TPU v7x, 128 devices: a whole 4x4x4 slice. The times are simulated.
128 devices in a mesh: row: 8 (over z_lo, x), col: 16 (over z_hi, y, core).
Axes of the slice: x: 4, y: 4, z: 4 (z_hi: 2, z_lo: 2; z = z_hi * 2 + z_lo), core: 2. Of those that a mesh axis runs over, the one named last changes fastest.
Arguments:
- amplitudes: float32 [2048, 8192], P('row', 'col'), may hold values from -6 to 6
- labels: int32 [16, 1], replicated, may hold values from 0 to 7, as said below
- integrals: float32 [8, 8192, 8192], P('row', None, 'col'), may hold values from -0.0625 to 0.0625
Outputs:
- residual: float32 [2048, 8192], P('row', 'col')
Inputs may be any that keep to these rules, and one draw needn't show every extreme that they name: No irreducible representation labels more than 4 tiles, and one labels exactly 4.
All inputs are finite; a program needn't handle non-finite values.
Results may differ from a plain program's by a relative error of at most 0.00007.
Values sent between devices are 32-bit elements; how exact they have to be, the bound alone decides.
No kernel may reach another device: no remote copies, remote signals or barrier semaphores. Data moves between devices by JAX's collectives and lax.ppermute only.
A program may use at most 128 MiB of HBM per device.

v0:
```python
import jax
import jax.numpy as jnp
from jax import lax
from jax.sharding import PartitionSpec as P

IRREPS = 8
TILE = 128


def on_device(amplitudes, labels, integrals):
    labels_flat = labels[:, 0]
    n_tiles = labels_flat.shape[0]
    cap_slots = max(2, n_tiles // 4)
    own_irreps = integrals.shape[0]
    local_tiles = amplitudes.shape[0] // TILE
    row_place = lax.axis_index("row")
    first_irrep = row_place * own_irreps
    one_hot = (labels_flat[:, None] == jnp.arange(IRREPS, dtype=jnp.int32)[None, :]).astype(
        jnp.int32
    )
    before = jnp.cumsum(one_hot, axis=0) - one_hot
    within_rank = jnp.sum(before * one_hot, axis=1)
    targets = first_irrep + jnp.arange(own_irreps, dtype=jnp.int32)
    slot_match = (labels_flat[None, None, :] == targets[:, None, None]) & (
        within_rank[None, None, :] == jnp.arange(cap_slots, dtype=jnp.int32)[None, :, None]
    )
    chosen = jnp.sum(
        jnp.where(slot_match, jnp.arange(n_tiles, dtype=jnp.int32)[None, None, :], 0), axis=2
    )
    slot_live = jnp.any(slot_match, axis=2)
    everything = lax.all_gather(amplitudes, "row", axis=0, tiled=True)
    row_tiles = everything.reshape(n_tiles, TILE, everything.shape[1])
    picked = jnp.take(row_tiles, chosen.reshape(-1), axis=0) * slot_live.reshape(-1)[
        :, None, None
    ].astype(jnp.float32)
    picked = picked.reshape(own_irreps, cap_slots * TILE, everything.shape[1])
    products = jnp.einsum(
        "gmk,gkn->gmn",
        lax.all_gather(picked, "col", axis=2, tiled=True),
        integrals,
        precision=lax.Precision.HIGHEST,
        preferred_element_type=jnp.float32,
    )
    my_tiles = row_place * local_tiles + jnp.arange(local_tiles, dtype=jnp.int32)
    my_labels = labels_flat[my_tiles]
    my_ranks = within_rank[my_tiles]
    collected = lax.all_gather(products, "row", axis=0, tiled=True)
    collected = collected.reshape(IRREPS * cap_slots, TILE, integrals.shape[2])
    residual = jnp.take(collected, my_labels * cap_slots + my_ranks, axis=0)
    residual = residual.reshape(local_tiles * TILE, integrals.shape[2])
    return residual


def solution(mesh):
    in_specs = (P("row", "col"), P(), P("row", None, "col"))
    out_specs = P("row", "col")
    return jax.shard_map(
        on_device, mesh=mesh, in_specs=in_specs, out_specs=out_specs, check_vma=False
    )
```

profile of v0, /device:TPU:0, one launch (start us, length us, event | category | flops | bytes accessed | tf_op | source)
XLA Modules:
  0.0 309.9 jit_solution(10101748702129379687)
XLA Ops:
  6.5 0.0 all-gather.5.cloned.1.call-start
  6.5 0.7 all-gather.5.cloned.1.call-update
  7.3 0.0 all-gather.7.cloned.1.call-start
  7.3 0.7 fusion.4
  8.1 0.8 select_reduce_fusion
  8.9 0.7 broadcast_compare_fusion
  9.6 0.1 fusion.6
  9.7 0.1 select_reduce_fusion.1
  9.9 0.1 broadcast_bitcast_fusion.1
  9.9 0.1 broadcast_bitcast_fusion
  10.0 54.2 %all-gather.5.cloned.1.call-done = f32[2048,512]{1,0:T(8,128)} async-done(((f32[256,512]{1,0:T(8,128)}), f32[2048,512]{1,0:T(8,128)}) %all-gather.5.cloned.1.call-update) | async-done | bytes 4194320 | tf_op jit(solution)/shard_map/all_gather | solution.py:31
  64.2 2.8 gather_fusion.2
  67.0 1.2 fusion.3
  68.2 0.0 all-gather.7.cloned.1.call-update
  68.2 0.0 copy-start
  68.2 0.0 all-gather.9.cloned.1.call-start
  68.3 109.2 %all-gather.7.cloned.1.call-done = f32[1,512,8192]{2,1,0:T(8,128)} async-done(((f32[1,512,512]{2,1,0:T(8,128)}), f32[1,512,8192]{2,1,0:T(8,128)}) %all-gather.7.cloned.1.call-update) | async-done | bytes 16777232 | tf_op jit(solution)/shard_map/all_gather | solution.py:39
  177.4 31.4 %fusion = f32[512,512]{1,0:T(8,128)} fusion(f32[1,8192,512]{2,1,0:T(8,128)} %param.5, f32[1,512,8192]{2,1,0:T(8,128)} %all-gather.7.cloned.1.call-done), kind=kOutput, calls=%fused_computation.4 | convolution fusion | flops 25769803776 | bytes 34603008 | tf_op jit(solution)/shard_map/gmk,gkn->gmn/dot_general | solution.py:37
  208.8 0.0 all-gather.9.cloned.1.call-update
  208.9 0.6 gather_fusion.1
  209.5 0.0 copy-done
  209.5 0.6 gather_fusion
  210.2 0.1 broadcast_bitcast_fusion.2
  210.3 88.2 %all-gather.9.cloned.1.call-done = f32[4096,512]{1,0:T(8,128)} async-done(((f32[512,512]{1,0:T(8,128)}), f32[4096,512]{1,0:T(8,128)}) %all-gather.9.cloned.1.call-update) | async-done | bytes 8388624 | tf_op jit(solution)/shard_map/all_gather | solution.py:47
  298.5 4.0 %gather_fusion.3 = f32[2,128,512]{2,1,0:T(8,128)S(1)} fusion(f32[32,128,512]{2,1,0:T(8,128)} %bitcast.38, s32[1024]{0:T(1024)S(1)} %pad_clamp_fusion), kind=kCustom, calls=%fused_computation.3 | custom fusion | bytes 1048584 | tf_op jit(solution)/shard_map/jit(_take)/gather | solution.py:49
  302.4 0.9 bitcast_select_fusion.1
  (10 shorter events, 0.1 us)
Async XLA Ops:
  6.5 57.7 %all-gather.5.cloned.1.call-start = ((), (), s32[]{:S(2)}) async-start(), calls=%async_computation | async-start | bytes 4718592 | tf_op jit(solution)/shard_map/all_gather | solution.py:31
  7.3 170.2 %all-gather.7.cloned.1.call-start = ((), (), s32[]{:S(2)}) async-start(), calls=%async_computation.1 | async-start | bytes 17825792 | tf_op jit(solution)/shard_map/all_gather | solution.py:39
  68.2 141.3 %copy-start = (s32[16,1]{0,1:T(1,128)S(1)}, s32[16,1]{0,1:T(1,128)}, u32[]{:S(2)}) copy-start(s32[16,1]{0,1:T(1,128)} %param.4) | copy-start | bytes 196
  68.2 230.2 %all-gather.9.cloned.1.call-start = ((), (), s32[]{:S(2)}) async-start(), calls=%async_computation.2 | async-start | bytes 9437184 | tf_op jit(solution)/shard_map/all_gather | solution.py:47
Sparse Core Ops, SparseCore 0:
  9.0 55.1 all-gather.4
  68.3 109.0 all-gather.6
  209.0 89.4 all-gather.8
where the time goes:
time: 311 us; the launch traced here: 310 us
  waiting for transfers between devices  252 us (81%)
  matrix products  31.4 us (10%)
  between operations  13.2 us (4%)
  local copies, waits for them, and re-layouts  8.26 us (3%)
  other arithmetic  4.67 us (2%)
    all_gather x1, waiting for transfers between devices, on_device(): lax.all_gather(picked, 'col', axis=2, tiled=True)  109 us
    all_gather x1, waiting for transfers between devices, on_device(): collected = lax.all_gather(products, 'row', axis=0, tiled=True)  88.2 us
    all_gather x1, waiting for transfers between devices, on_device(): everything = lax.all_gather(amplitudes, 'row', axis=0, tiled=True)  54.2 us
    dot_general x1, matrix products, on_device(): jnp.einsum('gmk,gkn->gmn', lax.all_gather(picked, 'col', axis=2, tiled=Tr...  31.4 us
  transfers between devices with their start and end apart: 3, of which 3 were waited for; matrix products, arithmetic and copies ran while one was open for 1% of the time, Pallas kernels for 0%

commit v1 on v0

v1 whole, which is shorter than its diff:
```python
import functools

import jax
import jax.numpy as jnp
import numpy as np
from jax import lax
from jax.experimental import pallas as pl
from jax.experimental.pallas import tpu as pltpu
from jax.sharding import PartitionSpec as P

TILE = 128
SLOTS = 4
CHUNKS = (64, 64)

ROWS = [(zl, x) for zl in range(2) for x in range(4)]
COLS = [(zh, y, c) for zh in range(2) for y in range(4) for c in range(2)]


def shift_x(a, dx):
    return lax.ppermute(a, "row", [(zl * 4 + x, zl * 4 + (x + dx) % 4) for zl, x in ROWS])


def flip_z(a):
    return lax.ppermute(a, "row", [(zl * 4 + x, (1 - zl) * 4 + x) for zl, x in ROWS])


def shift_y(a, dy):
    return lax.ppermute(
        a, "col", [(zh * 8 + y * 2 + c, zh * 8 + (y + dy) % 4 * 2 + c) for zh, y, c in COLS]
    )


def flip_core(a):
    return lax.ppermute(a, "col", [(i, i ^ 1) for i in range(16)])


def cross_z(a):
    pairs = [
        ((zl * 4 + x) * 16 + zh * 8 + i, ((1 - zl) * 4 + x) * 16 + (1 - zh) * 8 + i)
        for zl, x in ROWS
        for zh in range(2)
        for i in range(8)
    ]
    return lax.ppermute(a, ("row", "col"), pairs)


def split(v):
    hi = v.astype(jnp.bfloat16)
    return hi, (v - hi.astype(jnp.float32)).astype(jnp.bfloat16)


def product_kernel(n, first, at_ref, *refs):
    pieces, (own_ref, far_ref), refs = refs[:n], refs[n : n + 2], refs[n + 2 :]
    adds, (out_own, out_far) = refs[:2], refs[-2:]
    step = pl.program_id(0)

    for i, piece in enumerate(pieces):

        @pl.when(step == i)
        def _():
            a_hi, a_lo = split(piece[...])
            for j, (rhs, out) in enumerate(((own_ref, out_own), (far_ref, out_far))):
                b_hi, b_lo = split(rhs[...])
                dot = functools.partial(jnp.dot, preferred_element_type=jnp.float32)
                term = dot(a_hi, b_hi) + (dot(a_hi, b_lo) + dot(a_lo, b_hi))
                if i == 0:
                    out[...] = term if first else adds[j][...] + term
                else:
                    out[...] += term


def products(pieces, at, own, far, sums, after=()):
    n = len(pieces)
    m, width = pieces[0].shape
    cols = own.shape[1]
    whole = lambda shape: pl.BlockSpec(shape, lambda s, at: (0, 0))
    return pl.pallas_call(
        functools.partial(product_kernel, n, not sums),
        grid_spec=pltpu.PrefetchScalarGridSpec(
            num_scalar_prefetch=1,
            grid=(n,),
            in_specs=[whole((m, width))] * n
            + [
                pl.BlockSpec((width, cols), lambda s, at: (at[s], 0)),
                pl.BlockSpec((width, cols), lambda s, at: (at[s], 0)),
            ]
            + [whole((m, cols))] * len(sums)
            + [pl.BlockSpec(memory_space=pl.ANY)] * len(after),
            out_specs=[whole((m, cols))] * 2,
        ),
        out_shape=[jax.ShapeDtypeStruct((m, cols), jnp.float32)] * 2,
        compiler_params=pltpu.CompilerParams(vmem_limit_bytes=32 * 1024 * 1024),
        cost_estimate=pl.CostEstimate(
            flops=12 * n * m * width * cols,
            bytes_accessed=8 * n * width * cols + 4 * n * m * width,
            transcendentals=0,
        ),
        name="products",
    )(at, *pieces, own, far, *sums, *after)


def small_kernel(body, plan, shapes, operands, after=(), name=None):
    def kernel(plan_ref, *refs):
        body(plan_ref, refs[: len(operands)], refs[len(operands) + len(after) :])

    out = pl.pallas_call(
        kernel,
        in_specs=[pl.BlockSpec(memory_space=pltpu.SMEM)]
        + [pl.BlockSpec(memory_space=pltpu.VMEM)] * len(operands)
        + [pl.BlockSpec(memory_space=pl.ANY)] * len(after),
        out_specs=[pl.BlockSpec(memory_space=pltpu.VMEM)] * len(shapes),
        out_shape=[jax.ShapeDtypeStruct(s, jnp.float32) for s in shapes],
        compiler_params=pltpu.CompilerParams(vmem_limit_bytes=24 * 1024 * 1024),
        cost_estimate=pl.CostEstimate(
            flops=0, bytes_accessed=4 * sum(int(np.prod(s)) for s in shapes), transcendentals=0
        ),
        name=name,
    )(plan, *operands, *after)
    return out


def gather_rows(own):
    h = own.shape[1] // 2
    other = flip_z(own)
    below, above = shift_x(own, 1), shift_x(own, -1)
    below_o, above_o = shift_x(other, 1), shift_x(other, -1)
    far = [shift_x(below[:, :h], 1), shift_x(above[:, h:], -1)]
    far_o = [shift_x(below_o[:, :h], 1), shift_x(above_o[:, h:], -1)]
    return [[own], [other], [above], [above_o], far, far_o, [below], [below_o]]


def pick(plan, parts, after):
    m = parts[0][0].shape[1]
    width = parts[0][0].shape[2]
    flat_parts = [p for part in parts for p in part]

    def body(plan_ref, ins, outs):
        for s in range(2 * SLOTS):
            place = plan_ref[s]
            out, lo = outs[s // SLOTS], s % SLOTS * m
            k = 0
            for i, part in enumerate(parts):
                refs = ins[k : k + len(part)]
                k += len(part)

                @pl.when(place // 2 == i)
                def _():
                    at = lo
                    for ref in refs:
                        out[at : at + ref.shape[1]] = ref[place % 2]
                        at += ref.shape[1]

    return small_kernel(
        body, plan, [(SLOTS * m, width)] * 2, flat_parts, after, name="pick"
    )


def wait_for(values, *others):
    return lax.optimization_barrier((tuple(values), others))[0]


def cols_first(b, crossing):
    return shift_y(b, 1), shift_y(b, -1), cross_z(crossing)


def cols_second(below, above, bz):
    h = bz.shape[0] // 2
    far = shift_y(below[:h], 1), shift_y(above[h:], -1)
    return shift_y(bz, 1), shift_y(bz, -1), jnp.concatenate(far, axis=0)


def cols_third(below_z, above_z):
    h = below_z.shape[0] // 2
    return jnp.concatenate([shift_y(below_z[:h], 1), shift_y(above_z[h:], -1)], axis=0)


GROUPS = [[(0, 0), (0, 3), (0, 1), (1, 0)], [(0, 2), (1, 3), (1, 1)], [(1, 2)]]


def share(plan_ref, ex, product, lo, hi, out, at, arrived=None):
    for i in range(4):
        slot = plan_ref[2 * SLOTS + ex % 4 * 4 + i]

        @pl.when(slot >= 0)
        def _():
            out[i, at : at + hi - lo] = product[slot, lo:hi]

        @pl.when(slot < 0)
        def _():
            if arrived is None:
                out[i, at : at + hi - lo] = jnp.zeros((hi - lo, product.shape[2]), jnp.float32)
            else:
                out[i, at : at + hi - lo] = arrived(i)


def return_far(plan, sums):
    m, cols = sums[0].shape[0] // SLOTS, sums[0].shape[1]
    h = m // 2

    def body(plan_ref, ins, outs):
        mine, theirs = ins
        product, lower, upper = outs
        for s in range(SLOTS):
            rows = slice(s * m, (s + 1) * m)
            product[s] = mine[rows] + theirs[rows]
        share(plan_ref, 2, product, 0, h, lower, 0)
        share(plan_ref, 2, product, h, m, upper, 0)

    product, lower, upper = small_kernel(
        body,
        plan,
        [(SLOTS, m, cols), (4, h, cols), (4, h, cols)],
        [sums[0], flip_core(sums[1])],
        name="return_far",
    )
    return product, shift_x(lower, 1), shift_x(upper, -1)


def return_near(plan, product, from_below, from_above):
    _, m, cols = product.shape
    h = m // 2

    def body(plan_ref, ins, outs):
        product, from_below, from_above = ins
        up, down = outs
        share(plan_ref, 1, product, 0, h, up, 0, lambda i: from_below[i])
        share(plan_ref, 1, product, h, m, up, h)
        share(plan_ref, -1, product, 0, h, down, 0)
        share(plan_ref, -1, product, h, m, down, h, lambda i: from_above[i])

    up, down = small_kernel(
        body, plan, [(4, m, cols)] * 2, [product, from_below, from_above], name="return_near"
    )
    return product, shift_x(up, 1), shift_x(down, -1)


def return_here(plan, product, from_below, from_above):
    _, m, cols = product.shape

    def body(plan_ref, ins, outs):
        product, from_below, from_above = ins
        (total,) = outs
        share(plan_ref, 0, product, 0, m, total, 0, lambda i: from_below[i] + from_above[i])

    (total,) = small_kernel(
        body, plan, [(4, m, cols)], [product, from_below, from_above], name="return_here"
    )
    return total, flip_z(total[2:])


def on_device(amplitudes, labels, integrals):
    flat = labels[:, 0]
    n_tiles = flat.shape[0]
    local_tiles = amplitudes.shape[0] // TILE
    width = amplitudes.shape[1]
    cols = integrals.shape[2]
    row = lax.axis_index("row")
    col = lax.axis_index("col")
    zl, x = row // 4, row % 4
    zh, y, core = col // 8, col // 2 % 4, col % 2

    ids = np.arange(n_tiles, dtype=np.int32)
    same = (flat[:, None] == flat[None, :]) & (ids[None, :] < ids[:, None])
    rank = jnp.sum(same.astype(jnp.int32), axis=1)
    place = (ids // 2 % 4 - x) % 4 * 4 + ((ids // 8) ^ zl) * 2 + ids % 2
    slot = np.arange(2 * SLOTS, dtype=np.int32)
    target = jnp.where(slot < SLOTS, row, (1 - zl) * 4 + x)
    hit = (flat[None, :] == target[:, None]) & (rank[None, :] == (slot % SLOTS)[:, None])
    wanted = jnp.sum(jnp.where(hit, place[None, :], 0), axis=1)
    held = jnp.where(flat == row, rank, -1)
    slots = jnp.sum(jnp.where(place[None, :] == ids[:, None], held[None, :], 0), axis=1)
    plan = jnp.concatenate([wanted, slots])

    tiles = amplitudes.reshape(local_tiles, TILE, width)
    starts = [sum(CHUNKS[:i]) for i in range(len(CHUNKS))]
    pieces = [tiles[:, s : s + m] for s, m in zip(starts, CHUNKS)]
    parts = gather_rows(pieces[0])

    own = integrals.reshape(16 * width, cols)
    far = flip_core(own)
    at = []
    for group in GROUPS:
        gz, gy = np.array(group, np.int32).T
        places = (zh ^ gz) * 4 + (y + gy) % 4
        at.append(places * 2 + core)

    def step(group, blocks, sums, after=()):
        return products(blocks, at[group], own, far, sums, after)

    out, last = [], None
    for k in range(len(CHUNKS)):
        b, crossing = pick(plan, parts, () if last is None else last["seen"])
        if k + 1 < len(CHUNKS):
            ahead = wait_for([pieces[k + 1]], parts[3][0])
            parts = gather_rows(ahead[0])
        below, above, bz = cols_first(b, crossing)
        if last is not None:
            sums = step(1, last["second"], last["sums"], (b,))
            sums = step(2, last["third"], sums)
            below, above, bz = wait_for([below, above, bz], sums[0])
        below_z, above_z, far_b = cols_second(below, above, bz)
        ready = []
        if last is not None:
            back = return_far(plan, sums)
            ready = [back[0]]
        sums = step(0, [b, below, above, bz], [])
        far_z = cols_third(*wait_for([below_z, above_z], sums[0], *ready))
        if last is not None:
            out.append(return_here(plan, *return_near(plan, *back)))
        last = dict(
            seen=(below_z,), second=[far_b, below_z, above_z], third=[far_z], sums=sums
        )
    sums = step(1, last["second"], last["sums"], [t for t, _ in out[-1:]])
    sums = step(2, last["third"], sums)
    out.append(return_here(plan, *return_near(plan, *return_far(plan, sums))))
    out = [total[:2] + more for total, more in out]
    return jnp.concatenate(out, axis=1).reshape(local_tiles * TILE, cols)


def solution(mesh):
    in_specs = (P("row", "col"), P(), P("row", None, "col"))
    out_specs = P("row", "col")
    return jax.shard_map(
        on_device, mesh=mesh, in_specs=in_specs, out_specs=out_specs, check_vma=False
    )
```

time: 311 us -> 202 us (0.65)
  waiting for transfers between devices: 252 us -> 60 us
  starting transfers between devices: 0.08 us -> 68.8 us
  Pallas kernels: 0 us -> 34.8 us
  matrix products: 31.4 us -> 0 us
  local copies, waits for them, and re-layouts: 8.26 us -> 30.9 us
  between operations: 13.2 us -> 0.54 us
    all_gather x3 -> x0, waiting for transfers between devices: 252 us -> none  [the longest x1 109 us: on_device(): lax.all_gather(picked, 'col', axis=2, tiled=True)]
    ppermute x0 -> x49, starting transfers between devices: none -> 68.8 us  [the longest x24 36.2 us: shift_x(): lax.ppermute(a, 'row', [(zl * 4 + x, zl * 4 + (x + dx) % 4) for zl, x in...]
    ppermute x0 -> x49, waiting for transfers between devices: none -> 60 us  [the longest x24 35.7 us: shift_x(): lax.ppermute(a, 'row', [(zl * 4 + x, zl * 4 + (x + dx) % 4) for zl, x in...]
    pallas_call x0 -> x14, Pallas kernels: none -> 34.8 us  [the longest x6 27.6 us: products(): pl.pallas_call(functools.partial(product_kernel, n, not sums), grid_spec=...]
    dot_general x1 -> x0, matrix products: 31.4 us -> none  [on_device(): jnp.einsum('gmk,gkn->gmn', lax.all_gather(picked, 'col', axis=2, tiled=Tr...]
    unnamed x2 -> x14, local copies, waits for them, and re-layouts: 0.01 us -> 29.5 us
    gather x4 -> x0, local copies, waits for them, and re-layouts: 8.04 us -> none  [the longest x1 3.96 us: on_device(): residual = jnp.take(collected, my_labels * cap_slots + my_ranks, axis=0)]
  transfers between devices with their start and end apart: 3 -> 49, of which waited for: 3 -> 17; matrix products, arithmetic and copies ran while one was open for 1% -> 3% of each run, Pallas kernels for 0% -> 13%
where the time goes in v1:
time: 202 us; the launch traced here: 201 us
  starting transfers between devices  68.8 us (34%)
  waiting for transfers between devices  60 us (30%)
  Pallas kernels  34.8 us (17%)
  local copies, waits for them, and re-layouts  30.9 us (15%)
  other arithmetic  5.75 us (3%)
    ppermute x24, starting transfers between devices, shift_x(): lax.ppermute(a, 'row', [(zl * 4 + x, zl * 4 + (x + dx) % 4) for zl, x in...  36.2 us
    ppermute x24, waiting for transfers between devices, shift_x(): lax.ppermute(a, 'row', [(zl * 4 + x, zl * 4 + (x + dx) % 4) for zl, x in...  35.7 us
    unnamed x14, local copies, waits for them, and re-layouts  29.5 us
    pallas_call x6, Pallas kernels, products(): pl.pallas_call(functools.partial(product_kernel, n, not sums), grid_spec=...  27.6 us
    ppermute x16, starting transfers between devices, shift_y(): lax.ppermute(a, 'col', [(zh * 8 + y * 2 + c, zh * 8 + (y + dy) % 4 * 2 +...  24.5 us
    ppermute x16, waiting for transfers between devices, shift_y(): lax.ppermute(a, 'col', [(zh * 8 + y * 2 + c, zh * 8 + (y + dy) % 4 * 2 +...  12 us
    ppermute x4, waiting for transfers between devices, flip_z(): lax.ppermute(a, 'row', [(zl * 4 + x, (1 - zl) * 4 + x) for zl, x in ROWS])  8.62 us
    pallas_call x8, Pallas kernels, small_kernel(): pl.pallas_call(kernel, in_specs=[pl.BlockSpec(memory_space=pltpu.SMEM)] +...  7.23 us
  transfers between devices with their start and end apart: 49, of which 17 were waited for; matrix products, arithmetic and copies ran while one was open for 3% of the time, Pallas kernels for 13%

profile of v1, /device:TPU:0, one launch (start us, length us, event | category | flops | bytes accessed | tf_op | source)
XLA Modules:
  0.0 200.8 jit_solution(1141924682037371991)
XLA Ops:
  1.1 2.1 %collective-permute-start = (f32[2,64,512]{2,1,0:T(8,128)S(1)}, f32[2,64,512]{2,1,0:T(8,128)S(1)}, u32[]{:S(2)}, u32[]{:S(2)}) collective-permute-start(f32[2,64,512]{2,1,0:T(8,128)S(1)} %get-tuple-element.73.refs_0_), channel_id=1, source_target_pairs={{0,64},{16,80},{32,96},{48,112},{64,0},{80,16},{96,32},{112,48},{1... | collective-permute-start | bytes 786440 | tf_op jit(solution)/shard_map/ppermute | solution.py:24
  4.6 1.7 collective-permute-start.1
  8.0 2.1 %collective-permute-done.refs_1_ = f32[2,64,512]{2,1,0:T(8,128)S(1)} collective-permute-done((f32[2,64,512]{2,1,0:T(8,128)S(1)}, f32[2,64,512]{2,1,0:T(8,128)S(1)}, u32[]{:S(2)}, u32[]{:S(2)}) %collective-permute-start) | collective-permute-done | bytes 262176 | tf_op jit(solution)/shard_map/ppermute | solution.py:24
  10.1 2.8 %collective-permute-start.2 = (f32[2,64,512]{2,1,0:T(8,128)S(1)}, f32[2,64,512]{2,1,0:T(8,128)S(1)}, u32[]{:S(2)}, u32[]{:S(2)}) collective-permute-start(f32[2,64,512]{2,1,0:T(8,128)S(1)} %collective-permute-done.refs_1_), channel_id=1, source_target_pairs={{0,48},{16,0},{32,16},{48,32},{64,112},{80,64},{96,80},{112,96},{1... | collective-permute-start | bytes 786440 | tf_op jit(solution)/shard_map/ppermute | solution.py:20
  15.3 2.6 %collective-permute-start.5 = (f32[2,32,512]{2,1,0:T(8,128)S(1)}, f32[2,32,512]{2,1,0:T(8,128)S(1)}, u32[]{:S(2)}, u32[]{:S(2)}) collective-permute-start(f32[2,32,512]{2,1,0:T(8,128)S(1)} %slice.90), channel_id=1, source_target_pairs={{0,48},{16,0},{32,16},{48,32},{64,112},{80,64},{96,80},{112,96},{1... | collective-permute-start | bytes 393224 | tf_op jit(solution)/shard_map/ppermute | solution.py:20
  17.8 1.8 collective-permute-done.2.refs_3_
  19.6 3.8 %collective-permute-start.8 = (f32[2,32,512]{2,1,0:T(8,128)S(1)}, f32[2,32,512]{2,1,0:T(8,128)S(1)}, u32[]{:S(2)}, u32[]{:S(2)}) collective-permute-start(f32[2,32,512]{2,1,0:T(8,128)S(1)} %slice.92), channel_id=1, source_target_pairs={{0,48},{16,0},{32,16},{48,32},{64,112},{80,64},{96,80},{112,96},{1... | collective-permute-start | bytes 393224 | tf_op jit(solution)/shard_map/ppermute | solution.py:20
  24.7 1.6 collective-permute-start.19
  26.3 3.3 %collective-permute-done.7.refs_6_ = f32[2,32,512]{2,1,0:T(8,128)S(1)} collective-permute-done((f32[2,32,512]{2,1,0:T(8,128)S(1)}, f32[2,32,512]{2,1,0:T(8,128)S(1)}, u32[]{:S(2)}, u32[]{:S(2)}) %collective-permute-start.7) | collective-permute-done | bytes 131104 | tf_op jit(solution)/shard_map/ppermute | solution.py:20
  29.6 1.8 pick.2
  31.4 3.8 %collective-permute-start.9 = (f32[256,512]{1,0:T(8,128)S(1)}, f32[256,512]{1,0:T(8,128)}, u32[]{:S(2)}, u32[]{:S(2)}) collective-permute-start(f32[256,512]{1,0:T(8,128)S(1)} %get-tuple-element.39), channel_id=1, source_target_pairs={{0,72},{1,73},{2,74},{3,75},{4,76},{5,77},{6,78},{7,79},{8,64},{9,... | collective-permute-start | bytes 1572872 | tf_op jit(solution)/shard_map/ppermute | solution.py:44
  35.2 3.2 %collective-permute-start.20 = (f32[2,64,512]{2,1,0:T(8,128)S(1)}, f32[2,64,512]{2,1,0:T(8,128)S(1)}, u32[]{:S(2)}, u32[]{:S(2)}) collective-permute-start(f32[2,64,512]{2,1,0:T(8,128)S(1)} %get-tuple-element.45.refs_0_), channel_id=1, source_target_pairs={{0,48},{16,0},{32,16},{48,32},{64,112},{80,64},{96,80},{112,96},{1... | collective-permute-start | bytes 786440 | tf_op jit(solution)/shard_map/ppermute | solution.py:20
  38.5 5.0 %collective-permute-done.22.refs_8_ = f32[2,64,512]{2,1,0:T(8,128)S(1)} collective-permute-done((f32[2,64,512]{2,1,0:T(8,128)S(1)}, f32[2,64,512]{2,1,0:T(8,128)S(1)}, u32[]{:S(2)}, u32[]{:S(2)}) %collective-permute-start.22) | collective-permute-done | bytes 262176 | tf_op jit(solution)/shard_map/ppermute | solution.py:20
  44.1 1.6 collective-permute-start.12
  46.2 3.0 %collective-permute-start.13 = (f32[256,512]{1,0:T(8,128)}, f32[256,512]{1,0:T(8,128)S(1)}, u32[]{:S(2)}, u32[]{:S(2)}) collective-permute-start(f32[256,512]{1,0:T(8,128)} %get-tuple-element.40.refs_0_), channel_id=1, source_target_pairs={{0,6},{1,7},{2,0},{3,1},{4,2},{5,3},{6,4},{7,5},{8,14},{9,15},{10,... | collective-permute-start | bytes 1572872 | tf_op jit(solution)/shard_map/ppermute | solution.py:28
  49.8 3.0 %collective-permute-start.11 = (f32[256,512]{1,0:T(8,128)}, f32[256,512]{1,0:T(8,128)S(1)}, u32[]{:S(2)}, u32[]{:S(2)}) collective-permute-start(f32[256,512]{1,0:T(8,128)} %collective-permute-done.9.refs_3_), channel_id=1, source_target_pairs={{0,6},{1,7},{2,0},{3,1},{4,2},{5,3},{6,4},{7,5},{8,14},{9,15},{10,... | collective-permute-start | bytes 1572872 | tf_op jit(solution)/shard_map/ppermute | solution.py:28
  53.5 6.2 %collective-permute-done.12.refs_1_ = f32[256,512]{1,0:T(8,128)S(1)} collective-permute-done((f32[256,512]{1,0:T(8,128)}, f32[256,512]{1,0:T(8,128)S(1)}, u32[]{:S(2)}, u32[]{:S(2)}) %collective-permute-start.12) | collective-permute-done | bytes 524320 | tf_op jit(solution)/shard_map/ppermute | solution.py:28
  59.7 1.7 collective-permute-start.23
  62.2 1.6 collective-permute-start.24
  63.8 2.1 %collective-permute-done.23.refs_4_ = f32[2,32,512]{2,1,0:T(8,128)S(1)} collective-permute-done((f32[2,32,512]{2,1,0:T(8,128)S(1)}, f32[2,32,512]{2,1,0:T(8,128)S(1)}, u32[]{:S(2)}, u32[]{:S(2)}) %collective-permute-start.23) | collective-permute-done | bytes 131104 | tf_op jit(solution)/shard_map/ppermute | solution.py:20
  66.4 4.0 %collective-permute-start.27 = (f32[2,32,512]{2,1,0:T(8,128)S(1)}, f32[2,32,512]{2,1,0:T(8,128)S(1)}, u32[]{:S(2)}, u32[]{:S(2)}) collective-permute-start(f32[2,32,512]{2,1,0:T(8,128)S(1)} %slice.99), channel_id=1, source_target_pairs={{0,48},{16,0},{32,16},{48,32},{64,112},{80,64},{96,80},{112,96},{1... | collective-permute-start | bytes 393224 | tf_op jit(solution)/shard_map/ppermute | solution.py:20
  70.6 2.9 %collective-permute-start.18 = (f32[128,512]{1,0:T(8,128)S(1)}, f32[128,512]{1,0:T(8,128)S(1)}, u32[]{:S(2)}, u32[]{:S(2)}) collective-permute-start(f32[128,512]{1,0:T(8,128)S(1)} %slice.94), channel_id=1, source_target_pairs={{0,6},{1,7},{2,0},{3,1},{4,2},{5,3},{6,4},{7,5},{8,14},{9,15},{10,... | collective-permute-start | bytes 786440 | tf_op jit(solution)/shard_map/ppermute | solution.py:28
  73.6 5.8 %copy-done = f32[1,8192,512]{2,1,0:T(8,128)S(1)} copy-done((f32[1,8192,512]{2,1,0:T(8,128)S(1)}, f32[1,8192,512]{2,1,0:T(8,128)}, u32[]{:S(2)}) %copy-start) | copy-done | bytes 16777240
  79.3 6.5 %products.6 = (f32[256,512]{1,0:T(8,128)S(1)}, f32[256,512]{1,0:T(8,128)S(1)}) custom-call(s32[4]{0:T(128)S(1)} %fusion.11.at_ref, f32[256,512]{1,0:T(8,128)} %get-tuple-element.40.refs_0_, f32[256,512]{1,0:T(8,128)S(1)} %collective-permute-done.12.refs_1_, f32[256,512]{1,0:T(8,128)S(1)} %collective-permute-done.13.refs_2_, ...), custom_call_target="tpu_custom_call" | custom-call | flops 3221225472 | bytes 10485760 | tf_op jit(solution)/shard_map/products/pallas_call | solution.py:77
  86.0 3.2 %collective-permute-start.16 = (f32[128,512]{1,0:T(8,128)S(1)}, f32[128,512]{1,0:T(8,128)S(1)}, u32[]{:S(2)}, u32[]{:S(2)}) collective-permute-start(f32[128,512]{1,0:T(8,128)S(1)} %slice.72), channel_id=1, source_target_pairs={{0,6},{1,7},{2,0},{3,1},{4,2},{5,3},{6,4},{7,5},{8,14},{9,15},{10,... | collective-permute-start | bytes 786440 | tf_op jit(solution)/shard_map/ppermute | solution.py:28
  90.4 3.2 %collective-permute-start.35 = (f32[256,512]{1,0:T(8,128)S(1)}, f32[256,512]{1,0:T(8,128)S(1)}, u32[]{:S(2)}, u32[]{:S(2)}) collective-permute-start(f32[256,512]{1,0:T(8,128)S(1)} %get-tuple-element.46.refs_7_.refs_0_), channel_id=1, source_target_pairs={{0,6},{1,7},{2,0},{3,1},{4,2},{5,3},{6,4},{7,5},{8,14},{9,15},{10,... | collective-permute-start | bytes 1572872 | tf_op jit(solution)/shard_map/ppermute | solution.py:28
  93.9 5.8 %copy-done.1 = f32[1,8192,512]{2,1,0:T(8,128)S(1)} copy-done((f32[1,8192,512]{2,1,0:T(8,128)S(1)}, f32[1,8192,512]{2,1,0:T(8,128)}, u32[]{:S(2)}) %copy-start.1) | copy-done | bytes 16777240
  99.7 5.1 %products.7 = (f32[256,512]{1,0:T(8,128)S(1)}, f32[256,512]{1,0:T(8,128)S(1)}) custom-call(s32[3]{0:T(128)S(1)} %fusion.9.at_ref, f32[256,512]{1,0:T(8,128)S(1)} %pad_maximum_fusion.1.refs_0_, f32[256,512]{1,0:T(8,128)S(1)} %collective-permute-done.10.refs_10_.refs_1_, f32[256,512]{1,0:T(8,128)S(1)} %collective-permute-done.11.refs_2_, ...), custom_call_target="tpu_custom_call" | custom-call | flops 2415919104 | bytes 7864320 | tf_op jit(solution)/shard_map/products/pallas_call | solution.py:77
  104.9 5.8 %copy-done.2 = f32[1,8192,512]{2,1,0:T(8,128)S(1)} copy-done((f32[1,8192,512]{2,1,0:T(8,128)S(1)}, f32[1,8192,512]{2,1,0:T(8,128)}, u32[]{:S(2)}) %copy-start.2) | copy-done | bytes 16777240
  110.7 2.3 %products.8 = (f32[256,512]{1,0:T(8,128)S(1)}, f32[256,512]{1,0:T(8,128)S(1)}) custom-call(s32[1]{0:T(128)S(6)} %add.109.at_ref, f32[256,512]{1,0:T(8,128)S(1)} %pad_maximum_fusion.refs_0_, f32[8192,512]{1,0:T(8,128)S(1)} %bitcast.11, f32[8192,512]{1,0:T(8,128)} %collective-permute-done.14.refs_5_.refs_4_.refs_2_, f32[256,512]{1,0:T(8,128)S(1)} %get-tuple-element.47.refs_3_, ...), custom_call_target="tpu_custom_call" | custom-call | flops 805306368 | bytes 2621440 | tf_op jit(solution)/shard_map/products/pallas_call | solution.py:77
  113.2 1.8 collective-permute-done.28.refs_1_
  115.7 3.2 %collective-permute-start.30 = (f32[4,32,512]{2,1,0:T(8,128)S(1)}, f32[4,32,512]{2,1,0:T(8,128)S(1)}, u32[]{:S(2)}, u32[]{:S(2)}) collective-permute-start(f32[4,32,512]{2,1,0:T(8,128)S(1)} %get-tuple-element.53), channel_id=1, source_target_pairs={{0,48},{16,0},{32,16},{48,32},{64,112},{80,64},{96,80},{112,96},{1... | collective-permute-start | bytes 786440 | tf_op jit(solution)/shard_map/ppermute | solution.py:20
  121.1 4.2 %collective-permute-done.29.refs_1_ = f32[4,32,512]{2,1,0:T(8,128)S(1)} collective-permute-done((f32[4,32,512]{2,1,0:T(8,128)S(1)}, f32[4,32,512]{2,1,0:T(8,128)S(1)}, u32[]{:S(2)}, u32[]{:S(2)}) %collective-permute-start.29) | collective-permute-done | bytes 262176 | tf_op jit(solution)/shard_map/ppermute | solution.py:20
  125.3 1.5 collective-permute-start.42
  129.1 2.0 collective-permute-start.32
  131.1 5.8 %copy-done.3 = f32[1,8192,512]{2,1,0:T(8,128)S(1)} copy-done((f32[1,8192,512]{2,1,0:T(8,128)S(1)}, f32[1,8192,512]{2,1,0:T(8,128)}, u32[]{:S(2)}) %copy-start.3) | copy-done | bytes 16777240
  136.8 6.3 %products.9 = (f32[256,512]{1,0:T(8,128)S(1)}, f32[256,512]{1,0:T(8,128)S(1)}) custom-call(s32[4]{0:T(128)S(1)} %fusion.11.at_ref, f32[256,512]{1,0:T(8,128)S(1)} %get-tuple-element.46.refs_7_.refs_0_, f32[256,512]{1,0:T(8,128)S(1)} %collective-permute-done.34.refs_1_, f32[256,512]{1,0:T(8,128)S(1)} %collective-permute-done.35.refs_2_, ...), custom_call_target="tpu_custom_call" | custom-call | flops 3221225472 | bytes 10485760 | tf_op jit(solution)/shard_map/products/pallas_call | solution.py:77
  143.8 2.8 %collective-permute-start.40 = (f32[128,512]{1,0:T(8,128)S(1)}, f32[128,512]{1,0:T(8,128)S(1)}, u32[]{:S(2)}, u32[]{:S(2)}) collective-permute-start(f32[128,512]{1,0:T(8,128)S(1)} %slice.83), channel_id=1, source_target_pairs={{0,6},{1,7},{2,0},{3,1},{4,2},{5,3},{6,4},{7,5},{8,14},{9,15},{10,... | collective-permute-start | bytes 786440 | tf_op jit(solution)/shard_map/ppermute | solution.py:28
  146.6 4.6 %collective-permute-done.39 = f32[128,512]{1,0:T(8,128)S(1)} collective-permute-done((f32[128,512]{1,0:T(8,128)S(1)}, f32[128,512]{1,0:T(8,128)S(1)}, u32[]{:S(2)}, u32[]{:S(2)}) %collective-permute-start.39) | collective-permute-done | bytes 262176 | tf_op jit(solution)/shard_map/ppermute | solution.py:28
  151.9 5.8 %copy-done.4 = f32[1,8192,512]{2,1,0:T(8,128)S(1)} copy-done((f32[1,8192,512]{2,1,0:T(8,128)S(1)}, f32[1,8192,512]{2,1,0:T(8,128)}, u32[]{:S(2)}) %copy-start.4) | copy-done | bytes 16777240
  157.6 5.1 %products.10 = (f32[256,512]{1,0:T(8,128)S(1)}, f32[256,512]{1,0:T(8,128)S(1)}) custom-call(s32[3]{0:T(128)S(1)} %fusion.9.at_ref, f32[256,512]{1,0:T(8,128)S(1)} %pad_maximum_fusion.3.refs_0_, f32[256,512]{1,0:T(8,128)S(1)} %collective-permute-done.37.refs_1_, f32[256,512]{1,0:T(8,128)S(1)} %collective-permute-done.38.refs_2_, f32[8192,512]{1,0:T(8,128)S(1)} %bitcast.13, ...), custom_call_target="tpu_custom_call" | custom-call | flops 2415919104 | bytes 7864320 | tf_op jit(solution)/shard_map/products/pallas_call | solution.py:77
  162.8 2.3 %products.11 = (f32[256,512]{1,0:T(8,128)S(1)}, f32[256,512]{1,0:T(8,128)S(1)}) custom-call(s32[1]{0:T(128)S(6)} %add.109.at_ref, f32[256,512]{1,0:T(8,128)S(1)} %pad_maximum_fusion.2.refs_0_, f32[8192,512]{1,0:T(8,128)S(1)} %bitcast.14, f32[8192,512]{1,0:T(8,128)} %collective-permute-done.14.refs_5_.refs_4_.refs_2_, ...), custom_call_target="tpu_custom_call" | custom-call | flops 805306368 | bytes 2621440 | tf_op jit(solution)/shard_map/products/pallas_call | solution.py:77
  165.2 1.9 collective-permute-done.43.refs_1_
  168.3 2.8 %collective-permute-start.45 = (f32[4,32,512]{2,1,0:T(8,128)S(1)}, f32[4,32,512]{2,1,0:T(8,128)S(1)}, u32[]{:S(2)}, u32[]{:S(2)}) collective-permute-start(f32[4,32,512]{2,1,0:T(8,128)S(1)} %get-tuple-element.70), channel_id=1, source_target_pairs={{0,48},{16,0},{32,16},{48,32},{64,112},{80,64},{96,80},{112,96},{1... | collective-permute-start | bytes 786440 | tf_op jit(solution)/shard_map/ppermute | solution.py:20
  171.1 6.3 %collective-permute-done.44.refs_1_ = f32[4,32,512]{2,1,0:T(8,128)S(1)} collective-permute-done((f32[4,32,512]{2,1,0:T(8,128)S(1)}, f32[4,32,512]{2,1,0:T(8,128)S(1)}, u32[]{:S(2)}, u32[]{:S(2)}) %collective-permute-start.44) | collective-permute-done | bytes 262176 | tf_op jit(solution)/shard_map/ppermute | solution.py:20
  178.3 3.2 %collective-permute-start.47 = (f32[4,64,512]{2,1,0:T(8,128)S(1)}, f32[4,64,512]{2,1,0:T(8,128)S(1)}, u32[]{:S(2)}, u32[]{:S(2)}) collective-permute-start(f32[4,64,512]{2,1,0:T(8,128)S(1)} %get-tuple-element.72), channel_id=1, source_target_pairs={{0,48},{16,0},{32,16},{48,32},{64,112},{80,64},{96,80},{112,96},{1... | collective-permute-start | bytes 1572872 | tf_op jit(solution)/shard_map/ppermute | solution.py:20
  181.6 11.0 %collective-permute-done.46.refs_1_ = f32[4,64,512]{2,1,0:T(8,128)S(1)} collective-permute-done((f32[4,64,512]{2,1,0:T(8,128)S(1)}, f32[4,64,512]{2,1,0:T(8,128)S(1)}, u32[]{:S(2)}, u32[]{:S(2)}) %collective-permute-start.46) | collective-permute-done | bytes 524320 | tf_op jit(solution)/shard_map/ppermute | solution.py:20
  193.4 6.5 %collective-permute-done.48 = f32[2,64,512]{2,1,0:T(8,128)S(1)} collective-permute-done((f32[2,64,512]{2,1,0:T(8,128)S(1)}, f32[2,64,512]{2,1,0:T(8,128)S(1)}, u32[]{:S(2)}, u32[]{:S(2)}) %collective-permute-start.48) | collective-permute-done | bytes 262176 | tf_op jit(solution)/shard_map/ppermute | solution.py:24
  (112 shorter events, 24.1 us)
Async XLA Ops:
  0.0 70.6 %collective-permute-start.14 = (f32[8192,512]{1,0:T(8,128)}, f32[8192,512]{1,0:T(8,128)}, u32[]{:S(2)}, u32[]{:S(2)}) collective-permute-start(f32[8192,512]{1,0:T(8,128)} %bitcast.8), channel_id=1, source_target_pairs={{0,1},{1,0},{2,3},{3,2},{4,5},{5,4},{6,7},{7,6},{8,9},{9,8},{10,11... | collective-permute-start | bytes 50331656 | tf_op jit(solution)/shard_map/ppermute | solution.py:34
  1.1 9.1 %collective-permute-start = (f32[2,64,512]{2,1,0:T(8,128)S(1)}, f32[2,64,512]{2,1,0:T(8,128)S(1)}, u32[]{:S(2)}, u32[]{:S(2)}) collective-permute-start(f32[2,64,512]{2,1,0:T(8,128)S(1)} %get-tuple-element.73.refs_0_), channel_id=1, source_target_pairs={{0,64},{16,80},{32,96},{48,112},{64,0},{80,16},{96,32},{112,48},{1... | collective-permute-start | bytes 786440 | tf_op jit(solution)/shard_map/ppermute | solution.py:24
  3.2 11.3 %collective-permute-start.3 = (f32[2,64,512]{2,1,0:T(8,128)S(1)}, f32[2,64,512]{2,1,0:T(8,128)S(1)}, u32[]{:S(2)}, u32[]{:S(2)}) collective-permute-start(f32[2,64,512]{2,1,0:T(8,128)S(1)} %get-tuple-element.73.refs_0_), channel_id=1, source_target_pairs={{0,16},{16,32},{32,48},{48,0},{64,80},{80,96},{96,112},{112,64},{1... | collective-permute-start | bytes 786440 | tf_op jit(solution)/shard_map/ppermute | solution.py:20
  4.6 10.6 %collective-permute-start.1 = (f32[2,64,512]{2,1,0:T(8,128)S(1)}, f32[2,64,512]{2,1,0:T(8,128)S(1)}, u32[]{:S(2)}, u32[]{:S(2)}) collective-permute-start(f32[2,64,512]{2,1,0:T(8,128)S(1)} %get-tuple-element.73.refs_0_), channel_id=1, source_target_pairs={{0,48},{16,0},{32,16},{48,32},{64,112},{80,64},{96,80},{112,96},{1... | collective-permute-start | bytes 786440 | tf_op jit(solution)/shard_map/ppermute | solution.py:20
  10.1 9.5 %collective-permute-start.2 = (f32[2,64,512]{2,1,0:T(8,128)S(1)}, f32[2,64,512]{2,1,0:T(8,128)S(1)}, u32[]{:S(2)}, u32[]{:S(2)}) collective-permute-start(f32[2,64,512]{2,1,0:T(8,128)S(1)} %collective-permute-done.refs_1_), channel_id=1, source_target_pairs={{0,48},{16,0},{32,16},{48,32},{64,112},{80,64},{96,80},{112,96},{1... | collective-permute-start | bytes 786440 | tf_op jit(solution)/shard_map/ppermute | solution.py:20
  12.9 10.5 %collective-permute-start.6 = (f32[2,64,512]{2,1,0:T(8,128)S(1)}, f32[2,64,512]{2,1,0:T(8,128)S(1)}, u32[]{:S(2)}, u32[]{:S(2)}) collective-permute-start(f32[2,64,512]{2,1,0:T(8,128)S(1)} %collective-permute-done.refs_1_), channel_id=1, source_target_pairs={{0,16},{16,32},{32,48},{48,0},{64,80},{80,96},{96,112},{112,64},{1... | collective-permute-start | bytes 786440 | tf_op jit(solution)/shard_map/ppermute | solution.py:20
  14.4 10.2 %collective-permute-start.4 = (f32[2,32,512]{2,1,0:T(8,128)S(1)}, f32[2,32,512]{2,1,0:T(8,128)S(1)}, u32[]{:S(2)}, u32[]{:S(2)}) collective-permute-start(f32[2,32,512]{2,1,0:T(8,128)S(1)} %slice.89), channel_id=1, source_target_pairs={{0,16},{16,32},{32,48},{48,0},{64,80},{80,96},{96,112},{112,64},{1... | collective-permute-start | bytes 393224 | tf_op jit(solution)/shard_map/ppermute | solution.py:20
  15.3 11.0 %collective-permute-start.5 = (f32[2,32,512]{2,1,0:T(8,128)S(1)}, f32[2,32,512]{2,1,0:T(8,128)S(1)}, u32[]{:S(2)}, u32[]{:S(2)}) collective-permute-start(f32[2,32,512]{2,1,0:T(8,128)S(1)} %slice.90), channel_id=1, source_target_pairs={{0,48},{16,0},{32,16},{48,32},{64,112},{80,64},{96,80},{112,96},{1... | collective-permute-start | bytes 393224 | tf_op jit(solution)/shard_map/ppermute | solution.py:20
  19.6 6.7 %collective-permute-start.8 = (f32[2,32,512]{2,1,0:T(8,128)S(1)}, f32[2,32,512]{2,1,0:T(8,128)S(1)}, u32[]{:S(2)}, u32[]{:S(2)}) collective-permute-start(f32[2,32,512]{2,1,0:T(8,128)S(1)} %slice.92), channel_id=1, source_target_pairs={{0,48},{16,0},{32,16},{48,32},{64,112},{80,64},{96,80},{112,96},{1... | collective-permute-start | bytes 393224 | tf_op jit(solution)/shard_map/ppermute | solution.py:20
  23.4 6.2 %collective-permute-start.7 = (f32[2,32,512]{2,1,0:T(8,128)S(1)}, f32[2,32,512]{2,1,0:T(8,128)S(1)}, u32[]{:S(2)}, u32[]{:S(2)}) collective-permute-start(f32[2,32,512]{2,1,0:T(8,128)S(1)} %slice.91), channel_id=1, source_target_pairs={{0,16},{16,32},{32,48},{48,0},{64,80},{80,96},{96,112},{112,64},{1... | collective-permute-start | bytes 393224 | tf_op jit(solution)/shard_map/ppermute | solution.py:20
  24.7 13.8 %collective-permute-start.19 = (f32[2,64,512]{2,1,0:T(8,128)S(1)}, f32[2,64,512]{2,1,0:T(8,128)S(1)}, u32[]{:S(2)}, u32[]{:S(2)}) collective-permute-start(f32[2,64,512]{2,1,0:T(8,128)S(1)} %get-tuple-element.45.refs_0_), channel_id=1, source_target_pairs={{0,64},{16,80},{32,96},{48,112},{64,0},{80,16},{96,32},{112,48},{1... | collective-permute-start | bytes 786440 | tf_op jit(solution)/shard_map/ppermute | solution.py:24
  31.4 17.8 %collective-permute-start.9 = (f32[256,512]{1,0:T(8,128)S(1)}, f32[256,512]{1,0:T(8,128)}, u32[]{:S(2)}, u32[]{:S(2)}) collective-permute-start(f32[256,512]{1,0:T(8,128)S(1)} %get-tuple-element.39), channel_id=1, source_target_pairs={{0,72},{1,73},{2,74},{3,75},{4,76},{5,77},{6,78},{7,79},{8,64},{9,... | collective-permute-start | bytes 1572872 | tf_op jit(solution)/shard_map/ppermute | solution.py:44
  35.2 8.2 %collective-permute-start.22 = (f32[2,64,512]{2,1,0:T(8,128)S(1)}, f32[2,64,512]{2,1,0:T(8,128)S(1)}, u32[]{:S(2)}, u32[]{:S(2)}) collective-permute-start(f32[2,64,512]{2,1,0:T(8,128)S(1)} %get-tuple-element.45.refs_0_), channel_id=1, source_target_pairs={{0,16},{16,32},{32,48},{48,0},{64,80},{80,96},{96,112},{112,64},{1... | collective-permute-start | bytes 786440 | tf_op jit(solution)/shard_map/ppermute | solution.py:20
  35.2 8.9 %collective-permute-start.20 = (f32[2,64,512]{2,1,0:T(8,128)S(1)}, f32[2,64,512]{2,1,0:T(8,128)S(1)}, u32[]{:S(2)}, u32[]{:S(2)}) collective-permute-start(f32[2,64,512]{2,1,0:T(8,128)S(1)} %get-tuple-element.45.refs_0_), channel_id=1, source_target_pairs={{0,48},{16,0},{32,16},{48,32},{64,112},{80,64},{96,80},{112,96},{1... | collective-permute-start | bytes 786440 | tf_op jit(solution)/shard_map/ppermute | solution.py:20
  38.4 7.8 %collective-permute-start.25 = (f32[2,64,512]{2,1,0:T(8,128)S(1)}, f32[2,64,512]{2,1,0:T(8,128)S(1)}, u32[]{:S(2)}, u32[]{:S(2)}) collective-permute-start(f32[2,64,512]{2,1,0:T(8,128)S(1)} %collective-permute-done.19.refs_1_), channel_id=1, source_target_pairs={{0,16},{16,32},{32,48},{48,0},{64,80},{80,96},{96,112},{112,64},{1... | collective-permute-start | bytes 786440 | tf_op jit(solution)/shard_map/ppermute | solution.py:20
  43.4 6.4 %collective-permute-start.21 = (f32[2,64,512]{2,1,0:T(8,128)S(1)}, f32[2,64,512]{2,1,0:T(8,128)S(1)}, u32[]{:S(2)}, u32[]{:S(2)}) collective-permute-start(f32[2,64,512]{2,1,0:T(8,128)S(1)} %collective-permute-done.19.refs_1_), channel_id=1, source_target_pairs={{0,48},{16,0},{32,16},{48,32},{64,112},{80,64},{96,80},{112,96},{1... | collective-permute-start | bytes 786440 | tf_op jit(solution)/shard_map/ppermute | solution.py:20
  44.1 15.5 %collective-permute-start.12 = (f32[256,512]{1,0:T(8,128)}, f32[256,512]{1,0:T(8,128)S(1)}, u32[]{:S(2)}, u32[]{:S(2)}) collective-permute-start(f32[256,512]{1,0:T(8,128)} %get-tuple-element.40.refs_0_), channel_id=1, source_target_pairs={{0,2},{1,3},{2,4},{3,5},{4,6},{5,7},{6,0},{7,1},{8,10},{9,11},{10,... | collective-permute-start | bytes 1572872 | tf_op jit(solution)/shard_map/ppermute | solution.py:28
  46.2 15.9 %collective-permute-start.13 = (f32[256,512]{1,0:T(8,128)}, f32[256,512]{1,0:T(8,128)S(1)}, u32[]{:S(2)}, u32[]{:S(2)}) collective-permute-start(f32[256,512]{1,0:T(8,128)} %get-tuple-element.40.refs_0_), channel_id=1, source_target_pairs={{0,6},{1,7},{2,0},{3,1},{4,2},{5,3},{6,4},{7,5},{8,14},{9,15},{10,... | collective-permute-start | bytes 1572872 | tf_op jit(solution)/shard_map/ppermute | solution.py:28
  49.2 17.1 %collective-permute-start.10 = (f32[256,512]{1,0:T(8,128)}, f32[256,512]{1,0:T(8,128)S(1)}, u32[]{:S(2)}, u32[]{:S(2)}) collective-permute-start(f32[256,512]{1,0:T(8,128)} %collective-permute-done.9.refs_3_), channel_id=1, source_target_pairs={{0,2},{1,3},{2,4},{3,5},{4,6},{5,7},{6,0},{7,1},{8,10},{9,11},{10,... | collective-permute-start | bytes 1572872 | tf_op jit(solution)/shard_map/ppermute | solution.py:28
  49.8 20.5 %collective-permute-start.11 = (f32[256,512]{1,0:T(8,128)}, f32[256,512]{1,0:T(8,128)S(1)}, u32[]{:S(2)}, u32[]{:S(2)}) collective-permute-start(f32[256,512]{1,0:T(8,128)} %collective-permute-done.9.refs_3_), channel_id=1, source_target_pairs={{0,6},{1,7},{2,0},{3,1},{4,2},{5,3},{6,4},{7,5},{8,14},{9,15},{10,... | collective-permute-start | bytes 1572872 | tf_op jit(solution)/shard_map/ppermute | solution.py:28
  59.7 6.2 %collective-permute-start.23 = (f32[2,32,512]{2,1,0:T(8,128)S(1)}, f32[2,32,512]{2,1,0:T(8,128)S(1)}, u32[]{:S(2)}, u32[]{:S(2)}) collective-permute-start(f32[2,32,512]{2,1,0:T(8,128)S(1)} %slice.96), channel_id=1, source_target_pairs={{0,16},{16,32},{32,48},{48,0},{64,80},{80,96},{96,112},{112,64},{1... | collective-permute-start | bytes 393224 | tf_op jit(solution)/shard_map/ppermute | solution.py:20
  62.2 27.1 %collective-permute-start.24 = (f32[2,32,512]{2,1,0:T(8,128)S(1)}, f32[2,32,512]{2,1,0:T(8,128)S(1)}, u32[]{:S(2)}, u32[]{:S(2)}) collective-permute-start(f32[2,32,512]{2,1,0:T(8,128)S(1)} %slice.97), channel_id=1, source_target_pairs={{0,48},{16,0},{32,16},{48,32},{64,112},{80,64},{96,80},{112,96},{1... | collective-permute-start | bytes 393224 | tf_op jit(solution)/shard_map/ppermute | solution.py:20
  65.8 23.5 %collective-permute-start.26 = (f32[2,32,512]{2,1,0:T(8,128)S(1)}, f32[2,32,512]{2,1,0:T(8,128)S(1)}, u32[]{:S(2)}, u32[]{:S(2)}) collective-permute-start(f32[2,32,512]{2,1,0:T(8,128)S(1)} %slice.98), channel_id=1, source_target_pairs={{0,16},{16,32},{32,48},{48,0},{64,80},{80,96},{96,112},{112,64},{1... | collective-permute-start | bytes 393224 | tf_op jit(solution)/shard_map/ppermute | solution.py:20
  66.4 22.9 %collective-permute-start.27 = (f32[2,32,512]{2,1,0:T(8,128)S(1)}, f32[2,32,512]{2,1,0:T(8,128)S(1)}, u32[]{:S(2)}, u32[]{:S(2)}) collective-permute-start(f32[2,32,512]{2,1,0:T(8,128)S(1)} %slice.99), channel_id=1, source_target_pairs={{0,48},{16,0},{32,16},{48,32},{64,112},{80,64},{96,80},{112,96},{1... | collective-permute-start | bytes 393224 | tf_op jit(solution)/shard_map/ppermute | solution.py:20
  70.3 15.6 %collective-permute-start.17 = (f32[128,512]{1,0:T(8,128)S(1)}, f32[128,512]{1,0:T(8,128)S(1)}, u32[]{:S(2)}, u32[]{:S(2)}) collective-permute-start(f32[128,512]{1,0:T(8,128)S(1)} %slice.93), channel_id=1, source_target_pairs={{0,2},{1,3},{2,4},{3,5},{4,6},{5,7},{6,0},{7,1},{8,10},{9,11},{10,... | collective-permute-start | bytes 786440 | tf_op jit(solution)/shard_map/ppermute | solution.py:28
  70.6 15.4 %collective-permute-start.18 = (f32[128,512]{1,0:T(8,128)S(1)}, f32[128,512]{1,0:T(8,128)S(1)}, u32[]{:S(2)}, u32[]{:S(2)}) collective-permute-start(f32[128,512]{1,0:T(8,128)S(1)} %slice.94), channel_id=1, source_target_pairs={{0,6},{1,7},{2,0},{3,1},{4,2},{5,3},{6,4},{7,5},{8,14},{9,15},{10,... | collective-permute-start | bytes 786440 | tf_op jit(solution)/shard_map/ppermute | solution.py:28
  85.9 18.9 %collective-permute-start.15 = (f32[128,512]{1,0:T(8,128)S(1)}, f32[128,512]{1,0:T(8,128)S(1)}, u32[]{:S(2)}, u32[]{:S(2)}) collective-permute-start(f32[128,512]{1,0:T(8,128)S(1)} %slice.71), channel_id=1, source_target_pairs={{0,2},{1,3},{2,4},{3,5},{4,6},{5,7},{6,0},{7,1},{8,10},{9,11},{10,... | collective-permute-start | bytes 786440 | tf_op jit(solution)/shard_map/ppermute | solution.py:28
  86.0 18.8 %collective-permute-start.16 = (f32[128,512]{1,0:T(8,128)S(1)}, f32[128,512]{1,0:T(8,128)S(1)}, u32[]{:S(2)}, u32[]{:S(2)}) collective-permute-start(f32[128,512]{1,0:T(8,128)S(1)} %slice.72), channel_id=1, source_target_pairs={{0,6},{1,7},{2,0},{3,1},{4,2},{5,3},{6,4},{7,5},{8,14},{9,15},{10,... | collective-permute-start | bytes 786440 | tf_op jit(solution)/shard_map/ppermute | solution.py:28
  90.4 22.7 %collective-permute-start.34 = (f32[256,512]{1,0:T(8,128)S(1)}, f32[256,512]{1,0:T(8,128)S(1)}, u32[]{:S(2)}, u32[]{:S(2)}) collective-permute-start(f32[256,512]{1,0:T(8,128)S(1)} %get-tuple-element.46.refs_7_.refs_0_), channel_id=1, source_target_pairs={{0,2},{1,3},{2,4},{3,5},{4,6},{5,7},{6,0},{7,1},{8,10},{9,11},{10,... | collective-permute-start | bytes 1572872 | tf_op jit(solution)/shard_map/ppermute | solution.py:28
  90.4 22.6 %collective-permute-start.35 = (f32[256,512]{1,0:T(8,128)S(1)}, f32[256,512]{1,0:T(8,128)S(1)}, u32[]{:S(2)}, u32[]{:S(2)}) collective-permute-start(f32[256,512]{1,0:T(8,128)S(1)} %get-tuple-element.46.refs_7_.refs_0_), channel_id=1, source_target_pairs={{0,6},{1,7},{2,0},{3,1},{4,2},{5,3},{6,4},{7,5},{8,14},{9,15},{10,... | collective-permute-start | bytes 1572872 | tf_op jit(solution)/shard_map/ppermute | solution.py:28
  93.7 19.4 %collective-permute-start.36 = (f32[256,512]{1,0:T(8,128)S(1)}, f32[256,512]{1,0:T(8,128)S(1)}, u32[]{:S(2)}, u32[]{:S(2)}) collective-permute-start(f32[256,512]{1,0:T(8,128)S(1)} %get-tuple-element.56), channel_id=1, source_target_pairs={{0,72},{1,73},{2,74},{3,75},{4,76},{5,77},{6,78},{7,79},{8,64},{9,... | collective-permute-start | bytes 1572872 | tf_op jit(solution)/shard_map/ppermute | solution.py:44
  112.9 2.0 collective-permute-start.28
  113.1 16.0 %collective-permute-start.37 = (f32[256,512]{1,0:T(8,128)S(1)}, f32[256,512]{1,0:T(8,128)S(1)}, u32[]{:S(2)}, u32[]{:S(2)}) collective-permute-start(f32[256,512]{1,0:T(8,128)S(1)} %collective-permute-done.36.refs_3_), channel_id=1, source_target_pairs={{0,2},{1,3},{2,4},{3,5},{4,6},{5,7},{6,0},{7,1},{8,10},{9,11},{10,... | collective-permute-start | bytes 1572872 | tf_op jit(solution)/shard_map/ppermute | solution.py:28
  115.6 9.6 %collective-permute-start.29 = (f32[4,32,512]{2,1,0:T(8,128)S(1)}, f32[4,32,512]{2,1,0:T(8,128)S(1)}, u32[]{:S(2)}, u32[]{:S(2)}) collective-permute-start(f32[4,32,512]{2,1,0:T(8,128)S(1)} %get-tuple-element.52), channel_id=1, source_target_pairs={{0,16},{16,32},{32,48},{48,0},{64,80},{80,96},{96,112},{112,64},{1... | collective-permute-start | bytes 786440 | tf_op jit(solution)/shard_map/ppermute | solution.py:20
  115.7 11.1 %collective-permute-start.30 = (f32[4,32,512]{2,1,0:T(8,128)S(1)}, f32[4,32,512]{2,1,0:T(8,128)S(1)}, u32[]{:S(2)}, u32[]{:S(2)}) collective-permute-start(f32[4,32,512]{2,1,0:T(8,128)S(1)} %get-tuple-element.53), channel_id=1, source_target_pairs={{0,48},{16,0},{32,16},{48,32},{64,112},{80,64},{96,80},{112,96},{1... | collective-permute-start | bytes 786440 | tf_op jit(solution)/shard_map/ppermute | solution.py:20
  118.9 24.2 %collective-permute-start.38 = (f32[256,512]{1,0:T(8,128)S(1)}, f32[256,512]{1,0:T(8,128)S(1)}, u32[]{:S(2)}, u32[]{:S(2)}) collective-permute-start(f32[256,512]{1,0:T(8,128)S(1)} %collective-permute-done.36.refs_3_), channel_id=1, source_target_pairs={{0,6},{1,7},{2,0},{3,1},{4,2},{5,3},{6,4},{7,5},{8,14},{9,15},{10,... | collective-permute-start | bytes 1572872 | tf_op jit(solution)/shard_map/ppermute | solution.py:28
  120.4 23.3 %collective-permute-start.41 = (f32[128,512]{1,0:T(8,128)S(1)}, f32[128,512]{1,0:T(8,128)S(1)}, u32[]{:S(2)}, u32[]{:S(2)}) collective-permute-start(f32[128,512]{1,0:T(8,128)S(1)} %slice.84), channel_id=1, source_target_pairs={{0,2},{1,3},{2,4},{3,5},{4,6},{5,7},{6,0},{7,1},{8,10},{9,11},{10,... | collective-permute-start | bytes 786440 | tf_op jit(solution)/shard_map/ppermute | solution.py:28
  125.3 21.3 %collective-permute-start.42 = (f32[128,512]{1,0:T(8,128)S(1)}, f32[128,512]{1,0:T(8,128)S(1)}, u32[]{:S(2)}, u32[]{:S(2)}) collective-permute-start(f32[128,512]{1,0:T(8,128)S(1)} %slice.85), channel_id=1, source_target_pairs={{0,6},{1,7},{2,0},{3,1},{4,2},{5,3},{6,4},{7,5},{8,14},{9,15},{10,... | collective-permute-start | bytes 786440 | tf_op jit(solution)/shard_map/ppermute | solution.py:28
  127.8 23.4 %collective-permute-start.31 = (f32[4,64,512]{2,1,0:T(8,128)S(1)}, f32[4,64,512]{2,1,0:T(8,128)S(1)}, u32[]{:S(2)}, u32[]{:S(2)}) collective-permute-start(f32[4,64,512]{2,1,0:T(8,128)S(1)} %get-tuple-element.54), channel_id=1, source_target_pairs={{0,16},{16,32},{32,48},{48,0},{64,80},{80,96},{96,112},{112,64},{1... | collective-permute-start | bytes 1572872 | tf_op jit(solution)/shard_map/ppermute | solution.py:20
  129.1 22.2 %collective-permute-start.32 = (f32[4,64,512]{2,1,0:T(8,128)S(1)}, f32[4,64,512]{2,1,0:T(8,128)S(1)}, u32[]{:S(2)}, u32[]{:S(2)}) collective-permute-start(f32[4,64,512]{2,1,0:T(8,128)S(1)} %get-tuple-element.55), channel_id=1, source_target_pairs={{0,48},{16,0},{32,16},{48,32},{64,112},{80,64},{96,80},{112,96},{1... | collective-permute-start | bytes 1572872 | tf_op jit(solution)/shard_map/ppermute | solution.py:20
  143.1 8.0 %collective-permute-start.39 = (f32[128,512]{1,0:T(8,128)S(1)}, f32[128,512]{1,0:T(8,128)S(1)}, u32[]{:S(2)}, u32[]{:S(2)}) collective-permute-start(f32[128,512]{1,0:T(8,128)S(1)} %slice.82), channel_id=1, source_target_pairs={{0,2},{1,3},{2,4},{3,5},{4,6},{5,7},{6,0},{7,1},{8,10},{9,11},{10,... | collective-permute-start | bytes 786440 | tf_op jit(solution)/shard_map/ppermute | solution.py:28
  143.8 7.4 %collective-permute-start.40 = (f32[128,512]{1,0:T(8,128)S(1)}, f32[128,512]{1,0:T(8,128)S(1)}, u32[]{:S(2)}, u32[]{:S(2)}) collective-permute-start(f32[128,512]{1,0:T(8,128)S(1)} %slice.83), channel_id=1, source_target_pairs={{0,6},{1,7},{2,0},{3,1},{4,2},{5,3},{6,4},{7,5},{8,14},{9,15},{10,... | collective-permute-start | bytes 786440 | tf_op jit(solution)/shard_map/ppermute | solution.py:28
  167.8 9.6 %collective-permute-start.44 = (f32[4,32,512]{2,1,0:T(8,128)S(1)}, f32[4,32,512]{2,1,0:T(8,128)S(1)}, u32[]{:S(2)}, u32[]{:S(2)}) collective-permute-start(f32[4,32,512]{2,1,0:T(8,128)S(1)} %get-tuple-element.69), channel_id=1, source_target_pairs={{0,16},{16,32},{32,48},{48,0},{64,80},{80,96},{96,112},{112,64},{1... | collective-permute-start | bytes 786440 | tf_op jit(solution)/shard_map/ppermute | solution.py:20
  168.3 9.1 %collective-permute-start.45 = (f32[4,32,512]{2,1,0:T(8,128)S(1)}, f32[4,32,512]{2,1,0:T(8,128)S(1)}, u32[]{:S(2)}, u32[]{:S(2)}) collective-permute-start(f32[4,32,512]{2,1,0:T(8,128)S(1)} %get-tuple-element.70), channel_id=1, source_target_pairs={{0,48},{16,0},{32,16},{48,32},{64,112},{80,64},{96,80},{112,96},{1... | collective-permute-start | bytes 786440 | tf_op jit(solution)/shard_map/ppermute | solution.py:20
  178.2 14.4 %collective-permute-start.46 = (f32[4,64,512]{2,1,0:T(8,128)S(1)}, f32[4,64,512]{2,1,0:T(8,128)S(1)}, u32[]{:S(2)}, u32[]{:S(2)}) collective-permute-start(f32[4,64,512]{2,1,0:T(8,128)S(1)} %get-tuple-element.71), channel_id=1, source_target_pairs={{0,16},{16,32},{32,48},{48,0},{64,80},{80,96},{96,112},{112,64},{1... | collective-permute-start | bytes 1572872 | tf_op jit(solution)/shard_map/ppermute | solution.py:20
  178.3 14.3 %collective-permute-start.47 = (f32[4,64,512]{2,1,0:T(8,128)S(1)}, f32[4,64,512]{2,1,0:T(8,128)S(1)}, u32[]{:S(2)}, u32[]{:S(2)}) collective-permute-start(f32[4,64,512]{2,1,0:T(8,128)S(1)} %get-tuple-element.72), channel_id=1, source_target_pairs={{0,48},{16,0},{32,16},{48,32},{64,112},{80,64},{96,80},{112,96},{1... | collective-permute-start | bytes 1572872 | tf_op jit(solution)/shard_map/ppermute | solution.py:20
  181.5 11.9 %collective-permute-start.33 = (f32[2,64,512]{2,1,0:T(8,128)S(1)}, f32[2,64,512]{2,1,0:T(8,128)S(1)}, u32[]{:S(2)}, u32[]{:S(2)}) collective-permute-start(f32[2,64,512]{2,1,0:T(8,128)S(1)} %slice.101), channel_id=1, source_target_pairs={{0,64},{16,80},{32,96},{48,112},{64,0},{80,16},{96,32},{112,48},{1... | collective-permute-start | bytes 786440 | tf_op jit(solution)/shard_map/ppermute | solution.py:24
  193.3 6.7 %collective-permute-start.48 = (f32[2,64,512]{2,1,0:T(8,128)S(1)}, f32[2,64,512]{2,1,0:T(8,128)S(1)}, u32[]{:S(2)}, u32[]{:S(2)}) collective-permute-start(f32[2,64,512]{2,1,0:T(8,128)S(1)} %slice.103), channel_id=1, source_target_pairs={{0,64},{16,80},{32,96},{48,112},{64,0},{80,16},{96,32},{112,48},{1... | collective-permute-start | bytes 786440 | tf_op jit(solution)/shard_map/ppermute | solution.py:24
  (8 other events, 57.1 us)

commit v2 on v1

v2 whole, which is shorter than its diff:
```python
import functools

import jax
import jax.numpy as jnp
import numpy as np
from jax import lax
from jax.experimental import pallas as pl
from jax.experimental.pallas import tpu as pltpu
from jax.sharding import PartitionSpec as P

TILE = 128
SLOTS = 4
CHUNKS = (64, 64)

PLACES = [
    (zl, x, zh, y, c)
    for zl in range(2)
    for x in range(4)
    for zh in range(2)
    for y in range(4)
    for c in range(2)
]


def send(a, to):
    index = {p: i for i, p in enumerate(PLACES)}
    return lax.ppermute(a, ("row", "col"), [(i, index[to(*p)]) for p, i in index.items()])


def other_of(i, ring):
    return (i + (1 if i % 2 == ring else 3)) % 4


def swap_x(a, ring):
    return send(a, lambda zl, x, zh, y, c: (zl, other_of(x, ring), zh, y, c))


def swap_y(a, ring):
    return send(a, lambda zl, x, zh, y, c: (zl, x, zh, other_of(y, ring), c))


def flip_z(a):
    return send(a, lambda zl, x, zh, y, c: (1 - zl, x, zh, y, c))


def cross_z(a):
    return send(a, lambda zl, x, zh, y, c: (1 - zl, x, 1 - zh, y, c))


def flip_core(a):
    return send(a, lambda zl, x, zh, y, c: (zl, x, zh, y, 1 - c))


def split(v):
    hi = v.astype(jnp.bfloat16)
    return hi, (v - hi.astype(jnp.float32)).astype(jnp.bfloat16)


def product_kernel(blocks, n_arrays, first, at_ref, *refs):
    arrays, (own_ref, far_ref), refs = refs[:n_arrays], refs[n_arrays : n_arrays + 2], refs[n_arrays + 2 :]
    adds, (out_own, out_far) = refs[:2], refs[-2:]
    step = pl.program_id(0)

    for i, block in enumerate(blocks):

        @pl.when(step == i)
        def _():
            parts = [arrays[array][lo : lo + size] for array, lo, size in block]
            a_hi, a_lo = split(parts[0] if len(parts) == 1 else jnp.concatenate(parts, axis=0))
            for j, (rhs, out) in enumerate(((own_ref, out_own), (far_ref, out_far))):
                b_hi, b_lo = split(rhs[...])
                dot = functools.partial(jnp.dot, preferred_element_type=jnp.float32)
                term = dot(a_hi, b_hi) + (dot(a_hi, b_lo) + dot(a_lo, b_hi))
                if i == 0:
                    out[...] = term if first else adds[j][...] + term
                else:
                    out[...] += term


def products(arrays, blocks, at, own, far, sums):
    n = len(blocks)
    m = sum(size for _, _, size in blocks[0])
    width = arrays[0].shape[1]
    cols = own.shape[1]
    whole = lambda shape: pl.BlockSpec(shape, lambda s, at: (0, 0))
    return pl.pallas_call(
        functools.partial(product_kernel, blocks, len(arrays), not sums),
        grid_spec=pltpu.PrefetchScalarGridSpec(
            num_scalar_prefetch=1,
            grid=(n,),
            in_specs=[whole(a.shape) for a in arrays]
            + [pl.BlockSpec((width, cols), lambda s, at: (at[s], 0))] * 2
            + [whole((m, cols))] * len(sums),
            out_specs=[whole((m, cols))] * 2,
        ),
        out_shape=[jax.ShapeDtypeStruct((m, cols), jnp.float32)] * 2,
        compiler_params=pltpu.CompilerParams(vmem_limit_bytes=50 * 1024 * 1024),
        cost_estimate=pl.CostEstimate(
            flops=12 * n * m * width * cols,
            bytes_accessed=8 * n * width * cols + 4 * n * m * width,
            transcendentals=0,
        ),
        name="products",
    )(at, *arrays, own, far, *sums)


def small_kernel(body, plan, shapes, operands, after=(), name=None):
    def kernel(plan_ref, *refs):
        body(plan_ref, refs[: len(operands)], refs[len(operands) + len(after) :])

    out = pl.pallas_call(
        kernel,
        in_specs=[pl.BlockSpec(memory_space=pltpu.SMEM)]
        + [pl.BlockSpec(memory_space=pltpu.VMEM)] * len(operands)
        + [pl.BlockSpec(memory_space=pl.ANY)] * len(after),
        out_specs=[pl.BlockSpec(memory_space=pltpu.VMEM)] * len(shapes),
        out_shape=[jax.ShapeDtypeStruct(s, jnp.float32) for s in shapes],
        compiler_params=pltpu.CompilerParams(vmem_limit_bytes=24 * 1024 * 1024),
        cost_estimate=pl.CostEstimate(
            flops=0, bytes_accessed=4 * sum(int(np.prod(s)) for s in shapes), transcendentals=0
        ),
        name=name,
    )(plan, *operands, *after)
    return out


def wait_for(value, *others):
    return lax.optimization_barrier((value, others))[0]


def gather_second(near, other, swap, pieces=1):
    return swap(join(other, half(near[1], 0, pieces)), 0), swap(join(other, half(near[0], 1, pieces)), 1)


def gather_third(both, rows, swap, pieces=1):
    return swap(half(both[1][:rows], 0, pieces), 0), swap(half(both[0][:rows], 1, pieces), 1)


def join(*arrays):
    return jnp.concatenate(arrays, axis=0)


def half(a, which, pieces):
    cut = a.reshape(pieces, 2, -1, a.shape[1])[:, which]
    return cut.reshape(-1, a.shape[1])


def pick(plan, m, arrays, after):
    width = arrays[0].shape[1]
    h = m // 2
    where = [
        [(0, 0, m)],
        [(1, 0, m)],
        [(2, 0, m)],
        [(4, 0, m)],
        [(4, 2 * m, h), (5, 2 * m, h)],
        [(6, 0, h), (7, 0, h)],
        [(3, 0, m)],
        [(5, 0, m)],
    ]

    def body(plan_ref, ins, outs):
        for s in range(2 * SLOTS):
            place = plan_ref[s]
            out, to = outs[s // SLOTS], s % SLOTS * m
            for i, parts in enumerate(where):

                @pl.when(place // 2 == i)
                def _():
                    at = to
                    for array, lo, size in parts:
                        rows = pl.ds(pl.multiple_of(lo + place % 2 * size, 8), size)
                        out[at : at + size] = ins[array][rows]
                        at += size

    return small_kernel(body, plan, [(SLOTS * m, width)] * 2, arrays, after, name="pick")


GROUPS = [[(0, 0), (0, 1), (0, 3), (1, 0)], [(1, 1), (1, 3), (0, 2)], [(1, 2)]]


def share(plan_ref, ring, dz, product, lo, hi, out, at, pitch, arrived=None):
    for j in range(2):
        slot = plan_ref[2 * SLOTS + ring * 4 + dz * 2 + j]
        rows = pl.ds(at + j * pitch, hi - lo)

        @pl.when(slot >= 0)
        def _():
            out[rows] = product[slot, lo:hi]

        @pl.when(slot < 0)
        def _():
            if arrived is None:
                out[rows] = jnp.zeros((hi - lo, product.shape[2]), jnp.float32)
            else:
                out[rows] = arrived(j)


def return_first(plan, sums, swapped):
    m, cols = sums[0].shape[0] // SLOTS, sums[0].shape[1]
    h = m // 2

    def body(plan_ref, ins, outs):
        mine, theirs = ins
        product, out_a, out_b = outs
        for s in range(SLOTS):
            rows = slice(s * m, (s + 1) * m)
            product[s] = mine[rows] + theirs[rows]
        share(plan_ref, 2, 1, product, 0, h, out_a, 0, h)
        share(plan_ref, 2, 1, product, h, m, out_b, 0, h)

    shapes = [(SLOTS, m, cols), (m, cols), (m, cols)]
    product, a, b = small_kernel(body, plan, shapes, [sums[0], swapped], name="return_first")
    return product, [swap_x(a, 0), swap_x(b, 1)]


def near_shares(plan_ref, dz, product, out_a, out_b, from_a, from_b):
    m = product.shape[1]
    h = m // 2
    share(plan_ref, 1, dz, product, 0, h, out_a, 0, m)
    share(plan_ref, 1, dz, product, h, m, out_a, h, m, from_b)
    share(plan_ref, 3, dz, product, 0, h, out_b, 0, m, from_a)
    share(plan_ref, 3, dz, product, h, m, out_b, h, m)


def return_second(plan, product, came):
    _, m, cols = product.shape
    h = m // 2

    def body(plan_ref, ins, outs):
        product, a, b = ins
        out_a, out_b = outs
        part = lambda ref: lambda j: ref[j * h : (j + 1) * h]
        near_shares(plan_ref, 1, product, out_a, out_b, part(a), part(b))
        share(plan_ref, 2, 0, product, 0, h, out_a, 2 * m, h)
        share(plan_ref, 2, 0, product, h, m, out_b, 2 * m, h)

    a, b = small_kernel(
        body, plan, [(3 * m, cols)] * 2, [product, *came], name="return_second"
    )
    return [swap_x(a, 0), swap_x(b, 1)]


def return_third(plan, product, came):
    _, m, cols = product.shape
    h = m // 2

    def body(plan_ref, ins, outs):
        product, a, b = ins
        out_a, out_b, across = outs
        part = lambda ref: lambda j: ref[2 * m + j * h : 2 * m + (j + 1) * h]
        near_shares(plan_ref, 0, product, out_a, out_b, part(a), part(b))
        both = lambda j: a[j * m : (j + 1) * m] + b[j * m : (j + 1) * m]
        share(plan_ref, 0, 1, product, 0, m, across, 0, m, both)

    a, b, across = small_kernel(
        body, plan, [(2 * m, cols)] * 3, [product, *came], name="return_third"
    )
    return [swap_x(a, 0), swap_x(b, 1), flip_z(across)]


def return_last(plan, product, came):
    _, m, cols = product.shape

    def body(plan_ref, ins, outs):
        product, *came = ins
        (total,) = outs
        rows = lambda j: slice(j * m, (j + 1) * m)
        arrived = lambda j: came[0][rows(j)] + came[1][rows(j)] + came[2][rows(j)]
        share(plan_ref, 0, 0, product, 0, m, total, 0, m, arrived)

    (total,) = small_kernel(body, plan, [(2 * m, cols)], [product, *came], name="return_last")
    return total


def on_device(amplitudes, labels, integrals):
    flat = labels[:, 0]
    n_tiles = flat.shape[0]
    local_tiles = amplitudes.shape[0] // TILE
    width = amplitudes.shape[1]
    cols = integrals.shape[2]
    row = lax.axis_index("row")
    col = lax.axis_index("col")
    zl, x = row // 4, row % 4
    zh, y, core = col // 8, col // 2 % 4, col % 2

    ids = np.arange(n_tiles, dtype=np.int32)
    same = (flat[:, None] == flat[None, :]) & (ids[None, :] < ids[:, None])
    rank = jnp.sum(same.astype(jnp.int32), axis=1)
    ring = (ids // 2 % 4 - x) * (1 - 2 * (x % 2)) % 4
    place = ring * 4 + ((ids // 8) ^ zl) * 2 + ids % 2
    slot = np.arange(2 * SLOTS, dtype=np.int32)
    target = jnp.where(slot < SLOTS, row, (1 - zl) * 4 + x)
    hit = (flat[None, :] == target[:, None]) & (rank[None, :] == (slot % SLOTS)[:, None])
    wanted = jnp.sum(jnp.where(hit, place[None, :], 0), axis=1)
    held = jnp.where(flat == row, rank, -1)
    slots = jnp.sum(jnp.where(place[None, :] == ids[:, None], held[None, :], 0), axis=1)
    plan = jnp.concatenate([wanted, slots])

    tiles = amplitudes.reshape(local_tiles, TILE, width)
    starts = [sum(CHUNKS[:i]) for i in range(len(CHUNKS))]
    pieces = [tiles[:, s : s + m].reshape(-1, width) for s, m in zip(starts, CHUNKS)]

    own = integrals.reshape(16 * width, cols)
    far = flip_core(own)
    at = []
    for group in GROUPS:
        gz, ring = np.array(group, np.int32).T
        places = (zh ^ gz) * 4 + (y + ring * (1 - 2 * (y % 2))) % 4
        at.append(places * 2 + core)

    def rows_first(piece):
        return [piece, flip_z(piece), swap_x(piece, 0), swap_x(piece, 1)]

    def rows_second(arrays):
        return arrays + list(gather_second(arrays[2:4], arrays[1], swap_x, local_tiles))

    def rows_third(arrays):
        rows = arrays[1].shape[0]
        return arrays + list(gather_third(arrays[4:6], rows, swap_x, local_tiles))

    def step(group, last):
        m, h = last["m"], last["m"] // 2
        if group == 0:
            arrays, blocks = last["first"], [[(i, 0, m)] for i in range(4)]
        elif group == 1:
            arrays, blocks = last["second"], [[(0, 0, m)], [(1, 0, m)], [(0, m, h), (1, m, h)]]
        else:
            arrays, blocks = last["third"], [[(0, 0, h), (1, 0, h)]]
        last["sums"] = products(arrays, blocks, at[group], own, far, last["sums"])
        return last["sums"]

    arrays = rows_third(rows_second(rows_first(pieces[0])))
    out, last = [], None
    for k, m in enumerate(CHUNKS):
        more = k + 1 < len(CHUNKS)
        after = () if last is None else (last["second"][0], last["sums"][0])
        b, crossing = pick(plan, m, arrays, after)
        this = dict(m=SLOTS * m, sums=[])
        if more:
            arrays = rows_first(wait_for(pieces[k + 1], b))
        near = [swap_y(b, 0), swap_y(b, 1)]
        bz = cross_z(crossing)
        this["first"] = [b, *near, bz]
        ready = arrays if more else []
        if last is not None:
            step(1, last)
            sums = step(2, last)
            swapped = flip_core(sums[1])
            ready = [*ready, sums[0]]
        near, bz = wait_for((near, bz), *ready)
        this["second"] = gather_second(near, bz, swap_y)
        if more:
            arrays = rows_second(wait_for(arrays, near[0]))
        ready = arrays[4:6] if more else []
        if last is not None:
            product, came = return_first(plan, sums, swapped)
        step(0, this)
        if last is not None:
            came = return_second(plan, product, came)
            ready = [*ready, product]
        both = wait_for(this["second"], this["sums"][0], *ready)
        this["third"] = gather_third(both, SLOTS * m, swap_y)
        if more:
            arrays = rows_third(arrays)
        if last is not None:
            came = return_third(plan, product, came)
            out.append(return_last(plan, product, came))
        last = this
    last["sums"] = wait_for(last["sums"], *out)
    step(1, last)
    sums = step(2, last)
    product, came = return_first(plan, sums, flip_core(sums[1]))
    came = return_third(plan, product, return_second(plan, product, came))
    out.append(return_last(plan, product, came))
    out = [o.reshape(local_tiles, -1, cols) for o in out]
    return jnp.concatenate(out, axis=1).reshape(local_tiles * TILE, cols)


def solution(mesh):
    in_specs = (P("row", "col"), P(), P("row", None, "col"))
    out_specs = P("row", "col")
    return jax.shard_map(
        on_device, mesh=mesh, in_specs=in_specs, out_specs=out_specs, check_vma=False
    )
```

time: 202 us -> 176 us (0.87)
  local copies, waits for them, and re-layouts: 30.9 us -> 8 us
  starting transfers between devices: 68.8 us -> 52.1 us
  waiting for transfers between devices: 60 us -> 66.9 us
  Pallas kernels: 34.8 us -> 39.9 us
    unnamed x14 -> x32, local copies, waits for them, and re-layouts: 29.5 us -> 3.18 us
    ppermute x49 -> x45, starting transfers between devices: 68.8 us -> 52.1 us  [send(): lax.ppermute(a, ('row', 'col'), [(i, index[to(*p)]) for p, i in index.ite...]
    ppermute x49 -> x45, waiting for transfers between devices: 60 us -> 66.9 us  [send(): lax.ppermute(a, ('row', 'col'), [(i, index[to(*p)]) for p, i in index.ite...]
    pallas_call x6, Pallas kernels: 27.6 us -> 30.8 us  [products(): pl.pallas_call(functools.partial(product_kernel, blocks, len(arrays), not...]
    concatenate x4, other arithmetic: 0.14 us -> 2.66 us  [join(): return jnp.concatenate(arrays, axis=0)]
    another operation x0 -> x8, local copies, waits for them, and re-layouts: none -> 2.51 us  [half(): return cut.reshape(-1, a.shape[1])]
    pallas_call x8 -> x10, Pallas kernels: 7.23 us -> 9.1 us  [small_kernel(): pl.pallas_call(kernel, in_specs=[pl.BlockSpec(memory_space=pltpu.SMEM)] +...]
  transfers between devices with their start and end apart: 49 -> 45, of which waited for: 17 -> 25; matrix products, arithmetic and copies ran while one was open for 3% -> 7% of each run, Pallas kernels for 13% -> 20%
where the time goes in v2:
time: 176 us; the launch traced here: 175 us
  waiting for transfers between devices  66.9 us (38%)
  starting transfers between devices  52.1 us (30%)
  Pallas kernels  39.9 us (23%)
  local copies, waits for them, and re-layouts  8 us (5%)
  other arithmetic  7.53 us (4%)
    ppermute x45, waiting for transfers between devices, send(): lax.ppermute(a, ('row', 'col'), [(i, index[to(*p)]) for p, i in index.ite...  66.9 us
    ppermute x45, starting transfers between devices, send(): lax.ppermute(a, ('row', 'col'), [(i, index[to(*p)]) for p, i in index.ite...  52.1 us
    pallas_call x6, Pallas kernels, products(): pl.pallas_call(functools.partial(product_kernel, blocks, len(arrays), not...  30.8 us
    pallas_call x10, Pallas kernels, small_kernel(): pl.pallas_call(kernel, in_specs=[pl.BlockSpec(memory_space=pltpu.SMEM)] +...  9.1 us
  transfers between devices with their start and end apart: 45, of which 25 were waited for; matrix products, arithmetic and copies ran while one was open for 7% of the time, Pallas kernels for 20%

profile of v2, /device:TPU:0, one launch (start us, length us, event | category | flops | bytes accessed | tf_op | source)
XLA Modules:
  0.0 175.0 jit_solution(8248581458302229328)
XLA Ops:
  1.1 2.9 %collective-permute-start.2 = (f32[128,512]{1,0:T(8,128)S(1)}, f32[128,512]{1,0:T(8,128)S(1)}, u32[]{:S(2)}, u32[]{:S(2)}) collective-permute-start(f32[128,512]{1,0:T(8,128)S(1)} %bitcast.75), channel_id=1, source_target_pairs={{0,48},{1,49},{2,50},{3,51},{4,52},{5,53},{6,54},{7,55},{8,56},{9,... | collective-permute-start | bytes 786440 | tf_op jit(solution)/shard_map/ppermute | solution.py:27
  4.2 1.9 %collective-permute-start = (f32[128,512]{1,0:T(8,128)S(1)}, f32[128,512]{1,0:T(8,128)S(1)}, u32[]{:S(2)}, u32[]{:S(2)}) collective-permute-start(f32[128,512]{1,0:T(8,128)S(1)} %bitcast.77), channel_id=1, source_target_pairs={{0,64},{1,65},{2,66},{3,67},{4,68},{5,69},{6,70},{7,71},{8,72},{9,... | collective-permute-start | bytes 786440 | tf_op jit(solution)/shard_map/ppermute | solution.py:27
  6.8 4.3 %collective-permute-done.2.refs_3_ = f32[128,512]{1,0:T(8,128)S(1)} collective-permute-done((f32[128,512]{1,0:T(8,128)S(1)}, f32[128,512]{1,0:T(8,128)S(1)}, u32[]{:S(2)}, u32[]{:S(2)}) %collective-permute-start.2) | collective-permute-done | bytes 262176 | tf_op jit(solution)/shard_map/ppermute | solution.py:27
  11.1 1.3 collective-permute-done.1.refs_2_
  12.7 1.4 collective-permute-start.4
  17.1 7.2 %collective-permute-done.4.refs_5_ = f32[192,512]{1,0:T(8,128)S(1)} collective-permute-done((f32[192,512]{1,0:T(8,128)S(1)}, f32[192,512]{1,0:T(8,128)S(1)}, u32[]{:S(2)}, u32[]{:S(2)}) %collective-permute-start.4) | collective-permute-done | bytes 393248 | tf_op jit(solution)/shard_map/ppermute | solution.py:27
  25.0 1.4 collective-permute-start.6
  26.6 2.9 %collective-permute-done.5.refs_6_ = f32[64,512]{1,0:T(8,128)S(1)} collective-permute-done((f32[64,512]{1,0:T(8,128)S(1)}, f32[64,512]{1,0:T(8,128)S(1)}, u32[]{:S(2)}, u32[]{:S(2)}) %collective-permute-start.5) | collective-permute-done | bytes 131104 | tf_op jit(solution)/shard_map/ppermute | solution.py:27
  29.5 1.8 %collective-permute-done.6.refs_7_ = f32[64,512]{1,0:T(8,128)S(1)} collective-permute-done((f32[64,512]{1,0:T(8,128)S(1)}, f32[64,512]{1,0:T(8,128)S(1)}, u32[]{:S(2)}, u32[]{:S(2)}) %collective-permute-start.6) | collective-permute-done | bytes 131104 | tf_op jit(solution)/shard_map/ppermute | solution.py:27
  32.3 1.7 collective-permute-start.10
  34.0 1.6 collective-permute-start.7
  36.1 2.2 %collective-permute-start.8 = (f32[256,512]{1,0:T(8,128)S(1)}, f32[256,512]{1,0:T(8,128)S(1)}, u32[]{:S(2)}, u32[]{:S(2)}) collective-permute-start(f32[256,512]{1,0:T(8,128)S(1)} %get-tuple-element.54.refs_0_), channel_id=1, source_target_pairs={{0,6},{1,7},{2,4},{3,5},{4,2},{5,3},{6,0},{7,1},{8,14},{9,15},{10,... | collective-permute-start | bytes 1572872 | tf_op jit(solution)/shard_map/ppermute | solution.py:27
  38.8 3.7 %collective-permute-start.9 = (f32[256,512]{1,0:T(8,128)S(1)}, f32[256,512]{1,0:T(8,128)S(1)}, u32[]{:S(2)}, u32[]{:S(2)}) collective-permute-start(f32[256,512]{1,0:T(8,128)S(1)} %get-tuple-element.55), channel_id=1, source_target_pairs={{0,72},{1,73},{2,74},{3,75},{4,76},{5,77},{6,78},{7,79},{8,64},{9,... | collective-permute-start | bytes 1572872 | tf_op jit(solution)/shard_map/ppermute | solution.py:27
  42.5 1.6 collective-permute-start.12
  44.1 5.9 %collective-permute-done.12.refs_3_ = f32[128,512]{1,0:T(8,128)S(1)} collective-permute-done((f32[128,512]{1,0:T(8,128)S(1)}, f32[128,512]{1,0:T(8,128)S(1)}, u32[]{:S(2)}, u32[]{:S(2)}) %collective-permute-start.12) | collective-permute-done | bytes 262176 | tf_op jit(solution)/shard_map/ppermute | solution.py:27
  50.8 1.4 pad_maximum_fusion
  52.2 1.6 collective-permute-start.13
  53.8 2.2 %collective-permute-start.14 = (f32[384,512]{1,0:T(8,128)}, f32[384,512]{1,0:T(8,128)S(1)}, u32[]{:S(2)}, u32[]{:S(2)}) collective-permute-start(f32[384,512]{1,0:T(8,128)} %get-tuple-element.105), channel_id=1, source_target_pairs={{0,6},{1,7},{2,4},{3,5},{4,2},{5,3},{6,0},{7,1},{8,14},{9,15},{10,... | collective-permute-start | bytes 2359304 | tf_op jit(solution)/shard_map/ppermute | solution.py:27
  57.0 2.0 %collective-permute-start.17 = (f32[192,512]{1,0:T(8,128)}, f32[192,512]{1,0:T(8,128)S(1)}, u32[]{:S(2)}, u32[]{:S(2)}) collective-permute-start(f32[192,512]{1,0:T(8,128)} %get-tuple-element.109), channel_id=1, source_target_pairs={{0,48},{1,49},{2,50},{3,51},{4,52},{5,53},{6,54},{7,55},{8,56},{9,... | collective-permute-start | bytes 1179656 | tf_op jit(solution)/shard_map/ppermute | solution.py:27
  59.8 6.4 %collective-permute-done.17.refs_5_ = f32[192,512]{1,0:T(8,128)S(1)} collective-permute-done((f32[192,512]{1,0:T(8,128)}, f32[192,512]{1,0:T(8,128)S(1)}, u32[]{:S(2)}, u32[]{:S(2)}) %collective-permute-start.17) | collective-permute-done | bytes 393248 | tf_op jit(solution)/shard_map/ppermute | solution.py:27
  66.4 2.0 %collective-permute-done.16.refs_4_ = f32[192,512]{1,0:T(8,128)} collective-permute-done((f32[192,512]{1,0:T(8,128)}, f32[192,512]{1,0:T(8,128)}, u32[]{:S(2)}, u32[]{:S(2)}) %collective-permute-start.16) | collective-permute-done | bytes 393248 | tf_op jit(solution)/shard_map/ppermute | solution.py:27
  69.5 1.4 collective-permute-start.29
  72.9 6.9 %products.6 = (f32[256,512]{1,0:T(8,128)S(1)}, f32[256,512]{1,0:T(8,128)S(1)}) custom-call(s32[4]{0:T(128)S(1)} %multiply_add_fusion.1.at_ref, f32[256,512]{1,0:T(8,128)S(1)} %copy-done.11, f32[256,512]{1,0:T(8,128)S(1)} %collective-permute-done.7.refs_1_, f32[256,512]{1,0:T(8,128)S(1)} %copy-done.1, f32[256,512]{1,0:T(8,128)S(1)} %collective-permute-done.9.refs_3_, ...), custom_call_target="tpu_custom_call" | custom-call | flops 3221225472 | bytes 10485760 | tf_op jit(solution)/shard_map/products/pallas_call | solution.py:86
  79.9 2.6 %pick.3 = (f32[256,512]{1,0:T(8,128)}, f32[256,512]{1,0:T(8,128)}) custom-call(s32[24]{0:T(128)S(1)} %pad_add_fusion.plan_ref, f32[128,512]{1,0:T(8,128)S(1)} %bitcast.74, f32[128,512]{1,0:T(8,128)S(1)} %copy-done.3, f32[128,512]{1,0:T(8,128)S(1)} %copy-done.7, f32[128,512]{1,0:T(8,128)S(1)} %copy-done.9, f32[192,512]{1,0:T(8,128)} %collective-permute-done.16.refs_4_, ...), custom_call_target="tpu_custom_call" | custom-call | bytes 1048576 | tf_op jit(solution)/shard_map/pick/pallas_call | solution.py:111
  86.5 2.2 %collective-permute-start.19 = (f32[128,512]{1,0:T(8,128)}, f32[128,512]{1,0:T(8,128)}, u32[]{:S(2)}, u32[]{:S(2)}) collective-permute-start(f32[128,512]{1,0:T(8,128)} %slice_bitcast_fusion.4), channel_id=1, source_target_pairs={{0,6},{1,7},{2,4},{3,5},{4,2},{5,3},{6,0},{7,1},{8,14},{9,15},{10,... | collective-permute-start | bytes 786440 | tf_op jit(solution)/shard_map/ppermute | solution.py:27
  88.7 2.9 %collective-permute-start.32 = (f32[256,512]{1,0:T(8,128)}, f32[256,512]{1,0:T(8,128)S(1)}, u32[]{:S(2)}, u32[]{:S(2)}) collective-permute-start(f32[256,512]{1,0:T(8,128)} %get-tuple-element.81), channel_id=1, source_target_pairs={{0,72},{1,73},{2,74},{3,75},{4,76},{5,77},{6,78},{7,79},{8,64},{9,... | collective-permute-start | bytes 1572872 | tf_op jit(solution)/shard_map/ppermute | solution.py:27
  92.7 5.7 %products.7 = (f32[256,512]{1,0:T(8,128)S(1)}, f32[256,512]{1,0:T(8,128)S(1)}) custom-call(s32[3]{0:T(128)S(1)} %multiply_add_fusion.at_ref, f32[384,512]{1,0:T(8,128)S(1)} %collective-permute-done.13.refs_0_.refs_8_, f32[384,512]{1,0:T(8,128)S(1)} %collective-permute-done.14.refs_1_, f32[8192,512]{1,0:T(8,128)} %bitcast.87, ...), custom_call_target="tpu_custom_call" | custom-call | flops 2415919104 | bytes 7864320 | tf_op jit(solution)/shard_map/products/pallas_call | solution.py:86
  98.5 2.7 %products.8 = (f32[256,512]{1,0:T(8,128)S(1)}, f32[256,512]{1,0:T(8,128)S(1)}) custom-call(s32[1]{0:T(128)S(6)} %add.113.at_ref, f32[128,512]{1,0:T(8,128)S(1)} %collective-permute-done.18.refs_0_, f32[128,512]{1,0:T(8,128)} %collective-permute-done.19.refs_1_, f32[8192,512]{1,0:T(8,128)} %bitcast.88, f32[8192,512]{1,0:T(8,128)} %collective-permute-done.15.refs_5_.refs_3_, ...), custom_call_target="tpu_custom_call" | custom-call | flops 805306368 | bytes 2621440 | tf_op jit(solution)/shard_map/products/pallas_call | solution.py:86
  106.6 3.4 %collective-permute-done.21.refs_1_ = f32[64,512]{1,0:T(8,128)S(1)} collective-permute-done((f32[64,512]{1,0:T(8,128)S(1)}, f32[64,512]{1,0:T(8,128)S(1)}, u32[]{:S(2)}, u32[]{:S(2)}) %collective-permute-start.21) | collective-permute-done | bytes 131104 | tf_op jit(solution)/shard_map/ppermute | solution.py:27
  110.1 1.7 collective-permute-done.22.refs_2_
  112.6 1.9 %collective-permute-start.24 = (f32[192,512]{1,0:T(8,128)S(1)}, f32[192,512]{1,0:T(8,128)S(1)}, u32[]{:S(2)}, u32[]{:S(2)}) collective-permute-start(f32[192,512]{1,0:T(8,128)S(1)} %get-tuple-element.75), channel_id=1, source_target_pairs={{0,48},{1,49},{2,50},{3,51},{4,52},{5,53},{6,54},{7,55},{8,56},{9,... | collective-permute-start | bytes 1179656 | tf_op jit(solution)/shard_map/ppermute | solution.py:27
  114.6 7.2 %products.9 = (f32[256,512]{1,0:T(8,128)S(1)}, f32[256,512]{1,0:T(8,128)S(1)}) custom-call(s32[4]{0:T(128)S(1)} %multiply_add_fusion.1.at_ref, f32[256,512]{1,0:T(8,128)} %get-tuple-element.80.refs_0_, f32[256,512]{1,0:T(8,128)S(1)} %collective-permute-done.30.refs_1_, f32[256,512]{1,0:T(8,128)} %collective-permute-done.31.refs_2_, ...), custom_call_target="tpu_custom_call" | custom-call | flops 3221225472 | bytes 10485760 | tf_op jit(solution)/shard_map/products/pallas_call | solution.py:86
  122.4 1.3 collective-permute-done.24.refs_2_
  124.9 2.0 %collective-permute-start.26 = (f32[128,512]{1,0:T(8,128)S(1)}, f32[128,512]{1,0:T(8,128)S(1)}, u32[]{:S(2)}, u32[]{:S(2)}) collective-permute-start(f32[128,512]{1,0:T(8,128)S(1)} %get-tuple-element.77), channel_id=1, source_target_pairs={{0,48},{1,49},{2,50},{3,51},{4,52},{5,53},{6,54},{7,55},{8,56},{9,... | collective-permute-start | bytes 786440 | tf_op jit(solution)/shard_map/ppermute | solution.py:27
  128.0 2.3 %collective-permute-start.36 = (f32[128,512]{1,0:T(8,128)S(1)}, f32[128,512]{1,0:T(8,128)S(1)}, u32[]{:S(2)}, u32[]{:S(2)}) collective-permute-start(f32[128,512]{1,0:T(8,128)S(1)} %slice_bitcast_fusion), channel_id=1, source_target_pairs={{0,6},{1,7},{2,4},{3,5},{4,2},{5,3},{6,0},{7,1},{8,14},{9,15},{10,... | collective-permute-start | bytes 786440 | tf_op jit(solution)/shard_map/ppermute | solution.py:27
  130.8 1.7 collective-permute-done.26.refs_2_
  134.1 5.7 %products.10 = (f32[256,512]{1,0:T(8,128)S(1)}, f32[256,512]{1,0:T(8,128)S(1)}) custom-call(s32[3]{0:T(128)S(1)} %multiply_add_fusion.at_ref, f32[384,512]{1,0:T(8,128)S(1)} %collective-permute-done.33.refs_0_, f32[384,512]{1,0:T(8,128)S(1)} %collective-permute-done.34.refs_1_, f32[8192,512]{1,0:T(8,128)} %bitcast.90, ...), custom_call_target="tpu_custom_call" | custom-call | flops 2415919104 | bytes 7864320 | tf_op jit(solution)/shard_map/products/pallas_call | solution.py:86
  139.9 2.6 %products.11 = (f32[256,512]{1,0:T(8,128)S(1)}, f32[256,512]{1,0:T(8,128)S(1)}) custom-call(s32[1]{0:T(128)S(6)} %add.113.at_ref, f32[128,512]{1,0:T(8,128)S(1)} %collective-permute-done.35.refs_0_, f32[128,512]{1,0:T(8,128)S(1)} %collective-permute-done.36.refs_1_, f32[8192,512]{1,0:T(8,128)} %bitcast.91, ...), custom_call_target="tpu_custom_call" | custom-call | flops 805306368 | bytes 2621440 | tf_op jit(solution)/shard_map/products/pallas_call | solution.py:86
  142.5 1.9 %collective-permute-done.37.refs_1_ = f32[256,512]{1,0:T(8,128)S(1)} collective-permute-done((f32[256,512]{1,0:T(8,128)S(1)}, f32[256,512]{1,0:T(8,128)S(1)}, u32[]{:S(2)}, u32[]{:S(2)}) %collective-permute-start.37) | collective-permute-done | bytes 524320 | tf_op jit(solution)/shard_map/ppermute | solution.py:27
  146.1 1.2 collective-permute-start.39
  147.4 3.3 %collective-permute-done.38.refs_1_ = f32[64,512]{1,0:T(8,128)S(1)} collective-permute-done((f32[64,512]{1,0:T(8,128)S(1)}, f32[64,512]{1,0:T(8,128)S(1)}, u32[]{:S(2)}, u32[]{:S(2)}) %collective-permute-start.38) | collective-permute-done | bytes 131104 | tf_op jit(solution)/shard_map/ppermute | solution.py:27
  150.7 1.9 %collective-permute-done.39.refs_2_ = f32[64,512]{1,0:T(8,128)S(1)} collective-permute-done((f32[64,512]{1,0:T(8,128)S(1)}, f32[64,512]{1,0:T(8,128)S(1)}, u32[]{:S(2)}, u32[]{:S(2)}) %collective-permute-start.39) | collective-permute-done | bytes 131104 | tf_op jit(solution)/shard_map/ppermute | solution.py:27
  153.4 1.3 collective-permute-start.41
  154.7 8.7 %collective-permute-done.40.refs_1_ = f32[192,512]{1,0:T(8,128)S(1)} collective-permute-done((f32[192,512]{1,0:T(8,128)S(1)}, f32[192,512]{1,0:T(8,128)S(1)}, u32[]{:S(2)}, u32[]{:S(2)}) %collective-permute-start.40) | collective-permute-done | bytes 393248 | tf_op jit(solution)/shard_map/ppermute | solution.py:27
  163.4 1.3 collective-permute-done.41.refs_2_
  165.9 1.2 collective-permute-start.43
  167.2 4.7 %collective-permute-done.42.refs_1_ = f32[128,512]{1,0:T(8,128)S(1)} collective-permute-done((f32[128,512]{1,0:T(8,128)S(1)}, f32[128,512]{1,0:T(8,128)S(1)}, u32[]{:S(2)}, u32[]{:S(2)}) %collective-permute-start.42) | collective-permute-done | bytes 262176 | tf_op jit(solution)/shard_map/ppermute | solution.py:27
  171.9 1.7 collective-permute-done.43.refs_2_
  (128 shorter events, 35.5 us)
Async XLA Ops:
  0.0 70.8 %collective-permute-start.15 = (f32[8192,512]{1,0:T(8,128)}, f32[8192,512]{1,0:T(8,128)}, u32[]{:S(2)}, u32[]{:S(2)}) collective-permute-start(f32[8192,512]{1,0:T(8,128)} %bitcast.85), channel_id=1, source_target_pairs={{0,1},{1,0},{2,3},{3,2},{4,5},{5,4},{6,7},{7,6},{8,9},{9,8},{10,11... | collective-permute-start | bytes 50331656 | tf_op jit(solution)/shard_map/ppermute | solution.py:27
  1.1 52.7 %copy-start.4 = (f32[2,64,512]{2,1,0:T(8,128)}, f32[2,64,512]{2,1,0:T(8,128)S(1)}, u32[]{:S(2)}) copy-start(f32[2,64,512]{2,1,0:T(8,128)S(1)} %get-tuple-element.108) | copy-start | bytes 786436
  1.1 10.0 %collective-permute-start.2 = (f32[128,512]{1,0:T(8,128)S(1)}, f32[128,512]{1,0:T(8,128)S(1)}, u32[]{:S(2)}, u32[]{:S(2)}) collective-permute-start(f32[128,512]{1,0:T(8,128)S(1)} %bitcast.75), channel_id=1, source_target_pairs={{0,48},{1,49},{2,50},{3,51},{4,52},{5,53},{6,54},{7,55},{8,56},{9,... | collective-permute-start | bytes 786440 | tf_op jit(solution)/shard_map/ppermute | solution.py:27
  4.0 8.4 %collective-permute-start.1 = (f32[128,512]{1,0:T(8,128)S(1)}, f32[128,512]{1,0:T(8,128)S(1)}, u32[]{:S(2)}, u32[]{:S(2)}) collective-permute-start(f32[128,512]{1,0:T(8,128)S(1)} %bitcast.76), channel_id=1, source_target_pairs={{0,16},{1,17},{2,18},{3,19},{4,20},{5,21},{6,22},{7,23},{8,24},{9,... | collective-permute-start | bytes 786440 | tf_op jit(solution)/shard_map/ppermute | solution.py:27
  4.2 8.4 %collective-permute-start = (f32[128,512]{1,0:T(8,128)S(1)}, f32[128,512]{1,0:T(8,128)S(1)}, u32[]{:S(2)}, u32[]{:S(2)}) collective-permute-start(f32[128,512]{1,0:T(8,128)S(1)} %bitcast.77), channel_id=1, source_target_pairs={{0,64},{1,65},{2,66},{3,67},{4,68},{5,69},{6,70},{7,71},{8,72},{9,... | collective-permute-start | bytes 786440 | tf_op jit(solution)/shard_map/ppermute | solution.py:27
  12.7 11.7 %collective-permute-start.4 = (f32[192,512]{1,0:T(8,128)S(1)}, f32[192,512]{1,0:T(8,128)S(1)}, u32[]{:S(2)}, u32[]{:S(2)}) collective-permute-start(f32[192,512]{1,0:T(8,128)S(1)} %get-tuple-element.111), channel_id=1, source_target_pairs={{0,48},{1,49},{2,50},{3,51},{4,52},{5,53},{6,54},{7,55},{8,56},{9,... | collective-permute-start | bytes 1179656 | tf_op jit(solution)/shard_map/ppermute | solution.py:27
  14.2 10.8 %collective-permute-start.3 = (f32[192,512]{1,0:T(8,128)S(1)}, f32[192,512]{1,0:T(8,128)S(1)}, u32[]{:S(2)}, u32[]{:S(2)}) collective-permute-start(f32[192,512]{1,0:T(8,128)S(1)} %get-tuple-element.112), channel_id=1, source_target_pairs={{0,16},{1,17},{2,18},{3,19},{4,20},{5,21},{6,22},{7,23},{8,24},{9,... | collective-permute-start | bytes 1179656 | tf_op jit(solution)/shard_map/ppermute | solution.py:27
  24.4 5.0 %collective-permute-start.5 = (f32[64,512]{1,0:T(8,128)S(1)}, f32[64,512]{1,0:T(8,128)S(1)}, u32[]{:S(2)}, u32[]{:S(2)}) collective-permute-start(f32[64,512]{1,0:T(8,128)S(1)} %bitcast.106), channel_id=1, source_target_pairs={{0,16},{1,17},{2,18},{3,19},{4,20},{5,21},{6,22},{7,23},{8,24},{9,... | collective-permute-start | bytes 393224 | tf_op jit(solution)/shard_map/ppermute | solution.py:27
  25.0 6.3 %collective-permute-start.6 = (f32[64,512]{1,0:T(8,128)S(1)}, f32[64,512]{1,0:T(8,128)S(1)}, u32[]{:S(2)}, u32[]{:S(2)}) collective-permute-start(f32[64,512]{1,0:T(8,128)S(1)} %bitcast.108), channel_id=1, source_target_pairs={{0,48},{1,49},{2,50},{3,51},{4,52},{5,53},{6,54},{7,55},{8,56},{9,... | collective-permute-start | bytes 393224 | tf_op jit(solution)/shard_map/ppermute | solution.py:27
  32.3 26.6 %copy-start.10 = (f32[256,512]{1,0:T(8,128)}, f32[256,512]{1,0:T(8,128)S(1)}, u32[]{:S(2)}) copy-start(f32[256,512]{1,0:T(8,128)S(1)} %get-tuple-element.54.refs_0_) | copy-start | bytes 1572868
  32.3 6.5 %collective-permute-start.10 = (f32[128,512]{1,0:T(8,128)S(1)}, f32[128,512]{1,0:T(8,128)S(1)}, u32[]{:S(2)}, u32[]{:S(2)}) collective-permute-start(f32[128,512]{1,0:T(8,128)S(1)} %bitcast.71), channel_id=1, source_target_pairs={{0,64},{1,65},{2,66},{3,67},{4,68},{5,69},{6,70},{7,71},{8,72},{9,... | collective-permute-start | bytes 786440 | tf_op jit(solution)/shard_map/ppermute | solution.py:27
  34.0 16.1 %collective-permute-start.7 = (f32[256,512]{1,0:T(8,128)S(1)}, f32[256,512]{1,0:T(8,128)S(1)}, u32[]{:S(2)}, u32[]{:S(2)}) collective-permute-start(f32[256,512]{1,0:T(8,128)S(1)} %get-tuple-element.54.refs_0_), channel_id=1, source_target_pairs={{0,2},{1,3},{2,0},{3,1},{4,6},{5,7},{6,4},{7,5},{8,10},{9,11},{10,... | collective-permute-start | bytes 1572872 | tf_op jit(solution)/shard_map/ppermute | solution.py:27
  35.5 6.9 %collective-permute-start.11 = (f32[128,512]{1,0:T(8,128)S(1)}, f32[128,512]{1,0:T(8,128)S(1)}, u32[]{:S(2)}, u32[]{:S(2)}) collective-permute-start(f32[128,512]{1,0:T(8,128)S(1)} %bitcast.72), channel_id=1, source_target_pairs={{0,16},{1,17},{2,18},{3,19},{4,20},{5,21},{6,22},{7,23},{8,24},{9,... | collective-permute-start | bytes 786440 | tf_op jit(solution)/shard_map/ppermute | solution.py:27
  36.1 13.9 %collective-permute-start.8 = (f32[256,512]{1,0:T(8,128)S(1)}, f32[256,512]{1,0:T(8,128)S(1)}, u32[]{:S(2)}, u32[]{:S(2)}) collective-permute-start(f32[256,512]{1,0:T(8,128)S(1)} %get-tuple-element.54.refs_0_), channel_id=1, source_target_pairs={{0,6},{1,7},{2,4},{3,5},{4,2},{5,3},{6,0},{7,1},{8,14},{9,15},{10,... | collective-permute-start | bytes 1572872 | tf_op jit(solution)/shard_map/ppermute | solution.py:27
  38.8 12.0 %collective-permute-start.9 = (f32[256,512]{1,0:T(8,128)S(1)}, f32[256,512]{1,0:T(8,128)S(1)}, u32[]{:S(2)}, u32[]{:S(2)}) collective-permute-start(f32[256,512]{1,0:T(8,128)S(1)} %get-tuple-element.55), channel_id=1, source_target_pairs={{0,72},{1,73},{2,74},{3,75},{4,76},{5,77},{6,78},{7,79},{8,64},{9,... | collective-permute-start | bytes 1572872 | tf_op jit(solution)/shard_map/ppermute | solution.py:27
  42.5 7.6 %collective-permute-start.12 = (f32[128,512]{1,0:T(8,128)S(1)}, f32[128,512]{1,0:T(8,128)S(1)}, u32[]{:S(2)}, u32[]{:S(2)}) collective-permute-start(f32[128,512]{1,0:T(8,128)S(1)} %bitcast.73), channel_id=1, source_target_pairs={{0,48},{1,49},{2,50},{3,51},{4,52},{5,53},{6,54},{7,55},{8,56},{9,... | collective-permute-start | bytes 786440 | tf_op jit(solution)/shard_map/ppermute | solution.py:27
  52.2 27.7 %collective-permute-start.13 = (f32[384,512]{1,0:T(8,128)}, f32[384,512]{1,0:T(8,128)S(1)}, u32[]{:S(2)}, u32[]{:S(2)}) collective-permute-start(f32[384,512]{1,0:T(8,128)} %get-tuple-element.106), channel_id=1, source_target_pairs={{0,2},{1,3},{2,0},{3,1},{4,6},{5,7},{6,4},{7,5},{8,10},{9,11},{10,... | collective-permute-start | bytes 2359304 | tf_op jit(solution)/shard_map/ppermute | solution.py:27
  53.8 30.0 %collective-permute-start.14 = (f32[384,512]{1,0:T(8,128)}, f32[384,512]{1,0:T(8,128)S(1)}, u32[]{:S(2)}, u32[]{:S(2)}) collective-permute-start(f32[384,512]{1,0:T(8,128)} %get-tuple-element.105), channel_id=1, source_target_pairs={{0,6},{1,7},{2,4},{3,5},{4,2},{5,3},{6,0},{7,1},{8,14},{9,15},{10,... | collective-permute-start | bytes 2359304 | tf_op jit(solution)/shard_map/ppermute | solution.py:27
  57.0 9.3 %collective-permute-start.17 = (f32[192,512]{1,0:T(8,128)}, f32[192,512]{1,0:T(8,128)S(1)}, u32[]{:S(2)}, u32[]{:S(2)}) collective-permute-start(f32[192,512]{1,0:T(8,128)} %get-tuple-element.109), channel_id=1, source_target_pairs={{0,48},{1,49},{2,50},{3,51},{4,52},{5,53},{6,54},{7,55},{8,56},{9,... | collective-permute-start | bytes 1179656 | tf_op jit(solution)/shard_map/ppermute | solution.py:27
  58.9 9.5 %collective-permute-start.16 = (f32[192,512]{1,0:T(8,128)}, f32[192,512]{1,0:T(8,128)}, u32[]{:S(2)}, u32[]{:S(2)}) collective-permute-start(f32[192,512]{1,0:T(8,128)} %get-tuple-element.110), channel_id=1, source_target_pairs={{0,16},{1,17},{2,18},{3,19},{4,20},{5,21},{6,22},{7,23},{8,24},{9,... | collective-permute-start | bytes 1179656 | tf_op jit(solution)/shard_map/ppermute | solution.py:27
  66.3 13.5 %collective-permute-start.28 = (f32[64,512]{1,0:T(8,128)S(1)}, f32[64,512]{1,0:T(8,128)S(1)}, u32[]{:S(2)}, u32[]{:S(2)}) collective-permute-start(f32[64,512]{1,0:T(8,128)S(1)} %bitcast.105), channel_id=1, source_target_pairs={{0,16},{1,17},{2,18},{3,19},{4,20},{5,21},{6,22},{7,23},{8,24},{9,... | collective-permute-start | bytes 393224 | tf_op jit(solution)/shard_map/ppermute | solution.py:27
  69.4 22.2 %copy-start.14 = (s32[3]{0:T(128)S(1)}, s32[3]{0:T(128)}, u32[]{:S(2)}) copy-start(s32[3]{0:T(128)} %constant.163.clone) | copy-start | bytes 40
  69.5 10.4 %collective-permute-start.29 = (f32[64,512]{1,0:T(8,128)S(1)}, f32[64,512]{1,0:T(8,128)S(1)}, u32[]{:S(2)}, u32[]{:S(2)}) collective-permute-start(f32[64,512]{1,0:T(8,128)S(1)} %bitcast.107), channel_id=1, source_target_pairs={{0,48},{1,49},{2,50},{3,51},{4,52},{5,53},{6,54},{7,55},{8,56},{9,... | collective-permute-start | bytes 393224 | tf_op jit(solution)/shard_map/ppermute | solution.py:27
  82.5 18.8 %collective-permute-start.30 = (f32[256,512]{1,0:T(8,128)}, f32[256,512]{1,0:T(8,128)S(1)}, u32[]{:S(2)}, u32[]{:S(2)}) collective-permute-start(f32[256,512]{1,0:T(8,128)} %get-tuple-element.80.refs_0_), channel_id=1, source_target_pairs={{0,2},{1,3},{2,0},{3,1},{4,6},{5,7},{6,4},{7,5},{8,10},{9,11},{10,... | collective-permute-start | bytes 1572872 | tf_op jit(solution)/shard_map/ppermute | solution.py:27
  83.2 18.1 %collective-permute-start.31 = (f32[256,512]{1,0:T(8,128)}, f32[256,512]{1,0:T(8,128)}, u32[]{:S(2)}, u32[]{:S(2)}) collective-permute-start(f32[256,512]{1,0:T(8,128)} %get-tuple-element.80.refs_0_), channel_id=1, source_target_pairs={{0,6},{1,7},{2,4},{3,5},{4,2},{5,3},{6,0},{7,1},{8,14},{9,15},{10,... | collective-permute-start | bytes 1572872 | tf_op jit(solution)/shard_map/ppermute | solution.py:27
  84.5 13.9 %collective-permute-start.18 = (f32[128,512]{1,0:T(8,128)}, f32[128,512]{1,0:T(8,128)S(1)}, u32[]{:S(2)}, u32[]{:S(2)}) collective-permute-start(f32[128,512]{1,0:T(8,128)} %slice_bitcast_fusion.5), channel_id=1, source_target_pairs={{0,2},{1,3},{2,0},{3,1},{4,6},{5,7},{6,4},{7,5},{8,10},{9,11},{10,... | collective-permute-start | bytes 786440 | tf_op jit(solution)/shard_map/ppermute | solution.py:27
  86.5 12.0 %collective-permute-start.19 = (f32[128,512]{1,0:T(8,128)}, f32[128,512]{1,0:T(8,128)}, u32[]{:S(2)}, u32[]{:S(2)}) collective-permute-start(f32[128,512]{1,0:T(8,128)} %slice_bitcast_fusion.4), channel_id=1, source_target_pairs={{0,6},{1,7},{2,4},{3,5},{4,2},{5,3},{6,0},{7,1},{8,14},{9,15},{10,... | collective-permute-start | bytes 786440 | tf_op jit(solution)/shard_map/ppermute | solution.py:27
  88.7 12.6 %collective-permute-start.32 = (f32[256,512]{1,0:T(8,128)}, f32[256,512]{1,0:T(8,128)S(1)}, u32[]{:S(2)}, u32[]{:S(2)}) collective-permute-start(f32[256,512]{1,0:T(8,128)} %get-tuple-element.81), channel_id=1, source_target_pairs={{0,72},{1,73},{2,74},{3,75},{4,76},{5,77},{6,78},{7,79},{8,64},{9,... | collective-permute-start | bytes 1572872 | tf_op jit(solution)/shard_map/ppermute | solution.py:27
  101.2 2.7 %collective-permute-start.20 = (f32[256,512]{1,0:T(8,128)S(1)}, f32[256,512]{1,0:T(8,128)S(1)}, u32[]{:S(2)}, u32[]{:S(2)}) collective-permute-start(f32[256,512]{1,0:T(8,128)S(1)} %get-tuple-element.70), channel_id=1, source_target_pairs={{0,1},{1,0},{2,3},{3,2},{4,5},{5,4},{6,7},{7,6},{8,9},{9,8},{10,11... | collective-permute-start | bytes 1572872 | tf_op jit(solution)/shard_map/ppermute | solution.py:27
  102.5 24.4 %collective-permute-start.33 = (f32[384,512]{1,0:T(8,128)S(1)}, f32[384,512]{1,0:T(8,128)S(1)}, u32[]{:S(2)}, u32[]{:S(2)}) collective-permute-start(f32[384,512]{1,0:T(8,128)S(1)} %get-tuple-element.104), channel_id=1, source_target_pairs={{0,2},{1,3},{2,0},{3,1},{4,6},{5,7},{6,4},{7,5},{8,10},{9,11},{10,... | collective-permute-start | bytes 2359304 | tf_op jit(solution)/shard_map/ppermute | solution.py:27
  103.3 23.6 %collective-permute-start.34 = (f32[384,512]{1,0:T(8,128)S(1)}, f32[384,512]{1,0:T(8,128)S(1)}, u32[]{:S(2)}, u32[]{:S(2)}) collective-permute-start(f32[384,512]{1,0:T(8,128)S(1)} %get-tuple-element.103), channel_id=1, source_target_pairs={{0,6},{1,7},{2,4},{3,5},{4,2},{5,3},{6,0},{7,1},{8,14},{9,15},{10,... | collective-permute-start | bytes 2359304 | tf_op jit(solution)/shard_map/ppermute | solution.py:27
  104.5 5.5 %collective-permute-start.21 = (f32[64,512]{1,0:T(8,128)S(1)}, f32[64,512]{1,0:T(8,128)S(1)}, u32[]{:S(2)}, u32[]{:S(2)}) collective-permute-start(f32[64,512]{1,0:T(8,128)S(1)} %get-tuple-element.72), channel_id=1, source_target_pairs={{0,16},{1,17},{2,18},{3,19},{4,20},{5,21},{6,22},{7,23},{8,24},{9,... | collective-permute-start | bytes 393224 | tf_op jit(solution)/shard_map/ppermute | solution.py:27
  105.5 6.2 %collective-permute-start.22 = (f32[64,512]{1,0:T(8,128)S(1)}, f32[64,512]{1,0:T(8,128)S(1)}, u32[]{:S(2)}, u32[]{:S(2)}) collective-permute-start(f32[64,512]{1,0:T(8,128)S(1)} %get-tuple-element.73), channel_id=1, source_target_pairs={{0,48},{1,49},{2,50},{3,51},{4,52},{5,53},{6,54},{7,55},{8,56},{9,... | collective-permute-start | bytes 393224 | tf_op jit(solution)/shard_map/ppermute | solution.py:27
  112.5 9.8 %collective-permute-start.23 = (f32[192,512]{1,0:T(8,128)S(1)}, f32[192,512]{1,0:T(8,128)S(1)}, u32[]{:S(2)}, u32[]{:S(2)}) collective-permute-start(f32[192,512]{1,0:T(8,128)S(1)} %get-tuple-element.74), channel_id=1, source_target_pairs={{0,16},{1,17},{2,18},{3,19},{4,20},{5,21},{6,22},{7,23},{8,24},{9,... | collective-permute-start | bytes 1179656 | tf_op jit(solution)/shard_map/ppermute | solution.py:27
  112.6 11.0 %collective-permute-start.24 = (f32[192,512]{1,0:T(8,128)S(1)}, f32[192,512]{1,0:T(8,128)S(1)}, u32[]{:S(2)}, u32[]{:S(2)}) collective-permute-start(f32[192,512]{1,0:T(8,128)S(1)} %get-tuple-element.75), channel_id=1, source_target_pairs={{0,48},{1,49},{2,50},{3,51},{4,52},{5,53},{6,54},{7,55},{8,56},{9,... | collective-permute-start | bytes 1179656 | tf_op jit(solution)/shard_map/ppermute | solution.py:27
  124.4 6.5 %collective-permute-start.25 = (f32[128,512]{1,0:T(8,128)S(1)}, f32[128,512]{1,0:T(8,128)S(1)}, u32[]{:S(2)}, u32[]{:S(2)}) collective-permute-start(f32[128,512]{1,0:T(8,128)S(1)} %get-tuple-element.76), channel_id=1, source_target_pairs={{0,16},{1,17},{2,18},{3,19},{4,20},{5,21},{6,22},{7,23},{8,24},{9,... | collective-permute-start | bytes 786440 | tf_op jit(solution)/shard_map/ppermute | solution.py:27
  124.9 7.6 %collective-permute-start.26 = (f32[128,512]{1,0:T(8,128)S(1)}, f32[128,512]{1,0:T(8,128)S(1)}, u32[]{:S(2)}, u32[]{:S(2)}) collective-permute-start(f32[128,512]{1,0:T(8,128)S(1)} %get-tuple-element.77), channel_id=1, source_target_pairs={{0,48},{1,49},{2,50},{3,51},{4,52},{5,53},{6,54},{7,55},{8,56},{9,... | collective-permute-start | bytes 786440 | tf_op jit(solution)/shard_map/ppermute | solution.py:27
  126.9 6.4 %collective-permute-start.27 = (f32[128,512]{1,0:T(8,128)S(1)}, f32[128,512]{1,0:T(8,128)S(1)}, u32[]{:S(2)}, u32[]{:S(2)}) collective-permute-start(f32[128,512]{1,0:T(8,128)S(1)} %get-tuple-element.78), channel_id=1, source_target_pairs={{0,64},{1,65},{2,66},{3,67},{4,68},{5,69},{6,70},{7,71},{8,72},{9,... | collective-permute-start | bytes 786440 | tf_op jit(solution)/shard_map/ppermute | solution.py:27
  127.0 12.9 %collective-permute-start.35 = (f32[128,512]{1,0:T(8,128)S(1)}, f32[128,512]{1,0:T(8,128)S(1)}, u32[]{:S(2)}, u32[]{:S(2)}) collective-permute-start(f32[128,512]{1,0:T(8,128)S(1)} %slice_bitcast_fusion.1), channel_id=1, source_target_pairs={{0,2},{1,3},{2,0},{3,1},{4,6},{5,7},{6,4},{7,5},{8,10},{9,11},{10,... | collective-permute-start | bytes 786440 | tf_op jit(solution)/shard_map/ppermute | solution.py:27
  128.0 11.9 %collective-permute-start.36 = (f32[128,512]{1,0:T(8,128)S(1)}, f32[128,512]{1,0:T(8,128)S(1)}, u32[]{:S(2)}, u32[]{:S(2)}) collective-permute-start(f32[128,512]{1,0:T(8,128)S(1)} %slice_bitcast_fusion), channel_id=1, source_target_pairs={{0,6},{1,7},{2,4},{3,5},{4,2},{5,3},{6,0},{7,1},{8,14},{9,15},{10,... | collective-permute-start | bytes 786440 | tf_op jit(solution)/shard_map/ppermute | solution.py:27
  142.4 2.0 %collective-permute-start.37 = (f32[256,512]{1,0:T(8,128)S(1)}, f32[256,512]{1,0:T(8,128)S(1)}, u32[]{:S(2)}, u32[]{:S(2)}) collective-permute-start(f32[256,512]{1,0:T(8,128)S(1)} %get-tuple-element.94), channel_id=1, source_target_pairs={{0,1},{1,0},{2,3},{3,2},{4,5},{5,4},{6,7},{7,6},{8,9},{9,8},{10,11... | collective-permute-start | bytes 1572872 | tf_op jit(solution)/shard_map/ppermute | solution.py:27
  145.1 5.6 %collective-permute-start.38 = (f32[64,512]{1,0:T(8,128)S(1)}, f32[64,512]{1,0:T(8,128)S(1)}, u32[]{:S(2)}, u32[]{:S(2)}) collective-permute-start(f32[64,512]{1,0:T(8,128)S(1)} %get-tuple-element.96), channel_id=1, source_target_pairs={{0,16},{1,17},{2,18},{3,19},{4,20},{5,21},{6,22},{7,23},{8,24},{9,... | collective-permute-start | bytes 393224 | tf_op jit(solution)/shard_map/ppermute | solution.py:27
  146.1 6.5 %collective-permute-start.39 = (f32[64,512]{1,0:T(8,128)S(1)}, f32[64,512]{1,0:T(8,128)S(1)}, u32[]{:S(2)}, u32[]{:S(2)}) collective-permute-start(f32[64,512]{1,0:T(8,128)S(1)} %get-tuple-element.97), channel_id=1, source_target_pairs={{0,48},{1,49},{2,50},{3,51},{4,52},{5,53},{6,54},{7,55},{8,56},{9,... | collective-permute-start | bytes 393224 | tf_op jit(solution)/shard_map/ppermute | solution.py:27
  153.3 10.1 %collective-permute-start.40 = (f32[192,512]{1,0:T(8,128)S(1)}, f32[192,512]{1,0:T(8,128)S(1)}, u32[]{:S(2)}, u32[]{:S(2)}) collective-permute-start(f32[192,512]{1,0:T(8,128)S(1)} %get-tuple-element.98), channel_id=1, source_target_pairs={{0,16},{1,17},{2,18},{3,19},{4,20},{5,21},{6,22},{7,23},{8,24},{9,... | collective-permute-start | bytes 1179656 | tf_op jit(solution)/shard_map/ppermute | solution.py:27
  153.4 11.3 %collective-permute-start.41 = (f32[192,512]{1,0:T(8,128)S(1)}, f32[192,512]{1,0:T(8,128)S(1)}, u32[]{:S(2)}, u32[]{:S(2)}) collective-permute-start(f32[192,512]{1,0:T(8,128)S(1)} %get-tuple-element.99), channel_id=1, source_target_pairs={{0,48},{1,49},{2,50},{3,51},{4,52},{5,53},{6,54},{7,55},{8,56},{9,... | collective-permute-start | bytes 1179656 | tf_op jit(solution)/shard_map/ppermute | solution.py:27
  165.4 6.5 %collective-permute-start.42 = (f32[128,512]{1,0:T(8,128)S(1)}, f32[128,512]{1,0:T(8,128)S(1)}, u32[]{:S(2)}, u32[]{:S(2)}) collective-permute-start(f32[128,512]{1,0:T(8,128)S(1)} %get-tuple-element.100), channel_id=1, source_target_pairs={{0,16},{1,17},{2,18},{3,19},{4,20},{5,21},{6,22},{7,23},{8,24},{9,... | collective-permute-start | bytes 786440 | tf_op jit(solution)/shard_map/ppermute | solution.py:27
  165.9 7.6 %collective-permute-start.43 = (f32[128,512]{1,0:T(8,128)S(1)}, f32[128,512]{1,0:T(8,128)S(1)}, u32[]{:S(2)}, u32[]{:S(2)}) collective-permute-start(f32[128,512]{1,0:T(8,128)S(1)} %get-tuple-element.101), channel_id=1, source_target_pairs={{0,48},{1,49},{2,50},{3,51},{4,52},{5,53},{6,54},{7,55},{8,56},{9,... | collective-permute-start | bytes 786440 | tf_op jit(solution)/shard_map/ppermute | solution.py:27
  167.2 6.4 %collective-permute-start.44 = (f32[128,512]{1,0:T(8,128)S(1)}, f32[128,512]{1,0:T(8,128)S(1)}, u32[]{:S(2)}, u32[]{:S(2)}) collective-permute-start(f32[128,512]{1,0:T(8,128)S(1)} %get-tuple-element.102), channel_id=1, source_target_pairs={{0,64},{1,65},{2,66},{3,67},{4,68},{5,69},{6,70},{7,71},{8,72},{9,... | collective-permute-start | bytes 786440 | tf_op jit(solution)/shard_map/ppermute | solution.py:27
  (13 other events, 124.4 us)

commit v3 on v2

--- a/solution.py
+++ b/solution.py
@@ -238,7 +238,7 @@
     a, b = small_kernel(
         body, plan, [(3 * m, cols)] * 2, [product, *came], name="return_second"
     )
-    return [swap_x(a, 0), swap_x(b, 1)]
+    return a, [swap_x(a, 0), swap_x(b, 1)]
 
 
 def return_third(plan, product, came):
@@ -330,8 +330,15 @@
         last["sums"] = products(arrays, blocks, at[group], own, far, last["sums"])
         return last["sums"]
 
+    def finish(last, back):
+        sums = step(1, last)
+        if back is not None:
+            product, came = back
+            back = product, return_third(plan, product, wait_for(came, sums[0]))
+        return step(2, last), back
+
     arrays = rows_third(rows_second(rows_first(pieces[0])))
-    out, last = [], None
+    out, last, back = [], None, None
     for k, m in enumerate(CHUNKS):
         more = k + 1 < len(CHUNKS)
         after = () if last is None else (last["second"][0], last["sums"][0])
@@ -344,8 +351,7 @@
         this["first"] = [b, *near, bz]
         ready = arrays if more else []
         if last is not None:
-            step(1, last)
-            sums = step(2, last)
+            sums, back = finish(last, back)
             swapped = flip_core(sums[1])
             ready = [*ready, sums[0]]
         near, bz = wait_for((near, bz), *ready)
@@ -357,22 +363,22 @@
             product, came = return_first(plan, sums, swapped)
         step(0, this)
         if last is not None:
-            came = return_second(plan, product, came)
-            ready = [*ready, product]
+            if back is not None:
+                out.append(return_last(plan, *back))
+            sent, came = return_second(plan, product, wait_for(came, this["sums"][0], *out))
+            back = product, came
+            ready = [*ready, sent]
         both = wait_for(this["second"], this["sums"][0], *ready)
         this["third"] = gather_third(both, SLOTS * m, swap_y)
         if more:
-            arrays = rows_third(arrays)
-        if last is not None:
-            came = return_third(plan, product, came)
-            out.append(return_last(plan, product, came))
+            arrays = rows_third(wait_for(arrays, this["sums"][0]))
         last = this
-    last["sums"] = wait_for(last["sums"], *out)
-    step(1, last)
-    sums = step(2, last)
+    sums, back = finish(last, back)
     product, came = return_first(plan, sums, flip_core(sums[1]))
-    came = return_third(plan, product, return_second(plan, product, came))
-    out.append(return_last(plan, product, came))
+    if back is not None:
+        out.append(return_last(plan, *back))
+    came = return_second(plan, product, wait_for(came, *out))[1]
+    out.append(return_last(plan, product, return_third(plan, product, came)))
     out = [o.reshape(local_tiles, -1, cols) for o in out]
     return jnp.concatenate(out, axis=1).reshape(local_tiles * TILE, cols)
 

time: 176 us -> 168 us (0.955)
  waiting for transfers between devices: 66.9 us -> 58 us
  starting transfers between devices: 52.1 us -> 54 us
    ppermute x45, waiting for transfers between devices: 66.9 us -> 58 us  [send(): lax.ppermute(a, ('row', 'col'), [(i, index[to(*p)]) for p, i in index.ite...]
    ppermute x45, starting transfers between devices: 52.1 us -> 54 us  [send(): lax.ppermute(a, ('row', 'col'), [(i, index[to(*p)]) for p, i in index.ite...]
    slice x8, local copies, waits for them, and re-layouts: 0.08 us -> 1.89 us  [half(): cut = a.reshape(pieces, 2, -1, a.shape[1])[:, which]]
  transfers between devices with their start and end apart: 45 -> 45, of which waited for: 25 -> 22; matrix products, arithmetic and copies ran while one was open for 7% -> 7% of each run, Pallas kernels for 20% -> 22%
where the time goes in v3:
time: 168 us; the launch traced here: 167 us
  waiting for transfers between devices  58 us (35%)
  starting transfers between devices  54 us (32%)
  Pallas kernels  39.5 us (24%)
  local copies, waits for them, and re-layouts  8.84 us (5%)
  other arithmetic  6.58 us (4%)
    ppermute x45, waiting for transfers between devices, send(): lax.ppermute(a, ('row', 'col'), [(i, index[to(*p)]) for p, i in index.ite...  58 us
    ppermute x45, starting transfers between devices, send(): lax.ppermute(a, ('row', 'col'), [(i, index[to(*p)]) for p, i in index.ite...  54 us
    pallas_call x6, Pallas kernels, products(): pl.pallas_call(functools.partial(product_kernel, blocks, len(arrays), not...  31 us
    pallas_call x10, Pallas kernels, small_kernel(): pl.pallas_call(kernel, in_specs=[pl.BlockSpec(memory_space=pltpu.SMEM)] +...  8.46 us
  transfers between devices with their start and end apart: 45, of which 22 were waited for; matrix products, arithmetic and copies ran while one was open for 7% of the time, Pallas kernels for 22%

profile of v3, /device:TPU:0, one launch (start us, length us, event | category | flops | bytes accessed | tf_op | source)
XLA Modules:
  0.0 167.5 jit_solution(8376546157668867239)
XLA Ops:
  0.0 1.1 fusion.8
  1.1 1.7 collective-permute-start.1
  2.7 2.1 %collective-permute-start.2 = (f32[128,512]{1,0:T(8,128)S(1)}, f32[128,512]{1,0:T(8,128)S(1)}, u32[]{:S(2)}, u32[]{:S(2)}) collective-permute-start(f32[128,512]{1,0:T(8,128)S(1)} %bitcast.76), channel_id=1, source_target_pairs={{0,48},{1,49},{2,50},{3,51},{4,52},{5,53},{6,54},{7,55},{8,56},{9,... | collective-permute-start | bytes 786440 | tf_op jit(solution)/shard_map/ppermute | solution.py:27
  4.8 1.9 %collective-permute-start = (f32[128,512]{1,0:T(8,128)S(1)}, f32[128,512]{1,0:T(8,128)S(1)}, u32[]{:S(2)}, u32[]{:S(2)}) collective-permute-start(f32[128,512]{1,0:T(8,128)S(1)} %bitcast.77), channel_id=1, source_target_pairs={{0,64},{1,65},{2,66},{3,67},{4,68},{5,69},{6,70},{7,71},{8,72},{9,... | collective-permute-start | bytes 786440 | tf_op jit(solution)/shard_map/ppermute | solution.py:27
  7.4 2.5 %collective-permute-done.1.refs_2_ = f32[128,512]{1,0:T(8,128)S(1)} collective-permute-done((f32[128,512]{1,0:T(8,128)S(1)}, f32[128,512]{1,0:T(8,128)S(1)}, u32[]{:S(2)}, u32[]{:S(2)}) %collective-permute-start.1) | collective-permute-done | bytes 262176 | tf_op jit(solution)/shard_map/ppermute | solution.py:27
  9.9 2.5 %collective-permute-done.2.refs_3_ = f32[128,512]{1,0:T(8,128)S(1)} collective-permute-done((f32[128,512]{1,0:T(8,128)S(1)}, f32[128,512]{1,0:T(8,128)S(1)}, u32[]{:S(2)}, u32[]{:S(2)}) %collective-permute-start.2) | collective-permute-done | bytes 262176 | tf_op jit(solution)/shard_map/ppermute | solution.py:27
  17.3 7.8 %collective-permute-done.4.refs_5_ = f32[192,512]{1,0:T(8,128)S(1)} collective-permute-done((f32[192,512]{1,0:T(8,128)S(1)}, f32[192,512]{1,0:T(8,128)S(1)}, u32[]{:S(2)}, u32[]{:S(2)}) %collective-permute-start.4) | collective-permute-done | bytes 393248 | tf_op jit(solution)/shard_map/ppermute | solution.py:27
  25.6 1.5 collective-permute-start.6
  27.3 3.0 %collective-permute-done.5.refs_6_ = f32[64,512]{1,0:T(8,128)S(1)} collective-permute-done((f32[64,512]{1,0:T(8,128)S(1)}, f32[64,512]{1,0:T(8,128)S(1)}, u32[]{:S(2)}, u32[]{:S(2)}) %collective-permute-start.5) | collective-permute-done | bytes 131104 | tf_op jit(solution)/shard_map/ppermute | solution.py:27
  30.3 1.6 collective-permute-done.6.refs_7_
  32.9 1.6 collective-permute-start.10
  35.1 1.6 collective-permute-start.7
  36.6 2.2 %collective-permute-start.8 = (f32[256,512]{1,0:T(8,128)S(1)}, f32[256,512]{1,0:T(8,128)S(1)}, u32[]{:S(2)}, u32[]{:S(2)}) collective-permute-start(f32[256,512]{1,0:T(8,128)S(1)} %get-tuple-element.64.refs_0_), channel_id=1, source_target_pairs={{0,6},{1,7},{2,4},{3,5},{4,2},{5,3},{6,0},{7,1},{8,14},{9,15},{10,... | collective-permute-start | bytes 1572872 | tf_op jit(solution)/shard_map/ppermute | solution.py:27
  39.3 3.7 %collective-permute-start.9 = (f32[256,512]{1,0:T(8,128)S(1)}, f32[256,512]{1,0:T(8,128)S(1)}, u32[]{:S(2)}, u32[]{:S(2)}) collective-permute-start(f32[256,512]{1,0:T(8,128)S(1)} %get-tuple-element.65), channel_id=1, source_target_pairs={{0,72},{1,73},{2,74},{3,75},{4,76},{5,77},{6,78},{7,79},{8,64},{9,... | collective-permute-start | bytes 1572872 | tf_op jit(solution)/shard_map/ppermute | solution.py:27
  43.0 1.8 %collective-permute-start.12 = (f32[128,512]{1,0:T(8,128)S(1)}, f32[128,512]{1,0:T(8,128)S(1)}, u32[]{:S(2)}, u32[]{:S(2)}) collective-permute-start(f32[128,512]{1,0:T(8,128)S(1)} %bitcast.73), channel_id=1, source_target_pairs={{0,48},{1,49},{2,50},{3,51},{4,52},{5,53},{6,54},{7,55},{8,56},{9,... | collective-permute-start | bytes 786440 | tf_op jit(solution)/shard_map/ppermute | solution.py:27
  44.8 5.7 %collective-permute-done.12.refs_3_ = f32[128,512]{1,0:T(8,128)S(1)} collective-permute-done((f32[128,512]{1,0:T(8,128)S(1)}, f32[128,512]{1,0:T(8,128)S(1)}, u32[]{:S(2)}, u32[]{:S(2)}) %collective-permute-start.12) | collective-permute-done | bytes 262176 | tf_op jit(solution)/shard_map/ppermute | solution.py:27
  50.6 1.3 pad_maximum_fusion
  52.0 1.6 collective-permute-start.13
  53.6 2.3 %collective-permute-start.14 = (f32[384,512]{1,0:T(8,128)}, f32[384,512]{1,0:T(8,128)S(1)}, u32[]{:S(2)}, u32[]{:S(2)}) collective-permute-start(f32[384,512]{1,0:T(8,128)} %get-tuple-element.125), channel_id=1, source_target_pairs={{0,6},{1,7},{2,4},{3,5},{4,2},{5,3},{6,0},{7,1},{8,14},{9,15},{10,... | collective-permute-start | bytes 2359304 | tf_op jit(solution)/shard_map/ppermute | solution.py:27
  58.2 2.5 %collective-permute-start.17 = (f32[192,512]{1,0:T(8,128)S(1)}, f32[192,512]{1,0:T(8,128)S(1)}, u32[]{:S(2)}, u32[]{:S(2)}) collective-permute-start(f32[192,512]{1,0:T(8,128)S(1)} %get-tuple-element.129), channel_id=1, source_target_pairs={{0,48},{1,49},{2,50},{3,51},{4,52},{5,53},{6,54},{7,55},{8,56},{9,... | collective-permute-start | bytes 1179656 | tf_op jit(solution)/shard_map/ppermute | solution.py:27
  63.5 6.9 %products.6 = (f32[256,512]{1,0:T(8,128)S(1)}, f32[256,512]{1,0:T(8,128)S(1)}) custom-call(s32[4]{0:T(128)S(1)} %multiply_add_fusion.1.at_ref, f32[256,512]{1,0:T(8,128)S(1)} %copy-done.9, f32[256,512]{1,0:T(8,128)S(1)} %collective-permute-done.7.refs_1_, f32[256,512]{1,0:T(8,128)S(1)} %copy-done.1, f32[256,512]{1,0:T(8,128)S(1)} %collective-permute-done.9.refs_3_, ...), custom_call_target="tpu_custom_call" | custom-call | flops 3221225472 | bytes 10485760 | tf_op jit(solution)/shard_map/products/pallas_call | solution.py:86
  71.2 1.3 collective-permute-start.24
  75.5 1.9 %collective-permute-done.24.refs_7_ = f32[64,512]{1,0:T(8,128)S(1)} collective-permute-done((f32[64,512]{1,0:T(8,128)S(1)}, f32[64,512]{1,0:T(8,128)S(1)}, u32[]{:S(2)}, u32[]{:S(2)}) %collective-permute-start.24) | collective-permute-done | bytes 131104 | tf_op jit(solution)/shard_map/ppermute | solution.py:27
  77.5 2.2 %pick.3 = (f32[256,512]{1,0:T(8,128)}, f32[256,512]{1,0:T(8,128)}) custom-call(s32[24]{0:T(128)S(1)} %pad_add_fusion.plan_ref, f32[128,512]{1,0:T(8,128)S(1)} %bitcast.74, f32[128,512]{1,0:T(8,128)S(1)} %collective-permute-done.10.refs_1_, f32[128,512]{1,0:T(8,128)S(1)} %copy-done.5, f32[128,512]{1,0:T(8,128)S(1)} %copy-done.7, ...), custom_call_target="tpu_custom_call" | custom-call | bytes 1048576 | tf_op jit(solution)/shard_map/pick/pallas_call | solution.py:111
  81.0 3.0 %collective-permute-start.27 = (f32[256,512]{1,0:T(8,128)}, f32[256,512]{1,0:T(8,128)S(1)}, u32[]{:S(2)}, u32[]{:S(2)}) collective-permute-start(f32[256,512]{1,0:T(8,128)} %get-tuple-element.92), channel_id=1, source_target_pairs={{0,72},{1,73},{2,74},{3,75},{4,76},{5,77},{6,78},{7,79},{8,64},{9,... | collective-permute-start | bytes 1572872 | tf_op jit(solution)/shard_map/ppermute | solution.py:27
  85.1 5.7 %products.7 = (f32[256,512]{1,0:T(8,128)S(1)}, f32[256,512]{1,0:T(8,128)S(1)}) custom-call(s32[3]{0:T(128)S(1)} %multiply_add_fusion.at_ref, f32[384,512]{1,0:T(8,128)S(1)} %collective-permute-done.13.refs_0_.refs_8_, f32[384,512]{1,0:T(8,128)S(1)} %collective-permute-done.14.refs_1_, f32[8192,512]{1,0:T(8,128)} %bitcast.87, ...), custom_call_target="tpu_custom_call" | custom-call | flops 2415919104 | bytes 7864320 | tf_op jit(solution)/shard_map/products/pallas_call | solution.py:86
  90.9 2.8 %products.8 = (f32[256,512]{1,0:T(8,128)S(1)}, f32[256,512]{1,0:T(8,128)S(1)}) custom-call(s32[1]{0:T(128)S(6)} %add.113.at_ref, f32[128,512]{1,0:T(8,128)} %collective-permute-done.18.refs_0_, f32[128,512]{1,0:T(8,128)} %collective-permute-done.19.refs_1_, f32[8192,512]{1,0:T(8,128)} %bitcast.88, f32[8192,512]{1,0:T(8,128)} %collective-permute-done.15.refs_5_.refs_3_, ...), custom_call_target="tpu_custom_call" | custom-call | flops 805306368 | bytes 2621440 | tf_op jit(solution)/shard_map/products/pallas_call | solution.py:86
  95.0 1.2 collective-permute-start.30
  96.1 2.2 %collective-permute-start.31 = (f32[384,512]{1,0:T(8,128)S(1)}, f32[384,512]{1,0:T(8,128)S(1)}, u32[]{:S(2)}, u32[]{:S(2)}) collective-permute-start(f32[384,512]{1,0:T(8,128)S(1)} %get-tuple-element.123), channel_id=1, source_target_pairs={{0,6},{1,7},{2,4},{3,5},{4,2},{5,3},{6,0},{7,1},{8,14},{9,15},{10,... | collective-permute-start | bytes 2359304 | tf_op jit(solution)/shard_map/ppermute | solution.py:27
  100.2 7.2 %products.9 = (f32[256,512]{1,0:T(8,128)S(1)}, f32[256,512]{1,0:T(8,128)S(1)}) custom-call(s32[4]{0:T(128)S(1)} %multiply_add_fusion.1.at_ref, f32[256,512]{1,0:T(8,128)} %get-tuple-element.91.refs_0_, f32[256,512]{1,0:T(8,128)S(1)} %collective-permute-done.25.refs_1_, f32[256,512]{1,0:T(8,128)} %collective-permute-done.26.refs_2_, ...), custom_call_target="tpu_custom_call" | custom-call | flops 3221225472 | bytes 10485760 | tf_op jit(solution)/shard_map/products/pallas_call | solution.py:86
  108.2 6.8 %collective-permute-done.30.refs_0_ = f32[384,512]{1,0:T(8,128)S(1)} collective-permute-done((f32[384,512]{1,0:T(8,128)S(1)}, f32[384,512]{1,0:T(8,128)S(1)}, u32[]{:S(2)}, u32[]{:S(2)}) %collective-permute-start.30) | collective-permute-done | bytes 786464 | tf_op jit(solution)/shard_map/ppermute | solution.py:27
  115.0 2.0 %collective-permute-done.31.refs_1_ = f32[384,512]{1,0:T(8,128)S(1)} collective-permute-done((f32[384,512]{1,0:T(8,128)S(1)}, f32[384,512]{1,0:T(8,128)S(1)}, u32[]{:S(2)}, u32[]{:S(2)}) %collective-permute-start.31) | collective-permute-done | bytes 786464 | tf_op jit(solution)/shard_map/ppermute | solution.py:27
  117.2 2.3 %collective-permute-start.36 = (f32[128,512]{1,0:T(8,128)S(1)}, f32[128,512]{1,0:T(8,128)S(1)}, u32[]{:S(2)}, u32[]{:S(2)}) collective-permute-start(f32[128,512]{1,0:T(8,128)S(1)} %slice_bitcast_fusion), channel_id=1, source_target_pairs={{0,6},{1,7},{2,4},{3,5},{4,2},{5,3},{6,0},{7,1},{8,14},{9,15},{10,... | collective-permute-start | bytes 786440 | tf_op jit(solution)/shard_map/ppermute | solution.py:27
  120.8 5.8 %products.10 = (f32[256,512]{1,0:T(8,128)S(1)}, f32[256,512]{1,0:T(8,128)S(1)}) custom-call(s32[3]{0:T(128)S(1)} %multiply_add_fusion.at_ref, f32[384,512]{1,0:T(8,128)S(1)} %collective-permute-done.30.refs_0_, f32[384,512]{1,0:T(8,128)S(1)} %collective-permute-done.31.refs_1_, f32[8192,512]{1,0:T(8,128)} %bitcast.90, ...), custom_call_target="tpu_custom_call" | custom-call | flops 2415919104 | bytes 7864320 | tf_op jit(solution)/shard_map/products/pallas_call | solution.py:86
  126.6 2.6 %products.11 = (f32[256,512]{1,0:T(8,128)S(1)}, f32[256,512]{1,0:T(8,128)S(1)}) custom-call(s32[1]{0:T(128)S(6)} %add.113.at_ref, f32[128,512]{1,0:T(8,128)S(1)} %collective-permute-done.35.refs_0_, f32[128,512]{1,0:T(8,128)S(1)} %collective-permute-done.36.refs_1_, f32[8192,512]{1,0:T(8,128)} %bitcast.91, ...), custom_call_target="tpu_custom_call" | custom-call | flops 805306368 | bytes 2621440 | tf_op jit(solution)/shard_map/products/pallas_call | solution.py:86
  129.6 1.2 collective-permute-done.29.refs_2_
  132.1 1.4 collective-permute-start.33
  134.8 2.2 %collective-permute-start.39 = (f32[64,512]{1,0:T(8,128)S(1)}, f32[64,512]{1,0:T(8,128)S(1)}, u32[]{:S(2)}, u32[]{:S(2)}) collective-permute-start(f32[64,512]{1,0:T(8,128)S(1)} %get-tuple-element.115), channel_id=1, source_target_pairs={{0,48},{1,49},{2,50},{3,51},{4,52},{5,53},{6,54},{7,55},{8,56},{9,... | collective-permute-start | bytes 393224 | tf_op jit(solution)/shard_map/ppermute | solution.py:27
  137.0 3.2 %collective-permute-done.32.refs_1_ = f32[128,512]{1,0:T(8,128)S(1)} collective-permute-done((f32[128,512]{1,0:T(8,128)S(1)}, f32[128,512]{1,0:T(8,128)S(1)}, u32[]{:S(2)}, u32[]{:S(2)}) %collective-permute-start.32) | collective-permute-done | bytes 262176 | tf_op jit(solution)/shard_map/ppermute | solution.py:27
  140.2 2.2 %collective-permute-done.33.refs_2_ = f32[128,512]{1,0:T(8,128)S(1)} collective-permute-done((f32[128,512]{1,0:T(8,128)S(1)}, f32[128,512]{1,0:T(8,128)S(1)}, u32[]{:S(2)}, u32[]{:S(2)}) %collective-permute-start.33) | collective-permute-done | bytes 262176 | tf_op jit(solution)/shard_map/ppermute | solution.py:27
  144.5 2.3 %collective-permute-start.41 = (f32[192,512]{1,0:T(8,128)S(1)}, f32[192,512]{1,0:T(8,128)S(1)}, u32[]{:S(2)}, u32[]{:S(2)}) collective-permute-start(f32[192,512]{1,0:T(8,128)S(1)} %get-tuple-element.119), channel_id=1, source_target_pairs={{0,48},{1,49},{2,50},{3,51},{4,52},{5,53},{6,54},{7,55},{8,56},{9,... | collective-permute-start | bytes 1179656 | tf_op jit(solution)/shard_map/ppermute | solution.py:27
  146.8 7.1 %collective-permute-done.40.refs_1_ = f32[192,512]{1,0:T(8,128)S(1)} collective-permute-done((f32[192,512]{1,0:T(8,128)S(1)}, f32[192,512]{1,0:T(8,128)S(1)}, u32[]{:S(2)}, u32[]{:S(2)}) %collective-permute-start.40) | collective-permute-done | bytes 393248 | tf_op jit(solution)/shard_map/ppermute | solution.py:27
  154.0 1.5 collective-permute-done.41.refs_2_
  156.2 1.1 collective-permute-start.42
  157.3 2.4 %collective-permute-start.43 = (f32[128,512]{1,0:T(8,128)S(1)}, f32[128,512]{1,0:T(8,128)S(1)}, u32[]{:S(2)}, u32[]{:S(2)}) collective-permute-start(f32[128,512]{1,0:T(8,128)S(1)} %get-tuple-element.121), channel_id=1, source_target_pairs={{0,48},{1,49},{2,50},{3,51},{4,52},{5,53},{6,54},{7,55},{8,56},{9,... | collective-permute-start | bytes 786440 | tf_op jit(solution)/shard_map/ppermute | solution.py:27
  159.7 3.0 %collective-permute-done.42.refs_1_ = f32[128,512]{1,0:T(8,128)S(1)} collective-permute-done((f32[128,512]{1,0:T(8,128)S(1)}, f32[128,512]{1,0:T(8,128)S(1)}, u32[]{:S(2)}, u32[]{:S(2)}) %collective-permute-start.42) | collective-permute-done | bytes 262176 | tf_op jit(solution)/shard_map/ppermute | solution.py:27
  162.6 2.3 %collective-permute-done.43.refs_2_ = f32[128,512]{1,0:T(8,128)S(1)} collective-permute-done((f32[128,512]{1,0:T(8,128)S(1)}, f32[128,512]{1,0:T(8,128)S(1)}, u32[]{:S(2)}, u32[]{:S(2)}) %collective-permute-start.43) | collective-permute-done | bytes 262176 | tf_op jit(solution)/shard_map/ppermute | solution.py:27
  164.9 1.1 collective-permute-done.44.refs_3_
  (124 shorter events, 32.2 us)
Async XLA Ops:
  0.0 61.4 %collective-permute-start.15 = (f32[8192,512]{1,0:T(8,128)}, f32[8192,512]{1,0:T(8,128)}, u32[]{:S(2)}, u32[]{:S(2)}) collective-permute-start(f32[8192,512]{1,0:T(8,128)} %bitcast.85), channel_id=1, source_target_pairs={{0,1},{1,0},{2,3},{3,2},{4,5},{5,4},{6,7},{7,6},{8,9},{9,8},{10,11... | collective-permute-start | bytes 50331656 | tf_op jit(solution)/shard_map/ppermute | solution.py:27
  1.1 52.5 %copy-start.2 = (f32[2,64,512]{2,1,0:T(8,128)}, f32[2,64,512]{2,1,0:T(8,128)S(1)}, u32[]{:S(2)}) copy-start(f32[2,64,512]{2,1,0:T(8,128)S(1)} %get-tuple-element.128) | copy-start | bytes 786436
  1.1 8.8 %collective-permute-start.1 = (f32[128,512]{1,0:T(8,128)S(1)}, f32[128,512]{1,0:T(8,128)S(1)}, u32[]{:S(2)}, u32[]{:S(2)}) collective-permute-start(f32[128,512]{1,0:T(8,128)S(1)} %bitcast.75), channel_id=1, source_target_pairs={{0,16},{1,17},{2,18},{3,19},{4,20},{5,21},{6,22},{7,23},{8,24},{9,... | collective-permute-start | bytes 786440 | tf_op jit(solution)/shard_map/ppermute | solution.py:27
  2.7 9.6 %collective-permute-start.2 = (f32[128,512]{1,0:T(8,128)S(1)}, f32[128,512]{1,0:T(8,128)S(1)}, u32[]{:S(2)}, u32[]{:S(2)}) collective-permute-start(f32[128,512]{1,0:T(8,128)S(1)} %bitcast.76), channel_id=1, source_target_pairs={{0,48},{1,49},{2,50},{3,51},{4,52},{5,53},{6,54},{7,55},{8,56},{9,... | collective-permute-start | bytes 786440 | tf_op jit(solution)/shard_map/ppermute | solution.py:27
  4.8 8.3 %collective-permute-start = (f32[128,512]{1,0:T(8,128)S(1)}, f32[128,512]{1,0:T(8,128)S(1)}, u32[]{:S(2)}, u32[]{:S(2)}) collective-permute-start(f32[128,512]{1,0:T(8,128)S(1)} %bitcast.77), channel_id=1, source_target_pairs={{0,64},{1,65},{2,66},{3,67},{4,68},{5,69},{6,70},{7,71},{8,72},{9,... | collective-permute-start | bytes 786440 | tf_op jit(solution)/shard_map/ppermute | solution.py:27
  13.3 12.3 %collective-permute-start.3 = (f32[192,512]{1,0:T(8,128)S(1)}, f32[192,512]{1,0:T(8,128)S(1)}, u32[]{:S(2)}, u32[]{:S(2)}) collective-permute-start(f32[192,512]{1,0:T(8,128)S(1)} %get-tuple-element.132), channel_id=1, source_target_pairs={{0,16},{1,17},{2,18},{3,19},{4,20},{5,21},{6,22},{7,23},{8,24},{9,... | collective-permute-start | bytes 1179656 | tf_op jit(solution)/shard_map/ppermute | solution.py:27
  13.9 11.2 %collective-permute-start.4 = (f32[192,512]{1,0:T(8,128)S(1)}, f32[192,512]{1,0:T(8,128)S(1)}, u32[]{:S(2)}, u32[]{:S(2)}) collective-permute-start(f32[192,512]{1,0:T(8,128)S(1)} %get-tuple-element.131), channel_id=1, source_target_pairs={{0,48},{1,49},{2,50},{3,51},{4,52},{5,53},{6,54},{7,55},{8,56},{9,... | collective-permute-start | bytes 1179656 | tf_op jit(solution)/shard_map/ppermute | solution.py:27
  25.2 5.0 %collective-permute-start.5 = (f32[64,512]{1,0:T(8,128)S(1)}, f32[64,512]{1,0:T(8,128)S(1)}, u32[]{:S(2)}, u32[]{:S(2)}) collective-permute-start(f32[64,512]{1,0:T(8,128)S(1)} %bitcast.107), channel_id=1, source_target_pairs={{0,16},{1,17},{2,18},{3,19},{4,20},{5,21},{6,22},{7,23},{8,24},{9,... | collective-permute-start | bytes 393224 | tf_op jit(solution)/shard_map/ppermute | solution.py:27
  25.6 6.3 %collective-permute-start.6 = (f32[64,512]{1,0:T(8,128)S(1)}, f32[64,512]{1,0:T(8,128)S(1)}, u32[]{:S(2)}, u32[]{:S(2)}) collective-permute-start(f32[64,512]{1,0:T(8,128)S(1)} %bitcast.108), channel_id=1, source_target_pairs={{0,48},{1,49},{2,50},{3,51},{4,52},{5,53},{6,54},{7,55},{8,56},{9,... | collective-permute-start | bytes 393224 | tf_op jit(solution)/shard_map/ppermute | solution.py:27
  32.8 20.7 %copy-start.8 = (f32[256,512]{1,0:T(8,128)}, f32[256,512]{1,0:T(8,128)S(1)}, u32[]{:S(2)}) copy-start(f32[256,512]{1,0:T(8,128)S(1)} %get-tuple-element.64.refs_0_) | copy-start | bytes 1572868
  32.9 6.5 %collective-permute-start.10 = (f32[128,512]{1,0:T(8,128)S(1)}, f32[128,512]{1,0:T(8,128)S(1)}, u32[]{:S(2)}, u32[]{:S(2)}) collective-permute-start(f32[128,512]{1,0:T(8,128)S(1)} %bitcast.71), channel_id=1, source_target_pairs={{0,64},{1,65},{2,66},{3,67},{4,68},{5,69},{6,70},{7,71},{8,72},{9,... | collective-permute-start | bytes 786440 | tf_op jit(solution)/shard_map/ppermute | solution.py:27
  34.5 8.5 %collective-permute-start.11 = (f32[128,512]{1,0:T(8,128)S(1)}, f32[128,512]{1,0:T(8,128)S(1)}, u32[]{:S(2)}, u32[]{:S(2)}) collective-permute-start(f32[128,512]{1,0:T(8,128)S(1)} %bitcast.72), channel_id=1, source_target_pairs={{0,16},{1,17},{2,18},{3,19},{4,20},{5,21},{6,22},{7,23},{8,24},{9,... | collective-permute-start | bytes 786440 | tf_op jit(solution)/shard_map/ppermute | solution.py:27
  35.1 15.5 %collective-permute-start.7 = (f32[256,512]{1,0:T(8,128)S(1)}, f32[256,512]{1,0:T(8,128)S(1)}, u32[]{:S(2)}, u32[]{:S(2)}) collective-permute-start(f32[256,512]{1,0:T(8,128)S(1)} %get-tuple-element.64.refs_0_), channel_id=1, source_target_pairs={{0,2},{1,3},{2,0},{3,1},{4,6},{5,7},{6,4},{7,5},{8,10},{9,11},{10,... | collective-permute-start | bytes 1572872 | tf_op jit(solution)/shard_map/ppermute | solution.py:27
  36.6 13.9 %collective-permute-start.8 = (f32[256,512]{1,0:T(8,128)S(1)}, f32[256,512]{1,0:T(8,128)S(1)}, u32[]{:S(2)}, u32[]{:S(2)}) collective-permute-start(f32[256,512]{1,0:T(8,128)S(1)} %get-tuple-element.64.refs_0_), channel_id=1, source_target_pairs={{0,6},{1,7},{2,4},{3,5},{4,2},{5,3},{6,0},{7,1},{8,14},{9,15},{10,... | collective-permute-start | bytes 1572872 | tf_op jit(solution)/shard_map/ppermute | solution.py:27
  39.3 11.3 %collective-permute-start.9 = (f32[256,512]{1,0:T(8,128)S(1)}, f32[256,512]{1,0:T(8,128)S(1)}, u32[]{:S(2)}, u32[]{:S(2)}) collective-permute-start(f32[256,512]{1,0:T(8,128)S(1)} %get-tuple-element.65), channel_id=1, source_target_pairs={{0,72},{1,73},{2,74},{3,75},{4,76},{5,77},{6,78},{7,79},{8,64},{9,... | collective-permute-start | bytes 1572872 | tf_op jit(solution)/shard_map/ppermute | solution.py:27
  43.0 7.6 %collective-permute-start.12 = (f32[128,512]{1,0:T(8,128)S(1)}, f32[128,512]{1,0:T(8,128)S(1)}, u32[]{:S(2)}, u32[]{:S(2)}) collective-permute-start(f32[128,512]{1,0:T(8,128)S(1)} %bitcast.73), channel_id=1, source_target_pairs={{0,48},{1,49},{2,50},{3,51},{4,52},{5,53},{6,54},{7,55},{8,56},{9,... | collective-permute-start | bytes 786440 | tf_op jit(solution)/shard_map/ppermute | solution.py:27
  52.0 20.5 %collective-permute-start.13 = (f32[384,512]{1,0:T(8,128)}, f32[384,512]{1,0:T(8,128)S(1)}, u32[]{:S(2)}, u32[]{:S(2)}) collective-permute-start(f32[384,512]{1,0:T(8,128)} %get-tuple-element.126), channel_id=1, source_target_pairs={{0,2},{1,3},{2,0},{3,1},{4,6},{5,7},{6,4},{7,5},{8,10},{9,11},{10,... | collective-permute-start | bytes 2359304 | tf_op jit(solution)/shard_map/ppermute | solution.py:27
  53.6 18.9 %collective-permute-start.14 = (f32[384,512]{1,0:T(8,128)}, f32[384,512]{1,0:T(8,128)S(1)}, u32[]{:S(2)}, u32[]{:S(2)}) collective-permute-start(f32[384,512]{1,0:T(8,128)} %get-tuple-element.125), channel_id=1, source_target_pairs={{0,6},{1,7},{2,4},{3,5},{4,2},{5,3},{6,0},{7,1},{8,14},{9,15},{10,... | collective-permute-start | bytes 2359304 | tf_op jit(solution)/shard_map/ppermute | solution.py:27
  57.8 12.7 %collective-permute-start.16 = (f32[192,512]{1,0:T(8,128)S(1)}, f32[192,512]{1,0:T(8,128)S(1)}, u32[]{:S(2)}, u32[]{:S(2)}) collective-permute-start(f32[192,512]{1,0:T(8,128)S(1)} %get-tuple-element.130), channel_id=1, source_target_pairs={{0,16},{1,17},{2,18},{3,19},{4,20},{5,21},{6,22},{7,23},{8,24},{9,... | collective-permute-start | bytes 1179656 | tf_op jit(solution)/shard_map/ppermute | solution.py:27
  58.2 12.2 %collective-permute-start.17 = (f32[192,512]{1,0:T(8,128)S(1)}, f32[192,512]{1,0:T(8,128)S(1)}, u32[]{:S(2)}, u32[]{:S(2)}) collective-permute-start(f32[192,512]{1,0:T(8,128)S(1)} %get-tuple-element.129), channel_id=1, source_target_pairs={{0,48},{1,49},{2,50},{3,51},{4,52},{5,53},{6,54},{7,55},{8,56},{9,... | collective-permute-start | bytes 1179656 | tf_op jit(solution)/shard_map/ppermute | solution.py:27
  63.5 20.5 %copy-start.12 = (s32[3]{0:T(128)S(1)}, s32[3]{0:T(128)}, u32[]{:S(2)}) copy-start(s32[3]{0:T(128)} %constant.164.clone) | copy-start | bytes 40
  70.5 5.0 %collective-permute-start.23 = (f32[64,512]{1,0:T(8,128)S(1)}, f32[64,512]{1,0:T(8,128)S(1)}, u32[]{:S(2)}, u32[]{:S(2)}) collective-permute-start(f32[64,512]{1,0:T(8,128)S(1)} %bitcast.105), channel_id=1, source_target_pairs={{0,16},{1,17},{2,18},{3,19},{4,20},{5,21},{6,22},{7,23},{8,24},{9,... | collective-permute-start | bytes 393224 | tf_op jit(solution)/shard_map/ppermute | solution.py:27
  71.2 6.3 %collective-permute-start.24 = (f32[64,512]{1,0:T(8,128)S(1)}, f32[64,512]{1,0:T(8,128)S(1)}, u32[]{:S(2)}, u32[]{:S(2)}) collective-permute-start(f32[64,512]{1,0:T(8,128)S(1)} %bitcast.106), channel_id=1, source_target_pairs={{0,48},{1,49},{2,50},{3,51},{4,52},{5,53},{6,54},{7,55},{8,56},{9,... | collective-permute-start | bytes 393224 | tf_op jit(solution)/shard_map/ppermute | solution.py:27
  73.3 17.6 %collective-permute-start.18 = (f32[128,512]{1,0:T(8,128)}, f32[128,512]{1,0:T(8,128)}, u32[]{:S(2)}, u32[]{:S(2)}) collective-permute-start(f32[128,512]{1,0:T(8,128)} %slice_bitcast_fusion.5), channel_id=1, source_target_pairs={{0,2},{1,3},{2,0},{3,1},{4,6},{5,7},{6,4},{7,5},{8,10},{9,11},{10,... | collective-permute-start | bytes 786440 | tf_op jit(solution)/shard_map/ppermute | solution.py:27
  74.7 16.2 %collective-permute-start.19 = (f32[128,512]{1,0:T(8,128)}, f32[128,512]{1,0:T(8,128)}, u32[]{:S(2)}, u32[]{:S(2)}) collective-permute-start(f32[128,512]{1,0:T(8,128)} %slice_bitcast_fusion.4), channel_id=1, source_target_pairs={{0,6},{1,7},{2,4},{3,5},{4,2},{5,3},{6,0},{7,1},{8,14},{9,15},{10,... | collective-permute-start | bytes 786440 | tf_op jit(solution)/shard_map/ppermute | solution.py:27
  79.7 14.0 %collective-permute-start.25 = (f32[256,512]{1,0:T(8,128)}, f32[256,512]{1,0:T(8,128)S(1)}, u32[]{:S(2)}, u32[]{:S(2)}) collective-permute-start(f32[256,512]{1,0:T(8,128)} %get-tuple-element.91.refs_0_), channel_id=1, source_target_pairs={{0,2},{1,3},{2,0},{3,1},{4,6},{5,7},{6,4},{7,5},{8,10},{9,11},{10,... | collective-permute-start | bytes 1572872 | tf_op jit(solution)/shard_map/ppermute | solution.py:27
  80.4 13.4 %collective-permute-start.26 = (f32[256,512]{1,0:T(8,128)}, f32[256,512]{1,0:T(8,128)}, u32[]{:S(2)}, u32[]{:S(2)}) collective-permute-start(f32[256,512]{1,0:T(8,128)} %get-tuple-element.91.refs_0_), channel_id=1, source_target_pairs={{0,6},{1,7},{2,4},{3,5},{4,2},{5,3},{6,0},{7,1},{8,14},{9,15},{10,... | collective-permute-start | bytes 1572872 | tf_op jit(solution)/shard_map/ppermute | solution.py:27
  81.0 12.7 %collective-permute-start.27 = (f32[256,512]{1,0:T(8,128)}, f32[256,512]{1,0:T(8,128)S(1)}, u32[]{:S(2)}, u32[]{:S(2)}) collective-permute-start(f32[256,512]{1,0:T(8,128)} %get-tuple-element.92), channel_id=1, source_target_pairs={{0,72},{1,73},{2,74},{3,75},{4,76},{5,77},{6,78},{7,79},{8,64},{9,... | collective-permute-start | bytes 1572872 | tf_op jit(solution)/shard_map/ppermute | solution.py:27
  93.6 4.7 %collective-permute-start.20 = (f32[256,512]{1,0:T(8,128)S(1)}, f32[256,512]{1,0:T(8,128)S(1)}, u32[]{:S(2)}, u32[]{:S(2)}) collective-permute-start(f32[256,512]{1,0:T(8,128)S(1)} %get-tuple-element.80), channel_id=1, source_target_pairs={{0,1},{1,0},{2,3},{3,2},{4,5},{5,4},{6,7},{7,6},{8,9},{9,8},{10,11... | collective-permute-start | bytes 1572872 | tf_op jit(solution)/shard_map/ppermute | solution.py:27
  95.0 20.0 %collective-permute-start.30 = (f32[384,512]{1,0:T(8,128)S(1)}, f32[384,512]{1,0:T(8,128)S(1)}, u32[]{:S(2)}, u32[]{:S(2)}) collective-permute-start(f32[384,512]{1,0:T(8,128)S(1)} %get-tuple-element.124), channel_id=1, source_target_pairs={{0,2},{1,3},{2,0},{3,1},{4,6},{5,7},{6,4},{7,5},{8,10},{9,11},{10,... | collective-permute-start | bytes 2359304 | tf_op jit(solution)/shard_map/ppermute | solution.py:27
  96.1 20.9 %collective-permute-start.31 = (f32[384,512]{1,0:T(8,128)S(1)}, f32[384,512]{1,0:T(8,128)S(1)}, u32[]{:S(2)}, u32[]{:S(2)}) collective-permute-start(f32[384,512]{1,0:T(8,128)S(1)} %get-tuple-element.123), channel_id=1, source_target_pairs={{0,6},{1,7},{2,4},{3,5},{4,2},{5,3},{6,0},{7,1},{8,14},{9,15},{10,... | collective-permute-start | bytes 2359304 | tf_op jit(solution)/shard_map/ppermute | solution.py:27
  99.0 8.5 %collective-permute-start.21 = (f32[64,512]{1,0:T(8,128)S(1)}, f32[64,512]{1,0:T(8,128)S(1)}, u32[]{:S(2)}, u32[]{:S(2)}) collective-permute-start(f32[64,512]{1,0:T(8,128)S(1)} %get-tuple-element.82), channel_id=1, source_target_pairs={{0,16},{1,17},{2,18},{3,19},{4,20},{5,21},{6,22},{7,23},{8,24},{9,... | collective-permute-start | bytes 393224 | tf_op jit(solution)/shard_map/ppermute | solution.py:27
  99.3 8.2 %collective-permute-start.22 = (f32[64,512]{1,0:T(8,128)S(1)}, f32[64,512]{1,0:T(8,128)S(1)}, u32[]{:S(2)}, u32[]{:S(2)}) collective-permute-start(f32[64,512]{1,0:T(8,128)S(1)} %get-tuple-element.83), channel_id=1, source_target_pairs={{0,48},{1,49},{2,50},{3,51},{4,52},{5,53},{6,54},{7,55},{8,56},{9,... | collective-permute-start | bytes 393224 | tf_op jit(solution)/shard_map/ppermute | solution.py:27
  117.1 9.5 %collective-permute-start.35 = (f32[128,512]{1,0:T(8,128)S(1)}, f32[128,512]{1,0:T(8,128)S(1)}, u32[]{:S(2)}, u32[]{:S(2)}) collective-permute-start(f32[128,512]{1,0:T(8,128)S(1)} %slice_bitcast_fusion.1), channel_id=1, source_target_pairs={{0,2},{1,3},{2,0},{3,1},{4,6},{5,7},{6,4},{7,5},{8,10},{9,11},{10,... | collective-permute-start | bytes 786440 | tf_op jit(solution)/shard_map/ppermute | solution.py:27
  117.2 9.3 %collective-permute-start.36 = (f32[128,512]{1,0:T(8,128)S(1)}, f32[128,512]{1,0:T(8,128)S(1)}, u32[]{:S(2)}, u32[]{:S(2)}) collective-permute-start(f32[128,512]{1,0:T(8,128)S(1)} %slice_bitcast_fusion), channel_id=1, source_target_pairs={{0,6},{1,7},{2,4},{3,5},{4,2},{5,3},{6,0},{7,1},{8,14},{9,15},{10,... | collective-permute-start | bytes 786440 | tf_op jit(solution)/shard_map/ppermute | solution.py:27
  119.5 10.1 %collective-permute-start.28 = (f32[192,512]{1,0:T(8,128)S(1)}, f32[192,512]{1,0:T(8,128)S(1)}, u32[]{:S(2)}, u32[]{:S(2)}) collective-permute-start(f32[192,512]{1,0:T(8,128)S(1)} %get-tuple-element.96), channel_id=1, source_target_pairs={{0,16},{1,17},{2,18},{3,19},{4,20},{5,21},{6,22},{7,23},{8,24},{9,... | collective-permute-start | bytes 1179656 | tf_op jit(solution)/shard_map/ppermute | solution.py:27
  119.7 11.1 %collective-permute-start.29 = (f32[192,512]{1,0:T(8,128)S(1)}, f32[192,512]{1,0:T(8,128)S(1)}, u32[]{:S(2)}, u32[]{:S(2)}) collective-permute-start(f32[192,512]{1,0:T(8,128)S(1)} %get-tuple-element.97), channel_id=1, source_target_pairs={{0,48},{1,49},{2,50},{3,51},{4,52},{5,53},{6,54},{7,55},{8,56},{9,... | collective-permute-start | bytes 1179656 | tf_op jit(solution)/shard_map/ppermute | solution.py:27
  129.2 4.3 %collective-permute-start.37 = (f32[256,512]{1,0:T(8,128)S(1)}, f32[256,512]{1,0:T(8,128)S(1)}, u32[]{:S(2)}, u32[]{:S(2)}) collective-permute-start(f32[256,512]{1,0:T(8,128)S(1)} %get-tuple-element.112), channel_id=1, source_target_pairs={{0,1},{1,0},{2,3},{3,2},{4,5},{5,4},{6,7},{7,6},{8,9},{9,8},{10,11... | collective-permute-start | bytes 1572872 | tf_op jit(solution)/shard_map/ppermute | solution.py:27
  131.5 8.6 %collective-permute-start.32 = (f32[128,512]{1,0:T(8,128)S(1)}, f32[128,512]{1,0:T(8,128)S(1)}, u32[]{:S(2)}, u32[]{:S(2)}) collective-permute-start(f32[128,512]{1,0:T(8,128)S(1)} %get-tuple-element.105), channel_id=1, source_target_pairs={{0,16},{1,17},{2,18},{3,19},{4,20},{5,21},{6,22},{7,23},{8,24},{9,... | collective-permute-start | bytes 786440 | tf_op jit(solution)/shard_map/ppermute | solution.py:27
  132.1 10.2 %collective-permute-start.33 = (f32[128,512]{1,0:T(8,128)S(1)}, f32[128,512]{1,0:T(8,128)S(1)}, u32[]{:S(2)}, u32[]{:S(2)}) collective-permute-start(f32[128,512]{1,0:T(8,128)S(1)} %get-tuple-element.106), channel_id=1, source_target_pairs={{0,48},{1,49},{2,50},{3,51},{4,52},{5,53},{6,54},{7,55},{8,56},{9,... | collective-permute-start | bytes 786440 | tf_op jit(solution)/shard_map/ppermute | solution.py:27
  133.5 8.8 %collective-permute-start.34 = (f32[128,512]{1,0:T(8,128)S(1)}, f32[128,512]{1,0:T(8,128)S(1)}, u32[]{:S(2)}, u32[]{:S(2)}) collective-permute-start(f32[128,512]{1,0:T(8,128)S(1)} %get-tuple-element.107), channel_id=1, source_target_pairs={{0,64},{1,65},{2,66},{3,67},{4,68},{5,69},{6,70},{7,71},{8,72},{9,... | collective-permute-start | bytes 786440 | tf_op jit(solution)/shard_map/ppermute | solution.py:27
  134.2 8.8 %collective-permute-start.38 = (f32[64,512]{1,0:T(8,128)S(1)}, f32[64,512]{1,0:T(8,128)S(1)}, u32[]{:S(2)}, u32[]{:S(2)}) collective-permute-start(f32[64,512]{1,0:T(8,128)S(1)} %get-tuple-element.114), channel_id=1, source_target_pairs={{0,16},{1,17},{2,18},{3,19},{4,20},{5,21},{6,22},{7,23},{8,24},{9,... | collective-permute-start | bytes 393224 | tf_op jit(solution)/shard_map/ppermute | solution.py:27
  134.8 8.9 %collective-permute-start.39 = (f32[64,512]{1,0:T(8,128)S(1)}, f32[64,512]{1,0:T(8,128)S(1)}, u32[]{:S(2)}, u32[]{:S(2)}) collective-permute-start(f32[64,512]{1,0:T(8,128)S(1)} %get-tuple-element.115), channel_id=1, source_target_pairs={{0,48},{1,49},{2,50},{3,51},{4,52},{5,53},{6,54},{7,55},{8,56},{9,... | collective-permute-start | bytes 393224 | tf_op jit(solution)/shard_map/ppermute | solution.py:27
  144.4 9.5 %collective-permute-start.40 = (f32[192,512]{1,0:T(8,128)S(1)}, f32[192,512]{1,0:T(8,128)S(1)}, u32[]{:S(2)}, u32[]{:S(2)}) collective-permute-start(f32[192,512]{1,0:T(8,128)S(1)} %get-tuple-element.118), channel_id=1, source_target_pairs={{0,16},{1,17},{2,18},{3,19},{4,20},{5,21},{6,22},{7,23},{8,24},{9,... | collective-permute-start | bytes 1179656 | tf_op jit(solution)/shard_map/ppermute | solution.py:27
  144.5 10.9 %collective-permute-start.41 = (f32[192,512]{1,0:T(8,128)S(1)}, f32[192,512]{1,0:T(8,128)S(1)}, u32[]{:S(2)}, u32[]{:S(2)}) collective-permute-start(f32[192,512]{1,0:T(8,128)S(1)} %get-tuple-element.119), channel_id=1, source_target_pairs={{0,48},{1,49},{2,50},{3,51},{4,52},{5,53},{6,54},{7,55},{8,56},{9,... | collective-permute-start | bytes 1179656 | tf_op jit(solution)/shard_map/ppermute | solution.py:27
  156.2 6.5 %collective-permute-start.42 = (f32[128,512]{1,0:T(8,128)S(1)}, f32[128,512]{1,0:T(8,128)S(1)}, u32[]{:S(2)}, u32[]{:S(2)}) collective-permute-start(f32[128,512]{1,0:T(8,128)S(1)} %get-tuple-element.120), channel_id=1, source_target_pairs={{0,16},{1,17},{2,18},{3,19},{4,20},{5,21},{6,22},{7,23},{8,24},{9,... | collective-permute-start | bytes 786440 | tf_op jit(solution)/shard_map/ppermute | solution.py:27
  157.3 7.6 %collective-permute-start.43 = (f32[128,512]{1,0:T(8,128)S(1)}, f32[128,512]{1,0:T(8,128)S(1)}, u32[]{:S(2)}, u32[]{:S(2)}) collective-permute-start(f32[128,512]{1,0:T(8,128)S(1)} %get-tuple-element.121), channel_id=1, source_target_pairs={{0,48},{1,49},{2,50},{3,51},{4,52},{5,53},{6,54},{7,55},{8,56},{9,... | collective-permute-start | bytes 786440 | tf_op jit(solution)/shard_map/ppermute | solution.py:27
  159.7 6.4 %collective-permute-start.44 = (f32[128,512]{1,0:T(8,128)S(1)}, f32[128,512]{1,0:T(8,128)S(1)}, u32[]{:S(2)}, u32[]{:S(2)}) collective-permute-start(f32[128,512]{1,0:T(8,128)S(1)} %get-tuple-element.122), channel_id=1, source_target_pairs={{0,64},{1,65},{2,66},{3,67},{4,68},{5,69},{6,70},{7,71},{8,72},{9,... | collective-permute-start | bytes 786440 | tf_op jit(solution)/shard_map/ppermute | solution.py:27
  (11 other events, 92.1 us)

commit v4 on v3

--- a/solution.py
+++ b/solution.py
@@ -11,6 +11,7 @@
 TILE = 128
 SLOTS = 4
 CHUNKS = (64, 64)
+BRIEF = pl.CostEstimate(flops=1, bytes_accessed=1, transcendentals=0)
 
 PLACES = [
     (zl, x, zh, y, c)
@@ -56,52 +57,87 @@
     return hi, (v - hi.astype(jnp.float32)).astype(jnp.bfloat16)
 
 
-def product_kernel(blocks, n_arrays, first, at_ref, *refs):
-    arrays, (own_ref, far_ref), refs = refs[:n_arrays], refs[n_arrays : n_arrays + 2], refs[n_arrays + 2 :]
-    adds, (out_own, out_far) = refs[:2], refs[-2:]
-    step = pl.program_id(0)
-
-    for i, block in enumerate(blocks):
-
-        @pl.when(step == i)
-        def _():
-            parts = [arrays[array][lo : lo + size] for array, lo, size in block]
-            a_hi, a_lo = split(parts[0] if len(parts) == 1 else jnp.concatenate(parts, axis=0))
-            for j, (rhs, out) in enumerate(((own_ref, out_own), (far_ref, out_far))):
-                b_hi, b_lo = split(rhs[...])
-                dot = functools.partial(jnp.dot, preferred_element_type=jnp.float32)
-                term = dot(a_hi, b_hi) + (dot(a_hi, b_lo) + dot(a_lo, b_hi))
-                if i == 0:
-                    out[...] = term if first else adds[j][...] + term
-                else:
-                    out[...] += term
-
-
-def products(arrays, blocks, at, own, far, sums):
+def split_rows(a, width, at, first, parts=None):
+    n, cols = at.shape[0], a.shape[1]
+
+    def kernel(at_ref, a_ref, *refs):
+        def body(a, hi, lo):
+            hi[...], lo[...] = split(a[...])
+
+        pltpu.emit_pipeline(
+            body,
+            grid=(n,),
+            in_specs=[pl.BlockSpec((width, cols), lambda s: (at_ref[s], 0))],
+            out_specs=[pl.BlockSpec((width, cols), lambda s: (s, 0))] * 2,
+        )(a_ref, refs[-1].at[first], refs[-1].at[first + 1])
+
+    before = () if parts is None else (parts,)
+    anywhere = pl.BlockSpec(memory_space=pl.ANY)
+    return pl.pallas_call(
+        kernel,
+        in_specs=[pl.BlockSpec(memory_space=pltpu.SMEM), anywhere] + [anywhere] * len(before),
+        out_specs=anywhere,
+        out_shape=jax.ShapeDtypeStruct((4, n * width, cols), jnp.bfloat16),
+        input_output_aliases={2: 0} if before else {},
+        compiler_params=pltpu.CompilerParams(vmem_limit_bytes=50 * 1024 * 1024),
+        cost_estimate=BRIEF,
+        name="split_rows",
+    )(at, a, *before)
+
+
+def products(arrays, blocks, at, rhs, sums):
     n = len(blocks)
     m = sum(size for _, _, size in blocks[0])
     width = arrays[0].shape[1]
-    cols = own.shape[1]
-    whole = lambda shape: pl.BlockSpec(shape, lambda s, at: (0, 0))
+    cols = rhs.shape[2]
+    dot = functools.partial(jnp.dot, preferred_element_type=jnp.float32)
+
+    def kernel(at_ref, *refs):
+        ins, refs = refs[: len(arrays)], refs[len(arrays) :]
+        rhs_ref, *refs = refs
+        adds, (*outs, held, sems) = refs[: len(sums)], refs[len(sums) :]
+
+        def copies(i):
+            rows = pl.ds(pl.multiple_of(at_ref[i] * width, width), width)
+            return [
+                pltpu.make_async_copy(rhs_ref.at[j, rows], held.at[i, j], sems.at[i, j])
+                for j in range(4)
+            ]
+
+        for i in range(n):
+            for copy in copies(i):
+                copy.start()
+        for i, block in enumerate(blocks):
+            rows = [ins[array][lo : lo + size] for array, lo, size in block]
+            a_hi, a_lo = split(rows[0] if len(rows) == 1 else jnp.concatenate(rows, axis=0))
+            a_both = jnp.concatenate([a_hi, a_lo], axis=0)
+            for copy in copies(i):
+                copy.wait()
+            for j, out in enumerate(outs):
+                upper = dot(a_both, held[i, 2 * j])
+                term = upper[:m] + (upper[m:] + dot(a_hi, held[i, 2 * j + 1]))
+                if i == 0:
+                    out[...] = adds[j][...] + term if sums else term
+                else:
+                    out[...] += term
+
+    vmem = pl.BlockSpec(memory_space=pltpu.VMEM)
     return pl.pallas_call(
-        functools.partial(product_kernel, blocks, len(arrays), not sums),
-        grid_spec=pltpu.PrefetchScalarGridSpec(
-            num_scalar_prefetch=1,
-            grid=(n,),
-            in_specs=[whole(a.shape) for a in arrays]
-            + [pl.BlockSpec((width, cols), lambda s, at: (at[s], 0))] * 2
-            + [whole((m, cols))] * len(sums),
-            out_specs=[whole((m, cols))] * 2,
-        ),
+        kernel,
+        in_specs=[pl.BlockSpec(memory_space=pltpu.SMEM)]
+        + [vmem] * len(arrays)
+        + [pl.BlockSpec(memory_space=pl.ANY)]
+        + [vmem] * len(sums),
+        out_specs=[vmem] * 2,
         out_shape=[jax.ShapeDtypeStruct((m, cols), jnp.float32)] * 2,
+        scratch_shapes=[
+            pltpu.VMEM((n, 4, width, cols), jnp.bfloat16),
+            pltpu.SemaphoreType.DMA((n, 4)),
+        ],
         compiler_params=pltpu.CompilerParams(vmem_limit_bytes=50 * 1024 * 1024),
-        cost_estimate=pl.CostEstimate(
-            flops=12 * n * m * width * cols,
-            bytes_accessed=8 * n * width * cols + 4 * n * m * width,
-            transcendentals=0,
-        ),
+        cost_estimate=BRIEF,
         name="products",
-    )(at, *arrays, own, far, *sums)
+    )(at, *arrays, rhs, *sums)
 
 
 def small_kernel(body, plan, shapes, operands, after=(), name=None):
@@ -116,9 +152,7 @@
         out_specs=[pl.BlockSpec(memory_space=pltpu.VMEM)] * len(shapes),
         out_shape=[jax.ShapeDtypeStruct(s, jnp.float32) for s in shapes],
         compiler_params=pltpu.CompilerParams(vmem_limit_bytes=24 * 1024 * 1024),
-        cost_estimate=pl.CostEstimate(
-            flops=0, bytes_accessed=4 * sum(int(np.prod(s)) for s in shapes), transcendentals=0
-        ),
+        cost_estimate=BRIEF,
         name=name,
     )(plan, *operands, *after)
     return out
@@ -129,11 +163,13 @@
 
 
 def gather_second(near, other, swap, pieces=1):
-    return swap(join(other, half(near[1], 0, pieces)), 0), swap(join(other, half(near[0], 1, pieces)), 1)
+    going = [join(other, half(near[1 - i], i, pieces)) for i in range(2)]
+    return going, [swap(a, i) for i, a in enumerate(going)]
 
 
 def gather_third(both, rows, swap, pieces=1):
-    return swap(half(both[1][:rows], 0, pieces), 0), swap(half(both[0][:rows], 1, pieces), 1)
+    going = [half(both[1 - i][:rows], i, pieces) for i in range(2)]
+    return going, [swap(a, i) for i, a in enumerate(going)]
 
 
 def join(*arrays):
@@ -145,18 +181,18 @@
     return cut.reshape(-1, a.shape[1])
 
 
-def pick(plan, m, arrays, after):
+def pick(plan, start, m, arrays, after):
     width = arrays[0].shape[1]
     h = m // 2
     where = [
-        [(0, 0, m)],
-        [(1, 0, m)],
-        [(2, 0, m)],
-        [(4, 0, m)],
-        [(4, 2 * m, h), (5, 2 * m, h)],
-        [(6, 0, h), (7, 0, h)],
-        [(3, 0, m)],
-        [(5, 0, m)],
+        [(0, start, TILE, m)],
+        [(1, start, TILE, m)],
+        [(2, start, TILE, m)],
+        [(4, 0, m, m)],
+        [(4, 2 * m, h, h), (5, 2 * m, h, h)],
+        [(6, 0, h, h), (7, 0, h, h)],
+        [(3, start, TILE, m)],
+        [(5, 0, m, m)],
     ]
 
     def body(plan_ref, ins, outs):
@@ -168,8 +204,8 @@
                 @pl.when(place // 2 == i)
                 def _():
                     at = to
-                    for array, lo, size in parts:
-                        rows = pl.ds(pl.multiple_of(lo + place % 2 * size, 8), size)
+                    for array, lo, pitch, size in parts:
+                        rows = pl.ds(pl.multiple_of(lo + place % 2 * pitch, 8), size)
                         out[at : at + size] = ins[array][rows]
                         at += size
 
@@ -297,27 +333,31 @@
     slots = jnp.sum(jnp.where(place[None, :] == ids[:, None], held[None, :], 0), axis=1)
     plan = jnp.concatenate([wanted, slots])
 
-    tiles = amplitudes.reshape(local_tiles, TILE, width)
+    far = flip_core(integrals.reshape(16 * width, cols))
+    places = np.arange(8, dtype=np.int32) * 2 + core
+    rhs_own = split_rows(integrals.reshape(16 * width, cols), width, places, 0)
+
     starts = [sum(CHUNKS[:i]) for i in range(len(CHUNKS))]
-    pieces = [tiles[:, s : s + m].reshape(-1, width) for s, m in zip(starts, CHUNKS)]
-
-    own = integrals.reshape(16 * width, cols)
-    far = flip_core(own)
+    whole = [amplitudes, flip_z(amplitudes), swap_x(amplitudes, 0), swap_x(amplitudes, 1)]
+
+    def rows_second(k, *after):
+        start, m = starts[k], CHUNKS[k]
+        part = lambda a: a.reshape(-1, TILE, width)[:, start : start + m].reshape(-1, width)
+        other, *near = wait_for([part(a) for a in whole[1:]], *after)
+        return gather_second(near, other, swap_x, local_tiles)[1]
+
+    def rows_third(k, both, *after):
+        rows = local_tiles * CHUNKS[k]
+        return gather_third(wait_for(both, *after), rows, swap_x, local_tiles)[1]
+
+    rows = [rows_second(0)]
+    rows.append(rows_second(1, *rows[0]))
+    rows[0] += rows_third(0, rows[0], rhs_own)
+
     at = []
     for group in GROUPS:
         gz, ring = np.array(group, np.int32).T
-        places = (zh ^ gz) * 4 + (y + ring * (1 - 2 * (y % 2))) % 4
-        at.append(places * 2 + core)
-
-    def rows_first(piece):
-        return [piece, flip_z(piece), swap_x(piece, 0), swap_x(piece, 1)]
-
-    def rows_second(arrays):
-        return arrays + list(gather_second(arrays[2:4], arrays[1], swap_x, local_tiles))
-
-    def rows_third(arrays):
-        rows = arrays[1].shape[0]
-        return arrays + list(gather_third(arrays[4:6], rows, swap_x, local_tiles))
+        at.append((zh ^ gz) * 4 + (y + ring * (1 - 2 * (y % 2))) % 4)
 
     def step(group, last):
         m, h = last["m"], last["m"] // 2
@@ -327,53 +367,49 @@
             arrays, blocks = last["second"], [[(0, 0, m)], [(1, 0, m)], [(0, m, h), (1, m, h)]]
         else:
             arrays, blocks = last["third"], [[(0, 0, h), (1, 0, h)]]
-        last["sums"] = products(arrays, blocks, at[group], own, far, last["sums"])
+        where = at[group % 3]
+        if group == 3:
+            arrays = [*last["second"], *last["third"]]
+            blocks = [[(0, 0, m)], [(1, 0, m)], [(0, m, h), (1, m, h)], [(2, 0, h), (3, 0, h)]]
+            where = jnp.concatenate(at[1:])
+        last["sums"] = products(arrays, blocks, where, rhs, last["sums"])
         return last["sums"]
 
-    def finish(last, back):
-        sums = step(1, last)
-        if back is not None:
-            product, came = back
-            back = product, return_third(plan, product, wait_for(came, sums[0]))
-        return step(2, last), back
-
-    arrays = rows_third(rows_second(rows_first(pieces[0])))
+    def begin(k, *after):
+        b, crossing = pick(plan, starts[k], CHUNKS[k], whole + rows[k], after)
+        bz = cross_z(crossing)
+        return dict(m=SLOTS * CHUNKS[k], sums=[], first=[b, swap_y(b, 0), swap_y(b, 1), bz])
+
     out, last, back = [], None, None
-    for k, m in enumerate(CHUNKS):
-        more = k + 1 < len(CHUNKS)
-        after = () if last is None else (last["second"][0], last["sums"][0])
-        b, crossing = pick(plan, m, arrays, after)
-        this = dict(m=SLOTS * m, sums=[])
-        if more:
-            arrays = rows_first(wait_for(pieces[k + 1], b))
-        near = [swap_y(b, 0), swap_y(b, 1)]
-        bz = cross_z(crossing)
-        this["first"] = [b, *near, bz]
-        ready = arrays if more else []
+    this = begin(0)
+    rows[1] += rows_third(1, rows[1], this["first"][1])
+    rhs = split_rows(far, width, places, 2, rhs_own)
+    for k in range(len(CHUNKS)):
+        b, *near, bz = this["first"]
         if last is not None:
-            sums, back = finish(last, back)
-            swapped = flip_core(sums[1])
-            ready = [*ready, sums[0]]
-        near, bz = wait_for((near, bz), *ready)
-        this["second"] = gather_second(near, bz, swap_y)
-        if more:
-            arrays = rows_second(wait_for(arrays, near[0]))
-        ready = arrays[4:6] if more else []
+            near, bz = wait_for((near, bz), last["sums"][0], *last["going"])
+        going, this["second"] = gather_second(near, bz, swap_y)
+        later = None
+        if k + 1 < len(CHUNKS):
+            later = begin(k + 1, near[0])
+            this["first"] = wait_for(this["first"], later["first"][0])
         if last is not None:
-            product, came = return_first(plan, sums, swapped)
-        step(0, this)
-        if last is not None:
+            last["third"] = wait_for(last["third"], *going)
+            sums = step(3, last)
+            product, came = return_first(plan, sums, flip_core(sums[1]))
             if back is not None:
                 out.append(return_last(plan, *back))
-            sent, came = return_second(plan, product, wait_for(came, this["sums"][0], *out))
-            back = product, came
-            ready = [*ready, sent]
-        both = wait_for(this["second"], this["sums"][0], *ready)
-        this["third"] = gather_third(both, SLOTS * m, swap_y)
-        if more:
-            arrays = rows_third(wait_for(arrays, this["sums"][0]))
-        last = this
-    sums, back = finish(last, back)
+        ready = [step(0, this)[0]]
+        if last is not None:
+            sent, came = return_second(plan, product, wait_for(came, *ready, *out))
+            ready.append(sent)
+        this["going"], this["third"] = gather_third(wait_for(this["second"], *ready), this["m"], swap_y)
+        if later is None:
+            sums = step(1, this)
+        if last is not None:
+            back = product, return_third(plan, product, wait_for(came, sums[0]))
+        last, this = this, later
+    sums = step(2, last)
     product, came = return_first(plan, sums, flip_core(sums[1]))
     if back is not None:
         out.append(return_last(plan, *back))

time: 168 us -> 190 us (1.13)
  Pallas kernels: 39.5 us -> 53.9 us
  waiting for transfers between devices: 58 us -> 65.3 us
  starting transfers between devices: 54 us -> 47.8 us
  local copies, waits for them, and re-layouts: 8.84 us -> 13.8 us
    pallas_call x6 -> x7, Pallas kernels: 31 us -> 46.2 us  [the longest x5 26.5 us: products(): pl.pallas_call(kernel, in_specs=[pl.BlockSpec(memory_space=pltpu.SMEM)] +...]
    ppermute x45 -> x42, waiting for transfers between devices: 58 us -> 65.3 us  [send(): lax.ppermute(a, ('row', 'col'), [(i, index[to(*p)]) for p, i in index.ite...]
    ppermute x45 -> x42, starting transfers between devices: 54 us -> 47.8 us  [send(): lax.ppermute(a, ('row', 'col'), [(i, index[to(*p)]) for p, i in index.ite...]
    concatenate x4, other arithmetic: 1.71 us -> 4.79 us  [join(): return jnp.concatenate(arrays, axis=0)]
    slice x9 -> x11, local copies, waits for them, and re-layouts: 1.28 us -> 3.8 us  [the longest x3 2.24 us: rows_second(): a.reshape(-1, TILE, width)[:, start:start + m].reshape(-1, width)]
    unnamed x28 -> x62, local copies, waits for them, and re-layouts: 3.16 us -> 5.25 us
  transfers between devices with their start and end apart: 45 -> 42, of which waited for: 22 -> 23; matrix products, arithmetic and copies ran while one was open for 7% -> 8% of each run, Pallas kernels for 22% -> 27%
where the time goes in v4:
time: 190 us; the launch traced here: 189 us
  waiting for transfers between devices  65.3 us (34%)
  Pallas kernels  53.9 us (28%)
  starting transfers between devices  47.8 us (25%)
  local copies, waits for them, and re-layouts  13.8 us (7%)
  other arithmetic  7.69 us (4%)
    ppermute x42, waiting for transfers between devices, send(): lax.ppermute(a, ('row', 'col'), [(i, index[to(*p)]) for p, i in index.ite...  65.3 us
    ppermute x42, starting transfers between devices, send(): lax.ppermute(a, ('row', 'col'), [(i, index[to(*p)]) for p, i in index.ite...  47.8 us
    pallas_call x5, Pallas kernels, products(): pl.pallas_call(kernel, in_specs=[pl.BlockSpec(memory_space=pltpu.SMEM)] +...  26.5 us
    pallas_call x2, Pallas kernels, split_rows(): pl.pallas_call(kernel, in_specs=[pl.BlockSpec(memory_space=pltpu.SMEM), a...  19.7 us
    pallas_call x10, Pallas kernels, small_kernel(): pl.pallas_call(kernel, in_specs=[pl.BlockSpec(memory_space=pltpu.SMEM)] +...  7.71 us
    unnamed x62, local copies, waits for them, and re-layouts  5.25 us
    concatenate x4, other arithmetic, join(): return jnp.concatenate(arrays, axis=0)  4.79 us
  transfers between devices with their start and end apart: 42, of which 23 were waited for; matrix products, arithmetic and copies ran while one was open for 8% of the time, Pallas kernels for 27%

profile of v4, /device:TPU:0, one launch (start us, length us, event | category | flops | bytes accessed | tf_op | source)
XLA Modules:
  0.0 189.2 jit_solution(15146347470200342361)
XLA Ops:
  0.0 2.0 %collective-permute-start = (f32[256,512]{1,0:T(8,128)}, f32[256,512]{1,0:T(8,128)S(1)}, u32[]{:S(2)}, u32[]{:S(2)}) collective-permute-start(f32[256,512]{1,0:T(8,128)} %refs_0_.3), channel_id=1, source_target_pairs={{0,64},{1,65},{2,66},{3,67},{4,68},{5,69},{6,70},{7,71},{8,72},{9,... | collective-permute-start | bytes 1572872 | tf_op jit(solution)/shard_map/ppermute | solution.py:28
  2.0 1.5 collective-permute-start.1
  3.5 2.1 %collective-permute-start.2 = (f32[256,512]{1,0:T(8,128)}, f32[256,512]{1,0:T(8,128)S(1)}, u32[]{:S(2)}, u32[]{:S(2)}) collective-permute-start(f32[256,512]{1,0:T(8,128)} %refs_0_.3), channel_id=1, source_target_pairs={{0,48},{1,49},{2,50},{3,51},{4,52},{5,53},{6,54},{7,55},{8,56},{9,... | collective-permute-start | bytes 1572872 | tf_op jit(solution)/shard_map/ppermute | solution.py:28
  6.3 8.6 %collective-permute-done.refs_1_ = f32[256,512]{1,0:T(8,128)S(1)} collective-permute-done((f32[256,512]{1,0:T(8,128)}, f32[256,512]{1,0:T(8,128)S(1)}, u32[]{:S(2)}, u32[]{:S(2)}) %collective-permute-start) | collective-permute-done | bytes 524320 | tf_op jit(solution)/shard_map/ppermute | solution.py:28
  17.0 1.7 collective-permute-done.2.refs_3_
  20.3 2.1 %collective-permute-start.4 = (f32[192,512]{1,0:T(8,128)S(1)}, f32[192,512]{1,0:T(8,128)S(1)}, u32[]{:S(2)}, u32[]{:S(2)}) collective-permute-start(f32[192,512]{1,0:T(8,128)S(1)} %get-tuple-element.135), channel_id=1, source_target_pairs={{0,48},{1,49},{2,50},{3,51},{4,52},{5,53},{6,54},{7,55},{8,56},{9,... | collective-permute-start | bytes 1179656 | tf_op jit(solution)/shard_map/ppermute | solution.py:28
  23.4 9.9 %split_rows.2.refs_0_ = bf16[4,4096,512]{2,1,0:T(8,128)(2,1)} custom-call(s32[8]{0:T(128)S(1)} %multiply_add_fusion.at_ref, f32[8192,512]{1,0:T(8,128)} %bitcast.75), custom_call_target="tpu_custom_call" | custom-call | flops 1 | bytes 1 | tf_op jit(solution)/shard_map/split_rows/pallas_call | solution.py:76
  33.6 1.5 collective-permute-start.5
  36.5 2.1 %collective-permute-done.5.refs_6_ = f32[64,512]{1,0:T(8,128)S(1)} collective-permute-done((f32[64,512]{1,0:T(8,128)S(1)}, f32[64,512]{1,0:T(8,128)S(1)}, u32[]{:S(2)}, u32[]{:S(2)}) %collective-permute-start.5) | collective-permute-done | bytes 131104 | tf_op jit(solution)/shard_map/ppermute | solution.py:28
  38.6 2.7 %collective-permute-done.6.refs_7_ = f32[64,512]{1,0:T(8,128)S(1)} collective-permute-done((f32[64,512]{1,0:T(8,128)S(1)}, f32[64,512]{1,0:T(8,128)S(1)}, u32[]{:S(2)}, u32[]{:S(2)}) %collective-permute-start.6) | collective-permute-done | bytes 131104 | tf_op jit(solution)/shard_map/ppermute | solution.py:28
  42.4 1.7 collective-permute-start.10
  44.1 2.2 %collective-permute-start.8 = (f32[256,512]{1,0:T(8,128)S(1)}, f32[256,512]{1,0:T(8,128)S(1)}, u32[]{:S(2)}, u32[]{:S(2)}) collective-permute-start(f32[256,512]{1,0:T(8,128)S(1)} %get-tuple-element.77.refs_0_), channel_id=1, source_target_pairs={{0,6},{1,7},{2,4},{3,5},{4,2},{5,3},{6,0},{7,1},{8,14},{9,15},{10,... | collective-permute-start | bytes 1572872 | tf_op jit(solution)/shard_map/ppermute | solution.py:28
  46.3 2.5 %collective-permute-start.7 = (f32[256,512]{1,0:T(8,128)S(1)}, f32[256,512]{1,0:T(8,128)S(1)}, u32[]{:S(2)}, u32[]{:S(2)}) collective-permute-start(f32[256,512]{1,0:T(8,128)S(1)} %get-tuple-element.69), channel_id=1, source_target_pairs={{0,72},{1,73},{2,74},{3,75},{4,76},{5,77},{6,78},{7,79},{8,64},{9,... | collective-permute-start | bytes 1572872 | tf_op jit(solution)/shard_map/ppermute | solution.py:28
  50.6 2.8 %collective-permute-done.10.refs_8_.refs_1_ = f32[256,512]{1,0:T(8,128)S(1)} collective-permute-done((f32[256,512]{1,0:T(8,128)S(1)}, f32[256,512]{1,0:T(8,128)S(1)}, u32[]{:S(2)}, u32[]{:S(2)}) %collective-permute-start.10) | collective-permute-done | bytes 524320 | tf_op jit(solution)/shard_map/ppermute | solution.py:28
  53.5 2.5 %collective-permute-done.8.refs_2_ = f32[256,512]{1,0:T(8,128)S(1)} collective-permute-done((f32[256,512]{1,0:T(8,128)S(1)}, f32[256,512]{1,0:T(8,128)S(1)}, u32[]{:S(2)}, u32[]{:S(2)}) %collective-permute-start.8) | collective-permute-done | bytes 524320 | tf_op jit(solution)/shard_map/ppermute | solution.py:28
  56.0 1.9 collective-permute-done.7.refs_3_
  57.8 1.3 pad_maximum_fusion
  62.9 6.3 %collective-permute-done.12.refs_4_ = f32[192,512]{1,0:T(8,128)S(1)} collective-permute-done((f32[192,512]{1,0:T(8,128)S(1)}, f32[192,512]{1,0:T(8,128)S(1)}, u32[]{:S(2)}, u32[]{:S(2)}) %collective-permute-start.12) | collective-permute-done | bytes 393248 | tf_op jit(solution)/shard_map/ppermute | solution.py:28
  69.2 1.5 collective-permute-done.13.refs_5_
  73.8 2.9 %collective-permute-done.14.refs_6_ = f32[64,512]{1,0:T(8,128)S(1)} collective-permute-done((f32[64,512]{1,0:T(8,128)}, f32[64,512]{1,0:T(8,128)S(1)}, u32[]{:S(2)}, u32[]{:S(2)}) %collective-permute-start.14) | collective-permute-done | bytes 131104 | tf_op jit(solution)/shard_map/ppermute | solution.py:28
  76.6 2.5 %collective-permute-done.15.refs_7_ = f32[64,512]{1,0:T(8,128)} collective-permute-done((f32[64,512]{1,0:T(8,128)}, f32[64,512]{1,0:T(8,128)}, u32[]{:S(2)}, u32[]{:S(2)}) %collective-permute-start.15) | collective-permute-done | bytes 131104 | tf_op jit(solution)/shard_map/ppermute | solution.py:28
  82.1 1.4 pick.3
  83.6 2.1 %collective-permute-start.19 = (f32[256,512]{1,0:T(8,128)S(1)}, f32[256,512]{1,0:T(8,128)S(1)}, u32[]{:S(2)}, u32[]{:S(2)}) collective-permute-start(f32[256,512]{1,0:T(8,128)S(1)} %get-tuple-element.76.refs_0_), channel_id=1, source_target_pairs={{0,2},{1,3},{2,0},{3,1},{4,6},{5,7},{6,4},{7,5},{8,10},{9,11},{10,... | collective-permute-start | bytes 1572872 | tf_op jit(solution)/shard_map/ppermute | solution.py:28
  85.7 2.2 %collective-permute-start.20 = (f32[256,512]{1,0:T(8,128)S(1)}, f32[256,512]{1,0:T(8,128)S(1)}, u32[]{:S(2)}, u32[]{:S(2)}) collective-permute-start(f32[256,512]{1,0:T(8,128)S(1)} %get-tuple-element.76.refs_0_), channel_id=1, source_target_pairs={{0,6},{1,7},{2,4},{3,5},{4,2},{5,3},{6,0},{7,1},{8,14},{9,15},{10,... | collective-permute-start | bytes 1572872 | tf_op jit(solution)/shard_map/ppermute | solution.py:28
  87.8 2.8 %collective-permute-start.21 = (f32[256,512]{1,0:T(8,128)S(1)}, f32[256,512]{1,0:T(8,128)S(1)}, u32[]{:S(2)}, u32[]{:S(2)}) collective-permute-start(f32[256,512]{1,0:T(8,128)S(1)} %get-tuple-element.84), channel_id=1, source_target_pairs={{0,72},{1,73},{2,74},{3,75},{4,76},{5,77},{6,78},{7,79},{8,64},{9,... | collective-permute-start | bytes 1572872 | tf_op jit(solution)/shard_map/ppermute | solution.py:28
  90.7 9.8 %split_rows.3.refs_4_.refs_2_ = bf16[4,4096,512]{2,1,0:T(8,128)(2,1)} custom-call(s32[8]{0:T(128)S(1)} %multiply_add_fusion.at_ref, f32[8192,512]{1,0:T(8,128)} %collective-permute-done.16.a_ref, bf16[4,4096,512]{2,1,0:T(8,128)(2,1)} %split_rows.2.refs_0_), custom_call_target="tpu_custom_call", output_to_operand_aliasing={{}: (2, {})} | custom-call | flops 1 | bytes 1 | tf_op jit(solution)/shard_map/split_rows/pallas_call | solution.py:76
  100.5 6.0 %products.5 = (f32[256,512]{1,0:T(8,128)S(1)}, f32[256,512]{1,0:T(8,128)S(1)}) custom-call(s32[4]{0:T(128)S(1)} %fusion.1.at_ref, f32[256,512]{1,0:T(8,128)S(1)} %copy-done.15, f32[256,512]{1,0:T(8,128)S(1)} %collective-permute-done.10.refs_8_.refs_1_, f32[256,512]{1,0:T(8,128)S(1)} %copy-done.5, f32[256,512]{1,0:T(8,128)S(1)} %collective-permute-done.7.refs_3_, ...), custom_call_target="tpu_custom_call" | custom-call | flops 1 | bytes 1 | tf_op jit(solution)/shard_map/products/pallas_call | solution.py:125
  106.6 1.4 slice.110
  110.6 1.6 pad_maximum_fusion.2
  112.1 1.4 collective-permute-start.27
  113.6 2.2 %collective-permute-start.28 = (f32[384,512]{1,0:T(8,128)}, f32[384,512]{1,0:T(8,128)S(1)}, u32[]{:S(2)}, u32[]{:S(2)}) collective-permute-start(f32[384,512]{1,0:T(8,128)} %get-tuple-element.123), channel_id=1, source_target_pairs={{0,6},{1,7},{2,4},{3,5},{4,2},{5,3},{6,0},{7,1},{8,14},{9,15},{10,... | collective-permute-start | bytes 2359304 | tf_op jit(solution)/shard_map/ppermute | solution.py:28
  115.9 2.3 %collective-permute-done.17.refs_2_ = f32[128,512]{1,0:T(8,128)} collective-permute-done((f32[128,512]{1,0:T(8,128)}, f32[128,512]{1,0:T(8,128)}, u32[]{:S(2)}, u32[]{:S(2)}) %collective-permute-start.17) | collective-permute-done | bytes 262176 | tf_op jit(solution)/shard_map/ppermute | solution.py:28
  118.3 1.9 %collective-permute-done.18.refs_3_ = f32[128,512]{1,0:T(8,128)} collective-permute-done((f32[128,512]{1,0:T(8,128)}, f32[128,512]{1,0:T(8,128)}, u32[]{:S(2)}, u32[]{:S(2)}) %collective-permute-start.18) | collective-permute-done | bytes 262176 | tf_op jit(solution)/shard_map/ppermute | solution.py:28
  122.3 6.8 %products.6 = (f32[256,512]{1,0:T(8,128)S(1)}, f32[256,512]{1,0:T(8,128)S(1)}) custom-call(s32[4]{0:T(128)S(1)} %pad_add_fusion.1.at_ref, f32[384,512]{1,0:T(8,128)S(1)} %collective-permute-done.9.refs_0_, f32[384,512]{1,0:T(8,128)} %collective-permute-done.11.refs_1_, f32[128,512]{1,0:T(8,128)} %collective-permute-done.17.refs_2_, ...), custom_call_target="tpu_custom_call" | custom-call | flops 1 | bytes 1 | tf_op jit(solution)/shard_map/products/pallas_call | solution.py:125
  129.2 1.9 %collective-permute-done.22.refs_1_ = f32[256,512]{1,0:T(8,128)S(1)} collective-permute-done((f32[256,512]{1,0:T(8,128)S(1)}, f32[256,512]{1,0:T(8,128)S(1)}, u32[]{:S(2)}, u32[]{:S(2)}) %collective-permute-start.22) | collective-permute-done | bytes 524320 | tf_op jit(solution)/shard_map/ppermute | solution.py:28
  133.5 6.0 %products.7 = (f32[256,512]{1,0:T(8,128)S(1)}, f32[256,512]{1,0:T(8,128)S(1)}) custom-call(s32[4]{0:T(128)S(1)} %fusion.1.at_ref, f32[256,512]{1,0:T(8,128)S(1)} %copy-done.17, f32[256,512]{1,0:T(8,128)S(1)} %copy-done.7, f32[256,512]{1,0:T(8,128)S(1)} %copy-done.9, f32[256,512]{1,0:T(8,128)S(1)} %copy-done.1, bf16[4,4096,512]{2,1,0:T(8,128)(2,1)} %split_rows.3.refs_4_.refs_2_), custom_call_target="tpu_custom_call" | custom-call | flops 1 | bytes 1 | tf_op jit(solution)/shard_map/products/pallas_call | solution.py:125
  141.0 1.4 collective-permute-start.33
  143.1 2.3 %collective-permute-start.26 = (f32[192,512]{1,0:T(8,128)S(1)}, f32[192,512]{1,0:T(8,128)S(1)}, u32[]{:S(2)}, u32[]{:S(2)}) collective-permute-start(f32[192,512]{1,0:T(8,128)S(1)} %get-tuple-element.100), channel_id=1, source_target_pairs={{0,48},{1,49},{2,50},{3,51},{4,52},{5,53},{6,54},{7,55},{8,56},{9,... | collective-permute-start | bytes 1179656 | tf_op jit(solution)/shard_map/ppermute | solution.py:28
  145.5 5.1 %products.8 = (f32[256,512]{1,0:T(8,128)S(1)}, f32[256,512]{1,0:T(8,128)S(1)}) custom-call(s32[3]{0:T(128)S(1)} %fusion.at_ref, f32[384,512]{1,0:T(8,128)S(1)} %collective-permute-done.27.refs_0_, f32[384,512]{1,0:T(8,128)S(1)} %collective-permute-done.28.refs_1_, bf16[4,4096,512]{2,1,0:T(8,128)(2,1)} %split_rows.3.refs_4_.refs_2_, ...), custom_call_target="tpu_custom_call" | custom-call | flops 1 | bytes 1 | tf_op jit(solution)/shard_map/products/pallas_call | solution.py:125
  150.6 2.5 %products.9 = (f32[256,512]{1,0:T(8,128)S(1)}, f32[256,512]{1,0:T(8,128)S(1)}) custom-call(s32[1]{0:T(128)S(6)} %add.102.at_ref, f32[128,512]{1,0:T(8,128)S(1)} %collective-permute-done.32.refs_0_, f32[128,512]{1,0:T(8,128)S(1)} %collective-permute-done.33.refs_1_, bf16[4,4096,512]{2,1,0:T(8,128)(2,1)} %split_rows.3.refs_4_.refs_2_, ...), custom_call_target="tpu_custom_call" | custom-call | flops 1 | bytes 1 | tf_op jit(solution)/shard_map/products/pallas_call | solution.py:125
  155.0 2.5 %collective-permute-start.30 = (f32[128,512]{1,0:T(8,128)S(1)}, f32[128,512]{1,0:T(8,128)S(1)}, u32[]{:S(2)}, u32[]{:S(2)}) collective-permute-start(f32[128,512]{1,0:T(8,128)S(1)} %get-tuple-element.106), channel_id=1, source_target_pairs={{0,48},{1,49},{2,50},{3,51},{4,52},{5,53},{6,54},{7,55},{8,56},{9,... | collective-permute-start | bytes 786440 | tf_op jit(solution)/shard_map/ppermute | solution.py:28
  160.4 3.7 %collective-permute-done.29.refs_1_ = f32[128,512]{1,0:T(8,128)S(1)} collective-permute-done((f32[128,512]{1,0:T(8,128)S(1)}, f32[128,512]{1,0:T(8,128)S(1)}, u32[]{:S(2)}, u32[]{:S(2)}) %collective-permute-start.29) | collective-permute-done | bytes 262176 | tf_op jit(solution)/shard_map/ppermute | solution.py:28
  164.1 1.5 collective-permute-done.30.refs_2_
  168.1 1.3 collective-permute-start.38
  169.4 8.2 %collective-permute-done.37.refs_1_ = f32[192,512]{1,0:T(8,128)S(1)} collective-permute-done((f32[192,512]{1,0:T(8,128)S(1)}, f32[192,512]{1,0:T(8,128)S(1)}, u32[]{:S(2)}, u32[]{:S(2)}) %collective-permute-start.37) | collective-permute-done | bytes 393248 | tf_op jit(solution)/shard_map/ppermute | solution.py:28
  177.6 1.3 collective-permute-done.38.refs_2_
  181.2 4.9 %collective-permute-done.39.refs_1_ = f32[128,512]{1,0:T(8,128)S(1)} collective-permute-done((f32[128,512]{1,0:T(8,128)S(1)}, f32[128,512]{1,0:T(8,128)S(1)}, u32[]{:S(2)}, u32[]{:S(2)}) %collective-permute-start.39) | collective-permute-done | bytes 262176 | tf_op jit(solution)/shard_map/ppermute | solution.py:28
  186.1 1.7 collective-permute-done.40.refs_2_
  (157 shorter events, 39.9 us)
Async XLA Ops:
  0.0 87.8 %collective-permute-start.16 = (f32[8192,512]{1,0:T(8,128)}, f32[8192,512]{1,0:T(8,128)}, u32[]{:S(2)}, u32[]{:S(2)}) collective-permute-start(f32[8192,512]{1,0:T(8,128)} %bitcast.74), channel_id=1, source_target_pairs={{0,1},{1,0},{2,3},{3,2},{4,5},{5,4},{6,7},{7,6},{8,9},{9,8},{10,11... | collective-permute-start | bytes 50331656 | tf_op jit(solution)/shard_map/ppermute | solution.py:28
  0.0 14.8 %collective-permute-start = (f32[256,512]{1,0:T(8,128)}, f32[256,512]{1,0:T(8,128)S(1)}, u32[]{:S(2)}, u32[]{:S(2)}) collective-permute-start(f32[256,512]{1,0:T(8,128)} %refs_0_.3), channel_id=1, source_target_pairs={{0,64},{1,65},{2,66},{3,67},{4,68},{5,69},{6,70},{7,71},{8,72},{9,... | collective-permute-start | bytes 1572872 | tf_op jit(solution)/shard_map/ppermute | solution.py:28
  2.0 14.3 %collective-permute-start.1 = (f32[256,512]{1,0:T(8,128)}, f32[256,512]{1,0:T(8,128)S(1)}, u32[]{:S(2)}, u32[]{:S(2)}) collective-permute-start(f32[256,512]{1,0:T(8,128)} %refs_0_.3), channel_id=1, source_target_pairs={{0,16},{1,17},{2,18},{3,19},{4,20},{5,21},{6,22},{7,23},{8,24},{9,... | collective-permute-start | bytes 1572872 | tf_op jit(solution)/shard_map/ppermute | solution.py:28
  3.5 15.2 %collective-permute-start.2 = (f32[256,512]{1,0:T(8,128)}, f32[256,512]{1,0:T(8,128)S(1)}, u32[]{:S(2)}, u32[]{:S(2)}) collective-permute-start(f32[256,512]{1,0:T(8,128)} %refs_0_.3), channel_id=1, source_target_pairs={{0,48},{1,49},{2,50},{3,51},{4,52},{5,53},{6,54},{7,55},{8,56},{9,... | collective-permute-start | bytes 1572872 | tf_op jit(solution)/shard_map/ppermute | solution.py:28
  20.3 13.2 %collective-permute-start.3 = (f32[192,512]{1,0:T(8,128)}, f32[192,512]{1,0:T(8,128)S(1)}, u32[]{:S(2)}, u32[]{:S(2)}) collective-permute-start(f32[192,512]{1,0:T(8,128)} %get-tuple-element.136), channel_id=1, source_target_pairs={{0,16},{1,17},{2,18},{3,19},{4,20},{5,21},{6,22},{7,23},{8,24},{9,... | collective-permute-start | bytes 1179656 | tf_op jit(solution)/shard_map/ppermute | solution.py:28
  20.3 13.2 %collective-permute-start.4 = (f32[192,512]{1,0:T(8,128)S(1)}, f32[192,512]{1,0:T(8,128)S(1)}, u32[]{:S(2)}, u32[]{:S(2)}) collective-permute-start(f32[192,512]{1,0:T(8,128)S(1)} %get-tuple-element.135), channel_id=1, source_target_pairs={{0,48},{1,49},{2,50},{3,51},{4,52},{5,53},{6,54},{7,55},{8,56},{9,... | collective-permute-start | bytes 1179656 | tf_op jit(solution)/shard_map/ppermute | solution.py:28
  23.4 18.0 %copy-start.2 = (f32[256,512]{1,0:T(8,128)S(1)}, f32[256,512]{1,0:T(8,128)}, u32[]{:S(2)}) copy-start(f32[256,512]{1,0:T(8,128)} %refs_0_.3) | copy-start | bytes 1572868
  23.4 67.2 %copy-start.25 = (s32[4]{0:T(128)S(1)}, s32[4]{0:T(128)}, u32[]{:S(2)}) copy-start(s32[4]{0:T(128)} %constant.161.clone) | copy-start | bytes 52
  23.4 67.2 %copy-start.26 = (s32[4]{0:T(128)S(1)}, s32[4]{0:T(128)}, u32[]{:S(2)}) copy-start(s32[4]{0:T(128)} %constant.162.clone) | copy-start | bytes 52
  33.6 5.0 %collective-permute-start.5 = (f32[64,512]{1,0:T(8,128)S(1)}, f32[64,512]{1,0:T(8,128)S(1)}, u32[]{:S(2)}, u32[]{:S(2)}) collective-permute-start(f32[64,512]{1,0:T(8,128)S(1)} %bitcast.94), channel_id=1, source_target_pairs={{0,16},{1,17},{2,18},{3,19},{4,20},{5,21},{6,22},{7,23},{8,24},{9,... | collective-permute-start | bytes 393224 | tf_op jit(solution)/shard_map/ppermute | solution.py:28
  35.1 6.3 %collective-permute-start.6 = (f32[64,512]{1,0:T(8,128)S(1)}, f32[64,512]{1,0:T(8,128)S(1)}, u32[]{:S(2)}, u32[]{:S(2)}) collective-permute-start(f32[64,512]{1,0:T(8,128)S(1)} %bitcast.95), channel_id=1, source_target_pairs={{0,48},{1,49},{2,50},{3,51},{4,52},{5,53},{6,54},{7,55},{8,56},{9,... | collective-permute-start | bytes 393224 | tf_op jit(solution)/shard_map/ppermute | solution.py:28
  42.4 29.5 %copy-start.14 = (f32[256,512]{1,0:T(8,128)}, f32[256,512]{1,0:T(8,128)S(1)}, u32[]{:S(2)}) copy-start(f32[256,512]{1,0:T(8,128)S(1)} %get-tuple-element.77.refs_0_) | copy-start | bytes 1572868
  42.4 11.0 %collective-permute-start.10 = (f32[256,512]{1,0:T(8,128)S(1)}, f32[256,512]{1,0:T(8,128)S(1)}, u32[]{:S(2)}, u32[]{:S(2)}) collective-permute-start(f32[256,512]{1,0:T(8,128)S(1)} %get-tuple-element.77.refs_0_), channel_id=1, source_target_pairs={{0,2},{1,3},{2,0},{3,1},{4,6},{5,7},{6,4},{7,5},{8,10},{9,11},{10,... | collective-permute-start | bytes 1572872 | tf_op jit(solution)/shard_map/ppermute | solution.py:28
  44.1 11.9 %collective-permute-start.8 = (f32[256,512]{1,0:T(8,128)S(1)}, f32[256,512]{1,0:T(8,128)S(1)}, u32[]{:S(2)}, u32[]{:S(2)}) collective-permute-start(f32[256,512]{1,0:T(8,128)S(1)} %get-tuple-element.77.refs_0_), channel_id=1, source_target_pairs={{0,6},{1,7},{2,4},{3,5},{4,2},{5,3},{6,0},{7,1},{8,14},{9,15},{10,... | collective-permute-start | bytes 1572872 | tf_op jit(solution)/shard_map/ppermute | solution.py:28
  46.3 11.6 %collective-permute-start.7 = (f32[256,512]{1,0:T(8,128)S(1)}, f32[256,512]{1,0:T(8,128)S(1)}, u32[]{:S(2)}, u32[]{:S(2)}) collective-permute-start(f32[256,512]{1,0:T(8,128)S(1)} %get-tuple-element.69), channel_id=1, source_target_pairs={{0,72},{1,73},{2,74},{3,75},{4,76},{5,77},{6,78},{7,79},{8,64},{9,... | collective-permute-start | bytes 1572872 | tf_op jit(solution)/shard_map/ppermute | solution.py:28
  59.2 47.4 %collective-permute-start.11 = (f32[384,512]{1,0:T(8,128)}, f32[384,512]{1,0:T(8,128)}, u32[]{:S(2)}, u32[]{:S(2)}) collective-permute-start(f32[384,512]{1,0:T(8,128)} %get-tuple-element.125), channel_id=1, source_target_pairs={{0,6},{1,7},{2,4},{3,5},{4,2},{5,3},{6,0},{7,1},{8,14},{9,15},{10,... | collective-permute-start | bytes 2359304 | tf_op jit(solution)/shard_map/ppermute | solution.py:28
  60.2 46.3 %collective-permute-start.9 = (f32[384,512]{1,0:T(8,128)}, f32[384,512]{1,0:T(8,128)S(1)}, u32[]{:S(2)}, u32[]{:S(2)}) collective-permute-start(f32[384,512]{1,0:T(8,128)} %get-tuple-element.126), channel_id=1, source_target_pairs={{0,2},{1,3},{2,0},{3,1},{4,6},{5,7},{6,4},{7,5},{8,10},{9,11},{10,... | collective-permute-start | bytes 2359304 | tf_op jit(solution)/shard_map/ppermute | solution.py:28
  61.3 7.9 %collective-permute-start.12 = (f32[192,512]{1,0:T(8,128)S(1)}, f32[192,512]{1,0:T(8,128)S(1)}, u32[]{:S(2)}, u32[]{:S(2)}) collective-permute-start(f32[192,512]{1,0:T(8,128)S(1)} %get-tuple-element.134), channel_id=1, source_target_pairs={{0,16},{1,17},{2,18},{3,19},{4,20},{5,21},{6,22},{7,23},{8,24},{9,... | collective-permute-start | bytes 1179656 | tf_op jit(solution)/shard_map/ppermute | solution.py:28
  61.7 9.0 %collective-permute-start.13 = (f32[192,512]{1,0:T(8,128)S(1)}, f32[192,512]{1,0:T(8,128)S(1)}, u32[]{:S(2)}, u32[]{:S(2)}) collective-permute-start(f32[192,512]{1,0:T(8,128)S(1)} %get-tuple-element.133), channel_id=1, source_target_pairs={{0,48},{1,49},{2,50},{3,51},{4,52},{5,53},{6,54},{7,55},{8,56},{9,... | collective-permute-start | bytes 1179656 | tf_op jit(solution)/shard_map/ppermute | solution.py:28
  71.4 5.2 %collective-permute-start.14 = (f32[64,512]{1,0:T(8,128)}, f32[64,512]{1,0:T(8,128)S(1)}, u32[]{:S(2)}, u32[]{:S(2)}) collective-permute-start(f32[64,512]{1,0:T(8,128)} %bitcast.30), channel_id=1, source_target_pairs={{0,16},{1,17},{2,18},{3,19},{4,20},{5,21},{6,22},{7,23},{8,24},{9,... | collective-permute-start | bytes 393224 | tf_op jit(solution)/shard_map/ppermute | solution.py:28
  72.6 6.5 %collective-permute-start.15 = (f32[64,512]{1,0:T(8,128)}, f32[64,512]{1,0:T(8,128)}, u32[]{:S(2)}, u32[]{:S(2)}) collective-permute-start(f32[64,512]{1,0:T(8,128)} %bitcast.32), channel_id=1, source_target_pairs={{0,48},{1,49},{2,50},{3,51},{4,52},{5,53},{6,54},{7,55},{8,56},{9,... | collective-permute-start | bytes 393224 | tf_op jit(solution)/shard_map/ppermute | solution.py:28
  83.6 26.9 %collective-permute-start.19 = (f32[256,512]{1,0:T(8,128)S(1)}, f32[256,512]{1,0:T(8,128)S(1)}, u32[]{:S(2)}, u32[]{:S(2)}) collective-permute-start(f32[256,512]{1,0:T(8,128)S(1)} %get-tuple-element.76.refs_0_), channel_id=1, source_target_pairs={{0,2},{1,3},{2,0},{3,1},{4,6},{5,7},{6,4},{7,5},{8,10},{9,11},{10,... | collective-permute-start | bytes 1572872 | tf_op jit(solution)/shard_map/ppermute | solution.py:28
  85.7 24.8 %collective-permute-start.20 = (f32[256,512]{1,0:T(8,128)S(1)}, f32[256,512]{1,0:T(8,128)S(1)}, u32[]{:S(2)}, u32[]{:S(2)}) collective-permute-start(f32[256,512]{1,0:T(8,128)S(1)} %get-tuple-element.76.refs_0_), channel_id=1, source_target_pairs={{0,6},{1,7},{2,4},{3,5},{4,2},{5,3},{6,0},{7,1},{8,14},{9,15},{10,... | collective-permute-start | bytes 1572872 | tf_op jit(solution)/shard_map/ppermute | solution.py:28
  87.8 22.7 %collective-permute-start.21 = (f32[256,512]{1,0:T(8,128)S(1)}, f32[256,512]{1,0:T(8,128)S(1)}, u32[]{:S(2)}, u32[]{:S(2)}) collective-permute-start(f32[256,512]{1,0:T(8,128)S(1)} %get-tuple-element.84), channel_id=1, source_target_pairs={{0,72},{1,73},{2,74},{3,75},{4,76},{5,77},{6,78},{7,79},{8,64},{9,... | collective-permute-start | bytes 1572872 | tf_op jit(solution)/shard_map/ppermute | solution.py:28
  108.7 9.6 %collective-permute-start.17 = (f32[128,512]{1,0:T(8,128)}, f32[128,512]{1,0:T(8,128)}, u32[]{:S(2)}, u32[]{:S(2)}) collective-permute-start(f32[128,512]{1,0:T(8,128)} %slice_bitcast_fusion.5), channel_id=1, source_target_pairs={{0,2},{1,3},{2,0},{3,1},{4,6},{5,7},{6,4},{7,5},{8,10},{9,11},{10,... | collective-permute-start | bytes 786440 | tf_op jit(solution)/shard_map/ppermute | solution.py:28
  109.4 10.8 %collective-permute-start.18 = (f32[128,512]{1,0:T(8,128)}, f32[128,512]{1,0:T(8,128)}, u32[]{:S(2)}, u32[]{:S(2)}) collective-permute-start(f32[128,512]{1,0:T(8,128)} %slice_bitcast_fusion.4), channel_id=1, source_target_pairs={{0,6},{1,7},{2,4},{3,5},{4,2},{5,3},{6,0},{7,1},{8,14},{9,15},{10,... | collective-permute-start | bytes 786440 | tf_op jit(solution)/shard_map/ppermute | solution.py:28
  112.1 28.1 %collective-permute-start.27 = (f32[384,512]{1,0:T(8,128)}, f32[384,512]{1,0:T(8,128)S(1)}, u32[]{:S(2)}, u32[]{:S(2)}) collective-permute-start(f32[384,512]{1,0:T(8,128)} %get-tuple-element.124), channel_id=1, source_target_pairs={{0,2},{1,3},{2,0},{3,1},{4,6},{5,7},{6,4},{7,5},{8,10},{9,11},{10,... | collective-permute-start | bytes 2359304 | tf_op jit(solution)/shard_map/ppermute | solution.py:28
  113.6 19.9 %copy-start.1 = (f32[256,512]{1,0:T(8,128)S(1)}, f32[256,512]{1,0:T(8,128)}, u32[]{:S(2)}) copy-start(f32[256,512]{1,0:T(8,128)} %copy-done) | copy-start | bytes 1572868
  113.6 26.7 %collective-permute-start.28 = (f32[384,512]{1,0:T(8,128)}, f32[384,512]{1,0:T(8,128)S(1)}, u32[]{:S(2)}, u32[]{:S(2)}) collective-permute-start(f32[384,512]{1,0:T(8,128)} %get-tuple-element.123), channel_id=1, source_target_pairs={{0,6},{1,7},{2,4},{3,5},{4,2},{5,3},{6,0},{7,1},{8,14},{9,15},{10,... | collective-permute-start | bytes 2359304 | tf_op jit(solution)/shard_map/ppermute | solution.py:28
  115.8 17.7 %copy-start.7 = (f32[256,512]{1,0:T(8,128)S(1)}, f32[256,512]{1,0:T(8,128)}, u32[]{:S(2)}) copy-start(f32[256,512]{1,0:T(8,128)} %copy-done.6) | copy-start | bytes 1572868
  129.1 2.0 %collective-permute-start.22 = (f32[256,512]{1,0:T(8,128)S(1)}, f32[256,512]{1,0:T(8,128)S(1)}, u32[]{:S(2)}, u32[]{:S(2)}) collective-permute-start(f32[256,512]{1,0:T(8,128)S(1)} %get-tuple-element.92), channel_id=1, source_target_pairs={{0,1},{1,0},{2,3},{3,2},{4,5},{5,4},{6,7},{7,6},{8,9},{9,8},{10,11... | collective-permute-start | bytes 1572872 | tf_op jit(solution)/shard_map/ppermute | solution.py:28
  131.8 7.8 %collective-permute-start.23 = (f32[64,512]{1,0:T(8,128)S(1)}, f32[64,512]{1,0:T(8,128)S(1)}, u32[]{:S(2)}, u32[]{:S(2)}) collective-permute-start(f32[64,512]{1,0:T(8,128)S(1)} %get-tuple-element.94), channel_id=1, source_target_pairs={{0,16},{1,17},{2,18},{3,19},{4,20},{5,21},{6,22},{7,23},{8,24},{9,... | collective-permute-start | bytes 393224 | tf_op jit(solution)/shard_map/ppermute | solution.py:28
  132.4 7.2 %collective-permute-start.24 = (f32[64,512]{1,0:T(8,128)S(1)}, f32[64,512]{1,0:T(8,128)S(1)}, u32[]{:S(2)}, u32[]{:S(2)}) collective-permute-start(f32[64,512]{1,0:T(8,128)S(1)} %get-tuple-element.95), channel_id=1, source_target_pairs={{0,48},{1,49},{2,50},{3,51},{4,52},{5,53},{6,54},{7,55},{8,56},{9,... | collective-permute-start | bytes 393224 | tf_op jit(solution)/shard_map/ppermute | solution.py:28
  140.4 10.2 %collective-permute-start.32 = (f32[128,512]{1,0:T(8,128)S(1)}, f32[128,512]{1,0:T(8,128)S(1)}, u32[]{:S(2)}, u32[]{:S(2)}) collective-permute-start(f32[128,512]{1,0:T(8,128)S(1)} %slice_bitcast_fusion.1), channel_id=1, source_target_pairs={{0,2},{1,3},{2,0},{3,1},{4,6},{5,7},{6,4},{7,5},{8,10},{9,11},{10,... | collective-permute-start | bytes 786440 | tf_op jit(solution)/shard_map/ppermute | solution.py:28
  141.0 9.6 %collective-permute-start.33 = (f32[128,512]{1,0:T(8,128)S(1)}, f32[128,512]{1,0:T(8,128)S(1)}, u32[]{:S(2)}, u32[]{:S(2)}) collective-permute-start(f32[128,512]{1,0:T(8,128)S(1)} %slice_bitcast_fusion), channel_id=1, source_target_pairs={{0,6},{1,7},{2,4},{3,5},{4,2},{5,3},{6,0},{7,1},{8,14},{9,15},{10,... | collective-permute-start | bytes 786440 | tf_op jit(solution)/shard_map/ppermute | solution.py:28
  142.5 10.8 %collective-permute-start.25 = (f32[192,512]{1,0:T(8,128)S(1)}, f32[192,512]{1,0:T(8,128)S(1)}, u32[]{:S(2)}, u32[]{:S(2)}) collective-permute-start(f32[192,512]{1,0:T(8,128)S(1)} %get-tuple-element.99), channel_id=1, source_target_pairs={{0,16},{1,17},{2,18},{3,19},{4,20},{5,21},{6,22},{7,23},{8,24},{9,... | collective-permute-start | bytes 1179656 | tf_op jit(solution)/shard_map/ppermute | solution.py:28
  143.1 11.0 %collective-permute-start.26 = (f32[192,512]{1,0:T(8,128)S(1)}, f32[192,512]{1,0:T(8,128)S(1)}, u32[]{:S(2)}, u32[]{:S(2)}) collective-permute-start(f32[192,512]{1,0:T(8,128)S(1)} %get-tuple-element.100), channel_id=1, source_target_pairs={{0,48},{1,49},{2,50},{3,51},{4,52},{5,53},{6,54},{7,55},{8,56},{9,... | collective-permute-start | bytes 1179656 | tf_op jit(solution)/shard_map/ppermute | solution.py:28
  153.1 4.4 %collective-permute-start.34 = (f32[256,512]{1,0:T(8,128)S(1)}, f32[256,512]{1,0:T(8,128)S(1)}, u32[]{:S(2)}, u32[]{:S(2)}) collective-permute-start(f32[256,512]{1,0:T(8,128)S(1)} %get-tuple-element.112), channel_id=1, source_target_pairs={{0,1},{1,0},{2,3},{3,2},{4,5},{5,4},{6,7},{7,6},{8,9},{9,8},{10,11... | collective-permute-start | bytes 1572872 | tf_op jit(solution)/shard_map/ppermute | solution.py:28
  154.8 9.3 %collective-permute-start.29 = (f32[128,512]{1,0:T(8,128)S(1)}, f32[128,512]{1,0:T(8,128)S(1)}, u32[]{:S(2)}, u32[]{:S(2)}) collective-permute-start(f32[128,512]{1,0:T(8,128)S(1)} %get-tuple-element.105), channel_id=1, source_target_pairs={{0,16},{1,17},{2,18},{3,19},{4,20},{5,21},{6,22},{7,23},{8,24},{9,... | collective-permute-start | bytes 786440 | tf_op jit(solution)/shard_map/ppermute | solution.py:28
  155.0 10.6 %collective-permute-start.30 = (f32[128,512]{1,0:T(8,128)S(1)}, f32[128,512]{1,0:T(8,128)S(1)}, u32[]{:S(2)}, u32[]{:S(2)}) collective-permute-start(f32[128,512]{1,0:T(8,128)S(1)} %get-tuple-element.106), channel_id=1, source_target_pairs={{0,48},{1,49},{2,50},{3,51},{4,52},{5,53},{6,54},{7,55},{8,56},{9,... | collective-permute-start | bytes 786440 | tf_op jit(solution)/shard_map/ppermute | solution.py:28
  157.5 8.1 %collective-permute-start.31 = (f32[128,512]{1,0:T(8,128)S(1)}, f32[128,512]{1,0:T(8,128)S(1)}, u32[]{:S(2)}, u32[]{:S(2)}) collective-permute-start(f32[128,512]{1,0:T(8,128)S(1)} %get-tuple-element.107), channel_id=1, source_target_pairs={{0,64},{1,65},{2,66},{3,67},{4,68},{5,69},{6,70},{7,71},{8,72},{9,... | collective-permute-start | bytes 786440 | tf_op jit(solution)/shard_map/ppermute | solution.py:28
  158.2 8.1 %collective-permute-start.35 = (f32[64,512]{1,0:T(8,128)S(1)}, f32[64,512]{1,0:T(8,128)S(1)}, u32[]{:S(2)}, u32[]{:S(2)}) collective-permute-start(f32[64,512]{1,0:T(8,128)S(1)} %get-tuple-element.114), channel_id=1, source_target_pairs={{0,16},{1,17},{2,18},{3,19},{4,20},{5,21},{6,22},{7,23},{8,24},{9,... | collective-permute-start | bytes 393224 | tf_op jit(solution)/shard_map/ppermute | solution.py:28
  159.4 7.7 %collective-permute-start.36 = (f32[64,512]{1,0:T(8,128)S(1)}, f32[64,512]{1,0:T(8,128)S(1)}, u32[]{:S(2)}, u32[]{:S(2)}) collective-permute-start(f32[64,512]{1,0:T(8,128)S(1)} %get-tuple-element.115), channel_id=1, source_target_pairs={{0,48},{1,49},{2,50},{3,51},{4,52},{5,53},{6,54},{7,55},{8,56},{9,... | collective-permute-start | bytes 393224 | tf_op jit(solution)/shard_map/ppermute | solution.py:28
  167.8 9.8 %collective-permute-start.37 = (f32[192,512]{1,0:T(8,128)S(1)}, f32[192,512]{1,0:T(8,128)S(1)}, u32[]{:S(2)}, u32[]{:S(2)}) collective-permute-start(f32[192,512]{1,0:T(8,128)S(1)} %get-tuple-element.118), channel_id=1, source_target_pairs={{0,16},{1,17},{2,18},{3,19},{4,20},{5,21},{6,22},{7,23},{8,24},{9,... | collective-permute-start | bytes 1179656 | tf_op jit(solution)/shard_map/ppermute | solution.py:28
  168.1 10.8 %collective-permute-start.38 = (f32[192,512]{1,0:T(8,128)S(1)}, f32[192,512]{1,0:T(8,128)S(1)}, u32[]{:S(2)}, u32[]{:S(2)}) collective-permute-start(f32[192,512]{1,0:T(8,128)S(1)} %get-tuple-element.119), channel_id=1, source_target_pairs={{0,48},{1,49},{2,50},{3,51},{4,52},{5,53},{6,54},{7,55},{8,56},{9,... | collective-permute-start | bytes 1179656 | tf_op jit(solution)/shard_map/ppermute | solution.py:28
  179.6 6.5 %collective-permute-start.39 = (f32[128,512]{1,0:T(8,128)S(1)}, f32[128,512]{1,0:T(8,128)S(1)}, u32[]{:S(2)}, u32[]{:S(2)}) collective-permute-start(f32[128,512]{1,0:T(8,128)S(1)} %get-tuple-element.120), channel_id=1, source_target_pairs={{0,16},{1,17},{2,18},{3,19},{4,20},{5,21},{6,22},{7,23},{8,24},{9,... | collective-permute-start | bytes 786440 | tf_op jit(solution)/shard_map/ppermute | solution.py:28
  180.2 7.6 %collective-permute-start.40 = (f32[128,512]{1,0:T(8,128)S(1)}, f32[128,512]{1,0:T(8,128)S(1)}, u32[]{:S(2)}, u32[]{:S(2)}) collective-permute-start(f32[128,512]{1,0:T(8,128)S(1)} %get-tuple-element.121), channel_id=1, source_target_pairs={{0,48},{1,49},{2,50},{3,51},{4,52},{5,53},{6,54},{7,55},{8,56},{9,... | collective-permute-start | bytes 786440 | tf_op jit(solution)/shard_map/ppermute | solution.py:28
  181.0 6.7 %collective-permute-start.41 = (f32[128,512]{1,0:T(8,128)S(1)}, f32[128,512]{1,0:T(8,128)S(1)}, u32[]{:S(2)}, u32[]{:S(2)}) collective-permute-start(f32[128,512]{1,0:T(8,128)S(1)} %get-tuple-element.122), channel_id=1, source_target_pairs={{0,64},{1,65},{2,66},{3,67},{4,68},{5,69},{6,70},{7,71},{8,72},{9,... | collective-permute-start | bytes 786440 | tf_op jit(solution)/shard_map/ppermute | solution.py:28
  (25 other events, 195.6 us)

commit v5 on v3

--- a/solution.py
+++ b/solution.py
@@ -67,10 +67,13 @@
         def _():
             parts = [arrays[array][lo : lo + size] for array, lo, size in block]
             a_hi, a_lo = split(parts[0] if len(parts) == 1 else jnp.concatenate(parts, axis=0))
+            a_both = jnp.concatenate([a_hi, a_lo], axis=0)
+            m = a_hi.shape[0]
             for j, (rhs, out) in enumerate(((own_ref, out_own), (far_ref, out_far))):
                 b_hi, b_lo = split(rhs[...])
                 dot = functools.partial(jnp.dot, preferred_element_type=jnp.float32)
-                term = dot(a_hi, b_hi) + (dot(a_hi, b_lo) + dot(a_lo, b_hi))
+                upper = dot(a_both, b_hi)
+                term = upper[:m] + (upper[m:] + dot(a_hi, b_lo))
                 if i == 0:
                     out[...] = term if first else adds[j][...] + term
                 else:
@@ -82,16 +85,16 @@
     m = sum(size for _, _, size in blocks[0])
     width = arrays[0].shape[1]
     cols = own.shape[1]
-    whole = lambda shape: pl.BlockSpec(shape, lambda s, at: (0, 0))
+    vmem = pl.BlockSpec(memory_space=pltpu.VMEM)
     return pl.pallas_call(
         functools.partial(product_kernel, blocks, len(arrays), not sums),
         grid_spec=pltpu.PrefetchScalarGridSpec(
             num_scalar_prefetch=1,
             grid=(n,),
-            in_specs=[whole(a.shape) for a in arrays]
+            in_specs=[vmem] * len(arrays)
             + [pl.BlockSpec((width, cols), lambda s, at: (at[s], 0))] * 2
-            + [whole((m, cols))] * len(sums),
-            out_specs=[whole((m, cols))] * 2,
+            + [vmem] * len(sums),
+            out_specs=[vmem] * 2,
         ),
         out_shape=[jax.ShapeDtypeStruct((m, cols), jnp.float32)] * 2,
         compiler_params=pltpu.CompilerParams(vmem_limit_bytes=50 * 1024 * 1024),
@@ -309,8 +312,13 @@
         places = (zh ^ gz) * 4 + (y + ring * (1 - 2 * (y % 2))) % 4
         at.append(places * 2 + core)
 
-    def rows_first(piece):
-        return [piece, flip_z(piece), swap_x(piece, 0), swap_x(piece, 1)]
+    def rows_first(piece, before=None):
+        beside, later = (), ()
+        if before is not None:
+            beside, later = before[1:4], before[4:6]
+        other = flip_z(wait_for(piece, *beside))
+        own = wait_for(piece, *later)
+        return [piece, other, swap_x(own, 0), swap_x(own, 1)]
 
     def rows_second(arrays):
         return arrays + list(gather_second(arrays[2:4], arrays[1], swap_x, local_tiles))
@@ -345,11 +353,11 @@
         b, crossing = pick(plan, m, arrays, after)
         this = dict(m=SLOTS * m, sums=[])
         if more:
-            arrays = rows_first(wait_for(pieces[k + 1], b))
+            arrays = rows_first(pieces[k + 1], arrays)
         near = [swap_y(b, 0), swap_y(b, 1)]
         bz = cross_z(crossing)
         this["first"] = [b, *near, bz]
-        ready = arrays if more else []
+        ready = []
         if last is not None:
             sums, back = finish(last, back)
             swapped = flip_core(sums[1])

time: 168 us -> 167 us (level)
  starting transfers between devices: 54 us -> 50 us
  waiting for transfers between devices: 58 us -> 60.6 us
    ppermute x45, starting transfers between devices: 54 us -> 50 us  [send(): lax.ppermute(a, ('row', 'col'), [(i, index[to(*p)]) for p, i in index.ite...]
    ppermute x45, waiting for transfers between devices: 58 us -> 60.6 us  [send(): lax.ppermute(a, ('row', 'col'), [(i, index[to(*p)]) for p, i in index.ite...]
  transfers between devices with their start and end apart: 45 -> 45, of which waited for: 22 -> 23; matrix products, arithmetic and copies ran while one was open for 7% -> 7% of each run, Pallas kernels for 22% -> 23%
where the time goes in v5:
time: 167 us
  waiting for transfers between devices  60.6 us (36%)
  starting transfers between devices  50 us (30%)
  Pallas kernels  39.6 us (24%)
  local copies, waits for them, and re-layouts  9.51 us (6%)
  other arithmetic  6.57 us (4%)
    ppermute x45, waiting for transfers between devices, send(): lax.ppermute(a, ('row', 'col'), [(i, index[to(*p)]) for p, i in index.ite...  60.6 us
    ppermute x45, starting transfers between devices, send(): lax.ppermute(a, ('row', 'col'), [(i, index[to(*p)]) for p, i in index.ite...  50 us
    pallas_call x6, Pallas kernels, products(): pl.pallas_call(functools.partial(product_kernel, blocks, len(arrays), not...  30.5 us
    pallas_call x10, Pallas kernels, small_kernel(): pl.pallas_call(kernel, in_specs=[pl.BlockSpec(memory_space=pltpu.SMEM)] +...  9.08 us
  transfers between devices with their start and end apart: 45, of which 23 were waited for; matrix products, arithmetic and copies ran while one was open for 7% of the time, Pallas kernels for 23%

profile of v5, /device:TPU:0, one launch (start us, length us, event | category | flops | bytes accessed | tf_op | source)
XLA Modules:
  0.0 166.9 jit_solution(9801041303253521213)
XLA Ops:
  0.0 1.8 %fusion.8 = (f32[2,64,512]{2,1,0:T(8,128)S(1)}, f32[2,64,512]{2,1,0:T(8,128)}) fusion(f32[2,128,512]{2,1,0:T(8,128)} %bitcast.98), kind=kLoop, calls=%fused_computation.43 | loop fusion | bytes 1048576 | tf_op jit(solution)/shard_map/slice | solution.py:305
  1.8 1.6 collective-permute-start.1
  3.4 2.1 %collective-permute-start.2 = (f32[128,512]{1,0:T(8,128)S(1)}, f32[128,512]{1,0:T(8,128)S(1)}, u32[]{:S(2)}, u32[]{:S(2)}) collective-permute-start(f32[128,512]{1,0:T(8,128)S(1)} %bitcast.72), channel_id=1, source_target_pairs={{0,48},{1,49},{2,50},{3,51},{4,52},{5,53},{6,54},{7,55},{8,56},{9,... | collective-permute-start | bytes 786440 | tf_op jit(solution)/shard_map/ppermute | solution.py:27
  5.5 1.9 %collective-permute-start = (f32[128,512]{1,0:T(8,128)S(1)}, f32[128,512]{1,0:T(8,128)S(1)}, u32[]{:S(2)}, u32[]{:S(2)}) collective-permute-start(f32[128,512]{1,0:T(8,128)S(1)} %bitcast.73), channel_id=1, source_target_pairs={{0,64},{1,65},{2,66},{3,67},{4,68},{5,69},{6,70},{7,71},{8,72},{9,... | collective-permute-start | bytes 786440 | tf_op jit(solution)/shard_map/ppermute | solution.py:27
  8.0 2.5 %collective-permute-done.1.refs_2_ = f32[128,512]{1,0:T(8,128)S(1)} collective-permute-done((f32[128,512]{1,0:T(8,128)S(1)}, f32[128,512]{1,0:T(8,128)S(1)}, u32[]{:S(2)}, u32[]{:S(2)}) %collective-permute-start.1) | collective-permute-done | bytes 262176 | tf_op jit(solution)/shard_map/ppermute | solution.py:27
  10.5 2.5 %collective-permute-done.2.refs_3_ = f32[128,512]{1,0:T(8,128)S(1)} collective-permute-done((f32[128,512]{1,0:T(8,128)S(1)}, f32[128,512]{1,0:T(8,128)S(1)}, u32[]{:S(2)}, u32[]{:S(2)}) %collective-permute-start.2) | collective-permute-done | bytes 262176 | tf_op jit(solution)/shard_map/ppermute | solution.py:27
  17.9 7.8 %collective-permute-done.4.refs_5_ = f32[192,512]{1,0:T(8,128)S(1)} collective-permute-done((f32[192,512]{1,0:T(8,128)S(1)}, f32[192,512]{1,0:T(8,128)S(1)}, u32[]{:S(2)}, u32[]{:S(2)}) %collective-permute-start.4) | collective-permute-done | bytes 393248 | tf_op jit(solution)/shard_map/ppermute | solution.py:27
  26.2 1.5 collective-permute-start.6
  27.9 3.0 %collective-permute-done.5.refs_6_ = f32[64,512]{1,0:T(8,128)S(1)} collective-permute-done((f32[64,512]{1,0:T(8,128)S(1)}, f32[64,512]{1,0:T(8,128)S(1)}, u32[]{:S(2)}, u32[]{:S(2)}) %collective-permute-start.5) | collective-permute-done | bytes 131104 | tf_op jit(solution)/shard_map/ppermute | solution.py:27
  30.9 1.6 collective-permute-done.6.refs_7_
  33.5 1.7 collective-permute-start.7
  35.1 2.2 %collective-permute-start.8 = (f32[256,512]{1,0:T(8,128)S(1)}, f32[256,512]{1,0:T(8,128)S(1)}, u32[]{:S(2)}, u32[]{:S(2)}) collective-permute-start(f32[256,512]{1,0:T(8,128)S(1)} %get-tuple-element.65.refs_0_), channel_id=1, source_target_pairs={{0,6},{1,7},{2,4},{3,5},{4,2},{5,3},{6,0},{7,1},{8,14},{9,15},{10,... | collective-permute-start | bytes 1572872 | tf_op jit(solution)/shard_map/ppermute | solution.py:27
  37.3 3.7 %collective-permute-start.9 = (f32[256,512]{1,0:T(8,128)S(1)}, f32[256,512]{1,0:T(8,128)S(1)}, u32[]{:S(2)}, u32[]{:S(2)}) collective-permute-start(f32[256,512]{1,0:T(8,128)S(1)} %get-tuple-element.66), channel_id=1, source_target_pairs={{0,72},{1,73},{2,74},{3,75},{4,76},{5,77},{6,78},{7,79},{8,64},{9,... | collective-permute-start | bytes 1572872 | tf_op jit(solution)/shard_map/ppermute | solution.py:27
  41.0 3.1 %collective-permute-done.7.refs_1_ = f32[256,512]{1,0:T(8,128)S(1)} collective-permute-done((f32[256,512]{1,0:T(8,128)S(1)}, f32[256,512]{1,0:T(8,128)S(1)}, u32[]{:S(2)}, u32[]{:S(2)}) %collective-permute-start.7) | collective-permute-done | bytes 524320 | tf_op jit(solution)/shard_map/ppermute | solution.py:27
  44.9 1.7 %collective-permute-done.8.refs_2_ = f32[256,512]{1,0:T(8,128)S(1)} collective-permute-done((f32[256,512]{1,0:T(8,128)S(1)}, f32[256,512]{1,0:T(8,128)S(1)}, u32[]{:S(2)}, u32[]{:S(2)}) %collective-permute-start.8) | collective-permute-done | bytes 524320 | tf_op jit(solution)/shard_map/ppermute | solution.py:27
  46.6 1.6 collective-permute-start.15
  49.1 1.3 pad_maximum_fusion
  52.0 2.5 %collective-permute-done.15.refs_3_ = f32[128,512]{1,0:T(8,128)} collective-permute-done((f32[128,512]{1,0:T(8,128)}, f32[128,512]{1,0:T(8,128)}, u32[]{:S(2)}, u32[]{:S(2)}) %collective-permute-start.15) | collective-permute-done | bytes 262176 | tf_op jit(solution)/shard_map/ppermute | solution.py:27
  56.5 1.7 %collective-permute-start.17 = (f32[192,512]{1,0:T(8,128)S(1)}, f32[192,512]{1,0:T(8,128)S(1)}, u32[]{:S(2)}, u32[]{:S(2)}) collective-permute-start(f32[192,512]{1,0:T(8,128)S(1)} %get-tuple-element.131), channel_id=1, source_target_pairs={{0,48},{1,49},{2,50},{3,51},{4,52},{5,53},{6,54},{7,55},{8,56},{9,... | collective-permute-start | bytes 1179656 | tf_op jit(solution)/shard_map/ppermute | solution.py:27
  61.0 6.8 %products.6 = (f32[256,512]{1,0:T(8,128)S(1)}, f32[256,512]{1,0:T(8,128)S(1)}) custom-call(s32[4]{0:T(128)S(1)} %multiply_add_fusion.1.at_ref, f32[256,512]{1,0:T(8,128)S(1)} %copy-done.3, f32[256,512]{1,0:T(8,128)S(1)} %collective-permute-done.7.refs_1_, f32[256,512]{1,0:T(8,128)S(1)} %copy-done.1, f32[256,512]{1,0:T(8,128)S(1)} %collective-permute-done.9.refs_3_, ...), custom_call_target="tpu_custom_call" | custom-call | flops 3221225472 | bytes 10485760 | tf_op jit(solution)/shard_map/products/pallas_call | solution.py:89
  67.9 1.4 collective-permute-start.23
  69.4 1.7 %collective-permute-start.24 = (f32[64,512]{1,0:T(8,128)S(1)}, f32[64,512]{1,0:T(8,128)S(1)}, u32[]{:S(2)}, u32[]{:S(2)}) collective-permute-start(f32[64,512]{1,0:T(8,128)S(1)} %bitcast.100), channel_id=1, source_target_pairs={{0,48},{1,49},{2,50},{3,51},{4,52},{5,53},{6,54},{7,55},{8,56},{9,... | collective-permute-start | bytes 393224 | tf_op jit(solution)/shard_map/ppermute | solution.py:27
  72.6 2.2 %collective-permute-start.19 = (f32[128,512]{1,0:T(8,128)}, f32[128,512]{1,0:T(8,128)}, u32[]{:S(2)}, u32[]{:S(2)}) collective-permute-start(f32[128,512]{1,0:T(8,128)} %slice_bitcast_fusion.4), channel_id=1, source_target_pairs={{0,6},{1,7},{2,4},{3,5},{4,2},{5,3},{6,0},{7,1},{8,14},{9,15},{10,... | collective-permute-start | bytes 786440 | tf_op jit(solution)/shard_map/ppermute | solution.py:27
  75.6 2.8 %pick.3 = (f32[256,512]{1,0:T(8,128)}, f32[256,512]{1,0:T(8,128)}) custom-call(s32[24]{0:T(128)S(1)} %pad_add_fusion.plan_ref, f32[128,512]{1,0:T(8,128)} %bitcast.19.refs_0_, f32[128,512]{1,0:T(8,128)S(1)} %collective-permute-done.13.refs_1_, f32[128,512]{1,0:T(8,128)} %collective-permute-done.14.refs_2_, f32[128,512]{1,0:T(8,128)} %collective-permute-done.15.refs_3_, ...), custom_call_target="tpu_custom_call" | custom-call | bytes 1048576 | tf_op jit(solution)/shard_map/pick/pallas_call | solution.py:114
  79.0 1.7 collective-permute-start.26
  80.7 4.1 %collective-permute-start.27 = (f32[256,512]{1,0:T(8,128)}, f32[256,512]{1,0:T(8,128)S(1)}, u32[]{:S(2)}, u32[]{:S(2)}) collective-permute-start(f32[256,512]{1,0:T(8,128)} %get-tuple-element.94), channel_id=1, source_target_pairs={{0,72},{1,73},{2,74},{3,75},{4,76},{5,77},{6,78},{7,79},{8,64},{9,... | collective-permute-start | bytes 1572872 | tf_op jit(solution)/shard_map/ppermute | solution.py:27
  85.8 5.7 %products.7 = (f32[256,512]{1,0:T(8,128)S(1)}, f32[256,512]{1,0:T(8,128)S(1)}) custom-call(s32[3]{0:T(128)S(1)} %multiply_add_fusion.at_ref, f32[384,512]{1,0:T(8,128)S(1)} %collective-permute-done.10.refs_0_.refs_8_, f32[384,512]{1,0:T(8,128)S(1)} %collective-permute-done.11.refs_1_, f32[8192,512]{1,0:T(8,128)} %bitcast.81, ...), custom_call_target="tpu_custom_call" | custom-call | flops 2415919104 | bytes 7864320 | tf_op jit(solution)/shard_map/products/pallas_call | solution.py:89
  91.5 2.7 %products.8 = (f32[256,512]{1,0:T(8,128)S(1)}, f32[256,512]{1,0:T(8,128)S(1)}) custom-call(s32[1]{0:T(128)S(6)} %add.113.at_ref, f32[128,512]{1,0:T(8,128)} %collective-permute-done.18.refs_0_, f32[128,512]{1,0:T(8,128)} %collective-permute-done.19.refs_1_, f32[8192,512]{1,0:T(8,128)} %bitcast.82, f32[8192,512]{1,0:T(8,128)} %collective-permute-done.12.refs_5_.refs_3_, ...), custom_call_target="tpu_custom_call" | custom-call | flops 805306368 | bytes 2621440 | tf_op jit(solution)/shard_map/products/pallas_call | solution.py:89
  95.6 1.4 collective-permute-start.30
  97.0 1.1 collective-permute-start.31
  98.8 1.1 collective-permute-start.22
  99.9 7.1 %products.9 = (f32[256,512]{1,0:T(8,128)S(1)}, f32[256,512]{1,0:T(8,128)S(1)}) custom-call(s32[4]{0:T(128)S(1)} %multiply_add_fusion.1.at_ref, f32[256,512]{1,0:T(8,128)} %get-tuple-element.93.refs_0_, f32[256,512]{1,0:T(8,128)S(1)} %collective-permute-done.25.refs_1_, f32[256,512]{1,0:T(8,128)} %collective-permute-done.26.refs_2_, ...), custom_call_target="tpu_custom_call" | custom-call | flops 3221225472 | bytes 10485760 | tf_op jit(solution)/shard_map/products/pallas_call | solution.py:89
  107.8 7.8 %collective-permute-done.30.refs_0_ = f32[384,512]{1,0:T(8,128)S(1)} collective-permute-done((f32[384,512]{1,0:T(8,128)S(1)}, f32[384,512]{1,0:T(8,128)S(1)}, u32[]{:S(2)}, u32[]{:S(2)}) %collective-permute-start.30) | collective-permute-done | bytes 786464 | tf_op jit(solution)/shard_map/ppermute | solution.py:27
  115.6 2.3 %collective-permute-done.31.refs_1_ = f32[384,512]{1,0:T(8,128)S(1)} collective-permute-done((f32[384,512]{1,0:T(8,128)S(1)}, f32[384,512]{1,0:T(8,128)S(1)}, u32[]{:S(2)}, u32[]{:S(2)}) %collective-permute-start.31) | collective-permute-done | bytes 786464 | tf_op jit(solution)/shard_map/ppermute | solution.py:27
  118.1 1.1 collective-permute-start.36
  119.2 1.7 collective-permute-start.29
  120.9 5.7 %products.10 = (f32[256,512]{1,0:T(8,128)S(1)}, f32[256,512]{1,0:T(8,128)S(1)}) custom-call(s32[3]{0:T(128)S(1)} %multiply_add_fusion.at_ref, f32[384,512]{1,0:T(8,128)S(1)} %collective-permute-done.30.refs_0_, f32[384,512]{1,0:T(8,128)S(1)} %collective-permute-done.31.refs_1_, f32[8192,512]{1,0:T(8,128)} %bitcast.84, ...), custom_call_target="tpu_custom_call" | custom-call | flops 2415919104 | bytes 7864320 | tf_op jit(solution)/shard_map/products/pallas_call | solution.py:89
  126.9 2.5 %products.11 = (f32[256,512]{1,0:T(8,128)S(1)}, f32[256,512]{1,0:T(8,128)S(1)}) custom-call(s32[1]{0:T(128)S(6)} %add.113.at_ref, f32[128,512]{1,0:T(8,128)S(1)} %collective-permute-done.35.refs_0_, f32[128,512]{1,0:T(8,128)S(1)} %collective-permute-done.36.refs_1_, f32[8192,512]{1,0:T(8,128)} %bitcast.85, ...), custom_call_target="tpu_custom_call" | custom-call | flops 805306368 | bytes 2621440 | tf_op jit(solution)/shard_map/products/pallas_call | solution.py:89
  131.9 1.3 collective-permute-start.33
  134.8 2.0 %collective-permute-start.39 = (f32[64,512]{1,0:T(8,128)S(1)}, f32[64,512]{1,0:T(8,128)S(1)}, u32[]{:S(2)}, u32[]{:S(2)}) collective-permute-start(f32[64,512]{1,0:T(8,128)S(1)} %get-tuple-element.117), channel_id=1, source_target_pairs={{0,48},{1,49},{2,50},{3,51},{4,52},{5,53},{6,54},{7,55},{8,56},{9,... | collective-permute-start | bytes 393224 | tf_op jit(solution)/shard_map/ppermute | solution.py:27
  136.7 3.8 %collective-permute-done.32.refs_1_ = f32[128,512]{1,0:T(8,128)S(1)} collective-permute-done((f32[128,512]{1,0:T(8,128)S(1)}, f32[128,512]{1,0:T(8,128)S(1)}, u32[]{:S(2)}, u32[]{:S(2)}) %collective-permute-start.32) | collective-permute-done | bytes 262176 | tf_op jit(solution)/shard_map/ppermute | solution.py:27
  140.5 1.8 %collective-permute-done.33.refs_2_ = f32[128,512]{1,0:T(8,128)S(1)} collective-permute-done((f32[128,512]{1,0:T(8,128)S(1)}, f32[128,512]{1,0:T(8,128)S(1)}, u32[]{:S(2)}, u32[]{:S(2)}) %collective-permute-start.33) | collective-permute-done | bytes 262176 | tf_op jit(solution)/shard_map/ppermute | solution.py:27
  144.6 1.8 %collective-permute-start.41 = (f32[192,512]{1,0:T(8,128)S(1)}, f32[192,512]{1,0:T(8,128)S(1)}, u32[]{:S(2)}, u32[]{:S(2)}) collective-permute-start(f32[192,512]{1,0:T(8,128)S(1)} %get-tuple-element.121), channel_id=1, source_target_pairs={{0,48},{1,49},{2,50},{3,51},{4,52},{5,53},{6,54},{7,55},{8,56},{9,... | collective-permute-start | bytes 1179656 | tf_op jit(solution)/shard_map/ppermute | solution.py:27
  146.3 8.0 %collective-permute-done.40.refs_1_ = f32[192,512]{1,0:T(8,128)S(1)} collective-permute-done((f32[192,512]{1,0:T(8,128)S(1)}, f32[192,512]{1,0:T(8,128)S(1)}, u32[]{:S(2)}, u32[]{:S(2)}) %collective-permute-start.40) | collective-permute-done | bytes 393248 | tf_op jit(solution)/shard_map/ppermute | solution.py:27
  154.4 1.3 collective-permute-done.41.refs_2_
  156.9 2.1 %collective-permute-start.43 = (f32[128,512]{1,0:T(8,128)S(1)}, f32[128,512]{1,0:T(8,128)S(1)}, u32[]{:S(2)}, u32[]{:S(2)}) collective-permute-start(f32[128,512]{1,0:T(8,128)S(1)} %get-tuple-element.123), channel_id=1, source_target_pairs={{0,48},{1,49},{2,50},{3,51},{4,52},{5,53},{6,54},{7,55},{8,56},{9,... | collective-permute-start | bytes 786440 | tf_op jit(solution)/shard_map/ppermute | solution.py:27
  159.0 3.8 %collective-permute-done.42.refs_1_ = f32[128,512]{1,0:T(8,128)S(1)} collective-permute-done((f32[128,512]{1,0:T(8,128)S(1)}, f32[128,512]{1,0:T(8,128)S(1)}, u32[]{:S(2)}, u32[]{:S(2)}) %collective-permute-start.42) | collective-permute-done | bytes 262176 | tf_op jit(solution)/shard_map/ppermute | solution.py:27
  162.8 1.7 collective-permute-done.43.refs_2_
  (112 shorter events, 32.2 us)
Async XLA Ops:
  0.0 58.9 %collective-permute-start.12 = (f32[8192,512]{1,0:T(8,128)}, f32[8192,512]{1,0:T(8,128)}, u32[]{:S(2)}, u32[]{:S(2)}) collective-permute-start(f32[8192,512]{1,0:T(8,128)} %bitcast.79), channel_id=1, source_target_pairs={{0,1},{1,0},{2,3},{3,2},{4,5},{5,4},{6,7},{7,6},{8,9},{9,8},{10,11... | collective-permute-start | bytes 50331656 | tf_op jit(solution)/shard_map/ppermute | solution.py:27
  1.8 8.7 %collective-permute-start.1 = (f32[128,512]{1,0:T(8,128)S(1)}, f32[128,512]{1,0:T(8,128)S(1)}, u32[]{:S(2)}, u32[]{:S(2)}) collective-permute-start(f32[128,512]{1,0:T(8,128)S(1)} %bitcast.71), channel_id=1, source_target_pairs={{0,16},{1,17},{2,18},{3,19},{4,20},{5,21},{6,22},{7,23},{8,24},{9,... | collective-permute-start | bytes 786440 | tf_op jit(solution)/shard_map/ppermute | solution.py:27
  3.4 9.6 %collective-permute-start.2 = (f32[128,512]{1,0:T(8,128)S(1)}, f32[128,512]{1,0:T(8,128)S(1)}, u32[]{:S(2)}, u32[]{:S(2)}) collective-permute-start(f32[128,512]{1,0:T(8,128)S(1)} %bitcast.72), channel_id=1, source_target_pairs={{0,48},{1,49},{2,50},{3,51},{4,52},{5,53},{6,54},{7,55},{8,56},{9,... | collective-permute-start | bytes 786440 | tf_op jit(solution)/shard_map/ppermute | solution.py:27
  5.5 8.3 %collective-permute-start = (f32[128,512]{1,0:T(8,128)S(1)}, f32[128,512]{1,0:T(8,128)S(1)}, u32[]{:S(2)}, u32[]{:S(2)}) collective-permute-start(f32[128,512]{1,0:T(8,128)S(1)} %bitcast.73), channel_id=1, source_target_pairs={{0,64},{1,65},{2,66},{3,67},{4,68},{5,69},{6,70},{7,71},{8,72},{9,... | collective-permute-start | bytes 786440 | tf_op jit(solution)/shard_map/ppermute | solution.py:27
  13.9 12.3 %collective-permute-start.3 = (f32[192,512]{1,0:T(8,128)S(1)}, f32[192,512]{1,0:T(8,128)S(1)}, u32[]{:S(2)}, u32[]{:S(2)}) collective-permute-start(f32[192,512]{1,0:T(8,128)S(1)} %get-tuple-element.134), channel_id=1, source_target_pairs={{0,16},{1,17},{2,18},{3,19},{4,20},{5,21},{6,22},{7,23},{8,24},{9,... | collective-permute-start | bytes 1179656 | tf_op jit(solution)/shard_map/ppermute | solution.py:27
  14.5 11.2 %collective-permute-start.4 = (f32[192,512]{1,0:T(8,128)S(1)}, f32[192,512]{1,0:T(8,128)S(1)}, u32[]{:S(2)}, u32[]{:S(2)}) collective-permute-start(f32[192,512]{1,0:T(8,128)S(1)} %get-tuple-element.133), channel_id=1, source_target_pairs={{0,48},{1,49},{2,50},{3,51},{4,52},{5,53},{6,54},{7,55},{8,56},{9,... | collective-permute-start | bytes 1179656 | tf_op jit(solution)/shard_map/ppermute | solution.py:27
  25.8 5.0 %collective-permute-start.5 = (f32[64,512]{1,0:T(8,128)S(1)}, f32[64,512]{1,0:T(8,128)S(1)}, u32[]{:S(2)}, u32[]{:S(2)}) collective-permute-start(f32[64,512]{1,0:T(8,128)S(1)} %bitcast.101), channel_id=1, source_target_pairs={{0,16},{1,17},{2,18},{3,19},{4,20},{5,21},{6,22},{7,23},{8,24},{9,... | collective-permute-start | bytes 393224 | tf_op jit(solution)/shard_map/ppermute | solution.py:27
  26.2 6.3 %collective-permute-start.6 = (f32[64,512]{1,0:T(8,128)S(1)}, f32[64,512]{1,0:T(8,128)S(1)}, u32[]{:S(2)}, u32[]{:S(2)}) collective-permute-start(f32[64,512]{1,0:T(8,128)S(1)} %bitcast.102), channel_id=1, source_target_pairs={{0,48},{1,49},{2,50},{3,51},{4,52},{5,53},{6,54},{7,55},{8,56},{9,... | collective-permute-start | bytes 393224 | tf_op jit(solution)/shard_map/ppermute | solution.py:27
  33.5 17.7 %copy-start.2 = (f32[256,512]{1,0:T(8,128)}, f32[256,512]{1,0:T(8,128)S(1)}, u32[]{:S(2)}) copy-start(f32[256,512]{1,0:T(8,128)S(1)} %get-tuple-element.65.refs_0_) | copy-start | bytes 1572868
  33.5 10.6 %collective-permute-start.7 = (f32[256,512]{1,0:T(8,128)S(1)}, f32[256,512]{1,0:T(8,128)S(1)}, u32[]{:S(2)}, u32[]{:S(2)}) collective-permute-start(f32[256,512]{1,0:T(8,128)S(1)} %get-tuple-element.65.refs_0_), channel_id=1, source_target_pairs={{0,2},{1,3},{2,0},{3,1},{4,6},{5,7},{6,4},{7,5},{8,10},{9,11},{10,... | collective-permute-start | bytes 1572872 | tf_op jit(solution)/shard_map/ppermute | solution.py:27
  35.1 11.5 %collective-permute-start.8 = (f32[256,512]{1,0:T(8,128)S(1)}, f32[256,512]{1,0:T(8,128)S(1)}, u32[]{:S(2)}, u32[]{:S(2)}) collective-permute-start(f32[256,512]{1,0:T(8,128)S(1)} %get-tuple-element.65.refs_0_), channel_id=1, source_target_pairs={{0,6},{1,7},{2,4},{3,5},{4,2},{5,3},{6,0},{7,1},{8,14},{9,15},{10,... | collective-permute-start | bytes 1572872 | tf_op jit(solution)/shard_map/ppermute | solution.py:27
  37.3 11.7 %collective-permute-start.9 = (f32[256,512]{1,0:T(8,128)S(1)}, f32[256,512]{1,0:T(8,128)S(1)}, u32[]{:S(2)}, u32[]{:S(2)}) collective-permute-start(f32[256,512]{1,0:T(8,128)S(1)} %get-tuple-element.66), channel_id=1, source_target_pairs={{0,72},{1,73},{2,74},{3,75},{4,76},{5,77},{6,78},{7,79},{8,64},{9,... | collective-permute-start | bytes 1572872 | tf_op jit(solution)/shard_map/ppermute | solution.py:27
  41.0 10.1 %collective-permute-start.13 = (f32[128,512]{1,0:T(8,128)}, f32[128,512]{1,0:T(8,128)S(1)}, u32[]{:S(2)}, u32[]{:S(2)}) collective-permute-start(f32[128,512]{1,0:T(8,128)} %bitcast.19.refs_0_), channel_id=1, source_target_pairs={{0,64},{1,65},{2,66},{3,67},{4,68},{5,69},{6,70},{7,71},{8,72},{9,... | collective-permute-start | bytes 786440 | tf_op jit(solution)/shard_map/ppermute | solution.py:27
  44.1 7.9 %collective-permute-start.14 = (f32[128,512]{1,0:T(8,128)}, f32[128,512]{1,0:T(8,128)}, u32[]{:S(2)}, u32[]{:S(2)}) collective-permute-start(f32[128,512]{1,0:T(8,128)} %bitcast.19.refs_0_), channel_id=1, source_target_pairs={{0,16},{1,17},{2,18},{3,19},{4,20},{5,21},{6,22},{7,23},{8,24},{9,... | collective-permute-start | bytes 786440 | tf_op jit(solution)/shard_map/ppermute | solution.py:27
  46.6 7.9 %collective-permute-start.15 = (f32[128,512]{1,0:T(8,128)}, f32[128,512]{1,0:T(8,128)}, u32[]{:S(2)}, u32[]{:S(2)}) collective-permute-start(f32[128,512]{1,0:T(8,128)} %bitcast.19.refs_0_), channel_id=1, source_target_pairs={{0,48},{1,49},{2,50},{3,51},{4,52},{5,53},{6,54},{7,55},{8,56},{9,... | collective-permute-start | bytes 786440 | tf_op jit(solution)/shard_map/ppermute | solution.py:27
  50.4 20.7 %collective-permute-start.10 = (f32[384,512]{1,0:T(8,128)}, f32[384,512]{1,0:T(8,128)S(1)}, u32[]{:S(2)}, u32[]{:S(2)}) collective-permute-start(f32[384,512]{1,0:T(8,128)} %get-tuple-element.128), channel_id=1, source_target_pairs={{0,2},{1,3},{2,0},{3,1},{4,6},{5,7},{6,4},{7,5},{8,10},{9,11},{10,... | collective-permute-start | bytes 2359304 | tf_op jit(solution)/shard_map/ppermute | solution.py:27
  51.1 20.0 %collective-permute-start.11 = (f32[384,512]{1,0:T(8,128)}, f32[384,512]{1,0:T(8,128)S(1)}, u32[]{:S(2)}, u32[]{:S(2)}) collective-permute-start(f32[384,512]{1,0:T(8,128)} %get-tuple-element.127), channel_id=1, source_target_pairs={{0,6},{1,7},{2,4},{3,5},{4,2},{5,3},{6,0},{7,1},{8,14},{9,15},{10,... | collective-permute-start | bytes 2359304 | tf_op jit(solution)/shard_map/ppermute | solution.py:27
  56.5 11.4 %collective-permute-start.16 = (f32[192,512]{1,0:T(8,128)S(1)}, f32[192,512]{1,0:T(8,128)S(1)}, u32[]{:S(2)}, u32[]{:S(2)}) collective-permute-start(f32[192,512]{1,0:T(8,128)S(1)} %get-tuple-element.132), channel_id=1, source_target_pairs={{0,16},{1,17},{2,18},{3,19},{4,20},{5,21},{6,22},{7,23},{8,24},{9,... | collective-permute-start | bytes 1179656 | tf_op jit(solution)/shard_map/ppermute | solution.py:27
  56.5 11.3 %collective-permute-start.17 = (f32[192,512]{1,0:T(8,128)S(1)}, f32[192,512]{1,0:T(8,128)S(1)}, u32[]{:S(2)}, u32[]{:S(2)}) collective-permute-start(f32[192,512]{1,0:T(8,128)S(1)} %get-tuple-element.131), channel_id=1, source_target_pairs={{0,48},{1,49},{2,50},{3,51},{4,52},{5,53},{6,54},{7,55},{8,56},{9,... | collective-permute-start | bytes 1179656 | tf_op jit(solution)/shard_map/ppermute | solution.py:27
  61.0 23.7 %copy-start.6 = (s32[3]{0:T(128)S(1)}, s32[3]{0:T(128)}, u32[]{:S(2)}) copy-start(s32[3]{0:T(128)} %constant.164.clone) | copy-start | bytes 40
  61.0 23.7 %copy-start.7 = (s32[3]{0:T(128)S(1)}, s32[3]{0:T(128)}, u32[]{:S(2)}) copy-start(s32[3]{0:T(128)} %constant.163.clone) | copy-start | bytes 40
  67.9 6.9 %collective-permute-start.23 = (f32[64,512]{1,0:T(8,128)S(1)}, f32[64,512]{1,0:T(8,128)S(1)}, u32[]{:S(2)}, u32[]{:S(2)}) collective-permute-start(f32[64,512]{1,0:T(8,128)S(1)} %bitcast.99), channel_id=1, source_target_pairs={{0,16},{1,17},{2,18},{3,19},{4,20},{5,21},{6,22},{7,23},{8,24},{9,... | collective-permute-start | bytes 393224 | tf_op jit(solution)/shard_map/ppermute | solution.py:27
  69.4 6.3 %collective-permute-start.24 = (f32[64,512]{1,0:T(8,128)S(1)}, f32[64,512]{1,0:T(8,128)S(1)}, u32[]{:S(2)}, u32[]{:S(2)}) collective-permute-start(f32[64,512]{1,0:T(8,128)S(1)} %bitcast.100), channel_id=1, source_target_pairs={{0,48},{1,49},{2,50},{3,51},{4,52},{5,53},{6,54},{7,55},{8,56},{9,... | collective-permute-start | bytes 393224 | tf_op jit(solution)/shard_map/ppermute | solution.py:27
  71.9 19.7 %collective-permute-start.18 = (f32[128,512]{1,0:T(8,128)}, f32[128,512]{1,0:T(8,128)}, u32[]{:S(2)}, u32[]{:S(2)}) collective-permute-start(f32[128,512]{1,0:T(8,128)} %slice_bitcast_fusion.5), channel_id=1, source_target_pairs={{0,2},{1,3},{2,0},{3,1},{4,6},{5,7},{6,4},{7,5},{8,10},{9,11},{10,... | collective-permute-start | bytes 786440 | tf_op jit(solution)/shard_map/ppermute | solution.py:27
  72.6 18.9 %collective-permute-start.19 = (f32[128,512]{1,0:T(8,128)}, f32[128,512]{1,0:T(8,128)}, u32[]{:S(2)}, u32[]{:S(2)}) collective-permute-start(f32[128,512]{1,0:T(8,128)} %slice_bitcast_fusion.4), channel_id=1, source_target_pairs={{0,6},{1,7},{2,4},{3,5},{4,2},{5,3},{6,0},{7,1},{8,14},{9,15},{10,... | collective-permute-start | bytes 786440 | tf_op jit(solution)/shard_map/ppermute | solution.py:27
  78.4 15.9 %collective-permute-start.25 = (f32[256,512]{1,0:T(8,128)}, f32[256,512]{1,0:T(8,128)S(1)}, u32[]{:S(2)}, u32[]{:S(2)}) collective-permute-start(f32[256,512]{1,0:T(8,128)} %get-tuple-element.93.refs_0_), channel_id=1, source_target_pairs={{0,2},{1,3},{2,0},{3,1},{4,6},{5,7},{6,4},{7,5},{8,10},{9,11},{10,... | collective-permute-start | bytes 1572872 | tf_op jit(solution)/shard_map/ppermute | solution.py:27
  79.0 15.4 %collective-permute-start.26 = (f32[256,512]{1,0:T(8,128)}, f32[256,512]{1,0:T(8,128)}, u32[]{:S(2)}, u32[]{:S(2)}) collective-permute-start(f32[256,512]{1,0:T(8,128)} %get-tuple-element.93.refs_0_), channel_id=1, source_target_pairs={{0,6},{1,7},{2,4},{3,5},{4,2},{5,3},{6,0},{7,1},{8,14},{9,15},{10,... | collective-permute-start | bytes 1572872 | tf_op jit(solution)/shard_map/ppermute | solution.py:27
  80.7 13.7 %collective-permute-start.27 = (f32[256,512]{1,0:T(8,128)}, f32[256,512]{1,0:T(8,128)S(1)}, u32[]{:S(2)}, u32[]{:S(2)}) collective-permute-start(f32[256,512]{1,0:T(8,128)} %get-tuple-element.94), channel_id=1, source_target_pairs={{0,72},{1,73},{2,74},{3,75},{4,76},{5,77},{6,78},{7,79},{8,64},{9,... | collective-permute-start | bytes 1572872 | tf_op jit(solution)/shard_map/ppermute | solution.py:27
  94.2 3.8 %collective-permute-start.20 = (f32[256,512]{1,0:T(8,128)S(1)}, f32[256,512]{1,0:T(8,128)S(1)}, u32[]{:S(2)}, u32[]{:S(2)}) collective-permute-start(f32[256,512]{1,0:T(8,128)S(1)} %get-tuple-element.82), channel_id=1, source_target_pairs={{0,1},{1,0},{2,3},{3,2},{4,5},{5,4},{6,7},{7,6},{8,9},{9,8},{10,11... | collective-permute-start | bytes 1572872 | tf_op jit(solution)/shard_map/ppermute | solution.py:27
  95.6 20.0 %collective-permute-start.30 = (f32[384,512]{1,0:T(8,128)S(1)}, f32[384,512]{1,0:T(8,128)S(1)}, u32[]{:S(2)}, u32[]{:S(2)}) collective-permute-start(f32[384,512]{1,0:T(8,128)S(1)} %get-tuple-element.126), channel_id=1, source_target_pairs={{0,2},{1,3},{2,0},{3,1},{4,6},{5,7},{6,4},{7,5},{8,10},{9,11},{10,... | collective-permute-start | bytes 2359304 | tf_op jit(solution)/shard_map/ppermute | solution.py:27
  97.0 20.9 %collective-permute-start.31 = (f32[384,512]{1,0:T(8,128)S(1)}, f32[384,512]{1,0:T(8,128)S(1)}, u32[]{:S(2)}, u32[]{:S(2)}) collective-permute-start(f32[384,512]{1,0:T(8,128)S(1)} %get-tuple-element.125), channel_id=1, source_target_pairs={{0,6},{1,7},{2,4},{3,5},{4,2},{5,3},{6,0},{7,1},{8,14},{9,15},{10,... | collective-permute-start | bytes 2359304 | tf_op jit(solution)/shard_map/ppermute | solution.py:27
  98.7 8.3 %collective-permute-start.21 = (f32[64,512]{1,0:T(8,128)S(1)}, f32[64,512]{1,0:T(8,128)S(1)}, u32[]{:S(2)}, u32[]{:S(2)}) collective-permute-start(f32[64,512]{1,0:T(8,128)S(1)} %get-tuple-element.84), channel_id=1, source_target_pairs={{0,16},{1,17},{2,18},{3,19},{4,20},{5,21},{6,22},{7,23},{8,24},{9,... | collective-permute-start | bytes 393224 | tf_op jit(solution)/shard_map/ppermute | solution.py:27
  98.8 8.3 %collective-permute-start.22 = (f32[64,512]{1,0:T(8,128)S(1)}, f32[64,512]{1,0:T(8,128)S(1)}, u32[]{:S(2)}, u32[]{:S(2)}) collective-permute-start(f32[64,512]{1,0:T(8,128)S(1)} %get-tuple-element.85), channel_id=1, source_target_pairs={{0,48},{1,49},{2,50},{3,51},{4,52},{5,53},{6,54},{7,55},{8,56},{9,... | collective-permute-start | bytes 393224 | tf_op jit(solution)/shard_map/ppermute | solution.py:27
  117.9 8.7 %collective-permute-start.35 = (f32[128,512]{1,0:T(8,128)S(1)}, f32[128,512]{1,0:T(8,128)S(1)}, u32[]{:S(2)}, u32[]{:S(2)}) collective-permute-start(f32[128,512]{1,0:T(8,128)S(1)} %slice_bitcast_fusion.1), channel_id=1, source_target_pairs={{0,2},{1,3},{2,0},{3,1},{4,6},{5,7},{6,4},{7,5},{8,10},{9,11},{10,... | collective-permute-start | bytes 786440 | tf_op jit(solution)/shard_map/ppermute | solution.py:27
  118.1 8.9 %collective-permute-start.36 = (f32[128,512]{1,0:T(8,128)S(1)}, f32[128,512]{1,0:T(8,128)S(1)}, u32[]{:S(2)}, u32[]{:S(2)}) collective-permute-start(f32[128,512]{1,0:T(8,128)S(1)} %slice_bitcast_fusion), channel_id=1, source_target_pairs={{0,6},{1,7},{2,4},{3,5},{4,2},{5,3},{6,0},{7,1},{8,14},{9,15},{10,... | collective-permute-start | bytes 786440 | tf_op jit(solution)/shard_map/ppermute | solution.py:27
  119.2 10.4 %collective-permute-start.28 = (f32[192,512]{1,0:T(8,128)S(1)}, f32[192,512]{1,0:T(8,128)S(1)}, u32[]{:S(2)}, u32[]{:S(2)}) collective-permute-start(f32[192,512]{1,0:T(8,128)S(1)} %get-tuple-element.98), channel_id=1, source_target_pairs={{0,16},{1,17},{2,18},{3,19},{4,20},{5,21},{6,22},{7,23},{8,24},{9,... | collective-permute-start | bytes 1179656 | tf_op jit(solution)/shard_map/ppermute | solution.py:27
  119.2 11.3 %collective-permute-start.29 = (f32[192,512]{1,0:T(8,128)S(1)}, f32[192,512]{1,0:T(8,128)S(1)}, u32[]{:S(2)}, u32[]{:S(2)}) collective-permute-start(f32[192,512]{1,0:T(8,128)S(1)} %get-tuple-element.99), channel_id=1, source_target_pairs={{0,48},{1,49},{2,50},{3,51},{4,52},{5,53},{6,54},{7,55},{8,56},{9,... | collective-permute-start | bytes 1179656 | tf_op jit(solution)/shard_map/ppermute | solution.py:27
  129.5 3.7 %collective-permute-start.37 = (f32[256,512]{1,0:T(8,128)S(1)}, f32[256,512]{1,0:T(8,128)S(1)}, u32[]{:S(2)}, u32[]{:S(2)}) collective-permute-start(f32[256,512]{1,0:T(8,128)S(1)} %get-tuple-element.114), channel_id=1, source_target_pairs={{0,1},{1,0},{2,3},{3,2},{4,5},{5,4},{6,7},{7,6},{8,9},{9,8},{10,11... | collective-permute-start | bytes 1572872 | tf_op jit(solution)/shard_map/ppermute | solution.py:27
  131.2 9.2 %collective-permute-start.32 = (f32[128,512]{1,0:T(8,128)S(1)}, f32[128,512]{1,0:T(8,128)S(1)}, u32[]{:S(2)}, u32[]{:S(2)}) collective-permute-start(f32[128,512]{1,0:T(8,128)S(1)} %get-tuple-element.107), channel_id=1, source_target_pairs={{0,16},{1,17},{2,18},{3,19},{4,20},{5,21},{6,22},{7,23},{8,24},{9,... | collective-permute-start | bytes 786440 | tf_op jit(solution)/shard_map/ppermute | solution.py:27
  131.9 10.4 %collective-permute-start.33 = (f32[128,512]{1,0:T(8,128)S(1)}, f32[128,512]{1,0:T(8,128)S(1)}, u32[]{:S(2)}, u32[]{:S(2)}) collective-permute-start(f32[128,512]{1,0:T(8,128)S(1)} %get-tuple-element.108), channel_id=1, source_target_pairs={{0,48},{1,49},{2,50},{3,51},{4,52},{5,53},{6,54},{7,55},{8,56},{9,... | collective-permute-start | bytes 786440 | tf_op jit(solution)/shard_map/ppermute | solution.py:27
  133.1 9.1 %collective-permute-start.34 = (f32[128,512]{1,0:T(8,128)S(1)}, f32[128,512]{1,0:T(8,128)S(1)}, u32[]{:S(2)}, u32[]{:S(2)}) collective-permute-start(f32[128,512]{1,0:T(8,128)S(1)} %get-tuple-element.109), channel_id=1, source_target_pairs={{0,64},{1,65},{2,66},{3,67},{4,68},{5,69},{6,70},{7,71},{8,72},{9,... | collective-permute-start | bytes 786440 | tf_op jit(solution)/shard_map/ppermute | solution.py:27
  133.8 9.1 %collective-permute-start.38 = (f32[64,512]{1,0:T(8,128)S(1)}, f32[64,512]{1,0:T(8,128)S(1)}, u32[]{:S(2)}, u32[]{:S(2)}) collective-permute-start(f32[64,512]{1,0:T(8,128)S(1)} %get-tuple-element.116), channel_id=1, source_target_pairs={{0,16},{1,17},{2,18},{3,19},{4,20},{5,21},{6,22},{7,23},{8,24},{9,... | collective-permute-start | bytes 393224 | tf_op jit(solution)/shard_map/ppermute | solution.py:27
  134.8 9.0 %collective-permute-start.39 = (f32[64,512]{1,0:T(8,128)S(1)}, f32[64,512]{1,0:T(8,128)S(1)}, u32[]{:S(2)}, u32[]{:S(2)}) collective-permute-start(f32[64,512]{1,0:T(8,128)S(1)} %get-tuple-element.117), channel_id=1, source_target_pairs={{0,48},{1,49},{2,50},{3,51},{4,52},{5,53},{6,54},{7,55},{8,56},{9,... | collective-permute-start | bytes 393224 | tf_op jit(solution)/shard_map/ppermute | solution.py:27
  144.5 9.9 %collective-permute-start.40 = (f32[192,512]{1,0:T(8,128)S(1)}, f32[192,512]{1,0:T(8,128)S(1)}, u32[]{:S(2)}, u32[]{:S(2)}) collective-permute-start(f32[192,512]{1,0:T(8,128)S(1)} %get-tuple-element.120), channel_id=1, source_target_pairs={{0,16},{1,17},{2,18},{3,19},{4,20},{5,21},{6,22},{7,23},{8,24},{9,... | collective-permute-start | bytes 1179656 | tf_op jit(solution)/shard_map/ppermute | solution.py:27
  144.6 11.1 %collective-permute-start.41 = (f32[192,512]{1,0:T(8,128)S(1)}, f32[192,512]{1,0:T(8,128)S(1)}, u32[]{:S(2)}, u32[]{:S(2)}) collective-permute-start(f32[192,512]{1,0:T(8,128)S(1)} %get-tuple-element.121), channel_id=1, source_target_pairs={{0,48},{1,49},{2,50},{3,51},{4,52},{5,53},{6,54},{7,55},{8,56},{9,... | collective-permute-start | bytes 1179656 | tf_op jit(solution)/shard_map/ppermute | solution.py:27
  156.4 6.5 %collective-permute-start.42 = (f32[128,512]{1,0:T(8,128)S(1)}, f32[128,512]{1,0:T(8,128)S(1)}, u32[]{:S(2)}, u32[]{:S(2)}) collective-permute-start(f32[128,512]{1,0:T(8,128)S(1)} %get-tuple-element.122), channel_id=1, source_target_pairs={{0,16},{1,17},{2,18},{3,19},{4,20},{5,21},{6,22},{7,23},{8,24},{9,... | collective-permute-start | bytes 786440 | tf_op jit(solution)/shard_map/ppermute | solution.py:27
  156.9 7.6 %collective-permute-start.43 = (f32[128,512]{1,0:T(8,128)S(1)}, f32[128,512]{1,0:T(8,128)S(1)}, u32[]{:S(2)}, u32[]{:S(2)}) collective-permute-start(f32[128,512]{1,0:T(8,128)S(1)} %get-tuple-element.123), channel_id=1, source_target_pairs={{0,48},{1,49},{2,50},{3,51},{4,52},{5,53},{6,54},{7,55},{8,56},{9,... | collective-permute-start | bytes 786440 | tf_op jit(solution)/shard_map/ppermute | solution.py:27
  159.0 6.4 %collective-permute-start.44 = (f32[128,512]{1,0:T(8,128)S(1)}, f32[128,512]{1,0:T(8,128)S(1)}, u32[]{:S(2)}, u32[]{:S(2)}) collective-permute-start(f32[128,512]{1,0:T(8,128)S(1)} %get-tuple-element.124), channel_id=1, source_target_pairs={{0,64},{1,65},{2,66},{3,67},{4,68},{5,69},{6,70},{7,71},{8,72},{9,... | collective-permute-start | bytes 786440 | tf_op jit(solution)/shard_map/ppermute | solution.py:27
  (5 other events, 28.2 us)

commit v6 on v5

--- a/solution.py
+++ b/solution.py
@@ -11,6 +11,9 @@
 TILE = 128
 SLOTS = 4
 CHUNKS = (64, 64)
+SPLIT_MIB = 40
+PRODUCTS_MIB = 16
+SMALL_MIB = 8
 
 PLACES = [
     (zl, x, zh, y, c)
@@ -56,55 +59,65 @@
     return hi, (v - hi.astype(jnp.float32)).astype(jnp.bfloat16)
 
 
-def product_kernel(blocks, n_arrays, first, at_ref, *refs):
-    arrays, (own_ref, far_ref), refs = refs[:n_arrays], refs[n_arrays : n_arrays + 2], refs[n_arrays + 2 :]
-    adds, (out_own, out_far) = refs[:2], refs[-2:]
-    step = pl.program_id(0)
-
-    for i, block in enumerate(blocks):
-
-        @pl.when(step == i)
-        def _():
-            parts = [arrays[array][lo : lo + size] for array, lo, size in block]
-            a_hi, a_lo = split(parts[0] if len(parts) == 1 else jnp.concatenate(parts, axis=0))
-            a_both = jnp.concatenate([a_hi, a_lo], axis=0)
-            m = a_hi.shape[0]
-            for j, (rhs, out) in enumerate(((own_ref, out_own), (far_ref, out_far))):
-                b_hi, b_lo = split(rhs[...])
-                dot = functools.partial(jnp.dot, preferred_element_type=jnp.float32)
-                upper = dot(a_both, b_hi)
-                term = upper[:m] + (upper[m:] + dot(a_hi, b_lo))
-                if i == 0:
-                    out[...] = term if first else adds[j][...] + term
-                else:
-                    out[...] += term
-
-
-def products(arrays, blocks, at, own, far, sums):
+def split_rows(a, width, at, name):
+    n, cols = at.shape[0], a.shape[1]
+
+    def kernel(at_ref, a_ref, hi_ref, lo_ref):
+        rows = pl.ds(pl.multiple_of(pl.program_id(0) * width, width), width)
+        hi_ref[rows], lo_ref[rows] = split(a_ref[...])
+
+    return pl.pallas_call(
+        kernel,
+        grid_spec=pltpu.PrefetchScalarGridSpec(
+            num_scalar_prefetch=1,
+            grid=(n,),
+            in_specs=[pl.BlockSpec((width, cols), lambda s, at: (at[s], 0))],
+            out_specs=[pl.BlockSpec(memory_space=pltpu.VMEM)] * 2,
+        ),
+        out_shape=[jax.ShapeDtypeStruct((n * width, cols), jnp.bfloat16)] * 2,
+        compiler_params=pltpu.CompilerParams(vmem_limit_bytes=SPLIT_MIB * 1024 * 1024),
+        name=name,
+    )(at, a)
+
+
+def products(arrays, blocks, at, rhs, sums):
     n = len(blocks)
     m = sum(size for _, _, size in blocks[0])
     width = arrays[0].shape[1]
-    cols = own.shape[1]
+    cols = rhs[0].shape[1]
+    dot = functools.partial(jnp.dot, preferred_element_type=jnp.float32)
+
+    def kernel(at_ref, *refs):
+        ins, refs = refs[: len(arrays)], refs[len(arrays) :]
+        parts, adds, outs = refs[:4], refs[4:-2], refs[-2:]
+        for i, block in enumerate(blocks):
+            rows = [ins[array][lo : lo + size] for array, lo, size in block]
+            a_hi, a_lo = split(rows[0] if len(rows) == 1 else jnp.concatenate(rows, axis=0))
+            a_both = jnp.concatenate([a_hi, a_lo], axis=0)
+            deep = pl.ds(pl.multiple_of(at_ref[i] * width, width), width)
+            for j, out in enumerate(outs):
+                upper = dot(a_both, parts[2 * j][deep])
+                term = upper[:m] + (upper[m:] + dot(a_hi, parts[2 * j + 1][deep]))
+                if i == 0:
+                    out[...] = adds[j][...] + term if sums else term
+                else:
+                    out[...] += term
+
     vmem = pl.BlockSpec(memory_space=pltpu.VMEM)
     return pl.pallas_call(
-        functools.partial(product_kernel, blocks, len(arrays), not sums),
-        grid_spec=pltpu.PrefetchScalarGridSpec(
-            num_scalar_prefetch=1,
-            grid=(n,),
-            in_specs=[vmem] * len(arrays)
-            + [pl.BlockSpec((width, cols), lambda s, at: (at[s], 0))] * 2
-            + [vmem] * len(sums),
-            out_specs=[vmem] * 2,
-        ),
+        kernel,
+        in_specs=[pl.BlockSpec(memory_space=pltpu.SMEM)]
+        + [vmem] * (len(arrays) + 4 + len(sums)),
+        out_specs=[vmem] * 2,
         out_shape=[jax.ShapeDtypeStruct((m, cols), jnp.float32)] * 2,
-        compiler_params=pltpu.CompilerParams(vmem_limit_bytes=50 * 1024 * 1024),
+        compiler_params=pltpu.CompilerParams(vmem_limit_bytes=PRODUCTS_MIB * 1024 * 1024),
         cost_estimate=pl.CostEstimate(
             flops=12 * n * m * width * cols,
             bytes_accessed=8 * n * width * cols + 4 * n * m * width,
             transcendentals=0,
         ),
         name="products",
-    )(at, *arrays, own, far, *sums)
+    )(at, *arrays, *rhs, *sums)
 
 
 def small_kernel(body, plan, shapes, operands, after=(), name=None):
@@ -118,7 +131,7 @@
         + [pl.BlockSpec(memory_space=pl.ANY)] * len(after),
         out_specs=[pl.BlockSpec(memory_space=pltpu.VMEM)] * len(shapes),
         out_shape=[jax.ShapeDtypeStruct(s, jnp.float32) for s in shapes],
-        compiler_params=pltpu.CompilerParams(vmem_limit_bytes=24 * 1024 * 1024),
+        compiler_params=pltpu.CompilerParams(vmem_limit_bytes=SMALL_MIB * 1024 * 1024),
         cost_estimate=pl.CostEstimate(
             flops=0, bytes_accessed=4 * sum(int(np.prod(s)) for s in shapes), transcendentals=0
         ),
@@ -259,20 +272,27 @@
     a, b, across = small_kernel(
         body, plan, [(2 * m, cols)] * 3, [product, *came], name="return_third"
     )
-    return [swap_x(a, 0), swap_x(b, 1), flip_z(across)]
-
-
-def return_last(plan, product, came):
+    return across, [swap_x(a, 0), swap_x(b, 1), flip_z(across)]
+
+
+def return_last(plan, product, came, earlier=None):
     _, m, cols = product.shape
+    start = 0 if earlier is None else earlier.shape[0] // 2
+    pitch = start + m
 
     def body(plan_ref, ins, outs):
-        product, *came = ins
+        product, a, b, c, *before = ins
         (total,) = outs
         rows = lambda j: slice(j * m, (j + 1) * m)
-        arrived = lambda j: came[0][rows(j)] + came[1][rows(j)] + came[2][rows(j)]
-        share(plan_ref, 0, 0, product, 0, m, total, 0, m, arrived)
-
-    (total,) = small_kernel(body, plan, [(2 * m, cols)], [product, *came], name="return_last")
+        arrived = lambda j: a[rows(j)] + b[rows(j)] + c[rows(j)]
+        share(plan_ref, 0, 0, product, 0, m, total, start, pitch, arrived)
+        for j in range(2 if before else 0):
+            total[j * pitch : j * pitch + start] = before[0][j * start : (j + 1) * start]
+
+    before = [] if earlier is None else [earlier]
+    (total,) = small_kernel(
+        body, plan, [(2 * pitch, cols)], [product, *came, *before], name="return_last"
+    )
     return total
 
 
@@ -306,11 +326,15 @@
 
     own = integrals.reshape(16 * width, cols)
     far = flip_core(own)
+    deep = np.arange(8, dtype=np.int32) * 2 + core
+    rhs_own = split_rows(own, width, deep, "split_own")
+    rhs_far = split_rows(far, width, deep, "split_far")
+    rhs = [*rhs_own, *rhs_far]
     at = []
     for group in GROUPS:
         gz, ring = np.array(group, np.int32).T
         places = (zh ^ gz) * 4 + (y + ring * (1 - 2 * (y % 2))) % 4
-        at.append(places * 2 + core)
+        at.append(places)
 
     def rows_first(piece, before=None):
         beside, later = (), ()
@@ -335,18 +359,20 @@
             arrays, blocks = last["second"], [[(0, 0, m)], [(1, 0, m)], [(0, m, h), (1, m, h)]]
         else:
             arrays, blocks = last["third"], [[(0, 0, h), (1, 0, h)]]
-        last["sums"] = products(arrays, blocks, at[group], own, far, last["sums"])
+        last["sums"] = products(arrays, blocks, at[group], rhs, last["sums"])
         return last["sums"]
 
     def finish(last, back):
         sums = step(1, last)
         if back is not None:
             product, came = back
-            back = product, return_third(plan, product, wait_for(came, sums[0]))
+            sent, came = return_third(plan, product, wait_for(came, sums[0]))
+            last["sums"] = wait_for(sums, sent)
+            back = product, came
         return step(2, last), back
 
-    arrays = rows_third(rows_second(rows_first(pieces[0])))
-    out, last, back = [], None, None
+    arrays = rows_third(wait_for(rows_second(rows_first(pieces[0])), rhs_own[0]))
+    last, back = None, None
     for k, m in enumerate(CHUNKS):
         more = k + 1 < len(CHUNKS)
         after = () if last is None else (last["second"][0], last["sums"][0])
@@ -357,7 +383,7 @@
         near = [swap_y(b, 0), swap_y(b, 1)]
         bz = cross_z(crossing)
         this["first"] = [b, *near, bz]
-        ready = []
+        ready = [] if k else rhs_far[:1]
         if last is not None:
             sums, back = finish(last, back)
             swapped = flip_core(sums[1])
@@ -371,11 +397,9 @@
             product, came = return_first(plan, sums, swapped)
         step(0, this)
         if last is not None:
-            if back is not None:
-                out.append(return_last(plan, *back))
-            sent, came = return_second(plan, product, wait_for(came, this["sums"][0], *out))
+            sent, came = return_second(plan, product, wait_for(came, this["sums"][0]))
             back = product, came
-            ready = [*ready, sent]
+            ready = [*ready, *came]
         both = wait_for(this["second"], this["sums"][0], *ready)
         this["third"] = gather_third(both, SLOTS * m, swap_y)
         if more:
@@ -383,12 +407,9 @@
         last = this
     sums, back = finish(last, back)
     product, came = return_first(plan, sums, flip_core(sums[1]))
-    if back is not None:
-        out.append(return_last(plan, *back))
-    came = return_second(plan, product, wait_for(came, *out))[1]
-    out.append(return_last(plan, product, return_third(plan, product, came)))
-    out = [o.reshape(local_tiles, -1, cols) for o in out]
-    return jnp.concatenate(out, axis=1).reshape(local_tiles * TILE, cols)
+    result = return_last(plan, *back)
+    came = return_second(plan, product, wait_for(came, result))[1]
+    return return_last(plan, product, return_third(plan, product, came)[1], result)
 
 
 def solution(mesh):

time: 167 us -> 176 us (1.054)
  local copies, waits for them, and re-layouts: 9.51 us -> 21.2 us
  waiting for transfers between devices: 60.6 us -> 53.5 us
  starting transfers between devices: 50 us -> 55.8 us
  other arithmetic: 6.57 us -> 2.48 us
  Pallas kernels: 39.6 us -> 41.8 us
    unnamed x16 -> x60, local copies, waits for them, and re-layouts: 3.13 us -> 17.2 us
    ppermute x45, waiting for transfers between devices: 60.6 us -> 53.5 us  [send(): lax.ppermute(a, ('row', 'col'), [(i, index[to(*p)]) for p, i in index.ite...]
    ppermute x45, starting transfers between devices: 50 us -> 55.8 us  [send(): lax.ppermute(a, ('row', 'col'), [(i, index[to(*p)]) for p, i in index.ite...]
    slice x8, local copies, waits for them, and re-layouts: 1.89 us -> 0.08 us  [half(): cut = a.reshape(pieces, 2, -1, a.shape[1])[:, which]]
    pallas_call x6 -> x8, Pallas kernels: 30.5 us -> 31.8 us  [the longest x6 18.4 us: products(): pl.pallas_call(kernel, in_specs=[pl.BlockSpec(memory_space=pltpu.SMEM)] +...]
  transfers between devices with their start and end apart: 45 -> 45, of which waited for: 23 -> 21; matrix products, arithmetic and copies ran while one was open for 7% -> 4% of each run, Pallas kernels for 23% -> 22%
where the time goes in v6:
time: 176 us
  starting transfers between devices  55.8 us (32%)
  waiting for transfers between devices  53.5 us (30%)
  Pallas kernels  41.8 us (24%)
  local copies, waits for them, and re-layouts  21.2 us (12%)
  other arithmetic  2.48 us (1%)
    ppermute x45, starting transfers between devices, send(): lax.ppermute(a, ('row', 'col'), [(i, index[to(*p)]) for p, i in index.ite...  55.8 us
    ppermute x45, waiting for transfers between devices, send(): lax.ppermute(a, ('row', 'col'), [(i, index[to(*p)]) for p, i in index.ite...  53.5 us
    pallas_call x6, Pallas kernels, products(): pl.pallas_call(kernel, in_specs=[pl.BlockSpec(memory_space=pltpu.SMEM)] +...  18.4 us
    unnamed x60, local copies, waits for them, and re-layouts  17.2 us
    pallas_call x2, Pallas kernels, split_rows(): pl.pallas_call(kernel, grid_spec=pltpu.PrefetchScalarGridSpec(num_scalar_...  13.5 us
    pallas_call x10, Pallas kernels, small_kernel(): pl.pallas_call(kernel, in_specs=[pl.BlockSpec(memory_space=pltpu.SMEM)] +...  9.94 us
  transfers between devices with their start and end apart: 45, of which 21 were waited for; matrix products, arithmetic and copies ran while one was open for 4% of the time, Pallas kernels for 22%

profile of v6, /device:TPU:0, one launch (start us, length us, event | category | flops | bytes accessed | tf_op | source)
XLA Modules:
  0.0 175.5 jit_solution(9616252255755771490)
XLA Ops:
  1.1 2.9 %collective-permute-start.2 = (f32[128,512]{1,0:T(8,128)S(1)}, f32[128,512]{1,0:T(8,128)S(1)}, u32[]{:S(2)}, u32[]{:S(2)}) collective-permute-start(f32[128,512]{1,0:T(8,128)S(1)} %bitcast.71), channel_id=1, source_target_pairs={{0,48},{1,49},{2,50},{3,51},{4,52},{5,53},{6,54},{7,55},{8,56},{9,... | collective-permute-start | bytes 786440 | tf_op jit(solution)/shard_map/ppermute | solution.py:30
  4.2 1.9 %collective-permute-start = (f32[128,512]{1,0:T(8,128)S(1)}, f32[128,512]{1,0:T(8,128)S(1)}, u32[]{:S(2)}, u32[]{:S(2)}) collective-permute-start(f32[128,512]{1,0:T(8,128)S(1)} %bitcast.73), channel_id=1, source_target_pairs={{0,64},{1,65},{2,66},{3,67},{4,68},{5,69},{6,70},{7,71},{8,72},{9,... | collective-permute-start | bytes 786440 | tf_op jit(solution)/shard_map/ppermute | solution.py:30
  7.7 3.3 %collective-permute-done.2.refs_3_ = f32[128,512]{1,0:T(8,128)S(1)} collective-permute-done((f32[128,512]{1,0:T(8,128)S(1)}, f32[128,512]{1,0:T(8,128)S(1)}, u32[]{:S(2)}, u32[]{:S(2)}) %collective-permute-start.2) | collective-permute-done | bytes 262176 | tf_op jit(solution)/shard_map/ppermute | solution.py:30
  11.1 1.3 collective-permute-done.1.refs_2_
  12.7 1.4 collective-permute-start.4
  14.7 6.6 %split_own.1 = (bf16[4096,512]{1,0:T(8,128)(2,1)S(1)}, bf16[4096,512]{1,0:T(8,128)(2,1)S(1)}) custom-call(s32[8]{0:T(128)S(1)} %multiply_add_fusion.at_ref, f32[8192,512]{1,0:T(8,128)} %bitcast.80), custom_call_target="tpu_custom_call" | custom-call | tf_op jit(solution)/shard_map/split_own/pallas_call | solution.py:69
  21.3 2.0 %copy-done = bf16[4096,512]{1,0:T(8,128)(2,1)} copy-done((bf16[4096,512]{1,0:T(8,128)(2,1)}, bf16[4096,512]{1,0:T(8,128)(2,1)S(1)}, u32[]{:S(2)}) %copy-start) | copy-done | bytes 4194328
  23.3 2.0 %copy-done.4 = bf16[4096,512]{1,0:T(8,128)(2,1)} copy-done((bf16[4096,512]{1,0:T(8,128)(2,1)}, bf16[4096,512]{1,0:T(8,128)(2,1)S(1)}, u32[]{:S(2)}) %copy-start.4) | copy-done | bytes 4194328
  25.6 2.6 %collective-permute-start.9 = (f32[64,512]{1,0:T(8,128)S(1)}, f32[64,512]{1,0:T(8,128)S(1)}, u32[]{:S(2)}, u32[]{:S(2)}) collective-permute-start(f32[64,512]{1,0:T(8,128)S(1)} %bitcast.94), channel_id=1, source_target_pairs={{0,48},{1,49},{2,50},{3,51},{4,52},{5,53},{6,54},{7,55},{8,56},{9,... | collective-permute-start | bytes 393224 | tf_op jit(solution)/shard_map/ppermute | solution.py:30
  28.8 3.0 %collective-permute-done.9.refs_7_ = f32[64,512]{1,0:T(8,128)S(1)} collective-permute-done((f32[64,512]{1,0:T(8,128)S(1)}, f32[64,512]{1,0:T(8,128)S(1)}, u32[]{:S(2)}, u32[]{:S(2)}) %collective-permute-start.9) | collective-permute-done | bytes 131104 | tf_op jit(solution)/shard_map/ppermute | solution.py:30
  31.9 1.4 collective-permute-done.8.refs_6_
  33.3 1.8 %pick.2 = (f32[256,512]{1,0:T(8,128)}, f32[256,512]{1,0:T(8,128)S(1)}) custom-call(s32[24]{0:T(128)S(1)} %pad_add_fusion.plan_ref, f32[128,512]{1,0:T(8,128)S(1)} %bitcast.74, f32[128,512]{1,0:T(8,128)S(1)} %collective-permute-done.refs_1_, f32[128,512]{1,0:T(8,128)S(1)} %collective-permute-done.1.refs_2_, f32[128,512]{1,0:T(8,128)S(1)} %collective-permute-done.2.refs_3_, ...), custom_call_target="tpu_custom_call" | custom-call | bytes 1048576 | tf_op jit(solution)/shard_map/pick/pallas_call | solution.py:127
  35.1 3.9 %collective-permute-start.12 = (f32[256,512]{1,0:T(8,128)S(1)}, f32[256,512]{1,0:T(8,128)S(1)}, u32[]{:S(2)}, u32[]{:S(2)}) collective-permute-start(f32[256,512]{1,0:T(8,128)S(1)} %get-tuple-element.87), channel_id=1, source_target_pairs={{0,72},{1,73},{2,74},{3,75},{4,76},{5,77},{6,78},{7,79},{8,64},{9,... | collective-permute-start | bytes 1572872 | tf_op jit(solution)/shard_map/ppermute | solution.py:30
  39.0 3.0 %collective-permute-start.11 = (f32[256,512]{1,0:T(8,128)}, f32[256,512]{1,0:T(8,128)S(1)}, u32[]{:S(2)}, u32[]{:S(2)}) collective-permute-start(f32[256,512]{1,0:T(8,128)} %get-tuple-element.86.refs_0_), channel_id=1, source_target_pairs={{0,6},{1,7},{2,4},{3,5},{4,2},{5,3},{6,0},{7,1},{8,14},{9,15},{10,... | collective-permute-start | bytes 1572872 | tf_op jit(solution)/shard_map/ppermute | solution.py:30
  43.3 5.2 %collective-permute-done.12.refs_3_ = f32[256,512]{1,0:T(8,128)S(1)} collective-permute-done((f32[256,512]{1,0:T(8,128)S(1)}, f32[256,512]{1,0:T(8,128)S(1)}, u32[]{:S(2)}, u32[]{:S(2)}) %collective-permute-start.12) | collective-permute-done | bytes 524320 | tf_op jit(solution)/shard_map/ppermute | solution.py:30
  49.2 6.9 %split_far.1 = (bf16[4096,512]{1,0:T(8,128)(2,1)S(1)}, bf16[4096,512]{1,0:T(8,128)(2,1)S(1)}) custom-call(s32[8]{0:T(128)S(1)} %multiply_add_fusion.at_ref, f32[8192,512]{1,0:T(8,128)} %collective-permute-done.13.a_ref), custom_call_target="tpu_custom_call" | custom-call | tf_op jit(solution)/shard_map/split_far/pallas_call | solution.py:69
  58.7 3.1 %collective-permute-start.22 = (f32[384,512]{1,0:T(8,128)S(1)}, f32[384,512]{1,0:T(8,128)S(1)}, u32[]{:S(2)}, u32[]{:S(2)}) collective-permute-start(f32[384,512]{1,0:T(8,128)S(1)} %get-tuple-element.151), channel_id=1, source_target_pairs={{0,6},{1,7},{2,4},{3,5},{4,2},{5,3},{6,0},{7,1},{8,14},{9,15},{10,... | collective-permute-start | bytes 2359304 | tf_op jit(solution)/shard_map/ppermute | solution.py:30
  62.0 1.9 %collective-permute-start.15 = (f32[192,512]{1,0:T(8,128)S(1)}, f32[192,512]{1,0:T(8,128)S(1)}, u32[]{:S(2)}, u32[]{:S(2)}) collective-permute-start(f32[192,512]{1,0:T(8,128)S(1)} %get-tuple-element.155), channel_id=1, source_target_pairs={{0,48},{1,49},{2,50},{3,51},{4,52},{5,53},{6,54},{7,55},{8,56},{9,... | collective-permute-start | bytes 1179656 | tf_op jit(solution)/shard_map/ppermute | solution.py:30
  65.0 4.6 %products.6 = (f32[256,512]{1,0:T(8,128)S(1)}, f32[256,512]{1,0:T(8,128)S(1)}) custom-call(s32[4]{0:T(128)S(1)} %fusion.at_ref, f32[256,512]{1,0:T(8,128)} %get-tuple-element.86.refs_0_, f32[256,512]{1,0:T(8,128)S(1)} %copy-done.12, f32[256,512]{1,0:T(8,128)S(1)} %collective-permute-done.11.refs_2_, f32[256,512]{1,0:T(8,128)S(1)} %collective-permute-done.12.refs_3_, ...), custom_call_target="tpu_custom_call" | custom-call | flops 3221225472 | bytes 10485760 | tf_op jit(solution)/shard_map/products/pallas_call | solution.py:107
  69.7 1.4 collective-permute-done.15.refs_5_
  74.0 4.3 %collective-permute-done.17.refs_7_ = f32[64,512]{1,0:T(8,128)S(1)} collective-permute-done((f32[64,512]{1,0:T(8,128)S(1)}, f32[64,512]{1,0:T(8,128)S(1)}, u32[]{:S(2)}, u32[]{:S(2)}) %collective-permute-start.17) | collective-permute-done | bytes 131104 | tf_op jit(solution)/shard_map/ppermute | solution.py:30
  78.3 2.0 %pick.3 = (f32[256,512]{1,0:T(8,128)}, f32[256,512]{1,0:T(8,128)}) custom-call(s32[24]{0:T(128)S(1)} %pad_add_fusion.plan_ref, f32[128,512]{1,0:T(8,128)S(1)} %bitcast.70, f32[128,512]{1,0:T(8,128)S(1)} %collective-permute-done.5.refs_1_, f32[128,512]{1,0:T(8,128)S(1)} %copy-done.18, f32[128,512]{1,0:T(8,128)S(1)} %copy-done.16, ...), custom_call_target="tpu_custom_call" | custom-call | bytes 1048576 | tf_op jit(solution)/shard_map/pick/pallas_call | solution.py:127
  85.1 2.0 %collective-permute-start.24 = (f32[128,512]{1,0:T(8,128)}, f32[128,512]{1,0:T(8,128)}, u32[]{:S(2)}, u32[]{:S(2)}) collective-permute-start(f32[128,512]{1,0:T(8,128)} %slice_bitcast_fusion.4), channel_id=1, source_target_pairs={{0,6},{1,7},{2,4},{3,5},{4,2},{5,3},{6,0},{7,1},{8,14},{9,15},{10,... | collective-permute-start | bytes 786440 | tf_op jit(solution)/shard_map/ppermute | solution.py:30
  87.2 3.2 %collective-permute-start.21 = (f32[256,512]{1,0:T(8,128)}, f32[256,512]{1,0:T(8,128)S(1)}, u32[]{:S(2)}, u32[]{:S(2)}) collective-permute-start(f32[256,512]{1,0:T(8,128)} %get-tuple-element.106), channel_id=1, source_target_pairs={{0,72},{1,73},{2,74},{3,75},{4,76},{5,77},{6,78},{7,79},{8,64},{9,... | collective-permute-start | bytes 1572872 | tf_op jit(solution)/shard_map/ppermute | solution.py:30
  90.5 2.2 %copy-done.2 = bf16[4096,512]{1,0:T(8,128)(2,1)S(1)} copy-done((bf16[4096,512]{1,0:T(8,128)(2,1)S(1)}, bf16[4096,512]{1,0:T(8,128)(2,1)}, u32[]{:S(2)}) %copy-start.2) | copy-done | bytes 4194328
  92.6 2.2 %copy-done.6 = bf16[4096,512]{1,0:T(8,128)(2,1)S(1)} copy-done((bf16[4096,512]{1,0:T(8,128)(2,1)S(1)}, bf16[4096,512]{1,0:T(8,128)(2,1)}, u32[]{:S(2)}) %copy-start.6) | copy-done | bytes 4194328
  94.8 2.2 %copy-done.8 = bf16[4096,512]{1,0:T(8,128)(2,1)S(1)} copy-done((bf16[4096,512]{1,0:T(8,128)(2,1)S(1)}, bf16[4096,512]{1,0:T(8,128)(2,1)}, u32[]{:S(2)}) %copy-start.8) | copy-done | bytes 4194328
  97.0 2.2 %copy-done.10 = bf16[4096,512]{1,0:T(8,128)(2,1)S(1)} copy-done((bf16[4096,512]{1,0:T(8,128)(2,1)S(1)}, bf16[4096,512]{1,0:T(8,128)(2,1)}, u32[]{:S(2)}) %copy-start.10) | copy-done | bytes 4194328
  100.2 3.1 %products.7 = (f32[256,512]{1,0:T(8,128)S(1)}, f32[256,512]{1,0:T(8,128)S(1)}) custom-call(s32[3]{0:T(128)S(1)} %fusion.1.at_ref, f32[384,512]{1,0:T(8,128)S(1)} %collective-permute-done.18.refs_8_.refs_0_, f32[384,512]{1,0:T(8,128)S(1)} %collective-permute-done.22.refs_1_, bf16[4096,512]{1,0:T(8,128)(2,1)S(1)} %copy-done.2, ...), custom_call_target="tpu_custom_call" | custom-call | flops 2415919104 | bytes 7864320 | tf_op jit(solution)/shard_map/products/pallas_call | solution.py:107
  103.4 1.9 %products.8 = (f32[256,512]{1,0:T(8,128)S(1)}, f32[256,512]{1,0:T(8,128)S(1)}) custom-call(s32[1]{0:T(128)S(6)} %add.98.at_ref, f32[128,512]{1,0:T(8,128)S(1)} %collective-permute-done.23.refs_0_, f32[128,512]{1,0:T(8,128)} %collective-permute-done.24.refs_1_, bf16[4096,512]{1,0:T(8,128)(2,1)S(1)} %copy-done.2, bf16[4096,512]{1,0:T(8,128)(2,1)S(1)} %copy-done.6, ...), custom_call_target="tpu_custom_call" | custom-call | flops 805306368 | bytes 2621440 | tf_op jit(solution)/shard_map/products/pallas_call | solution.py:107
  109.4 1.6 collective-permute-start.29
  111.0 4.6 %products.9 = (f32[256,512]{1,0:T(8,128)S(1)}, f32[256,512]{1,0:T(8,128)S(1)}) custom-call(s32[4]{0:T(128)S(1)} %fusion.at_ref, f32[256,512]{1,0:T(8,128)} %get-tuple-element.105.refs_0_, f32[256,512]{1,0:T(8,128)} %collective-permute-done.19.refs_1_, f32[256,512]{1,0:T(8,128)S(1)} %collective-permute-done.20.refs_2_, ...), custom_call_target="tpu_custom_call" | custom-call | flops 3221225472 | bytes 10485760 | tf_op jit(solution)/shard_map/products/pallas_call | solution.py:107
  118.9 8.3 %collective-permute-done.30.refs_1_ = f32[192,512]{1,0:T(8,128)S(1)} collective-permute-done((f32[192,512]{1,0:T(8,128)S(1)}, f32[192,512]{1,0:T(8,128)S(1)}, u32[]{:S(2)}, u32[]{:S(2)}) %collective-permute-start.30) | collective-permute-done | bytes 393248 | tf_op jit(solution)/shard_map/ppermute | solution.py:30
  127.2 2.0 %collective-permute-done.31.refs_2_ = f32[192,512]{1,0:T(8,128)S(1)} collective-permute-done((f32[192,512]{1,0:T(8,128)S(1)}, f32[192,512]{1,0:T(8,128)S(1)}, u32[]{:S(2)}, u32[]{:S(2)}) %collective-permute-start.31) | collective-permute-done | bytes 393248 | tf_op jit(solution)/shard_map/ppermute | solution.py:30
  129.3 1.8 %collective-permute-start.32 = (f32[128,512]{1,0:T(8,128)S(1)}, f32[128,512]{1,0:T(8,128)S(1)}, u32[]{:S(2)}, u32[]{:S(2)}) collective-permute-start(f32[128,512]{1,0:T(8,128)S(1)} %slice_bitcast_fusion.1), channel_id=1, source_target_pairs={{0,2},{1,3},{2,0},{3,1},{4,6},{5,7},{6,4},{7,5},{8,10},{9,11},{10,... | collective-permute-start | bytes 786440 | tf_op jit(solution)/shard_map/ppermute | solution.py:30
  131.2 2.1 %collective-permute-start.33 = (f32[128,512]{1,0:T(8,128)S(1)}, f32[128,512]{1,0:T(8,128)S(1)}, u32[]{:S(2)}, u32[]{:S(2)}) collective-permute-start(f32[128,512]{1,0:T(8,128)S(1)} %slice_bitcast_fusion), channel_id=1, source_target_pairs={{0,6},{1,7},{2,4},{3,5},{4,2},{5,3},{6,0},{7,1},{8,14},{9,15},{10,... | collective-permute-start | bytes 786440 | tf_op jit(solution)/shard_map/ppermute | solution.py:30
  133.3 3.1 %products.10 = (f32[256,512]{1,0:T(8,128)S(1)}, f32[256,512]{1,0:T(8,128)S(1)}) custom-call(s32[3]{0:T(128)S(1)} %fusion.1.at_ref, f32[384,512]{1,0:T(8,128)S(1)} %collective-permute-done.25.refs_0_, f32[384,512]{1,0:T(8,128)S(1)} %collective-permute-done.26.refs_1_, bf16[4096,512]{1,0:T(8,128)(2,1)S(1)} %copy-done.3, bf16[4096,512]{1,0:T(8,128)(2,1)S(1)} %copy-done.6, ...), custom_call_target="tpu_custom_call" | custom-call | flops 2415919104 | bytes 7864320 | tf_op jit(solution)/shard_map/products/pallas_call | solution.py:107
  137.2 1.7 collective-permute-done.33.refs_1_
  141.2 1.6 collective-permute-start.39
  143.5 1.4 collective-permute-start.35
  144.9 2.2 %collective-permute-start.36 = (f32[64,512]{1,0:T(8,128)S(1)}, f32[64,512]{1,0:T(8,128)S(1)}, u32[]{:S(2)}, u32[]{:S(2)}) collective-permute-start(f32[64,512]{1,0:T(8,128)S(1)} %get-tuple-element.139), channel_id=1, source_target_pairs={{0,48},{1,49},{2,50},{3,51},{4,52},{5,53},{6,54},{7,55},{8,56},{9,... | collective-permute-start | bytes 393224 | tf_op jit(solution)/shard_map/ppermute | solution.py:30
  147.0 2.1 %collective-permute-done.37.refs_1_ = f32[128,512]{1,0:T(8,128)S(1)} collective-permute-done((f32[128,512]{1,0:T(8,128)S(1)}, f32[128,512]{1,0:T(8,128)S(1)}, u32[]{:S(2)}, u32[]{:S(2)}) %collective-permute-start.37) | collective-permute-done | bytes 262176 | tf_op jit(solution)/shard_map/ppermute | solution.py:30
  149.1 1.3 collective-permute-done.38.refs_2_
  155.1 8.9 %collective-permute-done.40.refs_1_ = f32[192,512]{1,0:T(8,128)S(1)} collective-permute-done((f32[192,512]{1,0:T(8,128)S(1)}, f32[192,512]{1,0:T(8,128)S(1)}, u32[]{:S(2)}, u32[]{:S(2)}) %collective-permute-start.40) | collective-permute-done | bytes 393248 | tf_op jit(solution)/shard_map/ppermute | solution.py:30
  167.4 1.8 %collective-permute-start.44 = (f32[128,512]{1,0:T(8,128)S(1)}, f32[128,512]{1,0:T(8,128)S(1)}, u32[]{:S(2)}, u32[]{:S(2)}) collective-permute-start(f32[128,512]{1,0:T(8,128)S(1)} %get-tuple-element.148), channel_id=1, source_target_pairs={{0,64},{1,65},{2,66},{3,67},{4,68},{5,69},{6,70},{7,71},{8,72},{9,... | collective-permute-start | bytes 786440 | tf_op jit(solution)/shard_map/ppermute | solution.py:30
  169.2 3.2 %collective-permute-done.42.refs_1_ = f32[128,512]{1,0:T(8,128)S(1)} collective-permute-done((f32[128,512]{1,0:T(8,128)S(1)}, f32[128,512]{1,0:T(8,128)S(1)}, u32[]{:S(2)}, u32[]{:S(2)}) %collective-permute-start.42) | collective-permute-done | bytes 262176 | tf_op jit(solution)/shard_map/ppermute | solution.py:30
  172.4 1.7 collective-permute-done.43.refs_2_
  174.1 1.4 return_last.3
  (158 shorter events, 38.0 us)
Async XLA Ops:
  0.0 49.1 %collective-permute-start.13 = (f32[8192,512]{1,0:T(8,128)}, f32[8192,512]{1,0:T(8,128)}, u32[]{:S(2)}, u32[]{:S(2)}) collective-permute-start(f32[8192,512]{1,0:T(8,128)} %bitcast.79), channel_id=1, source_target_pairs={{0,1},{1,0},{2,3},{3,2},{4,5},{5,4},{6,7},{7,6},{8,9},{9,8},{10,11... | collective-permute-start | bytes 50331656 | tf_op jit(solution)/shard_map/ppermute | solution.py:30
  1.1 48.0 %copy-start.13 = (f32[2,64,512]{2,1,0:T(8,128)}, f32[2,64,512]{2,1,0:T(8,128)S(1)}, u32[]{:S(2)}) copy-start(f32[2,64,512]{2,1,0:T(8,128)S(1)} %get-tuple-element.154) | copy-start | bytes 786436
  1.1 10.0 %collective-permute-start.2 = (f32[128,512]{1,0:T(8,128)S(1)}, f32[128,512]{1,0:T(8,128)S(1)}, u32[]{:S(2)}, u32[]{:S(2)}) collective-permute-start(f32[128,512]{1,0:T(8,128)S(1)} %bitcast.71), channel_id=1, source_target_pairs={{0,48},{1,49},{2,50},{3,51},{4,52},{5,53},{6,54},{7,55},{8,56},{9,... | collective-permute-start | bytes 786440 | tf_op jit(solution)/shard_map/ppermute | solution.py:30
  4.0 8.4 %collective-permute-start.1 = (f32[128,512]{1,0:T(8,128)S(1)}, f32[128,512]{1,0:T(8,128)S(1)}, u32[]{:S(2)}, u32[]{:S(2)}) collective-permute-start(f32[128,512]{1,0:T(8,128)S(1)} %bitcast.72), channel_id=1, source_target_pairs={{0,16},{1,17},{2,18},{3,19},{4,20},{5,21},{6,22},{7,23},{8,24},{9,... | collective-permute-start | bytes 786440 | tf_op jit(solution)/shard_map/ppermute | solution.py:30
  4.2 8.4 %collective-permute-start = (f32[128,512]{1,0:T(8,128)S(1)}, f32[128,512]{1,0:T(8,128)S(1)}, u32[]{:S(2)}, u32[]{:S(2)}) collective-permute-start(f32[128,512]{1,0:T(8,128)S(1)} %bitcast.73), channel_id=1, source_target_pairs={{0,64},{1,65},{2,66},{3,67},{4,68},{5,69},{6,70},{7,71},{8,72},{9,... | collective-permute-start | bytes 786440 | tf_op jit(solution)/shard_map/ppermute | solution.py:30
  12.7 12.9 %collective-permute-start.4 = (f32[192,512]{1,0:T(8,128)S(1)}, f32[192,512]{1,0:T(8,128)S(1)}, u32[]{:S(2)}, u32[]{:S(2)}) collective-permute-start(f32[192,512]{1,0:T(8,128)S(1)} %get-tuple-element.157), channel_id=1, source_target_pairs={{0,48},{1,49},{2,50},{3,51},{4,52},{5,53},{6,54},{7,55},{8,56},{9,... | collective-permute-start | bytes 1179656 | tf_op jit(solution)/shard_map/ppermute | solution.py:30
  14.2 11.4 %collective-permute-start.3 = (f32[192,512]{1,0:T(8,128)S(1)}, f32[192,512]{1,0:T(8,128)S(1)}, u32[]{:S(2)}, u32[]{:S(2)}) collective-permute-start(f32[192,512]{1,0:T(8,128)S(1)} %get-tuple-element.158), channel_id=1, source_target_pairs={{0,16},{1,17},{2,18},{3,19},{4,20},{5,21},{6,22},{7,23},{8,24},{9,... | collective-permute-start | bytes 1179656 | tf_op jit(solution)/shard_map/ppermute | solution.py:30
  25.6 6.3 %collective-permute-start.9 = (f32[64,512]{1,0:T(8,128)S(1)}, f32[64,512]{1,0:T(8,128)S(1)}, u32[]{:S(2)}, u32[]{:S(2)}) collective-permute-start(f32[64,512]{1,0:T(8,128)S(1)} %bitcast.94), channel_id=1, source_target_pairs={{0,48},{1,49},{2,50},{3,51},{4,52},{5,53},{6,54},{7,55},{8,56},{9,... | collective-permute-start | bytes 393224 | tf_op jit(solution)/shard_map/ppermute | solution.py:30
  28.3 5.0 %collective-permute-start.8 = (f32[64,512]{1,0:T(8,128)S(1)}, f32[64,512]{1,0:T(8,128)S(1)}, u32[]{:S(2)}, u32[]{:S(2)}) collective-permute-start(f32[64,512]{1,0:T(8,128)S(1)} %bitcast.95), channel_id=1, source_target_pairs={{0,16},{1,17},{2,18},{3,19},{4,20},{5,21},{6,22},{7,23},{8,24},{9,... | collective-permute-start | bytes 393224 | tf_op jit(solution)/shard_map/ppermute | solution.py:30
  35.1 13.3 %collective-permute-start.12 = (f32[256,512]{1,0:T(8,128)S(1)}, f32[256,512]{1,0:T(8,128)S(1)}, u32[]{:S(2)}, u32[]{:S(2)}) collective-permute-start(f32[256,512]{1,0:T(8,128)S(1)} %get-tuple-element.87), channel_id=1, source_target_pairs={{0,72},{1,73},{2,74},{3,75},{4,76},{5,77},{6,78},{7,79},{8,64},{9,... | collective-permute-start | bytes 1572872 | tf_op jit(solution)/shard_map/ppermute | solution.py:30
  39.0 17.1 %collective-permute-start.11 = (f32[256,512]{1,0:T(8,128)}, f32[256,512]{1,0:T(8,128)S(1)}, u32[]{:S(2)}, u32[]{:S(2)}) collective-permute-start(f32[256,512]{1,0:T(8,128)} %get-tuple-element.86.refs_0_), channel_id=1, source_target_pairs={{0,6},{1,7},{2,4},{3,5},{4,2},{5,3},{6,0},{7,1},{8,14},{9,15},{10,... | collective-permute-start | bytes 1572872 | tf_op jit(solution)/shard_map/ppermute | solution.py:30
  42.0 14.1 %collective-permute-start.10 = (f32[256,512]{1,0:T(8,128)}, f32[256,512]{1,0:T(8,128)S(1)}, u32[]{:S(2)}, u32[]{:S(2)}) collective-permute-start(f32[256,512]{1,0:T(8,128)} %get-tuple-element.86.refs_0_), channel_id=1, source_target_pairs={{0,2},{1,3},{2,0},{3,1},{4,6},{5,7},{6,4},{7,5},{8,10},{9,11},{10,... | collective-permute-start | bytes 1572872 | tf_op jit(solution)/shard_map/ppermute | solution.py:30
  42.2 14.0 %collective-permute-start.7 = (f32[128,512]{1,0:T(8,128)S(1)}, f32[128,512]{1,0:T(8,128)S(1)}, u32[]{:S(2)}, u32[]{:S(2)}) collective-permute-start(f32[128,512]{1,0:T(8,128)S(1)} %bitcast.67), channel_id=1, source_target_pairs={{0,48},{1,49},{2,50},{3,51},{4,52},{5,53},{6,54},{7,55},{8,56},{9,... | collective-permute-start | bytes 786440 | tf_op jit(solution)/shard_map/ppermute | solution.py:30
  48.5 7.7 %collective-permute-start.6 = (f32[128,512]{1,0:T(8,128)S(1)}, f32[128,512]{1,0:T(8,128)S(1)}, u32[]{:S(2)}, u32[]{:S(2)}) collective-permute-start(f32[128,512]{1,0:T(8,128)S(1)} %bitcast.68), channel_id=1, source_target_pairs={{0,16},{1,17},{2,18},{3,19},{4,20},{5,21},{6,22},{7,23},{8,24},{9,... | collective-permute-start | bytes 786440 | tf_op jit(solution)/shard_map/ppermute | solution.py:30
  49.1 7.0 %collective-permute-start.5 = (f32[128,512]{1,0:T(8,128)S(1)}, f32[128,512]{1,0:T(8,128)S(1)}, u32[]{:S(2)}, u32[]{:S(2)}) collective-permute-start(f32[128,512]{1,0:T(8,128)S(1)} %bitcast.69), channel_id=1, source_target_pairs={{0,64},{1,65},{2,66},{3,67},{4,68},{5,69},{6,70},{7,71},{8,72},{9,... | collective-permute-start | bytes 786440 | tf_op jit(solution)/shard_map/ppermute | solution.py:30
  58.7 24.0 %collective-permute-start.22 = (f32[384,512]{1,0:T(8,128)S(1)}, f32[384,512]{1,0:T(8,128)S(1)}, u32[]{:S(2)}, u32[]{:S(2)}) collective-permute-start(f32[384,512]{1,0:T(8,128)S(1)} %get-tuple-element.151), channel_id=1, source_target_pairs={{0,6},{1,7},{2,4},{3,5},{4,2},{5,3},{6,0},{7,1},{8,14},{9,15},{10,... | collective-permute-start | bytes 2359304 | tf_op jit(solution)/shard_map/ppermute | solution.py:30
  61.8 16.6 %collective-permute-start.18 = (f32[384,512]{1,0:T(8,128)S(1)}, f32[384,512]{1,0:T(8,128)S(1)}, u32[]{:S(2)}, u32[]{:S(2)}) collective-permute-start(f32[384,512]{1,0:T(8,128)S(1)} %get-tuple-element.152), channel_id=1, source_target_pairs={{0,2},{1,3},{2,0},{3,1},{4,6},{5,7},{6,4},{7,5},{8,10},{9,11},{10,... | collective-permute-start | bytes 2359304 | tf_op jit(solution)/shard_map/ppermute | solution.py:30
  62.0 9.1 %collective-permute-start.15 = (f32[192,512]{1,0:T(8,128)S(1)}, f32[192,512]{1,0:T(8,128)S(1)}, u32[]{:S(2)}, u32[]{:S(2)}) collective-permute-start(f32[192,512]{1,0:T(8,128)S(1)} %get-tuple-element.155), channel_id=1, source_target_pairs={{0,48},{1,49},{2,50},{3,51},{4,52},{5,53},{6,54},{7,55},{8,56},{9,... | collective-permute-start | bytes 1179656 | tf_op jit(solution)/shard_map/ppermute | solution.py:30
  63.9 8.1 %collective-permute-start.14 = (f32[192,512]{1,0:T(8,128)S(1)}, f32[192,512]{1,0:T(8,128)S(1)}, u32[]{:S(2)}, u32[]{:S(2)}) collective-permute-start(f32[192,512]{1,0:T(8,128)S(1)} %get-tuple-element.156), channel_id=1, source_target_pairs={{0,16},{1,17},{2,18},{3,19},{4,20},{5,21},{6,22},{7,23},{8,24},{9,... | collective-permute-start | bytes 1179656 | tf_op jit(solution)/shard_map/ppermute | solution.py:30
  69.6 20.8 %copy-start.22 = (s32[3]{0:T(128)S(1)}, s32[3]{0:T(128)}, u32[]{:S(2)}) copy-start(s32[3]{0:T(128)} %constant.164.clone) | copy-start | bytes 40
  69.6 20.8 %copy-start.23 = (s32[3]{0:T(128)S(1)}, s32[3]{0:T(128)}, u32[]{:S(2)}) copy-start(s32[3]{0:T(128)} %constant.163.clone) | copy-start | bytes 40
  72.1 6.3 %collective-permute-start.17 = (f32[64,512]{1,0:T(8,128)S(1)}, f32[64,512]{1,0:T(8,128)S(1)}, u32[]{:S(2)}, u32[]{:S(2)}) collective-permute-start(f32[64,512]{1,0:T(8,128)S(1)} %bitcast.96), channel_id=1, source_target_pairs={{0,48},{1,49},{2,50},{3,51},{4,52},{5,53},{6,54},{7,55},{8,56},{9,... | collective-permute-start | bytes 393224 | tf_op jit(solution)/shard_map/ppermute | solution.py:30
  73.2 5.1 %collective-permute-start.16 = (f32[64,512]{1,0:T(8,128)S(1)}, f32[64,512]{1,0:T(8,128)S(1)}, u32[]{:S(2)}, u32[]{:S(2)}) collective-permute-start(f32[64,512]{1,0:T(8,128)S(1)} %bitcast.97), channel_id=1, source_target_pairs={{0,16},{1,17},{2,18},{3,19},{4,20},{5,21},{6,22},{7,23},{8,24},{9,... | collective-permute-start | bytes 393224 | tf_op jit(solution)/shard_map/ppermute | solution.py:30
  80.4 25.1 %collective-permute-start.20 = (f32[256,512]{1,0:T(8,128)}, f32[256,512]{1,0:T(8,128)S(1)}, u32[]{:S(2)}, u32[]{:S(2)}) collective-permute-start(f32[256,512]{1,0:T(8,128)} %get-tuple-element.105.refs_0_), channel_id=1, source_target_pairs={{0,6},{1,7},{2,4},{3,5},{4,2},{5,3},{6,0},{7,1},{8,14},{9,15},{10,... | collective-permute-start | bytes 1572872 | tf_op jit(solution)/shard_map/ppermute | solution.py:30
  81.6 23.9 %collective-permute-start.19 = (f32[256,512]{1,0:T(8,128)}, f32[256,512]{1,0:T(8,128)}, u32[]{:S(2)}, u32[]{:S(2)}) collective-permute-start(f32[256,512]{1,0:T(8,128)} %get-tuple-element.105.refs_0_), channel_id=1, source_target_pairs={{0,2},{1,3},{2,0},{3,1},{4,6},{5,7},{6,4},{7,5},{8,10},{9,11},{10,... | collective-permute-start | bytes 1572872 | tf_op jit(solution)/shard_map/ppermute | solution.py:30
  83.5 19.9 %collective-permute-start.23 = (f32[128,512]{1,0:T(8,128)}, f32[128,512]{1,0:T(8,128)S(1)}, u32[]{:S(2)}, u32[]{:S(2)}) collective-permute-start(f32[128,512]{1,0:T(8,128)} %slice_bitcast_fusion.5), channel_id=1, source_target_pairs={{0,2},{1,3},{2,0},{3,1},{4,6},{5,7},{6,4},{7,5},{8,10},{9,11},{10,... | collective-permute-start | bytes 786440 | tf_op jit(solution)/shard_map/ppermute | solution.py:30
  85.1 18.3 %collective-permute-start.24 = (f32[128,512]{1,0:T(8,128)}, f32[128,512]{1,0:T(8,128)}, u32[]{:S(2)}, u32[]{:S(2)}) collective-permute-start(f32[128,512]{1,0:T(8,128)} %slice_bitcast_fusion.4), channel_id=1, source_target_pairs={{0,6},{1,7},{2,4},{3,5},{4,2},{5,3},{6,0},{7,1},{8,14},{9,15},{10,... | collective-permute-start | bytes 786440 | tf_op jit(solution)/shard_map/ppermute | solution.py:30
  87.2 18.3 %collective-permute-start.21 = (f32[256,512]{1,0:T(8,128)}, f32[256,512]{1,0:T(8,128)S(1)}, u32[]{:S(2)}, u32[]{:S(2)}) collective-permute-start(f32[256,512]{1,0:T(8,128)} %get-tuple-element.106), channel_id=1, source_target_pairs={{0,72},{1,73},{2,74},{3,75},{4,76},{5,77},{6,78},{7,79},{8,64},{9,... | collective-permute-start | bytes 1572872 | tf_op jit(solution)/shard_map/ppermute | solution.py:30
  105.4 2.7 %collective-permute-start.27 = (f32[256,512]{1,0:T(8,128)S(1)}, f32[256,512]{1,0:T(8,128)S(1)}, u32[]{:S(2)}, u32[]{:S(2)}) collective-permute-start(f32[256,512]{1,0:T(8,128)S(1)} %get-tuple-element.117), channel_id=1, source_target_pairs={{0,1},{1,0},{2,3},{3,2},{4,5},{5,4},{6,7},{7,6},{8,9},{9,8},{10,11... | collective-permute-start | bytes 1572872 | tf_op jit(solution)/shard_map/ppermute | solution.py:30
  106.8 22.5 %collective-permute-start.26 = (f32[384,512]{1,0:T(8,128)S(1)}, f32[384,512]{1,0:T(8,128)S(1)}, u32[]{:S(2)}, u32[]{:S(2)}) collective-permute-start(f32[384,512]{1,0:T(8,128)S(1)} %get-tuple-element.149), channel_id=1, source_target_pairs={{0,6},{1,7},{2,4},{3,5},{4,2},{5,3},{6,0},{7,1},{8,14},{9,15},{10,... | collective-permute-start | bytes 2359304 | tf_op jit(solution)/shard_map/ppermute | solution.py:30
  108.0 21.2 %collective-permute-start.25 = (f32[384,512]{1,0:T(8,128)S(1)}, f32[384,512]{1,0:T(8,128)S(1)}, u32[]{:S(2)}, u32[]{:S(2)}) collective-permute-start(f32[384,512]{1,0:T(8,128)S(1)} %get-tuple-element.150), channel_id=1, source_target_pairs={{0,2},{1,3},{2,0},{3,1},{4,6},{5,7},{6,4},{7,5},{8,10},{9,11},{10,... | collective-permute-start | bytes 2359304 | tf_op jit(solution)/shard_map/ppermute | solution.py:30
  108.7 6.9 %collective-permute-start.28 = (f32[64,512]{1,0:T(8,128)S(1)}, f32[64,512]{1,0:T(8,128)S(1)}, u32[]{:S(2)}, u32[]{:S(2)}) collective-permute-start(f32[64,512]{1,0:T(8,128)S(1)} %get-tuple-element.119), channel_id=1, source_target_pairs={{0,16},{1,17},{2,18},{3,19},{4,20},{5,21},{6,22},{7,23},{8,24},{9,... | collective-permute-start | bytes 393224 | tf_op jit(solution)/shard_map/ppermute | solution.py:30
  109.4 6.4 %collective-permute-start.29 = (f32[64,512]{1,0:T(8,128)S(1)}, f32[64,512]{1,0:T(8,128)S(1)}, u32[]{:S(2)}, u32[]{:S(2)}) collective-permute-start(f32[64,512]{1,0:T(8,128)S(1)} %get-tuple-element.120), channel_id=1, source_target_pairs={{0,48},{1,49},{2,50},{3,51},{4,52},{5,53},{6,54},{7,55},{8,56},{9,... | collective-permute-start | bytes 393224 | tf_op jit(solution)/shard_map/ppermute | solution.py:30
  116.5 10.7 %collective-permute-start.30 = (f32[192,512]{1,0:T(8,128)S(1)}, f32[192,512]{1,0:T(8,128)S(1)}, u32[]{:S(2)}, u32[]{:S(2)}) collective-permute-start(f32[192,512]{1,0:T(8,128)S(1)} %get-tuple-element.123), channel_id=1, source_target_pairs={{0,16},{1,17},{2,18},{3,19},{4,20},{5,21},{6,22},{7,23},{8,24},{9,... | collective-permute-start | bytes 1179656 | tf_op jit(solution)/shard_map/ppermute | solution.py:30
  117.8 11.4 %collective-permute-start.31 = (f32[192,512]{1,0:T(8,128)S(1)}, f32[192,512]{1,0:T(8,128)S(1)}, u32[]{:S(2)}, u32[]{:S(2)}) collective-permute-start(f32[192,512]{1,0:T(8,128)S(1)} %get-tuple-element.124), channel_id=1, source_target_pairs={{0,48},{1,49},{2,50},{3,51},{4,52},{5,53},{6,54},{7,55},{8,56},{9,... | collective-permute-start | bytes 1179656 | tf_op jit(solution)/shard_map/ppermute | solution.py:30
  129.3 7.8 %collective-permute-start.32 = (f32[128,512]{1,0:T(8,128)S(1)}, f32[128,512]{1,0:T(8,128)S(1)}, u32[]{:S(2)}, u32[]{:S(2)}) collective-permute-start(f32[128,512]{1,0:T(8,128)S(1)} %slice_bitcast_fusion.1), channel_id=1, source_target_pairs={{0,2},{1,3},{2,0},{3,1},{4,6},{5,7},{6,4},{7,5},{8,10},{9,11},{10,... | collective-permute-start | bytes 786440 | tf_op jit(solution)/shard_map/ppermute | solution.py:30
  131.2 7.7 %collective-permute-start.33 = (f32[128,512]{1,0:T(8,128)S(1)}, f32[128,512]{1,0:T(8,128)S(1)}, u32[]{:S(2)}, u32[]{:S(2)}) collective-permute-start(f32[128,512]{1,0:T(8,128)S(1)} %slice_bitcast_fusion), channel_id=1, source_target_pairs={{0,6},{1,7},{2,4},{3,5},{4,2},{5,3},{6,0},{7,1},{8,14},{9,15},{10,... | collective-permute-start | bytes 786440 | tf_op jit(solution)/shard_map/ppermute | solution.py:30
  139.8 3.0 %collective-permute-start.34 = (f32[256,512]{1,0:T(8,128)S(1)}, f32[256,512]{1,0:T(8,128)S(1)}, u32[]{:S(2)}, u32[]{:S(2)}) collective-permute-start(f32[256,512]{1,0:T(8,128)S(1)} %get-tuple-element.136), channel_id=1, source_target_pairs={{0,1},{1,0},{2,3},{3,2},{4,5},{5,4},{6,7},{7,6},{8,9},{9,8},{10,11... | collective-permute-start | bytes 1572872 | tf_op jit(solution)/shard_map/ppermute | solution.py:30
  139.9 9.2 %collective-permute-start.37 = (f32[128,512]{1,0:T(8,128)S(1)}, f32[128,512]{1,0:T(8,128)S(1)}, u32[]{:S(2)}, u32[]{:S(2)}) collective-permute-start(f32[128,512]{1,0:T(8,128)S(1)} %get-tuple-element.140), channel_id=1, source_target_pairs={{0,16},{1,17},{2,18},{3,19},{4,20},{5,21},{6,22},{7,23},{8,24},{9,... | collective-permute-start | bytes 786440 | tf_op jit(solution)/shard_map/ppermute | solution.py:30
  140.0 10.4 %collective-permute-start.38 = (f32[128,512]{1,0:T(8,128)S(1)}, f32[128,512]{1,0:T(8,128)S(1)}, u32[]{:S(2)}, u32[]{:S(2)}) collective-permute-start(f32[128,512]{1,0:T(8,128)S(1)} %get-tuple-element.141), channel_id=1, source_target_pairs={{0,48},{1,49},{2,50},{3,51},{4,52},{5,53},{6,54},{7,55},{8,56},{9,... | collective-permute-start | bytes 786440 | tf_op jit(solution)/shard_map/ppermute | solution.py:30
  141.2 9.2 %collective-permute-start.39 = (f32[128,512]{1,0:T(8,128)S(1)}, f32[128,512]{1,0:T(8,128)S(1)}, u32[]{:S(2)}, u32[]{:S(2)}) collective-permute-start(f32[128,512]{1,0:T(8,128)S(1)} %get-tuple-element.132), channel_id=1, source_target_pairs={{0,64},{1,65},{2,66},{3,67},{4,68},{5,69},{6,70},{7,71},{8,72},{9,... | collective-permute-start | bytes 786440 | tf_op jit(solution)/shard_map/ppermute | solution.py:30
  143.5 8.0 %collective-permute-start.35 = (f32[64,512]{1,0:T(8,128)S(1)}, f32[64,512]{1,0:T(8,128)S(1)}, u32[]{:S(2)}, u32[]{:S(2)}) collective-permute-start(f32[64,512]{1,0:T(8,128)S(1)} %get-tuple-element.138), channel_id=1, source_target_pairs={{0,16},{1,17},{2,18},{3,19},{4,20},{5,21},{6,22},{7,23},{8,24},{9,... | collective-permute-start | bytes 393224 | tf_op jit(solution)/shard_map/ppermute | solution.py:30
  144.9 7.8 %collective-permute-start.36 = (f32[64,512]{1,0:T(8,128)S(1)}, f32[64,512]{1,0:T(8,128)S(1)}, u32[]{:S(2)}, u32[]{:S(2)}) collective-permute-start(f32[64,512]{1,0:T(8,128)S(1)} %get-tuple-element.139), channel_id=1, source_target_pairs={{0,48},{1,49},{2,50},{3,51},{4,52},{5,53},{6,54},{7,55},{8,56},{9,... | collective-permute-start | bytes 393224 | tf_op jit(solution)/shard_map/ppermute | solution.py:30
  153.4 10.6 %collective-permute-start.40 = (f32[192,512]{1,0:T(8,128)S(1)}, f32[192,512]{1,0:T(8,128)S(1)}, u32[]{:S(2)}, u32[]{:S(2)}) collective-permute-start(f32[192,512]{1,0:T(8,128)S(1)} %get-tuple-element.144), channel_id=1, source_target_pairs={{0,16},{1,17},{2,18},{3,19},{4,20},{5,21},{6,22},{7,23},{8,24},{9,... | collective-permute-start | bytes 1179656 | tf_op jit(solution)/shard_map/ppermute | solution.py:30
  154.0 11.3 %collective-permute-start.41 = (f32[192,512]{1,0:T(8,128)S(1)}, f32[192,512]{1,0:T(8,128)S(1)}, u32[]{:S(2)}, u32[]{:S(2)}) collective-permute-start(f32[192,512]{1,0:T(8,128)S(1)} %get-tuple-element.145), channel_id=1, source_target_pairs={{0,48},{1,49},{2,50},{3,51},{4,52},{5,53},{6,54},{7,55},{8,56},{9,... | collective-permute-start | bytes 1179656 | tf_op jit(solution)/shard_map/ppermute | solution.py:30
  166.0 6.5 %collective-permute-start.42 = (f32[128,512]{1,0:T(8,128)S(1)}, f32[128,512]{1,0:T(8,128)S(1)}, u32[]{:S(2)}, u32[]{:S(2)}) collective-permute-start(f32[128,512]{1,0:T(8,128)S(1)} %get-tuple-element.146), channel_id=1, source_target_pairs={{0,16},{1,17},{2,18},{3,19},{4,20},{5,21},{6,22},{7,23},{8,24},{9,... | collective-permute-start | bytes 786440 | tf_op jit(solution)/shard_map/ppermute | solution.py:30
  166.5 7.6 %collective-permute-start.43 = (f32[128,512]{1,0:T(8,128)S(1)}, f32[128,512]{1,0:T(8,128)S(1)}, u32[]{:S(2)}, u32[]{:S(2)}) collective-permute-start(f32[128,512]{1,0:T(8,128)S(1)} %get-tuple-element.147), channel_id=1, source_target_pairs={{0,48},{1,49},{2,50},{3,51},{4,52},{5,53},{6,54},{7,55},{8,56},{9,... | collective-permute-start | bytes 786440 | tf_op jit(solution)/shard_map/ppermute | solution.py:30
  167.4 6.7 %collective-permute-start.44 = (f32[128,512]{1,0:T(8,128)S(1)}, f32[128,512]{1,0:T(8,128)S(1)}, u32[]{:S(2)}, u32[]{:S(2)}) collective-permute-start(f32[128,512]{1,0:T(8,128)S(1)} %get-tuple-element.148), channel_id=1, source_target_pairs={{0,64},{1,65},{2,66},{3,67},{4,68},{5,69},{6,70},{7,71},{8,72},{9,... | collective-permute-start | bytes 786440 | tf_op jit(solution)/shard_map/ppermute | solution.py:30
  (27 other events, 199.2 us)

commit v7 on v5

--- a/solution.py
+++ b/solution.py
@@ -11,6 +11,7 @@
 TILE = 128
 SLOTS = 4
 CHUNKS = (64, 64)
+BRIEF = pl.CostEstimate(flops=1, bytes_accessed=1, transcendentals=0)
 
 PLACES = [
     (zl, x, zh, y, c)
@@ -98,11 +99,7 @@
         ),
         out_shape=[jax.ShapeDtypeStruct((m, cols), jnp.float32)] * 2,
         compiler_params=pltpu.CompilerParams(vmem_limit_bytes=50 * 1024 * 1024),
-        cost_estimate=pl.CostEstimate(
-            flops=12 * n * m * width * cols,
-            bytes_accessed=8 * n * width * cols + 4 * n * m * width,
-            transcendentals=0,
-        ),
+        cost_estimate=BRIEF,
         name="products",
     )(at, *arrays, own, far, *sums)
 
@@ -132,7 +129,8 @@
 
 
 def gather_second(near, other, swap, pieces=1):
-    return swap(join(other, half(near[1], 0, pieces)), 0), swap(join(other, half(near[0], 1, pieces)), 1)
+    going = [join(other, half(near[1 - i], i, pieces)) for i in range(2)]
+    return going, [swap(a, i) for i, a in enumerate(going)]
 
 
 def gather_third(both, rows, swap, pieces=1):
@@ -321,7 +319,7 @@
         return [piece, other, swap_x(own, 0), swap_x(own, 1)]
 
     def rows_second(arrays):
-        return arrays + list(gather_second(arrays[2:4], arrays[1], swap_x, local_tiles))
+        return arrays + gather_second(arrays[2:4], arrays[1], swap_x, local_tiles)[1]
 
     def rows_third(arrays):
         rows = arrays[1].shape[0]
@@ -350,20 +348,25 @@
     for k, m in enumerate(CHUNKS):
         more = k + 1 < len(CHUNKS)
         after = () if last is None else (last["second"][0], last["sums"][0])
+        if more:
+            later = rows_first(pieces[k + 1], arrays)
+            after = (*after, later[1])
         b, crossing = pick(plan, m, arrays, after)
         this = dict(m=SLOTS * m, sums=[])
         if more:
-            arrays = rows_first(pieces[k + 1], arrays)
+            arrays = later
         near = [swap_y(b, 0), swap_y(b, 1)]
         bz = cross_z(crossing)
         this["first"] = [b, *near, bz]
         ready = []
         if last is not None:
-            sums, back = finish(last, back)
+            ready = [*ready, step(1, last)[0]]
+        near, bz = wait_for((near, bz), *ready)
+        going, this["second"] = gather_second(near, bz, swap_y)
+        if last is not None:
+            last["third"] = wait_for(last["third"], *going)
+            sums = step(2, last)
             swapped = flip_core(sums[1])
-            ready = [*ready, sums[0]]
-        near, bz = wait_for((near, bz), *ready)
-        this["second"] = gather_second(near, bz, swap_y)
         if more:
             arrays = rows_second(wait_for(arrays, near[0]))
         ready = arrays[4:6] if more else []

time: 167 us -> 167 us (level)
  waiting for transfers between devices: 60.6 us -> 53.2 us
  starting transfers between devices: 50 us -> 56.7 us
  other arithmetic: 6.57 us -> 8.7 us
    ppermute x45, waiting for transfers between devices: 60.6 us -> 53.2 us  [send(): lax.ppermute(a, ('row', 'col'), [(i, index[to(*p)]) for p, i in index.ite...]
    ppermute x45, starting transfers between devices: 50 us -> 56.7 us  [send(): lax.ppermute(a, ('row', 'col'), [(i, index[to(*p)]) for p, i in index.ite...]
    concatenate x4, other arithmetic: 1.7 us -> 3.83 us  [join(): return jnp.concatenate(arrays, axis=0)]
    slice x8, local copies, waits for them, and re-layouts: 1.89 us -> 0.08 us  [half(): cut = a.reshape(pieces, 2, -1, a.shape[1])[:, which]]
    unnamed x16 -> x32, local copies, waits for them, and re-layouts: 3.13 us -> 3.91 us
  transfers between devices with their start and end apart: 45 -> 45, of which waited for: 23 -> 22; matrix products, arithmetic and copies ran while one was open for 7% -> 8% of each run, Pallas kernels for 23% -> 22%
where the time goes in v7:
time: 167 us; the launch traced here: 166 us
  starting transfers between devices  56.7 us (34%)
  waiting for transfers between devices  53.2 us (32%)
  Pallas kernels  38.2 us (23%)
  local copies, waits for them, and re-layouts  8.75 us (5%)
  other arithmetic  8.7 us (5%)
    ppermute x45, starting transfers between devices, send(): lax.ppermute(a, ('row', 'col'), [(i, index[to(*p)]) for p, i in index.ite...  56.7 us
    ppermute x45, waiting for transfers between devices, send(): lax.ppermute(a, ('row', 'col'), [(i, index[to(*p)]) for p, i in index.ite...  53.2 us
    pallas_call x6, Pallas kernels, products(): pl.pallas_call(functools.partial(product_kernel, blocks, len(arrays), not...  30.3 us
    pallas_call x10, Pallas kernels, small_kernel(): pl.pallas_call(kernel, in_specs=[pl.BlockSpec(memory_space=pltpu.SMEM)] +...  7.9 us
    unnamed x32, local copies, waits for them, and re-layouts  3.91 us
    concatenate x4, other arithmetic, join(): return jnp.concatenate(arrays, axis=0)  3.83 us
  transfers between devices with their start and end apart: 45, of which 22 were waited for; matrix products, arithmetic and copies ran while one was open for 8% of the time, Pallas kernels for 22%

profile of v7, /device:TPU:0, one launch (start us, length us, event | category | flops | bytes accessed | tf_op | source)
XLA Modules:
  0.0 166.2 jit_solution(5253436950125444065)
XLA Ops:
  1.1 2.9 %collective-permute-start.2 = (f32[128,512]{1,0:T(8,128)S(1)}, f32[128,512]{1,0:T(8,128)S(1)}, u32[]{:S(2)}, u32[]{:S(2)}) collective-permute-start(f32[128,512]{1,0:T(8,128)S(1)} %bitcast.76), channel_id=1, source_target_pairs={{0,48},{1,49},{2,50},{3,51},{4,52},{5,53},{6,54},{7,55},{8,56},{9,... | collective-permute-start | bytes 786440 | tf_op jit(solution)/shard_map/ppermute | solution.py:28
  4.2 1.9 %collective-permute-start = (f32[128,512]{1,0:T(8,128)S(1)}, f32[128,512]{1,0:T(8,128)S(1)}, u32[]{:S(2)}, u32[]{:S(2)}) collective-permute-start(f32[128,512]{1,0:T(8,128)S(1)} %bitcast.78), channel_id=1, source_target_pairs={{0,64},{1,65},{2,66},{3,67},{4,68},{5,69},{6,70},{7,71},{8,72},{9,... | collective-permute-start | bytes 786440 | tf_op jit(solution)/shard_map/ppermute | solution.py:28
  6.8 4.3 %collective-permute-done.2.refs_3_ = f32[128,512]{1,0:T(8,128)S(1)} collective-permute-done((f32[128,512]{1,0:T(8,128)S(1)}, f32[128,512]{1,0:T(8,128)S(1)}, u32[]{:S(2)}, u32[]{:S(2)}) %collective-permute-start.2) | collective-permute-done | bytes 262176 | tf_op jit(solution)/shard_map/ppermute | solution.py:28
  11.1 1.3 collective-permute-done.1.refs_2_
  12.7 1.4 collective-permute-start.4
  16.3 1.8 %collective-permute-start.7 = (f32[128,512]{1,0:T(8,128)S(1)}, f32[128,512]{1,0:T(8,128)S(1)}, u32[]{:S(2)}, u32[]{:S(2)}) collective-permute-start(f32[128,512]{1,0:T(8,128)S(1)} %bitcast.72), channel_id=1, source_target_pairs={{0,64},{1,65},{2,66},{3,67},{4,68},{5,69},{6,70},{7,71},{8,72},{9,... | collective-permute-start | bytes 786440 | tf_op jit(solution)/shard_map/ppermute | solution.py:28
  19.0 5.4 %collective-permute-done.4.refs_5_ = f32[192,512]{1,0:T(8,128)S(1)} collective-permute-done((f32[192,512]{1,0:T(8,128)S(1)}, f32[192,512]{1,0:T(8,128)S(1)}, u32[]{:S(2)}, u32[]{:S(2)}) %collective-permute-start.4) | collective-permute-done | bytes 393248 | tf_op jit(solution)/shard_map/ppermute | solution.py:28
  25.0 1.4 collective-permute-start.6
  26.6 2.9 %collective-permute-done.5.refs_6_ = f32[64,512]{1,0:T(8,128)S(1)} collective-permute-done((f32[64,512]{1,0:T(8,128)S(1)}, f32[64,512]{1,0:T(8,128)S(1)}, u32[]{:S(2)}, u32[]{:S(2)}) %collective-permute-start.5) | collective-permute-done | bytes 131104 | tf_op jit(solution)/shard_map/ppermute | solution.py:28
  29.5 1.8 %collective-permute-done.6.refs_7_ = f32[64,512]{1,0:T(8,128)S(1)} collective-permute-done((f32[64,512]{1,0:T(8,128)S(1)}, f32[64,512]{1,0:T(8,128)S(1)}, u32[]{:S(2)}, u32[]{:S(2)}) %collective-permute-start.6) | collective-permute-done | bytes 131104 | tf_op jit(solution)/shard_map/ppermute | solution.py:28
  32.3 3.8 %collective-permute-start.10 = (f32[256,512]{1,0:T(8,128)S(1)}, f32[256,512]{1,0:T(8,128)S(1)}, u32[]{:S(2)}, u32[]{:S(2)}) collective-permute-start(f32[256,512]{1,0:T(8,128)S(1)} %get-tuple-element.69), channel_id=1, source_target_pairs={{0,72},{1,73},{2,74},{3,75},{4,76},{5,77},{6,78},{7,79},{8,64},{9,... | collective-permute-start | bytes 1572872 | tf_op jit(solution)/shard_map/ppermute | solution.py:28
  36.1 3.0 %collective-permute-start.9 = (f32[256,512]{1,0:T(8,128)S(1)}, f32[256,512]{1,0:T(8,128)S(1)}, u32[]{:S(2)}, u32[]{:S(2)}) collective-permute-start(f32[256,512]{1,0:T(8,128)S(1)} %get-tuple-element.68.refs_0_), channel_id=1, source_target_pairs={{0,6},{1,7},{2,4},{3,5},{4,2},{5,3},{6,0},{7,1},{8,14},{9,15},{10,... | collective-permute-start | bytes 1572872 | tf_op jit(solution)/shard_map/ppermute | solution.py:28
  39.2 1.6 collective-permute-start.15
  40.9 4.7 %collective-permute-done.10.refs_3_ = f32[256,512]{1,0:T(8,128)S(1)} collective-permute-done((f32[256,512]{1,0:T(8,128)S(1)}, f32[256,512]{1,0:T(8,128)S(1)}, u32[]{:S(2)}, u32[]{:S(2)}) %collective-permute-start.10) | collective-permute-done | bytes 524320 | tf_op jit(solution)/shard_map/ppermute | solution.py:28
  46.1 2.2 %collective-permute-done.9.refs_2_ = f32[256,512]{1,0:T(8,128)S(1)} collective-permute-done((f32[256,512]{1,0:T(8,128)S(1)}, f32[256,512]{1,0:T(8,128)S(1)}, u32[]{:S(2)}, u32[]{:S(2)}) %collective-permute-start.9) | collective-permute-done | bytes 524320 | tf_op jit(solution)/shard_map/ppermute | solution.py:28
  48.3 1.5 collective-permute-done.8.refs_1_
  49.8 1.4 pad_maximum_fusion
  52.6 3.0 %collective-permute-start.12 = (f32[384,512]{1,0:T(8,128)}, f32[384,512]{1,0:T(8,128)S(1)}, u32[]{:S(2)}, u32[]{:S(2)}) collective-permute-start(f32[384,512]{1,0:T(8,128)} %get-tuple-element.131), channel_id=1, source_target_pairs={{0,6},{1,7},{2,4},{3,5},{4,2},{5,3},{6,0},{7,1},{8,14},{9,15},{10,... | collective-permute-start | bytes 2359304 | tf_op jit(solution)/shard_map/ppermute | solution.py:28
  56.6 2.0 %collective-permute-start.17 = (f32[192,512]{1,0:T(8,128)}, f32[192,512]{1,0:T(8,128)}, u32[]{:S(2)}, u32[]{:S(2)}) collective-permute-start(f32[192,512]{1,0:T(8,128)} %get-tuple-element.135), channel_id=1, source_target_pairs={{0,48},{1,49},{2,50},{3,51},{4,52},{5,53},{6,54},{7,55},{8,56},{9,... | collective-permute-start | bytes 1179656 | tf_op jit(solution)/shard_map/ppermute | solution.py:28
  60.6 6.8 %products.6 = (f32[256,512]{1,0:T(8,128)S(1)}, f32[256,512]{1,0:T(8,128)S(1)}) custom-call(s32[4]{0:T(128)S(1)} %multiply_add_fusion.1.at_ref, f32[256,512]{1,0:T(8,128)S(1)} %copy-done.7, f32[256,512]{1,0:T(8,128)S(1)} %collective-permute-done.8.refs_1_, f32[256,512]{1,0:T(8,128)S(1)} %collective-permute-done.9.refs_2_, ...), custom_call_target="tpu_custom_call" | custom-call | flops 1 | bytes 1 | tf_op jit(solution)/shard_map/products/pallas_call | solution.py:90
  70.6 1.5 collective-permute-start.20
  72.1 2.6 %collective-permute-done.21.refs_7_ = f32[64,512]{1,0:T(8,128)S(1)} collective-permute-done((f32[64,512]{1,0:T(8,128)S(1)}, f32[64,512]{1,0:T(8,128)S(1)}, u32[]{:S(2)}, u32[]{:S(2)}) %collective-permute-start.21) | collective-permute-done | bytes 131104 | tf_op jit(solution)/shard_map/ppermute | solution.py:28
  75.7 1.6 pick.3
  78.0 3.0 %collective-permute-start.24 = (f32[256,512]{1,0:T(8,128)S(1)}, f32[256,512]{1,0:T(8,128)S(1)}, u32[]{:S(2)}, u32[]{:S(2)}) collective-permute-start(f32[256,512]{1,0:T(8,128)S(1)} %get-tuple-element.88), channel_id=1, source_target_pairs={{0,72},{1,73},{2,74},{3,75},{4,76},{5,77},{6,78},{7,79},{8,64},{9,... | collective-permute-start | bytes 1572872 | tf_op jit(solution)/shard_map/ppermute | solution.py:28
  81.7 1.7 %collective-permute-start.18 = (f32[128,512]{1,0:T(8,128)}, f32[128,512]{1,0:T(8,128)}, u32[]{:S(2)}, u32[]{:S(2)}) collective-permute-start(f32[128,512]{1,0:T(8,128)} %slice_bitcast_fusion.5), channel_id=1, source_target_pairs={{0,2},{1,3},{2,0},{3,1},{4,6},{5,7},{6,4},{7,5},{8,10},{9,11},{10,... | collective-permute-start | bytes 786440 | tf_op jit(solution)/shard_map/ppermute | solution.py:28
  84.2 3.0 %collective-permute-start.19 = (f32[128,512]{1,0:T(8,128)}, f32[128,512]{1,0:T(8,128)}, u32[]{:S(2)}, u32[]{:S(2)}) collective-permute-start(f32[128,512]{1,0:T(8,128)} %slice_bitcast_fusion.4), channel_id=1, source_target_pairs={{0,6},{1,7},{2,4},{3,5},{4,2},{5,3},{6,0},{7,1},{8,14},{9,15},{10,... | collective-permute-start | bytes 786440 | tf_op jit(solution)/shard_map/ppermute | solution.py:28
  87.2 5.7 %products.7 = (f32[256,512]{1,0:T(8,128)S(1)}, f32[256,512]{1,0:T(8,128)S(1)}) custom-call(s32[3]{0:T(128)S(1)} %multiply_add_fusion.at_ref, f32[384,512]{1,0:T(8,128)S(1)} %collective-permute-done.11.refs_8_.refs_0_, f32[384,512]{1,0:T(8,128)S(1)} %collective-permute-done.12.refs_1_, f32[8192,512]{1,0:T(8,128)} %bitcast.88, ...), custom_call_target="tpu_custom_call" | custom-call | flops 1 | bytes 1 | tf_op jit(solution)/shard_map/products/pallas_call | solution.py:90
  93.0 1.4 pad_maximum_fusion.2
  96.8 2.7 %products.8 = (f32[256,512]{1,0:T(8,128)S(1)}, f32[256,512]{1,0:T(8,128)S(1)}) custom-call(s32[1]{0:T(128)S(6)} %add.113.at_ref, f32[128,512]{1,0:T(8,128)} %collective-permute-done.18.refs_0_, f32[128,512]{1,0:T(8,128)} %collective-permute-done.19.refs_1_, f32[8192,512]{1,0:T(8,128)} %bitcast.89, f32[8192,512]{1,0:T(8,128)} %collective-permute-done.13.refs_5_.refs_3_, ...), custom_call_target="tpu_custom_call" | custom-call | flops 1 | bytes 1 | tf_op jit(solution)/shard_map/products/pallas_call | solution.py:90
  99.6 1.9 %collective-permute-done.25.refs_1_ = f32[256,512]{1,0:T(8,128)S(1)} collective-permute-done((f32[256,512]{1,0:T(8,128)S(1)}, f32[256,512]{1,0:T(8,128)S(1)}, u32[]{:S(2)}, u32[]{:S(2)}) %collective-permute-start.25) | collective-permute-done | bytes 524320 | tf_op jit(solution)/shard_map/ppermute | solution.py:28
  102.2 1.5 collective-permute-start.26
  103.7 1.9 %collective-permute-start.27 = (f32[64,512]{1,0:T(8,128)S(1)}, f32[64,512]{1,0:T(8,128)S(1)}, u32[]{:S(2)}, u32[]{:S(2)}) collective-permute-start(f32[64,512]{1,0:T(8,128)S(1)} %get-tuple-element.101), channel_id=1, source_target_pairs={{0,48},{1,49},{2,50},{3,51},{4,52},{5,53},{6,54},{7,55},{8,56},{9,... | collective-permute-start | bytes 393224 | tf_op jit(solution)/shard_map/ppermute | solution.py:28
  105.6 6.8 %products.9 = (f32[256,512]{1,0:T(8,128)S(1)}, f32[256,512]{1,0:T(8,128)S(1)}) custom-call(s32[4]{0:T(128)S(1)} %multiply_add_fusion.1.at_ref, f32[256,512]{1,0:T(8,128)S(1)} %copy-done.9, f32[256,512]{1,0:T(8,128)S(1)} %collective-permute-done.22.refs_1_, f32[256,512]{1,0:T(8,128)S(1)} %collective-permute-done.23.refs_2_, ...), custom_call_target="tpu_custom_call" | custom-call | flops 1 | bytes 1 | tf_op jit(solution)/shard_map/products/pallas_call | solution.py:90
  113.3 2.1 %collective-permute-start.35 = (f32[128,512]{1,0:T(8,128)S(1)}, f32[128,512]{1,0:T(8,128)S(1)}, u32[]{:S(2)}, u32[]{:S(2)}) collective-permute-start(f32[128,512]{1,0:T(8,128)S(1)} %slice_bitcast_fusion.1), channel_id=1, source_target_pairs={{0,2},{1,3},{2,0},{3,1},{4,6},{5,7},{6,4},{7,5},{8,10},{9,11},{10,... | collective-permute-start | bytes 786440 | tf_op jit(solution)/shard_map/ppermute | solution.py:28
  115.4 3.0 %collective-permute-start.36 = (f32[128,512]{1,0:T(8,128)S(1)}, f32[128,512]{1,0:T(8,128)S(1)}, u32[]{:S(2)}, u32[]{:S(2)}) collective-permute-start(f32[128,512]{1,0:T(8,128)S(1)} %slice_bitcast_fusion), channel_id=1, source_target_pairs={{0,6},{1,7},{2,4},{3,5},{4,2},{5,3},{6,0},{7,1},{8,14},{9,15},{10,... | collective-permute-start | bytes 786440 | tf_op jit(solution)/shard_map/ppermute | solution.py:28
  119.8 5.7 %products.10 = (f32[256,512]{1,0:T(8,128)S(1)}, f32[256,512]{1,0:T(8,128)S(1)}) custom-call(s32[3]{0:T(128)S(1)} %multiply_add_fusion.at_ref, f32[384,512]{1,0:T(8,128)S(1)} %collective-permute-done.30.refs_0_, f32[384,512]{1,0:T(8,128)S(1)} %collective-permute-done.31.refs_1_, f32[8192,512]{1,0:T(8,128)} %bitcast.91, ...), custom_call_target="tpu_custom_call" | custom-call | flops 1 | bytes 1 | tf_op jit(solution)/shard_map/products/pallas_call | solution.py:90
  125.5 2.5 %products.11 = (f32[256,512]{1,0:T(8,128)S(1)}, f32[256,512]{1,0:T(8,128)S(1)}) custom-call(s32[1]{0:T(128)S(6)} %add.113.at_ref, f32[128,512]{1,0:T(8,128)S(1)} %collective-permute-done.35.refs_0_, f32[128,512]{1,0:T(8,128)S(1)} %collective-permute-done.36.refs_1_, f32[8192,512]{1,0:T(8,128)} %bitcast.92, ...), custom_call_target="tpu_custom_call" | custom-call | flops 1 | bytes 1 | tf_op jit(solution)/shard_map/products/pallas_call | solution.py:90
  128.1 1.6 collective-permute-done.29.refs_2_
  131.1 1.3 collective-permute-start.33
  134.0 1.9 %collective-permute-start.39 = (f32[64,512]{1,0:T(8,128)S(1)}, f32[64,512]{1,0:T(8,128)S(1)}, u32[]{:S(2)}, u32[]{:S(2)}) collective-permute-start(f32[64,512]{1,0:T(8,128)S(1)} %get-tuple-element.121), channel_id=1, source_target_pairs={{0,48},{1,49},{2,50},{3,51},{4,52},{5,53},{6,54},{7,55},{8,56},{9,... | collective-permute-start | bytes 393224 | tf_op jit(solution)/shard_map/ppermute | solution.py:28
  135.9 3.1 %collective-permute-done.32.refs_1_ = f32[128,512]{1,0:T(8,128)S(1)} collective-permute-done((f32[128,512]{1,0:T(8,128)S(1)}, f32[128,512]{1,0:T(8,128)S(1)}, u32[]{:S(2)}, u32[]{:S(2)}) %collective-permute-start.32) | collective-permute-done | bytes 262176 | tf_op jit(solution)/shard_map/ppermute | solution.py:28
  139.0 2.4 %collective-permute-done.33.refs_2_ = f32[128,512]{1,0:T(8,128)S(1)} collective-permute-done((f32[128,512]{1,0:T(8,128)S(1)}, f32[128,512]{1,0:T(8,128)S(1)}, u32[]{:S(2)}, u32[]{:S(2)}) %collective-permute-start.33) | collective-permute-done | bytes 262176 | tf_op jit(solution)/shard_map/ppermute | solution.py:28
  143.6 2.0 %collective-permute-start.41 = (f32[192,512]{1,0:T(8,128)S(1)}, f32[192,512]{1,0:T(8,128)S(1)}, u32[]{:S(2)}, u32[]{:S(2)}) collective-permute-start(f32[192,512]{1,0:T(8,128)S(1)} %get-tuple-element.125), channel_id=1, source_target_pairs={{0,48},{1,49},{2,50},{3,51},{4,52},{5,53},{6,54},{7,55},{8,56},{9,... | collective-permute-start | bytes 1179656 | tf_op jit(solution)/shard_map/ppermute | solution.py:28
  145.6 7.5 %collective-permute-done.40.refs_1_ = f32[192,512]{1,0:T(8,128)S(1)} collective-permute-done((f32[192,512]{1,0:T(8,128)S(1)}, f32[192,512]{1,0:T(8,128)S(1)}, u32[]{:S(2)}, u32[]{:S(2)}) %collective-permute-start.40) | collective-permute-done | bytes 393248 | tf_op jit(solution)/shard_map/ppermute | solution.py:28
  153.2 1.3 collective-permute-done.41.refs_2_
  156.1 2.3 %collective-permute-start.43 = (f32[128,512]{1,0:T(8,128)S(1)}, f32[128,512]{1,0:T(8,128)S(1)}, u32[]{:S(2)}, u32[]{:S(2)}) collective-permute-start(f32[128,512]{1,0:T(8,128)S(1)} %get-tuple-element.127), channel_id=1, source_target_pairs={{0,48},{1,49},{2,50},{3,51},{4,52},{5,53},{6,54},{7,55},{8,56},{9,... | collective-permute-start | bytes 786440 | tf_op jit(solution)/shard_map/ppermute | solution.py:28
  158.4 3.2 %collective-permute-done.42.refs_1_ = f32[128,512]{1,0:T(8,128)S(1)} collective-permute-done((f32[128,512]{1,0:T(8,128)S(1)}, f32[128,512]{1,0:T(8,128)S(1)}, u32[]{:S(2)}, u32[]{:S(2)}) %collective-permute-start.42) | collective-permute-done | bytes 262176 | tf_op jit(solution)/shard_map/ppermute | solution.py:28
  161.6 2.0 %collective-permute-done.43.refs_2_ = f32[128,512]{1,0:T(8,128)S(1)} collective-permute-done((f32[128,512]{1,0:T(8,128)S(1)}, f32[128,512]{1,0:T(8,128)S(1)}, u32[]{:S(2)}, u32[]{:S(2)}) %collective-permute-start.43) | collective-permute-done | bytes 262176 | tf_op jit(solution)/shard_map/ppermute | solution.py:28
  (128 shorter events, 33.1 us)
Async XLA Ops:
  0.0 59.5 %collective-permute-start.13 = (f32[8192,512]{1,0:T(8,128)}, f32[8192,512]{1,0:T(8,128)}, u32[]{:S(2)}, u32[]{:S(2)}) collective-permute-start(f32[8192,512]{1,0:T(8,128)} %bitcast.86), channel_id=1, source_target_pairs={{0,1},{1,0},{2,3},{3,2},{4,5},{5,4},{6,7},{7,6},{8,9},{9,8},{10,11... | collective-permute-start | bytes 50331656 | tf_op jit(solution)/shard_map/ppermute | solution.py:28
  1.1 50.9 %copy-start = (f32[2,64,512]{2,1,0:T(8,128)}, f32[2,64,512]{2,1,0:T(8,128)S(1)}, u32[]{:S(2)}) copy-start(f32[2,64,512]{2,1,0:T(8,128)S(1)} %get-tuple-element.134) | copy-start | bytes 786436
  1.1 10.0 %collective-permute-start.2 = (f32[128,512]{1,0:T(8,128)S(1)}, f32[128,512]{1,0:T(8,128)S(1)}, u32[]{:S(2)}, u32[]{:S(2)}) collective-permute-start(f32[128,512]{1,0:T(8,128)S(1)} %bitcast.76), channel_id=1, source_target_pairs={{0,48},{1,49},{2,50},{3,51},{4,52},{5,53},{6,54},{7,55},{8,56},{9,... | collective-permute-start | bytes 786440 | tf_op jit(solution)/shard_map/ppermute | solution.py:28
  4.0 8.4 %collective-permute-start.1 = (f32[128,512]{1,0:T(8,128)S(1)}, f32[128,512]{1,0:T(8,128)S(1)}, u32[]{:S(2)}, u32[]{:S(2)}) collective-permute-start(f32[128,512]{1,0:T(8,128)S(1)} %bitcast.77), channel_id=1, source_target_pairs={{0,16},{1,17},{2,18},{3,19},{4,20},{5,21},{6,22},{7,23},{8,24},{9,... | collective-permute-start | bytes 786440 | tf_op jit(solution)/shard_map/ppermute | solution.py:28
  4.2 8.4 %collective-permute-start = (f32[128,512]{1,0:T(8,128)S(1)}, f32[128,512]{1,0:T(8,128)S(1)}, u32[]{:S(2)}, u32[]{:S(2)}) collective-permute-start(f32[128,512]{1,0:T(8,128)S(1)} %bitcast.78), channel_id=1, source_target_pairs={{0,64},{1,65},{2,66},{3,67},{4,68},{5,69},{6,70},{7,71},{8,72},{9,... | collective-permute-start | bytes 786440 | tf_op jit(solution)/shard_map/ppermute | solution.py:28
  12.7 11.7 %collective-permute-start.4 = (f32[192,512]{1,0:T(8,128)S(1)}, f32[192,512]{1,0:T(8,128)S(1)}, u32[]{:S(2)}, u32[]{:S(2)}) collective-permute-start(f32[192,512]{1,0:T(8,128)S(1)} %get-tuple-element.137), channel_id=1, source_target_pairs={{0,48},{1,49},{2,50},{3,51},{4,52},{5,53},{6,54},{7,55},{8,56},{9,... | collective-permute-start | bytes 1179656 | tf_op jit(solution)/shard_map/ppermute | solution.py:28
  14.2 10.8 %collective-permute-start.3 = (f32[192,512]{1,0:T(8,128)S(1)}, f32[192,512]{1,0:T(8,128)S(1)}, u32[]{:S(2)}, u32[]{:S(2)}) collective-permute-start(f32[192,512]{1,0:T(8,128)S(1)} %get-tuple-element.138), channel_id=1, source_target_pairs={{0,16},{1,17},{2,18},{3,19},{4,20},{5,21},{6,22},{7,23},{8,24},{9,... | collective-permute-start | bytes 1179656 | tf_op jit(solution)/shard_map/ppermute | solution.py:28
  16.3 10.3 %collective-permute-start.7 = (f32[128,512]{1,0:T(8,128)S(1)}, f32[128,512]{1,0:T(8,128)S(1)}, u32[]{:S(2)}, u32[]{:S(2)}) collective-permute-start(f32[128,512]{1,0:T(8,128)S(1)} %bitcast.72), channel_id=1, source_target_pairs={{0,64},{1,65},{2,66},{3,67},{4,68},{5,69},{6,70},{7,71},{8,72},{9,... | collective-permute-start | bytes 786440 | tf_op jit(solution)/shard_map/ppermute | solution.py:28
  24.4 5.0 %collective-permute-start.5 = (f32[64,512]{1,0:T(8,128)S(1)}, f32[64,512]{1,0:T(8,128)S(1)}, u32[]{:S(2)}, u32[]{:S(2)}) collective-permute-start(f32[64,512]{1,0:T(8,128)S(1)} %bitcast.106), channel_id=1, source_target_pairs={{0,16},{1,17},{2,18},{3,19},{4,20},{5,21},{6,22},{7,23},{8,24},{9,... | collective-permute-start | bytes 393224 | tf_op jit(solution)/shard_map/ppermute | solution.py:28
  25.0 6.3 %collective-permute-start.6 = (f32[64,512]{1,0:T(8,128)S(1)}, f32[64,512]{1,0:T(8,128)S(1)}, u32[]{:S(2)}, u32[]{:S(2)}) collective-permute-start(f32[64,512]{1,0:T(8,128)S(1)} %bitcast.107), channel_id=1, source_target_pairs={{0,48},{1,49},{2,50},{3,51},{4,52},{5,53},{6,54},{7,55},{8,56},{9,... | collective-permute-start | bytes 393224 | tf_op jit(solution)/shard_map/ppermute | solution.py:28
  32.3 20.4 %copy-start.6 = (f32[256,512]{1,0:T(8,128)}, f32[256,512]{1,0:T(8,128)S(1)}, u32[]{:S(2)}) copy-start(f32[256,512]{1,0:T(8,128)S(1)} %get-tuple-element.68.refs_0_) | copy-start | bytes 1572868
  32.3 13.2 %collective-permute-start.10 = (f32[256,512]{1,0:T(8,128)S(1)}, f32[256,512]{1,0:T(8,128)S(1)}, u32[]{:S(2)}, u32[]{:S(2)}) collective-permute-start(f32[256,512]{1,0:T(8,128)S(1)} %get-tuple-element.69), channel_id=1, source_target_pairs={{0,72},{1,73},{2,74},{3,75},{4,76},{5,77},{6,78},{7,79},{8,64},{9,... | collective-permute-start | bytes 1572872 | tf_op jit(solution)/shard_map/ppermute | solution.py:28
  36.1 12.2 %collective-permute-start.9 = (f32[256,512]{1,0:T(8,128)S(1)}, f32[256,512]{1,0:T(8,128)S(1)}, u32[]{:S(2)}, u32[]{:S(2)}) collective-permute-start(f32[256,512]{1,0:T(8,128)S(1)} %get-tuple-element.68.refs_0_), channel_id=1, source_target_pairs={{0,6},{1,7},{2,4},{3,5},{4,2},{5,3},{6,0},{7,1},{8,14},{9,15},{10,... | collective-permute-start | bytes 1572872 | tf_op jit(solution)/shard_map/ppermute | solution.py:28
  39.1 10.6 %collective-permute-start.8 = (f32[256,512]{1,0:T(8,128)S(1)}, f32[256,512]{1,0:T(8,128)S(1)}, u32[]{:S(2)}, u32[]{:S(2)}) collective-permute-start(f32[256,512]{1,0:T(8,128)S(1)} %get-tuple-element.68.refs_0_), channel_id=1, source_target_pairs={{0,2},{1,3},{2,0},{3,1},{4,6},{5,7},{6,4},{7,5},{8,10},{9,11},{10,... | collective-permute-start | bytes 1572872 | tf_op jit(solution)/shard_map/ppermute | solution.py:28
  39.2 12.2 %collective-permute-start.15 = (f32[128,512]{1,0:T(8,128)S(1)}, f32[128,512]{1,0:T(8,128)S(1)}, u32[]{:S(2)}, u32[]{:S(2)}) collective-permute-start(f32[128,512]{1,0:T(8,128)S(1)} %bitcast.73), channel_id=1, source_target_pairs={{0,48},{1,49},{2,50},{3,51},{4,52},{5,53},{6,54},{7,55},{8,56},{9,... | collective-permute-start | bytes 786440 | tf_op jit(solution)/shard_map/ppermute | solution.py:28
  45.5 6.4 %collective-permute-start.14 = (f32[128,512]{1,0:T(8,128)S(1)}, f32[128,512]{1,0:T(8,128)S(1)}, u32[]{:S(2)}, u32[]{:S(2)}) collective-permute-start(f32[128,512]{1,0:T(8,128)S(1)} %bitcast.74), channel_id=1, source_target_pairs={{0,16},{1,17},{2,18},{3,19},{4,20},{5,21},{6,22},{7,23},{8,24},{9,... | collective-permute-start | bytes 786440 | tf_op jit(solution)/shard_map/ppermute | solution.py:28
  51.2 21.0 %collective-permute-start.11 = (f32[384,512]{1,0:T(8,128)}, f32[384,512]{1,0:T(8,128)S(1)}, u32[]{:S(2)}, u32[]{:S(2)}) collective-permute-start(f32[384,512]{1,0:T(8,128)} %get-tuple-element.132), channel_id=1, source_target_pairs={{0,2},{1,3},{2,0},{3,1},{4,6},{5,7},{6,4},{7,5},{8,10},{9,11},{10,... | collective-permute-start | bytes 2359304 | tf_op jit(solution)/shard_map/ppermute | solution.py:28
  52.6 28.3 %collective-permute-start.12 = (f32[384,512]{1,0:T(8,128)}, f32[384,512]{1,0:T(8,128)S(1)}, u32[]{:S(2)}, u32[]{:S(2)}) collective-permute-start(f32[384,512]{1,0:T(8,128)} %get-tuple-element.131), channel_id=1, source_target_pairs={{0,6},{1,7},{2,4},{3,5},{4,2},{5,3},{6,0},{7,1},{8,14},{9,15},{10,... | collective-permute-start | bytes 2359304 | tf_op jit(solution)/shard_map/ppermute | solution.py:28
  56.6 10.8 %collective-permute-start.17 = (f32[192,512]{1,0:T(8,128)}, f32[192,512]{1,0:T(8,128)}, u32[]{:S(2)}, u32[]{:S(2)}) collective-permute-start(f32[192,512]{1,0:T(8,128)} %get-tuple-element.135), channel_id=1, source_target_pairs={{0,48},{1,49},{2,50},{3,51},{4,52},{5,53},{6,54},{7,55},{8,56},{9,... | collective-permute-start | bytes 1179656 | tf_op jit(solution)/shard_map/ppermute | solution.py:28
  58.6 8.9 %collective-permute-start.16 = (f32[192,512]{1,0:T(8,128)}, f32[192,512]{1,0:T(8,128)}, u32[]{:S(2)}, u32[]{:S(2)}) collective-permute-start(f32[192,512]{1,0:T(8,128)} %get-tuple-element.136), channel_id=1, source_target_pairs={{0,16},{1,17},{2,18},{3,19},{4,20},{5,21},{6,22},{7,23},{8,24},{9,... | collective-permute-start | bytes 1179656 | tf_op jit(solution)/shard_map/ppermute | solution.py:28
  60.6 20.3 %copy-start.15 = (s32[3]{0:T(128)S(1)}, s32[3]{0:T(128)}, u32[]{:S(2)}) copy-start(s32[3]{0:T(128)} %constant.163.clone) | copy-start | bytes 40
  68.5 6.3 %collective-permute-start.21 = (f32[64,512]{1,0:T(8,128)S(1)}, f32[64,512]{1,0:T(8,128)S(1)}, u32[]{:S(2)}, u32[]{:S(2)}) collective-permute-start(f32[64,512]{1,0:T(8,128)S(1)} %bitcast.108), channel_id=1, source_target_pairs={{0,48},{1,49},{2,50},{3,51},{4,52},{5,53},{6,54},{7,55},{8,56},{9,... | collective-permute-start | bytes 393224 | tf_op jit(solution)/shard_map/ppermute | solution.py:28
  70.6 5.0 %collective-permute-start.20 = (f32[64,512]{1,0:T(8,128)S(1)}, f32[64,512]{1,0:T(8,128)S(1)}, u32[]{:S(2)}, u32[]{:S(2)}) collective-permute-start(f32[64,512]{1,0:T(8,128)S(1)} %bitcast.109), channel_id=1, source_target_pairs={{0,16},{1,17},{2,18},{3,19},{4,20},{5,21},{6,22},{7,23},{8,24},{9,... | collective-permute-start | bytes 393224 | tf_op jit(solution)/shard_map/ppermute | solution.py:28
  77.3 15.6 %collective-permute-start.23 = (f32[256,512]{1,0:T(8,128)S(1)}, f32[256,512]{1,0:T(8,128)S(1)}, u32[]{:S(2)}, u32[]{:S(2)}) collective-permute-start(f32[256,512]{1,0:T(8,128)S(1)} %get-tuple-element.87.refs_0_), channel_id=1, source_target_pairs={{0,6},{1,7},{2,4},{3,5},{4,2},{5,3},{6,0},{7,1},{8,14},{9,15},{10,... | collective-permute-start | bytes 1572872 | tf_op jit(solution)/shard_map/ppermute | solution.py:28
  77.6 15.3 %collective-permute-start.22 = (f32[256,512]{1,0:T(8,128)S(1)}, f32[256,512]{1,0:T(8,128)S(1)}, u32[]{:S(2)}, u32[]{:S(2)}) collective-permute-start(f32[256,512]{1,0:T(8,128)S(1)} %get-tuple-element.87.refs_0_), channel_id=1, source_target_pairs={{0,2},{1,3},{2,0},{3,1},{4,6},{5,7},{6,4},{7,5},{8,10},{9,11},{10,... | collective-permute-start | bytes 1572872 | tf_op jit(solution)/shard_map/ppermute | solution.py:28
  78.0 14.9 %collective-permute-start.24 = (f32[256,512]{1,0:T(8,128)S(1)}, f32[256,512]{1,0:T(8,128)S(1)}, u32[]{:S(2)}, u32[]{:S(2)}) collective-permute-start(f32[256,512]{1,0:T(8,128)S(1)} %get-tuple-element.88), channel_id=1, source_target_pairs={{0,72},{1,73},{2,74},{3,75},{4,76},{5,77},{6,78},{7,79},{8,64},{9,... | collective-permute-start | bytes 1572872 | tf_op jit(solution)/shard_map/ppermute | solution.py:28
  81.7 13.0 %collective-permute-start.18 = (f32[128,512]{1,0:T(8,128)}, f32[128,512]{1,0:T(8,128)}, u32[]{:S(2)}, u32[]{:S(2)}) collective-permute-start(f32[128,512]{1,0:T(8,128)} %slice_bitcast_fusion.5), channel_id=1, source_target_pairs={{0,2},{1,3},{2,0},{3,1},{4,6},{5,7},{6,4},{7,5},{8,10},{9,11},{10,... | collective-permute-start | bytes 786440 | tf_op jit(solution)/shard_map/ppermute | solution.py:28
  84.2 10.5 %collective-permute-start.19 = (f32[128,512]{1,0:T(8,128)}, f32[128,512]{1,0:T(8,128)}, u32[]{:S(2)}, u32[]{:S(2)}) collective-permute-start(f32[128,512]{1,0:T(8,128)} %slice_bitcast_fusion.4), channel_id=1, source_target_pairs={{0,6},{1,7},{2,4},{3,5},{4,2},{5,3},{6,0},{7,1},{8,14},{9,15},{10,... | collective-permute-start | bytes 786440 | tf_op jit(solution)/shard_map/ppermute | solution.py:28
  94.4 18.9 %collective-permute-start.31 = (f32[384,512]{1,0:T(8,128)}, f32[384,512]{1,0:T(8,128)S(1)}, u32[]{:S(2)}, u32[]{:S(2)}) collective-permute-start(f32[384,512]{1,0:T(8,128)} %get-tuple-element.129), channel_id=1, source_target_pairs={{0,6},{1,7},{2,4},{3,5},{4,2},{5,3},{6,0},{7,1},{8,14},{9,15},{10,... | collective-permute-start | bytes 2359304 | tf_op jit(solution)/shard_map/ppermute | solution.py:28
  94.7 18.6 %collective-permute-start.30 = (f32[384,512]{1,0:T(8,128)}, f32[384,512]{1,0:T(8,128)S(1)}, u32[]{:S(2)}, u32[]{:S(2)}) collective-permute-start(f32[384,512]{1,0:T(8,128)} %get-tuple-element.130), channel_id=1, source_target_pairs={{0,2},{1,3},{2,0},{3,1},{4,6},{5,7},{6,4},{7,5},{8,10},{9,11},{10,... | collective-permute-start | bytes 2359304 | tf_op jit(solution)/shard_map/ppermute | solution.py:28
  99.6 2.0 %collective-permute-start.25 = (f32[256,512]{1,0:T(8,128)S(1)}, f32[256,512]{1,0:T(8,128)S(1)}, u32[]{:S(2)}, u32[]{:S(2)}) collective-permute-start(f32[256,512]{1,0:T(8,128)S(1)} %get-tuple-element.98), channel_id=1, source_target_pairs={{0,1},{1,0},{2,3},{3,2},{4,5},{5,4},{6,7},{7,6},{8,9},{9,8},{10,11... | collective-permute-start | bytes 1572872 | tf_op jit(solution)/shard_map/ppermute | solution.py:28
  102.2 10.3 %collective-permute-start.26 = (f32[64,512]{1,0:T(8,128)S(1)}, f32[64,512]{1,0:T(8,128)S(1)}, u32[]{:S(2)}, u32[]{:S(2)}) collective-permute-start(f32[64,512]{1,0:T(8,128)S(1)} %get-tuple-element.100), channel_id=1, source_target_pairs={{0,16},{1,17},{2,18},{3,19},{4,20},{5,21},{6,22},{7,23},{8,24},{9,... | collective-permute-start | bytes 393224 | tf_op jit(solution)/shard_map/ppermute | solution.py:28
  103.7 8.8 %collective-permute-start.27 = (f32[64,512]{1,0:T(8,128)S(1)}, f32[64,512]{1,0:T(8,128)S(1)}, u32[]{:S(2)}, u32[]{:S(2)}) collective-permute-start(f32[64,512]{1,0:T(8,128)S(1)} %get-tuple-element.101), channel_id=1, source_target_pairs={{0,48},{1,49},{2,50},{3,51},{4,52},{5,53},{6,54},{7,55},{8,56},{9,... | collective-permute-start | bytes 393224 | tf_op jit(solution)/shard_map/ppermute | solution.py:28
  113.3 12.1 %collective-permute-start.35 = (f32[128,512]{1,0:T(8,128)S(1)}, f32[128,512]{1,0:T(8,128)S(1)}, u32[]{:S(2)}, u32[]{:S(2)}) collective-permute-start(f32[128,512]{1,0:T(8,128)S(1)} %slice_bitcast_fusion.1), channel_id=1, source_target_pairs={{0,2},{1,3},{2,0},{3,1},{4,6},{5,7},{6,4},{7,5},{8,10},{9,11},{10,... | collective-permute-start | bytes 786440 | tf_op jit(solution)/shard_map/ppermute | solution.py:28
  115.4 10.0 %collective-permute-start.36 = (f32[128,512]{1,0:T(8,128)S(1)}, f32[128,512]{1,0:T(8,128)S(1)}, u32[]{:S(2)}, u32[]{:S(2)}) collective-permute-start(f32[128,512]{1,0:T(8,128)S(1)} %slice_bitcast_fusion), channel_id=1, source_target_pairs={{0,6},{1,7},{2,4},{3,5},{4,2},{5,3},{6,0},{7,1},{8,14},{9,15},{10,... | collective-permute-start | bytes 786440 | tf_op jit(solution)/shard_map/ppermute | solution.py:28
  118.5 11.3 %collective-permute-start.28 = (f32[192,512]{1,0:T(8,128)S(1)}, f32[192,512]{1,0:T(8,128)S(1)}, u32[]{:S(2)}, u32[]{:S(2)}) collective-permute-start(f32[192,512]{1,0:T(8,128)S(1)} %get-tuple-element.105), channel_id=1, source_target_pairs={{0,16},{1,17},{2,18},{3,19},{4,20},{5,21},{6,22},{7,23},{8,24},{9,... | collective-permute-start | bytes 1179656 | tf_op jit(solution)/shard_map/ppermute | solution.py:28
  118.7 11.1 %collective-permute-start.29 = (f32[192,512]{1,0:T(8,128)S(1)}, f32[192,512]{1,0:T(8,128)S(1)}, u32[]{:S(2)}, u32[]{:S(2)}) collective-permute-start(f32[192,512]{1,0:T(8,128)S(1)} %get-tuple-element.106), channel_id=1, source_target_pairs={{0,48},{1,49},{2,50},{3,51},{4,52},{5,53},{6,54},{7,55},{8,56},{9,... | collective-permute-start | bytes 1179656 | tf_op jit(solution)/shard_map/ppermute | solution.py:28
  128.0 4.3 %collective-permute-start.37 = (f32[256,512]{1,0:T(8,128)S(1)}, f32[256,512]{1,0:T(8,128)S(1)}, u32[]{:S(2)}, u32[]{:S(2)}) collective-permute-start(f32[256,512]{1,0:T(8,128)S(1)} %get-tuple-element.118), channel_id=1, source_target_pairs={{0,1},{1,0},{2,3},{3,2},{4,5},{5,4},{6,7},{7,6},{8,9},{9,8},{10,11... | collective-permute-start | bytes 1572872 | tf_op jit(solution)/shard_map/ppermute | solution.py:28
  130.4 8.6 %collective-permute-start.32 = (f32[128,512]{1,0:T(8,128)S(1)}, f32[128,512]{1,0:T(8,128)S(1)}, u32[]{:S(2)}, u32[]{:S(2)}) collective-permute-start(f32[128,512]{1,0:T(8,128)S(1)} %get-tuple-element.111), channel_id=1, source_target_pairs={{0,16},{1,17},{2,18},{3,19},{4,20},{5,21},{6,22},{7,23},{8,24},{9,... | collective-permute-start | bytes 786440 | tf_op jit(solution)/shard_map/ppermute | solution.py:28
  131.1 10.3 %collective-permute-start.33 = (f32[128,512]{1,0:T(8,128)S(1)}, f32[128,512]{1,0:T(8,128)S(1)}, u32[]{:S(2)}, u32[]{:S(2)}) collective-permute-start(f32[128,512]{1,0:T(8,128)S(1)} %get-tuple-element.112), channel_id=1, source_target_pairs={{0,48},{1,49},{2,50},{3,51},{4,52},{5,53},{6,54},{7,55},{8,56},{9,... | collective-permute-start | bytes 786440 | tf_op jit(solution)/shard_map/ppermute | solution.py:28
  132.3 9.0 %collective-permute-start.34 = (f32[128,512]{1,0:T(8,128)S(1)}, f32[128,512]{1,0:T(8,128)S(1)}, u32[]{:S(2)}, u32[]{:S(2)}) collective-permute-start(f32[128,512]{1,0:T(8,128)S(1)} %get-tuple-element.113), channel_id=1, source_target_pairs={{0,64},{1,65},{2,66},{3,67},{4,68},{5,69},{6,70},{7,71},{8,72},{9,... | collective-permute-start | bytes 786440 | tf_op jit(solution)/shard_map/ppermute | solution.py:28
  133.0 9.0 %collective-permute-start.38 = (f32[64,512]{1,0:T(8,128)S(1)}, f32[64,512]{1,0:T(8,128)S(1)}, u32[]{:S(2)}, u32[]{:S(2)}) collective-permute-start(f32[64,512]{1,0:T(8,128)S(1)} %get-tuple-element.120), channel_id=1, source_target_pairs={{0,16},{1,17},{2,18},{3,19},{4,20},{5,21},{6,22},{7,23},{8,24},{9,... | collective-permute-start | bytes 393224 | tf_op jit(solution)/shard_map/ppermute | solution.py:28
  134.0 8.8 %collective-permute-start.39 = (f32[64,512]{1,0:T(8,128)S(1)}, f32[64,512]{1,0:T(8,128)S(1)}, u32[]{:S(2)}, u32[]{:S(2)}) collective-permute-start(f32[64,512]{1,0:T(8,128)S(1)} %get-tuple-element.121), channel_id=1, source_target_pairs={{0,48},{1,49},{2,50},{3,51},{4,52},{5,53},{6,54},{7,55},{8,56},{9,... | collective-permute-start | bytes 393224 | tf_op jit(solution)/shard_map/ppermute | solution.py:28
  143.5 9.7 %collective-permute-start.40 = (f32[192,512]{1,0:T(8,128)S(1)}, f32[192,512]{1,0:T(8,128)S(1)}, u32[]{:S(2)}, u32[]{:S(2)}) collective-permute-start(f32[192,512]{1,0:T(8,128)S(1)} %get-tuple-element.124), channel_id=1, source_target_pairs={{0,16},{1,17},{2,18},{3,19},{4,20},{5,21},{6,22},{7,23},{8,24},{9,... | collective-permute-start | bytes 1179656 | tf_op jit(solution)/shard_map/ppermute | solution.py:28
  143.6 10.9 %collective-permute-start.41 = (f32[192,512]{1,0:T(8,128)S(1)}, f32[192,512]{1,0:T(8,128)S(1)}, u32[]{:S(2)}, u32[]{:S(2)}) collective-permute-start(f32[192,512]{1,0:T(8,128)S(1)} %get-tuple-element.125), channel_id=1, source_target_pairs={{0,48},{1,49},{2,50},{3,51},{4,52},{5,53},{6,54},{7,55},{8,56},{9,... | collective-permute-start | bytes 1179656 | tf_op jit(solution)/shard_map/ppermute | solution.py:28
  155.2 6.5 %collective-permute-start.42 = (f32[128,512]{1,0:T(8,128)S(1)}, f32[128,512]{1,0:T(8,128)S(1)}, u32[]{:S(2)}, u32[]{:S(2)}) collective-permute-start(f32[128,512]{1,0:T(8,128)S(1)} %get-tuple-element.126), channel_id=1, source_target_pairs={{0,16},{1,17},{2,18},{3,19},{4,20},{5,21},{6,22},{7,23},{8,24},{9,... | collective-permute-start | bytes 786440 | tf_op jit(solution)/shard_map/ppermute | solution.py:28
  156.1 7.6 %collective-permute-start.43 = (f32[128,512]{1,0:T(8,128)S(1)}, f32[128,512]{1,0:T(8,128)S(1)}, u32[]{:S(2)}, u32[]{:S(2)}) collective-permute-start(f32[128,512]{1,0:T(8,128)S(1)} %get-tuple-element.127), channel_id=1, source_target_pairs={{0,48},{1,49},{2,50},{3,51},{4,52},{5,53},{6,54},{7,55},{8,56},{9,... | collective-permute-start | bytes 786440 | tf_op jit(solution)/shard_map/ppermute | solution.py:28
  158.4 6.4 %collective-permute-start.44 = (f32[128,512]{1,0:T(8,128)S(1)}, f32[128,512]{1,0:T(8,128)S(1)}, u32[]{:S(2)}, u32[]{:S(2)}) collective-permute-start(f32[128,512]{1,0:T(8,128)S(1)} %get-tuple-element.128), channel_id=1, source_target_pairs={{0,64},{1,65},{2,66},{3,67},{4,68},{5,69},{6,70},{7,71},{8,72},{9,... | collective-permute-start | bytes 786440 | tf_op jit(solution)/shard_map/ppermute | solution.py:28
  (13 other events, 101.5 us)

commit v8 on v7

--- a/solution.py
+++ b/solution.py
@@ -10,7 +10,7 @@
 
 TILE = 128
 SLOTS = 4
-CHUNKS = (64, 64)
+CHUNKS = (80, 48)
 BRIEF = pl.CostEstimate(flops=1, bytes_accessed=1, transcendentals=0)
 
 PLACES = [

time: 167 us -> 174 us (1.042)
  waiting for transfers between devices: 53.2 us -> 63.9 us
  starting transfers between devices: 56.7 us -> 50.1 us
  local copies, waits for them, and re-layouts: 8.75 us -> 11.9 us
    ppermute x45, waiting for transfers between devices: 53.2 us -> 63.9 us  [send(): lax.ppermute(a, ('row', 'col'), [(i, index[to(*p)]) for p, i in index.ite...]
    ppermute x45, starting transfers between devices: 56.7 us -> 50.1 us  [send(): lax.ppermute(a, ('row', 'col'), [(i, index[to(*p)]) for p, i in index.ite...]
    unnamed x32 -> x28, local copies, waits for them, and re-layouts: 3.91 us -> 7.53 us
  transfers between devices with their start and end apart: 45 -> 45, of which waited for: 22 -> 25; matrix products, arithmetic and copies ran while one was open for 8% -> 7% of each run, Pallas kernels for 22% -> 19%
where the time goes in v8:
time: 174 us; the launch traced here: 173 us
  waiting for transfers between devices  63.9 us (37%)
  starting transfers between devices  50.1 us (29%)
  Pallas kernels  38.4 us (22%)
  local copies, waits for them, and re-layouts  11.9 us (7%)
  other arithmetic  8.32 us (5%)
    ppermute x45, waiting for transfers between devices, send(): lax.ppermute(a, ('row', 'col'), [(i, index[to(*p)]) for p, i in index.ite...  63.9 us
    ppermute x45, starting transfers between devices, send(): lax.ppermute(a, ('row', 'col'), [(i, index[to(*p)]) for p, i in index.ite...  50.1 us
    pallas_call x6, Pallas kernels, products(): pl.pallas_call(functools.partial(product_kernel, blocks, len(arrays), not...  30.4 us
    pallas_call x10, Pallas kernels, small_kernel(): pl.pallas_call(kernel, in_specs=[pl.BlockSpec(memory_space=pltpu.SMEM)] +...  7.97 us
    unnamed x28, local copies, waits for them, and re-layouts  7.53 us
  transfers between devices with their start and end apart: 45, of which 25 were waited for; matrix products, arithmetic and copies ran while one was open for 7% of the time, Pallas kernels for 19%

profile of v8, /device:TPU:0, one launch (start us, length us, event | category | flops | bytes accessed | tf_op | source)
XLA Modules:
  0.0 173.2 jit_solution(8703524269937167676)
XLA Ops:
  1.0 2.9 %collective-permute-start.2 = (f32[160,512]{1,0:T(8,128)S(1)}, f32[160,512]{1,0:T(8,128)S(1)}, u32[]{:S(2)}, u32[]{:S(2)}) collective-permute-start(f32[160,512]{1,0:T(8,128)S(1)} %bitcast.70), channel_id=1, source_target_pairs={{0,48},{1,49},{2,50},{3,51},{4,52},{5,53},{6,54},{7,55},{8,56},{9,... | collective-permute-start | bytes 983048 | tf_op jit(solution)/shard_map/ppermute | solution.py:28
  4.1 1.9 %collective-permute-start = (f32[160,512]{1,0:T(8,128)S(1)}, f32[160,512]{1,0:T(8,128)S(1)}, u32[]{:S(2)}, u32[]{:S(2)}) collective-permute-start(f32[160,512]{1,0:T(8,128)S(1)} %bitcast.72), channel_id=1, source_target_pairs={{0,64},{1,65},{2,66},{3,67},{4,68},{5,69},{6,70},{7,71},{8,72},{9,... | collective-permute-start | bytes 983048 | tf_op jit(solution)/shard_map/ppermute | solution.py:28
  6.1 6.3 %collective-permute-done.2.refs_3_ = f32[160,512]{1,0:T(8,128)S(1)} collective-permute-done((f32[160,512]{1,0:T(8,128)S(1)}, f32[160,512]{1,0:T(8,128)S(1)}, u32[]{:S(2)}, u32[]{:S(2)}) %collective-permute-start.2) | collective-permute-done | bytes 327712 | tf_op jit(solution)/shard_map/ppermute | solution.py:28
  14.8 1.4 collective-permute-start.4
  20.7 1.8 %collective-permute-start.7 = (f32[96,512]{1,0:T(8,128)S(1)}, f32[96,512]{1,0:T(8,128)S(1)}, u32[]{:S(2)}, u32[]{:S(2)}) collective-permute-start(f32[96,512]{1,0:T(8,128)S(1)} %bitcast.78), channel_id=1, source_target_pairs={{0,64},{1,65},{2,66},{3,67},{4,68},{5,69},{6,70},{7,71},{8,72},{9,... | collective-permute-start | bytes 589832 | tf_op jit(solution)/shard_map/ppermute | solution.py:28
  22.6 6.0 %collective-permute-done.4.refs_5_ = f32[240,512]{1,0:T(8,128)S(1)} collective-permute-done((f32[240,512]{1,0:T(8,128)S(1)}, f32[240,512]{1,0:T(8,128)S(1)}, u32[]{:S(2)}, u32[]{:S(2)}) %collective-permute-start.4) | collective-permute-done | bytes 491552 | tf_op jit(solution)/shard_map/ppermute | solution.py:28
  29.2 1.4 collective-permute-start.6
  30.8 3.2 %collective-permute-done.5.refs_6_ = f32[80,512]{1,0:T(8,128)S(1)} collective-permute-done((f32[80,512]{1,0:T(8,128)S(1)}, f32[80,512]{1,0:T(8,128)S(1)}, u32[]{:S(2)}, u32[]{:S(2)}) %collective-permute-start.5) | collective-permute-done | bytes 163872 | tf_op jit(solution)/shard_map/ppermute | solution.py:28
  34.0 1.8 %collective-permute-done.6.refs_7_ = f32[80,512]{1,0:T(8,128)S(1)} collective-permute-done((f32[80,512]{1,0:T(8,128)S(1)}, f32[80,512]{1,0:T(8,128)S(1)}, u32[]{:S(2)}, u32[]{:S(2)}) %collective-permute-start.6) | collective-permute-done | bytes 163872 | tf_op jit(solution)/shard_map/ppermute | solution.py:28
  36.8 4.0 %collective-permute-start.10 = (f32[320,512]{1,0:T(8,128)S(1)}, f32[320,512]{1,0:T(8,128)S(1)}, u32[]{:S(2)}, u32[]{:S(2)}) collective-permute-start(f32[320,512]{1,0:T(8,128)S(1)} %get-tuple-element.69), channel_id=1, source_target_pairs={{0,72},{1,73},{2,74},{3,75},{4,76},{5,77},{6,78},{7,79},{8,64},{9,... | collective-permute-start | bytes 1966088 | tf_op jit(solution)/shard_map/ppermute | solution.py:28
  40.8 3.0 %collective-permute-start.9 = (f32[320,512]{1,0:T(8,128)S(1)}, f32[320,512]{1,0:T(8,128)S(1)}, u32[]{:S(2)}, u32[]{:S(2)}) collective-permute-start(f32[320,512]{1,0:T(8,128)S(1)} %get-tuple-element.68.refs_0_), channel_id=1, source_target_pairs={{0,6},{1,7},{2,4},{3,5},{4,2},{5,3},{6,0},{7,1},{8,14},{9,15},{10,... | collective-permute-start | bytes 1966088 | tf_op jit(solution)/shard_map/ppermute | solution.py:28
  44.0 9.1 %collective-permute-done.10.refs_3_ = f32[320,512]{1,0:T(8,128)S(1)} collective-permute-done((f32[320,512]{1,0:T(8,128)S(1)}, f32[320,512]{1,0:T(8,128)S(1)}, u32[]{:S(2)}, u32[]{:S(2)}) %collective-permute-start.10) | collective-permute-done | bytes 655392 | tf_op jit(solution)/shard_map/ppermute | solution.py:28
  53.1 2.7 %collective-permute-done.9.refs_2_ = f32[320,512]{1,0:T(8,128)S(1)} collective-permute-done((f32[320,512]{1,0:T(8,128)S(1)}, f32[320,512]{1,0:T(8,128)S(1)}, u32[]{:S(2)}, u32[]{:S(2)}) %collective-permute-start.9) | collective-permute-done | bytes 655392 | tf_op jit(solution)/shard_map/ppermute | solution.py:28
  55.8 1.5 collective-permute-done.8.refs_1_
  57.4 1.5 pad_maximum_fusion
  58.9 1.5 collective-permute-start.12
  60.3 1.7 %collective-permute-start.15 = (f32[96,512]{1,0:T(8,128)S(1)}, f32[96,512]{1,0:T(8,128)S(1)}, u32[]{:S(2)}, u32[]{:S(2)}) collective-permute-start(f32[96,512]{1,0:T(8,128)S(1)} %bitcast.79), channel_id=1, source_target_pairs={{0,48},{1,49},{2,50},{3,51},{4,52},{5,53},{6,54},{7,55},{8,56},{9,... | collective-permute-start | bytes 589832 | tf_op jit(solution)/shard_map/ppermute | solution.py:28
  62.3 4.9 %collective-permute-done.15.refs_3_ = f32[96,512]{1,0:T(8,128)S(1)} collective-permute-done((f32[96,512]{1,0:T(8,128)S(1)}, f32[96,512]{1,0:T(8,128)S(1)}, u32[]{:S(2)}, u32[]{:S(2)}) %collective-permute-start.15) | collective-permute-done | bytes 196640 | tf_op jit(solution)/shard_map/ppermute | solution.py:28
  69.3 1.5 collective-permute-start.17
  73.7 7.4 %products.6 = (f32[320,512]{1,0:T(8,128)S(1)}, f32[320,512]{1,0:T(8,128)S(1)}) custom-call(s32[4]{0:T(128)S(1)} %multiply_add_fusion.1.at_ref, f32[320,512]{1,0:T(8,128)S(1)} %copy-done.5, f32[320,512]{1,0:T(8,128)S(1)} %copy-done.1, f32[320,512]{1,0:T(8,128)S(1)} %collective-permute-done.9.refs_2_, f32[320,512]{1,0:T(8,128)S(1)} %collective-permute-done.10.refs_3_, ...), custom_call_target="tpu_custom_call" | custom-call | flops 1 | bytes 1 | tf_op jit(solution)/shard_map/products/pallas_call | solution.py:90
  82.9 1.8 %collective-permute-start.21 = (f32[48,512]{1,0:T(8,128)S(1)}, f32[48,512]{1,0:T(8,128)S(1)}, u32[]{:S(2)}, u32[]{:S(2)}) collective-permute-start(f32[48,512]{1,0:T(8,128)S(1)} %bitcast.109), channel_id=1, source_target_pairs={{0,48},{1,49},{2,50},{3,51},{4,52},{5,53},{6,54},{7,55},{8,56},{9,... | collective-permute-start | bytes 294920 | tf_op jit(solution)/shard_map/ppermute | solution.py:28
  84.8 1.5 collective-permute-start.20
  87.4 1.4 collective-permute-done.21.refs_7_
  92.2 1.6 pick.3
  93.9 1.8 %collective-permute-start.23 = (f32[192,512]{1,0:T(8,128)S(1)}, f32[192,512]{1,0:T(8,128)S(1)}, u32[]{:S(2)}, u32[]{:S(2)}) collective-permute-start(f32[192,512]{1,0:T(8,128)S(1)} %get-tuple-element.87.refs_0_), channel_id=1, source_target_pairs={{0,6},{1,7},{2,4},{3,5},{4,2},{5,3},{6,0},{7,1},{8,14},{9,15},{10,... | collective-permute-start | bytes 1179656 | tf_op jit(solution)/shard_map/ppermute | solution.py:28
  95.7 1.5 collective-permute-start.22
  98.2 1.6 collective-permute-start.19
  101.0 6.4 %products.7 = (f32[320,512]{1,0:T(8,128)S(1)}, f32[320,512]{1,0:T(8,128)S(1)}) custom-call(s32[3]{0:T(128)S(1)} %multiply_add_fusion.at_ref, f32[480,512]{1,0:T(8,128)S(1)} %collective-permute-done.11.refs_8_.refs_0_, f32[480,512]{1,0:T(8,128)} %collective-permute-done.12.refs_1_, f32[8192,512]{1,0:T(8,128)} %bitcast.88, ...), custom_call_target="tpu_custom_call" | custom-call | flops 1 | bytes 1 | tf_op jit(solution)/shard_map/products/pallas_call | solution.py:90
  107.6 2.7 %products.8 = (f32[320,512]{1,0:T(8,128)S(1)}, f32[320,512]{1,0:T(8,128)S(1)}) custom-call(s32[1]{0:T(128)S(6)} %add.113.at_ref, f32[160,512]{1,0:T(8,128)S(1)} %collective-permute-done.18.refs_0_, f32[160,512]{1,0:T(8,128)S(1)} %collective-permute-done.19.refs_1_, f32[8192,512]{1,0:T(8,128)} %bitcast.89, ...), custom_call_target="tpu_custom_call" | custom-call | flops 1 | bytes 1 | tf_op jit(solution)/shard_map/products/pallas_call | solution.py:90
  110.4 1.8 %collective-permute-start.31 = (f32[288,512]{1,0:T(8,128)S(1)}, f32[288,512]{1,0:T(8,128)S(1)}, u32[]{:S(2)}, u32[]{:S(2)}) collective-permute-start(f32[288,512]{1,0:T(8,128)S(1)} %get-tuple-element.131), channel_id=1, source_target_pairs={{0,6},{1,7},{2,4},{3,5},{4,2},{5,3},{6,0},{7,1},{8,14},{9,15},{10,... | collective-permute-start | bytes 1769480 | tf_op jit(solution)/shard_map/ppermute | solution.py:28
  113.2 1.5 collective-permute-start.26
  114.7 1.5 collective-permute-start.27
  116.2 6.3 %products.9 = (f32[192,512]{1,0:T(8,128)S(1)}, f32[192,512]{1,0:T(8,128)S(1)}) custom-call(s32[4]{0:T(128)S(1)} %multiply_add_fusion.1.at_ref, f32[192,512]{1,0:T(8,128)S(1)} %get-tuple-element.87.refs_0_, f32[192,512]{1,0:T(8,128)S(1)} %collective-permute-done.22.refs_1_, f32[192,512]{1,0:T(8,128)S(1)} %collective-permute-done.23.refs_2_, ...), custom_call_target="tpu_custom_call" | custom-call | flops 1 | bytes 1 | tf_op jit(solution)/shard_map/products/pallas_call | solution.py:90
  123.3 4.1 %collective-permute-done.31.refs_1_ = f32[288,512]{1,0:T(8,128)S(1)} collective-permute-done((f32[288,512]{1,0:T(8,128)S(1)}, f32[288,512]{1,0:T(8,128)S(1)}, u32[]{:S(2)}, u32[]{:S(2)}) %collective-permute-start.31) | collective-permute-done | bytes 589856 | tf_op jit(solution)/shard_map/ppermute | solution.py:28
  128.0 1.6 collective-permute-start.29
  129.6 1.8 %collective-permute-start.36 = (f32[96,512]{1,0:T(8,128)S(1)}, f32[96,512]{1,0:T(8,128)S(1)}, u32[]{:S(2)}, u32[]{:S(2)}) collective-permute-start(f32[96,512]{1,0:T(8,128)S(1)} %slice_bitcast_fusion.4), channel_id=1, source_target_pairs={{0,6},{1,7},{2,4},{3,5},{4,2},{5,3},{6,0},{7,1},{8,14},{9,15},{10,... | collective-permute-start | bytes 589832 | tf_op jit(solution)/shard_map/ppermute | solution.py:28
  131.5 5.3 %products.10 = (f32[192,512]{1,0:T(8,128)S(1)}, f32[192,512]{1,0:T(8,128)S(1)}) custom-call(s32[3]{0:T(128)S(1)} %multiply_add_fusion.at_ref, f32[288,512]{1,0:T(8,128)S(1)} %collective-permute-done.30.refs_0_, f32[288,512]{1,0:T(8,128)S(1)} %collective-permute-done.31.refs_1_, f32[8192,512]{1,0:T(8,128)} %bitcast.91, ...), custom_call_target="tpu_custom_call" | custom-call | flops 1 | bytes 1 | tf_op jit(solution)/shard_map/products/pallas_call | solution.py:90
  136.8 2.3 %products.11 = (f32[192,512]{1,0:T(8,128)S(1)}, f32[192,512]{1,0:T(8,128)S(1)}) custom-call(s32[1]{0:T(128)S(6)} %add.113.at_ref, f32[96,512]{1,0:T(8,128)S(1)} %collective-permute-done.35.refs_0_, f32[96,512]{1,0:T(8,128)S(1)} %collective-permute-done.36.refs_1_, f32[8192,512]{1,0:T(8,128)} %bitcast.92, ...), custom_call_target="tpu_custom_call" | custom-call | flops 1 | bytes 1 | tf_op jit(solution)/shard_map/products/pallas_call | solution.py:90
  139.3 2.4 %collective-permute-done.29.refs_2_ = f32[240,512]{1,0:T(8,128)S(1)} collective-permute-done((f32[240,512]{1,0:T(8,128)S(1)}, f32[240,512]{1,0:T(8,128)S(1)}, u32[]{:S(2)}, u32[]{:S(2)}) %collective-permute-start.29) | collective-permute-done | bytes 491552 | tf_op jit(solution)/shard_map/ppermute | solution.py:28
  142.6 1.5 collective-permute-start.33
  146.1 1.8 %collective-permute-start.39 = (f32[48,512]{1,0:T(8,128)S(1)}, f32[48,512]{1,0:T(8,128)S(1)}, u32[]{:S(2)}, u32[]{:S(2)}) collective-permute-start(f32[48,512]{1,0:T(8,128)S(1)} %get-tuple-element.121), channel_id=1, source_target_pairs={{0,48},{1,49},{2,50},{3,51},{4,52},{5,53},{6,54},{7,55},{8,56},{9,... | collective-permute-start | bytes 294920 | tf_op jit(solution)/shard_map/ppermute | solution.py:28
  147.8 3.6 %collective-permute-done.32.refs_1_ = f32[160,512]{1,0:T(8,128)S(1)} collective-permute-done((f32[160,512]{1,0:T(8,128)S(1)}, f32[160,512]{1,0:T(8,128)S(1)}, u32[]{:S(2)}, u32[]{:S(2)}) %collective-permute-start.32) | collective-permute-done | bytes 327712 | tf_op jit(solution)/shard_map/ppermute | solution.py:28
  151.4 1.6 collective-permute-done.33.refs_2_
  155.0 1.7 collective-permute-start.41
  156.7 4.9 %collective-permute-done.40.refs_1_ = f32[144,512]{1,0:T(8,128)S(1)} collective-permute-done((f32[144,512]{1,0:T(8,128)S(1)}, f32[144,512]{1,0:T(8,128)S(1)}, u32[]{:S(2)}, u32[]{:S(2)}) %collective-permute-start.40) | collective-permute-done | bytes 294944 | tf_op jit(solution)/shard_map/ppermute | solution.py:28
  164.4 1.7 collective-permute-start.43
  166.1 3.2 %collective-permute-done.42.refs_1_ = f32[96,512]{1,0:T(8,128)S(1)} collective-permute-done((f32[96,512]{1,0:T(8,128)S(1)}, f32[96,512]{1,0:T(8,128)S(1)}, u32[]{:S(2)}, u32[]{:S(2)}) %collective-permute-start.42) | collective-permute-done | bytes 196640 | tf_op jit(solution)/shard_map/ppermute | solution.py:28
  169.3 1.9 %collective-permute-done.43.refs_2_ = f32[96,512]{1,0:T(8,128)S(1)} collective-permute-done((f32[96,512]{1,0:T(8,128)S(1)}, f32[96,512]{1,0:T(8,128)S(1)}, u32[]{:S(2)}, u32[]{:S(2)}) %collective-permute-start.43) | collective-permute-done | bytes 196640 | tf_op jit(solution)/shard_map/ppermute | solution.py:28
  (125 shorter events, 36.3 us)
Async XLA Ops:
  0.0 71.5 %collective-permute-start.13 = (f32[8192,512]{1,0:T(8,128)}, f32[8192,512]{1,0:T(8,128)}, u32[]{:S(2)}, u32[]{:S(2)}) collective-permute-start(f32[8192,512]{1,0:T(8,128)} %bitcast.86), channel_id=1, source_target_pairs={{0,1},{1,0},{2,3},{3,2},{4,5},{5,4},{6,7},{7,6},{8,9},{9,8},{10,11... | collective-permute-start | bytes 50331656 | tf_op jit(solution)/shard_map/ppermute | solution.py:28
  1.0 11.4 %collective-permute-start.2 = (f32[160,512]{1,0:T(8,128)S(1)}, f32[160,512]{1,0:T(8,128)S(1)}, u32[]{:S(2)}, u32[]{:S(2)}) collective-permute-start(f32[160,512]{1,0:T(8,128)S(1)} %bitcast.70), channel_id=1, source_target_pairs={{0,48},{1,49},{2,50},{3,51},{4,52},{5,53},{6,54},{7,55},{8,56},{9,... | collective-permute-start | bytes 983048 | tf_op jit(solution)/shard_map/ppermute | solution.py:28
  3.9 9.8 %collective-permute-start.1 = (f32[160,512]{1,0:T(8,128)S(1)}, f32[160,512]{1,0:T(8,128)S(1)}, u32[]{:S(2)}, u32[]{:S(2)}) collective-permute-start(f32[160,512]{1,0:T(8,128)S(1)} %bitcast.71), channel_id=1, source_target_pairs={{0,16},{1,17},{2,18},{3,19},{4,20},{5,21},{6,22},{7,23},{8,24},{9,... | collective-permute-start | bytes 983048 | tf_op jit(solution)/shard_map/ppermute | solution.py:28
  4.1 9.8 %collective-permute-start = (f32[160,512]{1,0:T(8,128)S(1)}, f32[160,512]{1,0:T(8,128)S(1)}, u32[]{:S(2)}, u32[]{:S(2)}) collective-permute-start(f32[160,512]{1,0:T(8,128)S(1)} %bitcast.72), channel_id=1, source_target_pairs={{0,64},{1,65},{2,66},{3,67},{4,68},{5,69},{6,70},{7,71},{8,72},{9,... | collective-permute-start | bytes 983048 | tf_op jit(solution)/shard_map/ppermute | solution.py:28
  14.8 13.7 %collective-permute-start.4 = (f32[240,512]{1,0:T(8,128)S(1)}, f32[240,512]{1,0:T(8,128)S(1)}, u32[]{:S(2)}, u32[]{:S(2)}) collective-permute-start(f32[240,512]{1,0:T(8,128)S(1)} %get-tuple-element.133), channel_id=1, source_target_pairs={{0,48},{1,49},{2,50},{3,51},{4,52},{5,53},{6,54},{7,55},{8,56},{9,... | collective-permute-start | bytes 1474568 | tf_op jit(solution)/shard_map/ppermute | solution.py:28
  16.2 12.9 %collective-permute-start.3 = (f32[240,512]{1,0:T(8,128)}, f32[240,512]{1,0:T(8,128)S(1)}, u32[]{:S(2)}, u32[]{:S(2)}) collective-permute-start(f32[240,512]{1,0:T(8,128)} %get-tuple-element.134), channel_id=1, source_target_pairs={{0,16},{1,17},{2,18},{3,19},{4,20},{5,21},{6,22},{7,23},{8,24},{9,... | collective-permute-start | bytes 1474568 | tf_op jit(solution)/shard_map/ppermute | solution.py:28
  18.2 51.1 %copy-start.2 = (f32[2,48,512]{2,1,0:T(8,128)}, f32[2,48,512]{2,1,0:T(8,128)S(1)}, u32[]{:S(2)}) copy-start(f32[2,48,512]{2,1,0:T(8,128)S(1)} %slice.111) | copy-start | bytes 589828
  20.7 10.1 %collective-permute-start.7 = (f32[96,512]{1,0:T(8,128)S(1)}, f32[96,512]{1,0:T(8,128)S(1)}, u32[]{:S(2)}, u32[]{:S(2)}) collective-permute-start(f32[96,512]{1,0:T(8,128)S(1)} %bitcast.78), channel_id=1, source_target_pairs={{0,64},{1,65},{2,66},{3,67},{4,68},{5,69},{6,70},{7,71},{8,72},{9,... | collective-permute-start | bytes 589832 | tf_op jit(solution)/shard_map/ppermute | solution.py:28
  28.6 5.4 %collective-permute-start.5 = (f32[80,512]{1,0:T(8,128)S(1)}, f32[80,512]{1,0:T(8,128)S(1)}, u32[]{:S(2)}, u32[]{:S(2)}) collective-permute-start(f32[80,512]{1,0:T(8,128)S(1)} %bitcast.107), channel_id=1, source_target_pairs={{0,16},{1,17},{2,18},{3,19},{4,20},{5,21},{6,22},{7,23},{8,24},{9,... | collective-permute-start | bytes 491528 | tf_op jit(solution)/shard_map/ppermute | solution.py:28
  29.2 6.6 %collective-permute-start.6 = (f32[80,512]{1,0:T(8,128)S(1)}, f32[80,512]{1,0:T(8,128)S(1)}, u32[]{:S(2)}, u32[]{:S(2)}) collective-permute-start(f32[80,512]{1,0:T(8,128)S(1)} %bitcast.108), channel_id=1, source_target_pairs={{0,48},{1,49},{2,50},{3,51},{4,52},{5,53},{6,54},{7,55},{8,56},{9,... | collective-permute-start | bytes 491528 | tf_op jit(solution)/shard_map/ppermute | solution.py:28
  36.8 32.5 %copy-start.4 = (f32[320,512]{1,0:T(8,128)}, f32[320,512]{1,0:T(8,128)S(1)}, u32[]{:S(2)}) copy-start(f32[320,512]{1,0:T(8,128)S(1)} %get-tuple-element.68.refs_0_) | copy-start | bytes 1966084
  36.8 16.3 %collective-permute-start.10 = (f32[320,512]{1,0:T(8,128)S(1)}, f32[320,512]{1,0:T(8,128)S(1)}, u32[]{:S(2)}, u32[]{:S(2)}) collective-permute-start(f32[320,512]{1,0:T(8,128)S(1)} %get-tuple-element.69), channel_id=1, source_target_pairs={{0,72},{1,73},{2,74},{3,75},{4,76},{5,77},{6,78},{7,79},{8,64},{9,... | collective-permute-start | bytes 1966088 | tf_op jit(solution)/shard_map/ppermute | solution.py:28
  40.8 15.0 %collective-permute-start.9 = (f32[320,512]{1,0:T(8,128)S(1)}, f32[320,512]{1,0:T(8,128)S(1)}, u32[]{:S(2)}, u32[]{:S(2)}) collective-permute-start(f32[320,512]{1,0:T(8,128)S(1)} %get-tuple-element.68.refs_0_), channel_id=1, source_target_pairs={{0,6},{1,7},{2,4},{3,5},{4,2},{5,3},{6,0},{7,1},{8,14},{9,15},{10,... | collective-permute-start | bytes 1966088 | tf_op jit(solution)/shard_map/ppermute | solution.py:28
  43.8 13.5 %collective-permute-start.8 = (f32[320,512]{1,0:T(8,128)S(1)}, f32[320,512]{1,0:T(8,128)S(1)}, u32[]{:S(2)}, u32[]{:S(2)}) collective-permute-start(f32[320,512]{1,0:T(8,128)S(1)} %get-tuple-element.68.refs_0_), channel_id=1, source_target_pairs={{0,2},{1,3},{2,0},{3,1},{4,6},{5,7},{6,4},{7,5},{8,10},{9,11},{10,... | collective-permute-start | bytes 1966088 | tf_op jit(solution)/shard_map/ppermute | solution.py:28
  57.3 14.2 %copy-start = (f32[320,512]{1,0:T(8,128)}, f32[320,512]{1,0:T(8,128)S(1)}, u32[]{:S(2)}) copy-start(f32[320,512]{1,0:T(8,128)S(1)} %collective-permute-done.8.refs_1_) | copy-start | bytes 1966084
  58.9 27.4 %collective-permute-start.12 = (f32[480,512]{1,0:T(8,128)}, f32[480,512]{1,0:T(8,128)}, u32[]{:S(2)}, u32[]{:S(2)}) collective-permute-start(f32[480,512]{1,0:T(8,128)} %get-tuple-element.129), channel_id=1, source_target_pairs={{0,6},{1,7},{2,4},{3,5},{4,2},{5,3},{6,0},{7,1},{8,14},{9,15},{10,... | collective-permute-start | bytes 2949128 | tf_op jit(solution)/shard_map/ppermute | solution.py:28
  60.3 26.0 %collective-permute-start.11 = (f32[480,512]{1,0:T(8,128)}, f32[480,512]{1,0:T(8,128)S(1)}, u32[]{:S(2)}, u32[]{:S(2)}) collective-permute-start(f32[480,512]{1,0:T(8,128)} %get-tuple-element.130), channel_id=1, source_target_pairs={{0,2},{1,3},{2,0},{3,1},{4,6},{5,7},{6,4},{7,5},{8,10},{9,11},{10,... | collective-permute-start | bytes 2949128 | tf_op jit(solution)/shard_map/ppermute | solution.py:28
  60.3 6.9 %collective-permute-start.15 = (f32[96,512]{1,0:T(8,128)S(1)}, f32[96,512]{1,0:T(8,128)S(1)}, u32[]{:S(2)}, u32[]{:S(2)}) collective-permute-start(f32[96,512]{1,0:T(8,128)S(1)} %bitcast.79), channel_id=1, source_target_pairs={{0,48},{1,49},{2,50},{3,51},{4,52},{5,53},{6,54},{7,55},{8,56},{9,... | collective-permute-start | bytes 589832 | tf_op jit(solution)/shard_map/ppermute | solution.py:28
  62.1 5.7 %collective-permute-start.14 = (f32[96,512]{1,0:T(8,128)S(1)}, f32[96,512]{1,0:T(8,128)S(1)}, u32[]{:S(2)}, u32[]{:S(2)}) collective-permute-start(f32[96,512]{1,0:T(8,128)S(1)} %bitcast.80), channel_id=1, source_target_pairs={{0,16},{1,17},{2,18},{3,19},{4,20},{5,21},{6,22},{7,23},{8,24},{9,... | collective-permute-start | bytes 589832 | tf_op jit(solution)/shard_map/ppermute | solution.py:28
  69.3 12.6 %collective-permute-start.17 = (f32[144,512]{1,0:T(8,128)}, f32[144,512]{1,0:T(8,128)S(1)}, u32[]{:S(2)}, u32[]{:S(2)}) collective-permute-start(f32[144,512]{1,0:T(8,128)} %get-tuple-element.135), channel_id=1, source_target_pairs={{0,48},{1,49},{2,50},{3,51},{4,52},{5,53},{6,54},{7,55},{8,56},{9,... | collective-permute-start | bytes 884744 | tf_op jit(solution)/shard_map/ppermute | solution.py:28
  70.8 11.1 %collective-permute-start.16 = (f32[144,512]{1,0:T(8,128)}, f32[144,512]{1,0:T(8,128)}, u32[]{:S(2)}, u32[]{:S(2)}) collective-permute-start(f32[144,512]{1,0:T(8,128)} %get-tuple-element.136), channel_id=1, source_target_pairs={{0,16},{1,17},{2,18},{3,19},{4,20},{5,21},{6,22},{7,23},{8,24},{9,... | collective-permute-start | bytes 884744 | tf_op jit(solution)/shard_map/ppermute | solution.py:28
  82.9 5.9 %collective-permute-start.21 = (f32[48,512]{1,0:T(8,128)S(1)}, f32[48,512]{1,0:T(8,128)S(1)}, u32[]{:S(2)}, u32[]{:S(2)}) collective-permute-start(f32[48,512]{1,0:T(8,128)S(1)} %bitcast.109), channel_id=1, source_target_pairs={{0,48},{1,49},{2,50},{3,51},{4,52},{5,53},{6,54},{7,55},{8,56},{9,... | collective-permute-start | bytes 294920 | tf_op jit(solution)/shard_map/ppermute | solution.py:28
  84.8 4.7 %collective-permute-start.20 = (f32[48,512]{1,0:T(8,128)S(1)}, f32[48,512]{1,0:T(8,128)S(1)}, u32[]{:S(2)}, u32[]{:S(2)}) collective-permute-start(f32[48,512]{1,0:T(8,128)S(1)} %bitcast.110), channel_id=1, source_target_pairs={{0,16},{1,17},{2,18},{3,19},{4,20},{5,21},{6,22},{7,23},{8,24},{9,... | collective-permute-start | bytes 294920 | tf_op jit(solution)/shard_map/ppermute | solution.py:28
  93.9 13.5 %collective-permute-start.23 = (f32[192,512]{1,0:T(8,128)S(1)}, f32[192,512]{1,0:T(8,128)S(1)}, u32[]{:S(2)}, u32[]{:S(2)}) collective-permute-start(f32[192,512]{1,0:T(8,128)S(1)} %get-tuple-element.87.refs_0_), channel_id=1, source_target_pairs={{0,6},{1,7},{2,4},{3,5},{4,2},{5,3},{6,0},{7,1},{8,14},{9,15},{10,... | collective-permute-start | bytes 1179656 | tf_op jit(solution)/shard_map/ppermute | solution.py:28
  95.7 11.7 %collective-permute-start.22 = (f32[192,512]{1,0:T(8,128)S(1)}, f32[192,512]{1,0:T(8,128)S(1)}, u32[]{:S(2)}, u32[]{:S(2)}) collective-permute-start(f32[192,512]{1,0:T(8,128)S(1)} %get-tuple-element.87.refs_0_), channel_id=1, source_target_pairs={{0,2},{1,3},{2,0},{3,1},{4,6},{5,7},{6,4},{7,5},{8,10},{9,11},{10,... | collective-permute-start | bytes 1179656 | tf_op jit(solution)/shard_map/ppermute | solution.py:28
  97.1 10.2 %collective-permute-start.24 = (f32[192,512]{1,0:T(8,128)S(1)}, f32[192,512]{1,0:T(8,128)S(1)}, u32[]{:S(2)}, u32[]{:S(2)}) collective-permute-start(f32[192,512]{1,0:T(8,128)S(1)} %get-tuple-element.88), channel_id=1, source_target_pairs={{0,72},{1,73},{2,74},{3,75},{4,76},{5,77},{6,78},{7,79},{8,64},{9,... | collective-permute-start | bytes 1179656 | tf_op jit(solution)/shard_map/ppermute | solution.py:28
  97.5 10.1 %collective-permute-start.18 = (f32[160,512]{1,0:T(8,128)S(1)}, f32[160,512]{1,0:T(8,128)S(1)}, u32[]{:S(2)}, u32[]{:S(2)}) collective-permute-start(f32[160,512]{1,0:T(8,128)S(1)} %slice_bitcast_fusion.1), channel_id=1, source_target_pairs={{0,2},{1,3},{2,0},{3,1},{4,6},{5,7},{6,4},{7,5},{8,10},{9,11},{10,... | collective-permute-start | bytes 983048 | tf_op jit(solution)/shard_map/ppermute | solution.py:28
  98.2 9.3 %collective-permute-start.19 = (f32[160,512]{1,0:T(8,128)S(1)}, f32[160,512]{1,0:T(8,128)S(1)}, u32[]{:S(2)}, u32[]{:S(2)}) collective-permute-start(f32[160,512]{1,0:T(8,128)S(1)} %slice_bitcast_fusion), channel_id=1, source_target_pairs={{0,6},{1,7},{2,4},{3,5},{4,2},{5,3},{6,0},{7,1},{8,14},{9,15},{10,... | collective-permute-start | bytes 983048 | tf_op jit(solution)/shard_map/ppermute | solution.py:28
  110.4 2.2 %collective-permute-start.25 = (f32[320,512]{1,0:T(8,128)S(1)}, f32[320,512]{1,0:T(8,128)S(1)}, u32[]{:S(2)}, u32[]{:S(2)}) collective-permute-start(f32[320,512]{1,0:T(8,128)S(1)} %get-tuple-element.98), channel_id=1, source_target_pairs={{0,1},{1,0},{2,3},{3,2},{4,5},{5,4},{6,7},{7,6},{8,9},{9,8},{10,11... | collective-permute-start | bytes 1966088 | tf_op jit(solution)/shard_map/ppermute | solution.py:28
  110.4 17.0 %collective-permute-start.31 = (f32[288,512]{1,0:T(8,128)S(1)}, f32[288,512]{1,0:T(8,128)S(1)}, u32[]{:S(2)}, u32[]{:S(2)}) collective-permute-start(f32[288,512]{1,0:T(8,128)S(1)} %get-tuple-element.131), channel_id=1, source_target_pairs={{0,6},{1,7},{2,4},{3,5},{4,2},{5,3},{6,0},{7,1},{8,14},{9,15},{10,... | collective-permute-start | bytes 1769480 | tf_op jit(solution)/shard_map/ppermute | solution.py:28
  112.2 15.4 %collective-permute-start.30 = (f32[288,512]{1,0:T(8,128)S(1)}, f32[288,512]{1,0:T(8,128)S(1)}, u32[]{:S(2)}, u32[]{:S(2)}) collective-permute-start(f32[288,512]{1,0:T(8,128)S(1)} %get-tuple-element.132), channel_id=1, source_target_pairs={{0,2},{1,3},{2,0},{3,1},{4,6},{5,7},{6,4},{7,5},{8,10},{9,11},{10,... | collective-permute-start | bytes 1769480 | tf_op jit(solution)/shard_map/ppermute | solution.py:28
  113.2 9.3 %collective-permute-start.26 = (f32[80,512]{1,0:T(8,128)S(1)}, f32[80,512]{1,0:T(8,128)S(1)}, u32[]{:S(2)}, u32[]{:S(2)}) collective-permute-start(f32[80,512]{1,0:T(8,128)S(1)} %get-tuple-element.100), channel_id=1, source_target_pairs={{0,16},{1,17},{2,18},{3,19},{4,20},{5,21},{6,22},{7,23},{8,24},{9,... | collective-permute-start | bytes 491528 | tf_op jit(solution)/shard_map/ppermute | solution.py:28
  114.7 7.8 %collective-permute-start.27 = (f32[80,512]{1,0:T(8,128)S(1)}, f32[80,512]{1,0:T(8,128)S(1)}, u32[]{:S(2)}, u32[]{:S(2)}) collective-permute-start(f32[80,512]{1,0:T(8,128)S(1)} %get-tuple-element.101), channel_id=1, source_target_pairs={{0,48},{1,49},{2,50},{3,51},{4,52},{5,53},{6,54},{7,55},{8,56},{9,... | collective-permute-start | bytes 491528 | tf_op jit(solution)/shard_map/ppermute | solution.py:28
  123.2 18.4 %collective-permute-start.28 = (f32[240,512]{1,0:T(8,128)S(1)}, f32[240,512]{1,0:T(8,128)S(1)}, u32[]{:S(2)}, u32[]{:S(2)}) collective-permute-start(f32[240,512]{1,0:T(8,128)S(1)} %get-tuple-element.105), channel_id=1, source_target_pairs={{0,16},{1,17},{2,18},{3,19},{4,20},{5,21},{6,22},{7,23},{8,24},{9,... | collective-permute-start | bytes 1474568 | tf_op jit(solution)/shard_map/ppermute | solution.py:28
  127.6 9.1 %collective-permute-start.35 = (f32[96,512]{1,0:T(8,128)S(1)}, f32[96,512]{1,0:T(8,128)S(1)}, u32[]{:S(2)}, u32[]{:S(2)}) collective-permute-start(f32[96,512]{1,0:T(8,128)S(1)} %slice_bitcast_fusion.5), channel_id=1, source_target_pairs={{0,2},{1,3},{2,0},{3,1},{4,6},{5,7},{6,4},{7,5},{8,10},{9,11},{10,... | collective-permute-start | bytes 589832 | tf_op jit(solution)/shard_map/ppermute | solution.py:28
  128.0 13.6 %collective-permute-start.29 = (f32[240,512]{1,0:T(8,128)S(1)}, f32[240,512]{1,0:T(8,128)S(1)}, u32[]{:S(2)}, u32[]{:S(2)}) collective-permute-start(f32[240,512]{1,0:T(8,128)S(1)} %get-tuple-element.106), channel_id=1, source_target_pairs={{0,48},{1,49},{2,50},{3,51},{4,52},{5,53},{6,54},{7,55},{8,56},{9,... | collective-permute-start | bytes 1474568 | tf_op jit(solution)/shard_map/ppermute | solution.py:28
  129.6 7.2 %collective-permute-start.36 = (f32[96,512]{1,0:T(8,128)S(1)}, f32[96,512]{1,0:T(8,128)S(1)}, u32[]{:S(2)}, u32[]{:S(2)}) collective-permute-start(f32[96,512]{1,0:T(8,128)S(1)} %slice_bitcast_fusion.4), channel_id=1, source_target_pairs={{0,6},{1,7},{2,4},{3,5},{4,2},{5,3},{6,0},{7,1},{8,14},{9,15},{10,... | collective-permute-start | bytes 589832 | tf_op jit(solution)/shard_map/ppermute | solution.py:28
  139.2 5.0 %collective-permute-start.37 = (f32[192,512]{1,0:T(8,128)S(1)}, f32[192,512]{1,0:T(8,128)S(1)}, u32[]{:S(2)}, u32[]{:S(2)}) collective-permute-start(f32[192,512]{1,0:T(8,128)S(1)} %get-tuple-element.118), channel_id=1, source_target_pairs={{0,1},{1,0},{2,3},{3,2},{4,5},{5,4},{6,7},{7,6},{8,9},{9,8},{10,11... | collective-permute-start | bytes 1179656 | tf_op jit(solution)/shard_map/ppermute | solution.py:28
  142.4 9.0 %collective-permute-start.32 = (f32[160,512]{1,0:T(8,128)S(1)}, f32[160,512]{1,0:T(8,128)S(1)}, u32[]{:S(2)}, u32[]{:S(2)}) collective-permute-start(f32[160,512]{1,0:T(8,128)S(1)} %get-tuple-element.111), channel_id=1, source_target_pairs={{0,16},{1,17},{2,18},{3,19},{4,20},{5,21},{6,22},{7,23},{8,24},{9,... | collective-permute-start | bytes 983048 | tf_op jit(solution)/shard_map/ppermute | solution.py:28
  142.6 10.4 %collective-permute-start.33 = (f32[160,512]{1,0:T(8,128)S(1)}, f32[160,512]{1,0:T(8,128)S(1)}, u32[]{:S(2)}, u32[]{:S(2)}) collective-permute-start(f32[160,512]{1,0:T(8,128)S(1)} %get-tuple-element.112), channel_id=1, source_target_pairs={{0,48},{1,49},{2,50},{3,51},{4,52},{5,53},{6,54},{7,55},{8,56},{9,... | collective-permute-start | bytes 983048 | tf_op jit(solution)/shard_map/ppermute | solution.py:28
  144.2 8.9 %collective-permute-start.34 = (f32[160,512]{1,0:T(8,128)S(1)}, f32[160,512]{1,0:T(8,128)S(1)}, u32[]{:S(2)}, u32[]{:S(2)}) collective-permute-start(f32[160,512]{1,0:T(8,128)S(1)} %get-tuple-element.113), channel_id=1, source_target_pairs={{0,64},{1,65},{2,66},{3,67},{4,68},{5,69},{6,70},{7,71},{8,72},{9,... | collective-permute-start | bytes 983048 | tf_op jit(solution)/shard_map/ppermute | solution.py:28
  144.8 8.8 %collective-permute-start.38 = (f32[48,512]{1,0:T(8,128)S(1)}, f32[48,512]{1,0:T(8,128)S(1)}, u32[]{:S(2)}, u32[]{:S(2)}) collective-permute-start(f32[48,512]{1,0:T(8,128)S(1)} %get-tuple-element.120), channel_id=1, source_target_pairs={{0,16},{1,17},{2,18},{3,19},{4,20},{5,21},{6,22},{7,23},{8,24},{9,... | collective-permute-start | bytes 294920 | tf_op jit(solution)/shard_map/ppermute | solution.py:28
  146.1 8.0 %collective-permute-start.39 = (f32[48,512]{1,0:T(8,128)S(1)}, f32[48,512]{1,0:T(8,128)S(1)}, u32[]{:S(2)}, u32[]{:S(2)}) collective-permute-start(f32[48,512]{1,0:T(8,128)S(1)} %get-tuple-element.121), channel_id=1, source_target_pairs={{0,48},{1,49},{2,50},{3,51},{4,52},{5,53},{6,54},{7,55},{8,56},{9,... | collective-permute-start | bytes 294920 | tf_op jit(solution)/shard_map/ppermute | solution.py:28
  154.8 6.8 %collective-permute-start.40 = (f32[144,512]{1,0:T(8,128)S(1)}, f32[144,512]{1,0:T(8,128)S(1)}, u32[]{:S(2)}, u32[]{:S(2)}) collective-permute-start(f32[144,512]{1,0:T(8,128)S(1)} %get-tuple-element.124), channel_id=1, source_target_pairs={{0,16},{1,17},{2,18},{3,19},{4,20},{5,21},{6,22},{7,23},{8,24},{9,... | collective-permute-start | bytes 884744 | tf_op jit(solution)/shard_map/ppermute | solution.py:28
  155.0 7.9 %collective-permute-start.41 = (f32[144,512]{1,0:T(8,128)S(1)}, f32[144,512]{1,0:T(8,128)S(1)}, u32[]{:S(2)}, u32[]{:S(2)}) collective-permute-start(f32[144,512]{1,0:T(8,128)S(1)} %get-tuple-element.125), channel_id=1, source_target_pairs={{0,48},{1,49},{2,50},{3,51},{4,52},{5,53},{6,54},{7,55},{8,56},{9,... | collective-permute-start | bytes 884744 | tf_op jit(solution)/shard_map/ppermute | solution.py:28
  163.6 5.7 %collective-permute-start.42 = (f32[96,512]{1,0:T(8,128)S(1)}, f32[96,512]{1,0:T(8,128)S(1)}, u32[]{:S(2)}, u32[]{:S(2)}) collective-permute-start(f32[96,512]{1,0:T(8,128)S(1)} %get-tuple-element.126), channel_id=1, source_target_pairs={{0,16},{1,17},{2,18},{3,19},{4,20},{5,21},{6,22},{7,23},{8,24},{9,... | collective-permute-start | bytes 589832 | tf_op jit(solution)/shard_map/ppermute | solution.py:28
  164.4 6.9 %collective-permute-start.43 = (f32[96,512]{1,0:T(8,128)S(1)}, f32[96,512]{1,0:T(8,128)S(1)}, u32[]{:S(2)}, u32[]{:S(2)}) collective-permute-start(f32[96,512]{1,0:T(8,128)S(1)} %get-tuple-element.127), channel_id=1, source_target_pairs={{0,48},{1,49},{2,50},{3,51},{4,52},{5,53},{6,54},{7,55},{8,56},{9,... | collective-permute-start | bytes 589832 | tf_op jit(solution)/shard_map/ppermute | solution.py:28
  166.1 5.7 %collective-permute-start.44 = (f32[96,512]{1,0:T(8,128)S(1)}, f32[96,512]{1,0:T(8,128)S(1)}, u32[]{:S(2)}, u32[]{:S(2)}) collective-permute-start(f32[96,512]{1,0:T(8,128)S(1)} %get-tuple-element.128), channel_id=1, source_target_pairs={{0,64},{1,65},{2,66},{3,67},{4,68},{5,69},{6,70},{7,71},{8,72},{9,... | collective-permute-start | bytes 589832 | tf_op jit(solution)/shard_map/ppermute | solution.py:28
  (11 other events, 33.3 us)
